TPU v7x, 32 devices: a whole 2x2x4 slice. The times are simulated.
32 devices in a mesh: mode: 4 (over z), ex: 4 (over y, x), ey: 2 (over core).
Axes of the slice: x: 2, y: 2, z: 4, core: 2. Of those that a mesh axis runs over, the one named last changes fastest.
Arguments:
- stream_speed: float32 [12, 12, 16, 4, 256], P(None, None, 'ex', 'ey', 'mode'), may hold values from -9 to 9, as said below
- normal_speed: float32 [12, 12, 16, 4, 256], P(None, None, 'ex', 'ey', 'mode'), may hold values from -9 to 9, as said below
Outputs:
- velocity_modes: float32 [12, 12, 16, 4, 512], P(None, None, 'ex', 'ey', 'mode')
Inputs may be any that keep to these rules, and one draw needn't show every extreme that they name: `stream_speed`: continuous across element faces (shared nodes carry equal values), periodic along the streamwise direction and zero on the walls. `normal_speed`: continuous across element faces (shared nodes carry equal values), periodic along the streamwise direction and zero on the walls.
All inputs are finite; a program needn't handle non-finite values.
Results may differ from a plain program's by a relative error of at most 0.00018.
Values sent between devices are 32-bit elements; how exact they have to be, the bound alone decides.
No kernel may reach another device: no remote copies, remote signals or barrier semaphores. Data moves between devices by JAX's collectives and lax.ppermute only.
A program may use at most 128 MiB of HBM per device.

v0:
```python
import functools
import math

import jax
import jax.numpy as jnp
import ml_dtypes
import numpy as np
from jax import lax
from jax.experimental import pallas as pl
from jax.experimental.pallas import tpu as pltpu
from jax.sharding import PartitionSpec as P

BF16 = ml_dtypes.bfloat16

element_width = 2.0
shift_base = 10.0
span_rate = 0.0125


def legendre_pair(degree, points):
    before = points * 0.0 + 1.0
    current = points.copy()
    for step in range(1, degree):
        upcoming = ((2 * step + 1) * points * current - step * before) / (step + 1)
        before = current
        current = upcoming
    return (current, before)


def legendre_slope(degree, points):
    current, before = legendre_pair(degree, points)
    return (current, degree * (points * current - before) / (points * points - 1.0))


def lobatto_points(order):
    guesses = -np.cos(np.pi * np.arange(1, order) / order)
    for step in range(60):
        current, slope = legendre_slope(order, guesses)
        second = (2.0 * guesses * slope - order * (order + 1) * current) / (1.0 - guesses * guesses)
        guesses = guesses - slope / second
    return guesses


def gauss_rule(count):
    guesses = -np.cos(np.pi * (np.arange(count) + 0.75) / (count + 0.5))
    for step in range(60):
        current, slope = legendre_slope(count, guesses)
        guesses = guesses - current / slope
    current, slope = legendre_slope(count, guesses)
    return (guesses, 2.0 / ((1.0 - guesses * guesses) * slope * slope))


def jacobi_eigen(matrix):
    size_n = matrix.shape[0]
    work = matrix.copy()
    vectors = np.eye(size_n)
    for sweep_number in range(20):
        for first in range(size_n):
            for second in range(first + 1, size_n):
                coupling = work[first, second]
                if abs(coupling) > 1e-300:
                    theta = (work[second, second] - work[first, first]) / (2.0 * coupling)
                    direction = 1.0 if theta >= 0.0 else -1.0
                    tangent = direction / (abs(theta) + np.sqrt(theta * theta + 1.0))
                    cosine = 1.0 / np.sqrt(tangent * tangent + 1.0)
                    sine = tangent * cosine
                    rotation = np.eye(size_n)
                    rotation[first, first] = cosine
                    rotation[second, second] = cosine
                    rotation[first, second] = sine
                    rotation[second, first] = -sine
                    work = rotation.T @ work @ rotation
                    vectors = vectors @ rotation
    diagonal_index = np.arange(size_n)
    return (work[diagonal_index, diagonal_index], vectors)


def extended_basis(stiffness, weights, left_width, centre_width, right_width):
    node_count = weights.shape[0]
    full_count = 3 * node_count - 2
    stiff_full = np.zeros((full_count, full_count))
    mass_full = np.zeros(full_count)
    for position, span_width in enumerate((left_width, centre_width, right_width)):
        if span_width > 0.0:
            first_node = position * (node_count - 1)
            stiff_full[
                first_node : first_node + node_count, first_node : first_node + node_count
            ] += stiffness * (2.0 / span_width)
            mass_full[first_node : first_node + node_count] += weights * (span_width / 2.0)
    low_index = node_count - 2
    high_index = low_index + node_count + 2
    stiff_ext = stiff_full[low_index:high_index, low_index:high_index].copy()
    mass_ext = mass_full[low_index:high_index].copy()
    frozen_list = []
    if left_width <= 0.0:
        frozen_list += [0, 1]
    if right_width <= 0.0:
        frozen_list += [node_count, node_count + 1]
    for frozen_index in frozen_list:
        stiff_ext[frozen_index, :] = 0.0
        stiff_ext[:, frozen_index] = 0.0
        stiff_ext[frozen_index, frozen_index] = 1.0
        mass_ext[frozen_index] = 1.0
    inverse_root = 1.0 / np.sqrt(mass_ext)
    lambdas, vectors = jacobi_eigen(inverse_root[:, None] * stiff_ext * inverse_root[None, :])
    return (inverse_root[:, None] * vectors, lambdas)


def spectral_tables(order, rows_total):
    inner_points = lobatto_points(order)
    points = np.concatenate([[-1.0], inner_points, [1.0]])
    values, unused_before = legendre_pair(order, points)
    weights = 2.0 / (order * (order + 1) * values**2)
    identity = np.eye(order + 1)
    point_gaps = points[:, None] - points[None, :] + identity
    derivative = values[:, None] / (values[None, :] * point_gaps) * (1.0 - identity)
    derivative[0, 0] = -order * (order + 1) / 4.0
    derivative[order, order] = order * (order + 1) / 4.0
    stiffness = derivative.T @ (weights[:, None] * derivative)
    gauss_points, gauss_weights = gauss_rule(3 * (order + 1) // 2)
    offsets = gauss_points[:, None, None] - points[None, None, :]
    numerators = np.prod(np.where(identity[None, :, :] > 0.5, 1.0, offsets), axis=2)
    denominators = np.prod(np.where(identity > 0.5, 1.0, points[:, None] - points[None, :]), axis=1)
    interp = numerators / denominators[None, :]
    heights = 0.6 + 1.4 * np.sin(np.pi * (np.arange(rows_total) + 0.5) / rows_total)
    basis_x, lambdas_x = extended_basis(
        stiffness, weights, element_width, element_width, element_width
    )
    basis_rows = []
    lambda_rows = []
    for row_number in range(rows_total):
        below = heights[row_number - 1] if row_number > 0 else 0.0
        above = heights[row_number + 1] if row_number < rows_total - 1 else 0.0
        basis_one, lambda_one = extended_basis(
            stiffness, weights, below, heights[row_number], above
        )
        basis_rows.append(basis_one)
        lambda_rows.append(lambda_one)
    return (
        derivative,
        interp,
        gauss_weights,
        weights,
        stiffness,
        basis_x,
        lambdas_x,
        np.stack(basis_rows),
        np.stack(lambda_rows),
        heights,
    )


PARTS = 8
LANES = 128


def ceil_to(count, step):
    return -(-count // step) * step


class Sizes:
    def __init__(self, mesh_shape, block_shape):
        self.n_mode, self.n_ex, self.n_ey = (mesh_shape[name] for name in ("mode", "ex", "ey"))
        self.nodes, _, self.elems, self.rows, self.planes = block_shape
        self.order = self.nodes - 1
        self.gauss = 3 * self.nodes // 2
        self.rows_total = self.rows * self.n_ey
        self.elems_total = self.elems * self.n_ex
        self.planes_total = self.planes * self.n_mode
        self.block_x = self.order * self.elems + 1
        full_y = self.order * self.rows + 1
        self.inner = [
            [j for j in range(full_y) if not (p == 0 and j == 0) and not (p == self.n_ey - 1 and j == full_y - 1)]
            for p in range(self.n_ey)
        ]
        self.block_y = max(len(found) for found in self.inner)
        share = -(-(self.block_x * self.block_y + 2) // self.n_mode)
        self.share = ceil_to(share, LANES if share > 64 else 32)
        self.lane_nodes = self.share * self.n_mode
        self.columns = 2 * self.planes
        self.spots = self.n_ex * self.n_ey
        self.own = self.columns // self.spots
        self.folds = self.own // PARTS
        self.fold_width = LANES // self.folds
        self.points = self.nodes + 2
        self.x_nodes = self.n_ex * self.block_x
        self.x_pad = ceil_to(self.x_nodes, 16)
        self.x_eig = self.elems_total * self.points
        self.y_eig = self.rows_total * self.points
        self.fine = ceil_to(self.gauss * self.gauss, 16)
        assert self.own == PARTS * self.folds and self.x_eig % 16 == 0
        assert max(self.y_eig, self.n_ey * self.block_y) <= self.fold_width
        assert 2 * self.planes == LANES


def high_low(table):
    high = np.asarray(table, np.float32).astype(BF16)
    low = (np.asarray(table, np.float64) - high.astype(np.float64)).astype(BF16)
    return high, low


def beside(table):
    high, low = high_low(table)
    return np.concatenate([high, high, low], 1)


def host_tables(sz):
    derivative, interp, gauss_weights, weights, stiffness, basis_x, lam_x, basis_y, lam_y, heights = spectral_tables(
        sz.order, sz.rows_total
    )
    nodes, fine, points = sz.nodes, sz.fine, sz.points
    gauss_count = sz.gauss**2
    lift = np.zeros((3 * fine, nodes * nodes))
    lift[:gauss_count] = np.kron(interp, interp)
    lift[fine : fine + gauss_count] = np.kron(interp @ derivative, interp)
    lift[2 * fine : 2 * fine + gauss_count] = np.kron(interp, interp @ derivative)
    back = np.zeros((sz.n_ey, nodes * sz.block_y, sz.rows * fine))
    weighted = interp.T * gauss_weights[None, :]
    for place in range(sz.n_ey):
        for f in range(sz.rows):
            for jj, j in enumerate(sz.inner[place]):
                b = j - sz.order * f
                if 0 <= b < nodes:
                    back[place, jj :: sz.block_y, f * fine : f * fine + gauss_count] = -np.kron(
                        weighted, weighted[b : b + 1]
                    )
    grid_x, grid_y = sz.order * sz.elems_total, sz.order * sz.rows_total + 1
    to_x, stiff_x, mass_x = np.zeros((sz.x_eig, grid_x)), np.zeros((grid_x, grid_x)), np.zeros(grid_x)
    for e in range(sz.elems_total):
        for t in range(points):
            to_x[e * points : (e + 1) * points, (sz.order * e + t - 1) % grid_x] += basis_x[t]
        index = (sz.order * e + np.arange(nodes)) % grid_x
        stiff_x[np.ix_(index, index)] += stiffness * (2.0 / element_width)
        mass_x[index] += weights * (element_width / 2.0)
    to_y, stiff_y, mass_y = np.zeros((sz.y_eig, grid_y)), np.zeros((grid_y, grid_y)), np.zeros(grid_y)
    for f in range(sz.rows_total):
        for t in range(points):
            y = sz.order * f + t - 1
            if 0 < y < grid_y - 1:
                to_y[f * points : (f + 1) * points, y] = basis_y[f][t]
        index = sz.order * f + np.arange(nodes)
        stiff_y[np.ix_(index, index)] += stiffness * (2.0 / heights[f])
        mass_y[index] += weights * (heights[f] / 2.0)
    stiff_xx, mass_xx = to_x @ stiff_x @ to_x.T, (to_x * mass_x) @ to_x.T
    stiff_yy, mass_yy = to_y @ stiff_y @ to_y.T, (to_y * mass_y) @ to_y.T
    list_x = [(sz.order * sz.elems * p + i) % grid_x for p in range(sz.n_ex) for i in range(sz.block_x)]
    block_x = np.zeros((sz.x_eig, sz.x_pad))
    block_x[:, : sz.x_nodes] = to_x[:, list_x]
    width, folds = sz.fold_width, sz.folds
    block_y = np.zeros((width, width))
    for place in range(sz.n_ey):
        for jj, j in enumerate(sz.inner[place]):
            block_y[place * sz.block_y + jj, : sz.y_eig] = to_y[:, sz.order * sz.rows * place + j]

    def folded(table):
        padded = np.zeros((width, width))
        padded[: table.shape[0], : table.shape[1]] = table
        return np.kron(np.eye(folds), padded)

    def one_dot(table):
        high, low = high_low(folded(table))
        return np.block([[high, low], [high, np.zeros_like(low)]]).astype(BF16)

    mass_pair, stiff_pair = high_low(folded(mass_yy)), high_low(folded(stiff_yy))
    heads = np.concatenate([mass_pair[0], stiff_pair[0]], 1)
    tails = np.concatenate([mass_pair[1], stiff_pair[1]], 1)
    lam_lanes = np.ones((1, folds, width))
    lam_lanes[:, :, : sz.y_eig] = lam_y.reshape(-1)
    planes_total = sz.planes_total
    turns = np.arange(planes_total)[None, :] * np.arange(planes_total // 2)[:, None] % planes_total
    angles = turns * (2.0 * math.pi / planes_total)
    waves = np.stack([np.cos(angles), -np.sin(angles)], 1).reshape(planes_total, planes_total) / planes_total
    return dict(
        heights=np.asarray(heights, np.float32),
        lift=beside(lift),
        back=np.stack([beside(table) for table in back]),
        waves=np.stack(high_low(waves)),
        in_y=one_dot(block_y),
        in_x=beside(block_x),
        pair_y=np.concatenate([heads, heads, tails], 0),
        pair_x=beside(np.concatenate([stiff_xx, mass_xx], 1)),
        out_y=one_dot(block_y.T),
        out_x=beside(block_x.T),
        lam_x=np.asarray(np.tile(lam_x, sz.elems_total)[:, None] * np.ones((1, LANES)), np.float32),
        lam_y=np.asarray(lam_lanes.reshape(1, LANES), np.float32),
    )


def split(value):
    high = value.astype(jnp.bfloat16)
    low = (value - high.astype(jnp.float32)).astype(jnp.bfloat16)
    return high, low


def dot(left, right):
    return lax.dot_general(left, right, (((1,), (0,)), ((), ())), preferred_element_type=jnp.float32)


def below(value):
    high, low = split(value)
    return jnp.concatenate([high, low, high], 0)


def along(value):
    return jnp.concatenate(split(value), 1)


def lane_index(shape):
    return lax.broadcasted_iota(jnp.int32, shape, len(shape) - 1)


def advect_kernel(sz, heights_ref, stream_ref, normal_ref, lift_ref, back_ref, out_ref, total_ref):
    place = lax.axis_index("ey")
    count, fine, rows = sz.nodes * sz.nodes, sz.fine, sz.rows
    spots = sz.elems * rows
    half = lane_index((fine, LANES)) < sz.planes
    column, step = sz.nodes * sz.block_y, sz.order * sz.block_y
    length = sz.block_x * sz.block_y
    total_ref[pl.ds(length // 8 * 8, sz.lane_nodes - length // 8 * 8), :] = jnp.zeros(
        (sz.lane_nodes - length // 8 * 8, LANES), jnp.float32
    )
    carry = None
    for e in range(sz.elems):
        speeds = jnp.concatenate(
            [
                ref[pl.ds(e * rows + f, count, stride=spots), :]
                for f in range(rows)
                for ref in (stream_ref, normal_ref)
            ],
            1,
        )
        values = dot(lift_ref[...], below(speeds))
        highs, lows = [], []
        for f in range(rows):
            height = heights_ref[place * rows + f]
            mine = values[:, f * LANES : (f + 1) * LANES]
            both, slope_x, slope_y = mine[:fine], mine[fine : 2 * fine], mine[2 * fine :]
            turned = pltpu.roll(both, sz.planes, 1)
            stream = jnp.where(half, both, turned)
            normal = jnp.where(half, turned, both)
            high, low = split((stream * (height * 0.5)) * slope_x + (normal * (element_width * 0.5)) * slope_y)
            highs.append(high)
            lows.append(low)
        weak = dot(back_ref[place], jnp.concatenate(highs + lows + highs, 0))
        if carry is not None:
            head = jnp.concatenate([carry, jnp.zeros((column - carry.shape[0], LANES), jnp.float32)], 0)
            weak = weak + head
        if e < sz.elems - 1:
            total_ref[pl.ds(e * step, step), :] = weak[:step]
            carry = weak[step:]
        else:
            total_ref[pl.ds(e * step, column), :] = weak
    for z in range(sz.n_mode):
        out_ref[z] = total_ref[pl.ds(z * sz.share, sz.share), :]


def transform_kernel(sz, weak_ref, waves_ref, out_ref, mixed_ref):
    turned = [weak_ref[z].T for z in range(sz.n_mode)]
    modes = sz.planes_total
    for k in range(2):
        signal = jnp.concatenate([piece[k * sz.planes : (k + 1) * sz.planes] for piece in turned], 0)
        high, low = split(signal)
        part = dot(waves_ref[0], high) + dot(waves_ref[0], low) + dot(waves_ref[1], high)
        for t in range(mixed_ref.shape[0]):
            tile = part[:, t * LANES : (t + 1) * LANES]
            mixed_ref[t, pl.ds(k, modes, stride=2), pl.ds(0, tile.shape[1])] = tile
    for t in range(mixed_ref.shape[0]):
        last = min(LANES, sz.share - t * LANES)
        out_ref[:, pl.ds(t * LANES, last)] = mixed_ref[t, :, pl.ds(0, last)]


def smooth_kernel(
    sz,
    terms_ref,
    in_y_ref,
    in_x_ref,
    pair_y_ref,
    pair_x_ref,
    out_y_ref,
    out_x_ref,
    lam_x_ref,
    lam_y_ref,
    out_ref,
    field_ref,
    first_ref,
    work_ref,
):
    width, folds, strip = sz.fold_width, sz.folds, sz.block_y
    tiles = -(-sz.lane_nodes // LANES)
    lanes = lane_index((PARTS, LANES))
    x_pad, x_eig = sz.x_pad, sz.x_eig
    device = (lax.axis_index("mode") * sz.n_ex + lax.axis_index("ex")) * sz.n_ey + lax.axis_index("ey")
    first_mode = device * (sz.own // 4)

    for c in range(PARTS):
        field_ref[pl.ds(c * x_pad + sz.x_nodes, x_pad - sz.x_nodes), :] = jnp.zeros(
            (x_pad - sz.x_nodes, LANES), jnp.float32
        )
    for p in range(sz.n_ex):
        held = {}
        for q in range(sz.n_ey):
            for fold in range(folds):
                whole = jnp.concatenate(
                    [
                        terms_ref[(z * sz.n_ex + p) * sz.n_ey + q, pl.ds(fold * PARTS, PARTS), :]
                        for z in range(sz.n_mode)
                    ],
                    1,
                )
                held[q, fold] = [whole[:, t * LANES : (t + 1) * LANES] for t in range(tiles)]
        for i in range(sz.block_x):
            start = i * strip
            t, r = start // LANES, start % LANES
            result = jnp.zeros((PARTS, LANES), jnp.float32)
            for fold in range(folds):
                for q in range(sz.n_ey):
                    source = held[q, fold][t]
                    if r + strip > LANES:
                        source = jnp.where(lanes >= r, source, held[q, fold][t + 1])
                    goal = fold * width + q * strip
                    moved = pltpu.roll(source, (goal - r) % LANES, 1) if goal != r else source
                    result = jnp.where((lanes >= goal) & (lanes < goal + strip), moved, result)
            field_ref[pl.ds(p * sz.block_x + i, PARTS, stride=x_pad), :] = result

    parts = dot(along(field_ref[...]), in_y_ref[...])
    field_ref[...] = parts[:, :LANES] + parts[:, LANES:]
    fold_of_lane = lane_index((1, LANES)) // width
    shifts, inverses = [], []
    for group in range(PARTS // 4):
        mode = (first_mode + fold_of_lane * (PARTS // 4) + group).astype(jnp.float32)
        shift = shift_base + (span_rate * mode) ** 2
        shifts.append(shift)
        inverses.append(1.0 / (lam_x_ref[...] + (lam_y_ref[...] + shift)))
    for c in range(0, PARTS, 2):
        pair = jnp.concatenate([field_ref[pl.ds((c + d) * x_pad, x_pad), :] for d in range(2)], 1)
        forced = dot(in_x_ref[...], below(pair))
        for d in range(2):
            mine = forced[:, d * LANES : (d + 1) * LANES]
            first_ref[pl.ds((c + d) * x_eig, x_eig), :] = mine
            work_ref[pl.ds((c + d) * x_eig, x_eig), :] = mine * inverses[(c + d) // 4]
    for c in range(0, PARTS, 2):
        shift = shifts[c // 4]
        masses, stiffs = [], []
        for d in range(2):
            high, low = split(work_ref[pl.ds((c + d) * x_eig, x_eig), :])
            both = dot(jnp.concatenate([high, low, high], 1), pair_y_ref[...])
            masses.append(both[:, :LANES])
            stiffs.append(both[:, LANES:] + shift * both[:, :LANES])
        stacked = jnp.concatenate([jnp.concatenate(masses, 1), jnp.concatenate(stiffs, 1)], 0)
        applied = dot(pair_x_ref[...], below(stacked))
        for d in range(2):
            rows = pl.ds((c + d) * x_eig, x_eig)
            total = (2.0 * first_ref[rows, :] - applied[:, d * LANES : (d + 1) * LANES]) * inverses[c // 4]
            parts = dot(along(total), out_y_ref[...])
            work_ref[rows, :] = parts[:, :LANES] + parts[:, LANES:]
        pair = jnp.concatenate([work_ref[pl.ds((c + d) * x_eig, x_eig), :] for d in range(2)], 1)
        solved = dot(out_x_ref[...], below(pair))
        for d in range(2):
            field_ref[pl.ds((c + d) * x_pad, x_pad), :] = solved[:, d * LANES : (d + 1) * LANES]

    for p in range(sz.n_ex):
        made = {}
        for i in range(sz.block_x):
            source = field_ref[pl.ds(p * sz.block_x + i, PARTS, stride=x_pad), :]
            for q in range(sz.n_ey):
                begin = i * strip + sz.inner[q][0]
                count = len(sz.inner[q])
                t, r = begin // LANES, begin % LANES
                for fold in range(folds):
                    origin = fold * width + q * strip
                    moved = pltpu.roll(source, (r - origin) % LANES, 1) if origin != r else source
                    for tile, low, high in ((t, r, r + count), (t + 1, 0, r + count - LANES)):
                        if high > 0:
                            old = made.get((q, fold, tile))
                            if old is None:
                                old = jnp.zeros((PARTS, LANES), jnp.float32)
                            made[q, fold, tile] = jnp.where((lanes >= low) & (lanes < high), moved, old)
        for (q, fold, tile), value in made.items():
            last = min(LANES, sz.lane_nodes - tile * LANES)
            out_ref[p * sz.n_ey + q, pl.ds(fold * PARTS, PARTS), pl.ds(tile * LANES, last)] = value[:, :last]


def spread_kernel(sz, solved_ref, out_ref, turned_ref):
    place = lax.axis_index("ey")
    turned_ref[...] = solved_ref[...].T
    spots = sz.elems * sz.rows
    for e in range(sz.elems):
        for f in range(sz.rows):
            for a in range(sz.nodes):
                start = sz.block_y * (sz.order * e + a) + sz.order * f
                out_ref[pl.ds(a * sz.nodes * spots + e * sz.rows + f, sz.nodes, stride=spots), :] = turned_ref[
                    pl.ds(start, sz.nodes), :
                ]
    blank = jnp.zeros((sz.elems, LANES), jnp.float32)

    @pl.when(place == 0)
    def _():
        for a in range(sz.nodes):
            out_ref[pl.ds(a * sz.nodes * spots, sz.elems, stride=sz.rows), :] = blank

    @pl.when(place == sz.n_ey - 1)
    def _():
        for a in range(sz.nodes):
            first = ((a + 1) * sz.nodes - 1) * spots + sz.rows - 1
            out_ref[pl.ds(first, sz.elems, stride=sz.rows), :] = blank


def call(kernel, out_shape, operands, scratch=(), scalars=0):
    vmem = pl.BlockSpec(memory_space=pltpu.VMEM)
    smem = pl.BlockSpec(memory_space=pltpu.SMEM)
    return pl.pallas_call(
        kernel,
        out_shape=jax.ShapeDtypeStruct(out_shape, jnp.float32),
        in_specs=[smem] * scalars + [vmem] * (len(operands) - scalars),
        out_specs=vmem,
        scratch_shapes=[pltpu.VMEM(shape, jnp.float32) for shape in scratch],
        compiler_params=pltpu.CompilerParams(vmem_limit_bytes=56 * 2**20),
    )(*operands)


def on_device(sz, tables, stream_speed, normal_speed):
    flat = sz.nodes * sz.nodes * sz.elems * sz.rows
    table = {name: jnp.asarray(value) for name, value in tables.items()}
    weak = call(
        functools.partial(advect_kernel, sz),
        (sz.n_mode, sz.share, LANES),
        [
            table["heights"],
            stream_speed.reshape(flat, sz.planes),
            normal_speed.reshape(flat, sz.planes),
            table["lift"],
            table["back"],
        ],
        [(sz.lane_nodes, LANES)],
        scalars=1,
    )
    weak = lax.all_to_all(weak, "mode", split_axis=0, concat_axis=0, tiled=True)
    spectra = call(
        functools.partial(transform_kernel, sz),
        (2 * sz.planes_total, sz.share),
        [weak, table["waves"]],
        [(-(-sz.share // LANES), 2 * sz.planes_total, LANES)],
    )
    everyone = ("mode", "ex", "ey")
    spectra = spectra.reshape(sz.n_mode * sz.spots, sz.own, sz.share)
    terms = lax.all_to_all(spectra, everyone, split_axis=0, concat_axis=0, tiled=True)
    names = ("in_y", "in_x", "pair_y", "pair_x", "out_y", "out_x", "lam_x", "lam_y")
    solved = call(
        functools.partial(smooth_kernel, sz),
        (sz.spots, sz.own, sz.lane_nodes),
        [terms] + [table[name] for name in names],
        [(PARTS * sz.x_pad, LANES), (PARTS * sz.x_eig, LANES), (PARTS * sz.x_eig, LANES)],
    )
    solved = lax.all_to_all(solved, ("ex", "ey"), split_axis=0, concat_axis=0, tiled=True)
    out = call(
        functools.partial(spread_kernel, sz),
        (flat, LANES),
        [solved.reshape(sz.columns, sz.lane_nodes)],
        [(sz.lane_nodes, LANES)],
    )
    return out.reshape(sz.nodes, sz.nodes, sz.elems, sz.rows, sz.columns)


def solution(mesh):
    spec = P(None, None, "ex", "ey", "mode")

    def whole(stream_speed, normal_speed):
        shape = stream_speed.shape
        counts = mesh.shape
        block = shape[:2] + (shape[2] // counts["ex"], shape[3] // counts["ey"], shape[4] // counts["mode"])
        sz = Sizes(counts, block)
        return jax.shard_map(
            functools.partial(on_device, sz, host_tables(sz)),
            mesh=mesh,
            in_specs=(spec, spec),
            out_specs=spec,
            check_vma=False,
        )(stream_speed, normal_speed)

    return whole
```

profile of v0, /device:TPU:0, one launch (start us, length us, event | category | flops | bytes accessed | tf_op | source)
XLA Modules:
  0.0 74.6 jit_solution(4286869747190752003)
XLA Ops:
  0.0 6.5 %shard_map.136 = f32[4,256,128]{2,1,0:T(8,128)} custom-call(f32[4]{0:T(128)} %constant.24.clone.heights_ref, f32[1152,64]{1,0:T(8,128)} %bitcast.7, f32[1152,64]{1,0:T(8,128)} %bitcast.8, bf16[1008,432]{1,0:T(8,128)(2,1)} %constant.25.clone.lift_ref, bf16[2,264,2016]{2,1,0:T(8,128)(2,1)} %constant.26.clone.back_ref), custom_call_target="tpu_custom_call" | custom-call | tf_op jit(solution)/shard_map/pallas_call | solution.py:511
  6.5 20.9 %all_to_all.15.weak_ref = f32[4,256,128]{2,1,0:T(8,128)} all-to-all(f32[4,256,128]{2,1,0:T(8,128)} %shard_map.136), channel_id=1, replica_groups=mesh['mode'=4,'ex'=4,'ey'=2] {'mode'}, dimensions={0} | all-to-all | bytes 1048576 | tf_op jit(solution)/shard_map/all_to_all | solution.py:537
  27.4 2.5 %shard_map.137 = f32[512,256]{1,0:T(8,128)} custom-call(f32[4,256,128]{2,1,0:T(8,128)} %all_to_all.15.weak_ref, bf16[2,256,256]{2,1,0:T(8,128)(2,1)} %constant.27.clone.waves_ref), custom_call_target="tpu_custom_call" | custom-call | tf_op jit(solution)/shard_map/pallas_call | solution.py:511
  29.9 19.4 %all_to_all.16.terms_ref = f32[32,16,256]{2,1,0:T(8,128)} all-to-all(f32[32,16,256]{2,1,0:T(8,128)} %bitcast.5), channel_id=1, replica_groups=mesh['mode'=4,'ex'=4,'ey'=2] {'mode','ex','ey'}, dimensions={0} | all-to-all | bytes 1048576 | tf_op jit(solution)/shard_map/all_to_all | solution.py:546
  49.3 9.3 %shard_map.138 = f32[8,16,1024]{2,1,0:T(8,128)} custom-call(f32[32,16,256]{2,1,0:T(8,128)} %all_to_all.16.terms_ref, bf16[256,256]{1,0:T(8,128)(2,1)} %constant.28.clone.in_y_ref, bf16[224,576]{1,0:T(8,128)(2,1)} %constant.29.clone.in_x_ref, bf16[384,256]{1,0:T(8,128)(2,1)} %constant.30.clone.pair_y_ref, bf16[224,1344]{1,0:T(8,128)(2,1)} %constant.31.clone.pair_x_ref, ...), custom_call_target="tpu_custom_call" | custom-call | tf_op jit(solution)/shard_map/pallas_call | solution.py:511
  58.6 13.9 %all_to_all.17 = f32[8,16,1024]{2,1,0:T(8,128)} all-to-all(f32[8,16,1024]{2,1,0:T(8,128)} %shard_map.138), channel_id=1, replica_groups=mesh['mode'=4,'ex'=4,'ey'=2] {'ex','ey'}, dimensions={0} | all-to-all | bytes 1048576 | tf_op jit(solution)/shard_map/all_to_all | solution.py:554
  72.5 2.1 %shard_map.139 = f32[1152,128]{1,0:T(8,128)} custom-call(f32[128,1024]{1,0:T(8,128)} %bitcast.6), custom_call_target="tpu_custom_call" | custom-call | tf_op jit(solution)/shard_map/pallas_call | solution.py:511
where the time goes:
time: 75 us; the launch traced here: 74.6 us
  blocking collectives  54.1 us (72%)
  Pallas kernels  20.4 us (27%)
    all_to_all x1, blocking collectives, on_device(): weak = lax.all_to_all(weak, 'mode', split_axis=0, concat_axis=0, tiled=True)  20.9 us
    pallas_call x4, Pallas kernels, call(): pl.pallas_call(kernel, out_shape=jax.ShapeDtypeStruct(out_shape, jnp.floa...  20.4 us
    all_to_all x1, blocking collectives, on_device(): lax.all_to_all(spectra, everyone, split_axis=0, concat_axis=0, tiled=True)  19.4 us
    all_to_all x1, blocking collectives, on_device(): lax.all_to_all(solved, ('ex', 'ey'), split_axis=0, concat_axis=0, tiled=T...  13.9 us

commit v1 on v0

--- a/solution.py
+++ b/solution.py
@@ -514,7 +514,7 @@
         in_specs=[smem] * scalars + [vmem] * (len(operands) - scalars),
         out_specs=vmem,
         scratch_shapes=[pltpu.VMEM(shape, jnp.float32) for shape in scratch],
-        compiler_params=pltpu.CompilerParams(vmem_limit_bytes=56 * 2**20),
+        compiler_params=pltpu.CompilerParams(vmem_limit_bytes=16 * 2**20),
     )(*operands)
 
 

time: 75 us -> 71.2 us (0.949)
  Pallas kernels: 20.4 us -> 12.5 us
  local copies, waits for them, and re-layouts: 0 us -> 5.67 us
  blocking collectives: 54.1 us -> 52.5 us
    pallas_call x4, Pallas kernels: 20.4 us -> 12.5 us  [call(): pl.pallas_call(kernel, out_shape=jax.ShapeDtypeStruct(out_shape, jnp.floa...]
    unnamed x0 -> x28, local copies, waits for them, and re-layouts: none -> 5.67 us
    all_to_all x1, blocking collectives: 13.9 us -> 12.7 us  [on_device(): lax.all_to_all(solved, ('ex', 'ey'), split_axis=0, concat_axis=0, tiled=T...]
where the time goes in v1:
time: 71.2 us; the launch traced here: 70.8 us
  blocking collectives  52.5 us (74%)
  Pallas kernels  12.5 us (18%)
  local copies, waits for them, and re-layouts  5.67 us (8%)
    all_to_all x1, blocking collectives, on_device(): weak = lax.all_to_all(weak, 'mode', split_axis=0, concat_axis=0, tiled=True)  20.7 us
    all_to_all x1, blocking collectives, on_device(): lax.all_to_all(spectra, everyone, split_axis=0, concat_axis=0, tiled=True)  19.1 us
    all_to_all x1, blocking collectives, on_device(): lax.all_to_all(solved, ('ex', 'ey'), split_axis=0, concat_axis=0, tiled=T...  12.7 us
    pallas_call x4, Pallas kernels, call(): pl.pallas_call(kernel, out_shape=jax.ShapeDtypeStruct(out_shape, jnp.floa...  12.5 us
    unnamed x28, local copies, waits for them, and re-layouts  5.67 us

profile of v1, /device:TPU:0, one launch (start us, length us, event | category | flops | bytes accessed | tf_op | source)
XLA Modules:
  0.0 70.8 jit_solution(8848368163024615068)
XLA Ops:
  0.0 1.6 %copy-done = bf16[2,264,2016]{2,1,0:T(8,128)(2,1)S(1)} copy-done((bf16[2,264,2016]{2,1,0:T(8,128)(2,1)S(1)}, bf16[2,264,2016]{2,1,0:T(8,128)(2,1)}, u32[]{:S(2)}) %copy-start) | copy-done | bytes 2128920
  1.6 1.2 %copy-done.1 = bf16[1008,432]{1,0:T(8,128)(2,1)S(1)} copy-done((bf16[1008,432]{1,0:T(8,128)(2,1)S(1)}, bf16[1008,432]{1,0:T(8,128)(2,1)}, u32[]{:S(2)}) %copy-start.1) | copy-done | bytes 870936
  2.8 1.1 %copy-done.3 = f32[12,12,4,2,64]{4,3,2,1,0:T(2,128)S(1)} copy-done((f32[12,12,4,2,64]{4,3,2,1,0:T(2,128)S(1)}, f32[12,12,4,2,64]{4,3,2,1,0:T(2,128)}, u32[]{:S(2)}) %copy-start.3) | copy-done | bytes 294936
  3.9 1.1 %copy-done.4 = f32[12,12,4,2,64]{4,3,2,1,0:T(2,128)S(1)} copy-done((f32[12,12,4,2,64]{4,3,2,1,0:T(2,128)S(1)}, f32[12,12,4,2,64]{4,3,2,1,0:T(2,128)}, u32[]{:S(2)}) %copy-start.4) | copy-done | bytes 294936
  5.0 0.7 copy-done.13
  5.6 4.0 %shard_map.136 = f32[4,256,128]{2,1,0:T(8,128)S(1)} custom-call(f32[4]{0:T(128)S(1)} %copy-done.13, f32[1152,64]{1,0:T(8,128)S(1)} %bitcast.7, f32[1152,64]{1,0:T(8,128)S(1)} %bitcast.8, bf16[1008,432]{1,0:T(8,128)(2,1)S(1)} %copy-done.1, bf16[2,264,2016]{2,1,0:T(8,128)(2,1)S(1)} %copy-done), custom_call_target="tpu_custom_call" | custom-call | tf_op jit(solution)/shard_map/pallas_call | solution.py:511
  9.6 0.0 copy-start.2
  9.6 0.0 copy-start.5
  9.7 0.0 copy-start.6
  9.7 0.0 copy-start.8
  9.7 0.0 copy-start.9
  9.7 0.0 copy-start.10
  9.7 0.0 copy-start.11
  9.7 0.0 copy-start.12
  9.7 20.7 %all_to_all.15.weak_ref = f32[4,256,128]{2,1,0:T(8,128)S(1)} all-to-all(f32[4,256,128]{2,1,0:T(8,128)S(1)} %shard_map.136), channel_id=1, replica_groups=mesh['mode'=4,'ex'=4,'ey'=2] {'mode'}, dimensions={0} | all-to-all | bytes 1048576 | tf_op jit(solution)/shard_map/all_to_all | solution.py:537
  30.5 0.0 copy-done.7
  30.5 0.6 shard_map.137
  31.1 19.1 %all_to_all.16.terms_ref = f32[32,16,256]{2,1,0:T(8,128)S(1)} all-to-all(f32[32,16,256]{2,1,0:T(8,128)S(1)} %bitcast.5), channel_id=1, replica_groups=mesh['mode'=4,'ex'=4,'ey'=2] {'mode','ex','ey'}, dimensions={0} | all-to-all | bytes 1048576 | tf_op jit(solution)/shard_map/all_to_all | solution.py:546
  50.1 0.0 copy-done.2
  50.1 0.0 copy-done.5
  50.1 0.0 copy-done.6
  50.2 6.9 %shard_map.138 = f32[8,16,1024]{2,1,0:T(8,128)S(1)} custom-call(f32[32,16,256]{2,1,0:T(8,128)S(1)} %all_to_all.16.terms_ref, bf16[256,256]{1,0:T(8,128)(2,1)S(1)} %copy-done.10, bf16[224,576]{1,0:T(8,128)(2,1)S(1)} %copy-done.6, bf16[384,256]{1,0:T(8,128)(2,1)S(1)} %copy-done.8, bf16[224,1344]{1,0:T(8,128)(2,1)S(1)} %copy-done.2, ...), custom_call_target="tpu_custom_call" | custom-call | tf_op jit(solution)/shard_map/pallas_call | solution.py:511
  57.1 12.7 %all_to_all.17 = f32[8,16,1024]{2,1,0:T(8,128)S(1)} all-to-all(f32[8,16,1024]{2,1,0:T(8,128)S(1)} %shard_map.138), channel_id=1, replica_groups=mesh['mode'=4,'ex'=4,'ey'=2] {'ex','ey'}, dimensions={0} | all-to-all | bytes 1048576 | tf_op jit(solution)/shard_map/all_to_all | solution.py:554
  69.7 1.1 %shard_map.139 = f32[1152,128]{1,0:T(8,128)} custom-call(f32[128,1024]{1,0:T(8,128)S(1)} %bitcast.6), custom_call_target="tpu_custom_call" | custom-call | tf_op jit(solution)/shard_map/pallas_call | solution.py:511
  (11 shorter events, 0.0 us)
Async XLA Ops:
  0.0 1.6 %copy-start = (bf16[2,264,2016]{2,1,0:T(8,128)(2,1)S(1)}, bf16[2,264,2016]{2,1,0:T(8,128)(2,1)}, u32[]{:S(2)}) copy-start(bf16[2,264,2016]{2,1,0:T(8,128)(2,1)} %constant.26.clone.back_ref) | copy-start | bytes 6386692
  1.6 1.2 %copy-start.1 = (bf16[1008,432]{1,0:T(8,128)(2,1)S(1)}, bf16[1008,432]{1,0:T(8,128)(2,1)}, u32[]{:S(2)}) copy-start(bf16[1008,432]{1,0:T(8,128)(2,1)} %constant.25.clone.lift_ref) | copy-start | bytes 2612740
  2.8 1.1 %copy-start.3 = (f32[12,12,4,2,64]{4,3,2,1,0:T(2,128)S(1)}, f32[12,12,4,2,64]{4,3,2,1,0:T(2,128)}, u32[]{:S(2)}) copy-start(f32[12,12,4,2,64]{4,3,2,1,0:T(2,128)} %param.14) | copy-start | bytes 884740
  3.9 1.1 %copy-start.4 = (f32[12,12,4,2,64]{4,3,2,1,0:T(2,128)S(1)}, f32[12,12,4,2,64]{4,3,2,1,0:T(2,128)}, u32[]{:S(2)}) copy-start(f32[12,12,4,2,64]{4,3,2,1,0:T(2,128)} %param.15) | copy-start | bytes 884740
  5.0 0.7 copy-start.13
  5.6 24.9 %copy-start.7 = (bf16[2,256,256]{2,1,0:T(8,128)(2,1)S(1)}, bf16[2,256,256]{2,1,0:T(8,128)(2,1)}, u32[]{:S(2)}) copy-start(bf16[2,256,256]{2,1,0:T(8,128)(2,1)} %constant.27.clone.waves_ref) | copy-start | bytes 786436
  9.6 40.5 %copy-start.2 = (bf16[224,1344]{1,0:T(8,128)(2,1)S(1)}, bf16[224,1344]{1,0:T(8,128)(2,1)}, u32[]{:S(2)}) copy-start(bf16[224,1344]{1,0:T(8,128)(2,1)} %constant.31.clone.pair_x_ref) | copy-start | bytes 1806340
  9.6 40.5 %copy-start.5 = (bf16[192,672]{1,0:T(8,128)(2,1)S(1)}, bf16[192,672]{1,0:T(8,128)(2,1)}, u32[]{:S(2)}) copy-start(bf16[192,672]{1,0:T(8,128)(2,1)} %constant.33.clone.out_x_ref) | copy-start | bytes 774148
  9.7 40.5 %copy-start.6 = (bf16[224,576]{1,0:T(8,128)(2,1)S(1)}, bf16[224,576]{1,0:T(8,128)(2,1)}, u32[]{:S(2)}) copy-start(bf16[224,576]{1,0:T(8,128)(2,1)} %constant.29.clone.in_x_ref) | copy-start | bytes 774148
  9.7 40.5 %copy-start.8 = (bf16[384,256]{1,0:T(8,128)(2,1)S(1)}, bf16[384,256]{1,0:T(8,128)(2,1)}, u32[]{:S(2)}) copy-start(bf16[384,256]{1,0:T(8,128)(2,1)} %constant.30.clone.pair_y_ref) | copy-start | bytes 589828
  9.7 40.5 %copy-start.9 = (bf16[256,256]{1,0:T(8,128)(2,1)S(1)}, bf16[256,256]{1,0:T(8,128)(2,1)}, u32[]{:S(2)}) copy-start(bf16[256,256]{1,0:T(8,128)(2,1)} %constant.32.clone.out_y_ref) | copy-start | bytes 393220
  9.7 40.5 %copy-start.10 = (bf16[256,256]{1,0:T(8,128)(2,1)S(1)}, bf16[256,256]{1,0:T(8,128)(2,1)}, u32[]{:S(2)}) copy-start(bf16[256,256]{1,0:T(8,128)(2,1)} %constant.28.clone.in_y_ref) | copy-start | bytes 393220
  9.7 40.5 %copy-start.11 = (f32[224,128]{1,0:T(8,128)S(1)}, f32[224,128]{1,0:T(8,128)}, u32[]{:S(2)}) copy-start(f32[224,128]{1,0:T(8,128)} %constant.34.clone.lam_x_ref) | copy-start | bytes 344068
  9.7 40.4 %copy-start.12 = (f32[1,128]{1,0:T(1,128)S(1)}, f32[1,128]{1,0:T(1,128)}, u32[]{:S(2)}) copy-start(f32[1,128]{1,0:T(1,128)} %constant.35.clone.lam_y_ref) | copy-start | bytes 1540

commit v2 on v1

--- a/solution.py
+++ b/solution.py
@@ -190,7 +190,7 @@
         self.fine = ceil_to(self.gauss * self.gauss, 16)
         assert self.own == PARTS * self.folds and self.x_eig % 16 == 0
         assert max(self.y_eig, self.n_ey * self.block_y) <= self.fold_width
-        assert 2 * self.planes == LANES
+        assert 2 * self.planes == LANES and self.n_ey == 2
 
 
 def high_low(table):
@@ -309,8 +309,35 @@
     return lax.broadcasted_iota(jnp.int32, shape, len(shape) - 1)
 
 
-def advect_kernel(sz, heights_ref, stream_ref, normal_ref, lift_ref, back_ref, out_ref, total_ref):
+def advect_kernel(
+    sz,
+    heights_ref,
+    stream_hbm,
+    normal_hbm,
+    lift_hbm,
+    back_hbm,
+    out_ref,
+    total_ref,
+    stream_ref,
+    normal_ref,
+    lift_ref,
+    back_ref,
+    arrived,
+):
     place = lax.axis_index("ey")
+    fetched = [
+        pltpu.make_async_copy(source, target, arrived.at[i])
+        for i, (source, target) in enumerate(
+            (
+                (stream_hbm, stream_ref),
+                (normal_hbm, normal_ref),
+                (lift_hbm, lift_ref),
+                (back_hbm.at[place], back_ref),
+            )
+        )
+    ]
+    for copy in fetched:
+        copy.start()
     count, fine, rows = sz.nodes * sz.nodes, sz.fine, sz.rows
     spots = sz.elems * rows
     half = lane_index((fine, LANES)) < sz.planes
@@ -320,6 +347,8 @@
         (sz.lane_nodes - length // 8 * 8, LANES), jnp.float32
     )
     carry = None
+    for copy in fetched[:3]:
+        copy.wait()
     for e in range(sz.elems):
         speeds = jnp.concatenate(
             [
@@ -341,7 +370,9 @@
             high, low = split((stream * (height * 0.5)) * slope_x + (normal * (element_width * 0.5)) * slope_y)
             highs.append(high)
             lows.append(low)
-        weak = dot(back_ref[place], jnp.concatenate(highs + lows + highs, 0))
+        if e == 0:
+            fetched[3].wait()
+        weak = dot(back_ref[...], jnp.concatenate(highs + lows + highs, 0))
         if carry is not None:
             head = jnp.concatenate([carry, jnp.zeros((column - carry.shape[0], LANES), jnp.float32)], 0)
             weak = weak + head
@@ -371,7 +402,8 @@
 
 def smooth_kernel(
     sz,
-    terms_ref,
+    mine_ref,
+    other_ref,
     in_y_ref,
     in_x_ref,
     pair_y_ref,
@@ -389,7 +421,8 @@
     tiles = -(-sz.lane_nodes // LANES)
     lanes = lane_index((PARTS, LANES))
     x_pad, x_eig = sz.x_pad, sz.x_eig
-    device = (lax.axis_index("mode") * sz.n_ex + lax.axis_index("ex")) * sz.n_ey + lax.axis_index("ey")
+    place = lax.axis_index("ey")
+    device = (lax.axis_index("mode") * sz.n_ex + lax.axis_index("ex")) * sz.n_ey + place
     first_mode = device * (sz.own // 4)
 
     for c in range(PARTS):
@@ -400,9 +433,10 @@
         held = {}
         for q in range(sz.n_ey):
             for fold in range(folds):
+                rows = pl.ds(pl.multiple_of(place * sz.own + fold * PARTS, PARTS), PARTS)
                 whole = jnp.concatenate(
                     [
-                        terms_ref[(z * sz.n_ex + p) * sz.n_ey + q, pl.ds(fold * PARTS, PARTS), :]
+                        jnp.where(place == q, mine_ref[z * sz.n_ex + p, rows, :], other_ref[z * sz.n_ex + p, rows, :])
                         for z in range(sz.n_mode)
                     ],
                     1,
@@ -477,12 +511,18 @@
                             made[q, fold, tile] = jnp.where((lanes >= low) & (lanes < high), moved, old)
         for (q, fold, tile), value in made.items():
             last = min(LANES, sz.lane_nodes - tile * LANES)
-            out_ref[p * sz.n_ey + q, pl.ds(fold * PARTS, PARTS), pl.ds(tile * LANES, last)] = value[:, :last]
-
-
-def spread_kernel(sz, solved_ref, out_ref, turned_ref):
+            out_ref[p, pl.ds(q * sz.own + fold * PARTS, PARTS), pl.ds(tile * LANES, last)] = value[:, :last]
+
+
+def spread_kernel(sz, mine_ref, other_ref, out_ref, turned_ref):
     place = lax.axis_index("ey")
-    turned_ref[...] = solved_ref[...].T
+    rows = pl.ds(pl.multiple_of(place * sz.own, PARTS), sz.own)
+    solved = [
+        jnp.where(place == q, mine_ref[p, rows, :], other_ref[p, rows, :])
+        for p in range(sz.n_ex)
+        for q in range(sz.n_ey)
+    ]
+    turned_ref[...] = jnp.concatenate(solved, 0).T
     spots = sz.elems * sz.rows
     for e in range(sz.elems):
         for f in range(sz.rows):
@@ -505,21 +545,21 @@
             out_ref[pl.ds(first, sz.elems, stride=sz.rows), :] = blank
 
 
-def call(kernel, out_shape, operands, scratch=(), scalars=0):
-    vmem = pl.BlockSpec(memory_space=pltpu.VMEM)
-    smem = pl.BlockSpec(memory_space=pltpu.SMEM)
+def call(kernel, out_shape, operands, scratch=(), spaces=None):
+    spaces = spaces or [pltpu.VMEM] * len(operands)
     return pl.pallas_call(
         kernel,
         out_shape=jax.ShapeDtypeStruct(out_shape, jnp.float32),
-        in_specs=[smem] * scalars + [vmem] * (len(operands) - scalars),
-        out_specs=vmem,
-        scratch_shapes=[pltpu.VMEM(shape, jnp.float32) for shape in scratch],
+        in_specs=[pl.BlockSpec(memory_space=space) for space in spaces],
+        out_specs=pl.BlockSpec(memory_space=pltpu.VMEM),
+        scratch_shapes=[pltpu.VMEM(each, jnp.float32) if isinstance(each, tuple) else each for each in scratch],
         compiler_params=pltpu.CompilerParams(vmem_limit_bytes=16 * 2**20),
     )(*operands)
 
 
 def on_device(sz, tables, stream_speed, normal_speed):
     flat = sz.nodes * sz.nodes * sz.elems * sz.rows
+    swap = [(q, sz.n_ey - 1 - q) for q in range(sz.n_ey)]
     table = {name: jnp.asarray(value) for name, value in tables.items()}
     weak = call(
         functools.partial(advect_kernel, sz),
@@ -531,8 +571,15 @@
             table["lift"],
             table["back"],
         ],
-        [(sz.lane_nodes, LANES)],
-        scalars=1,
+        [
+            (sz.lane_nodes, LANES),
+            (flat, sz.planes),
+            (flat, sz.planes),
+            pltpu.VMEM(tables["lift"].shape, jnp.bfloat16),
+            pltpu.VMEM(tables["back"].shape[1:], jnp.bfloat16),
+            pltpu.SemaphoreType.DMA((4,)),
+        ],
+        [pltpu.SMEM] + [pltpu.HBM] * 4,
     )
     weak = lax.all_to_all(weak, "mode", split_axis=0, concat_axis=0, tiled=True)
     spectra = call(
@@ -541,21 +588,20 @@
         [weak, table["waves"]],
         [(-(-sz.share // LANES), 2 * sz.planes_total, LANES)],
     )
-    everyone = ("mode", "ex", "ey")
-    spectra = spectra.reshape(sz.n_mode * sz.spots, sz.own, sz.share)
-    terms = lax.all_to_all(spectra, everyone, split_axis=0, concat_axis=0, tiled=True)
+    spectra = spectra.reshape(sz.n_mode * sz.n_ex, sz.n_ey * sz.own, sz.share)
+    terms = lax.all_to_all(spectra, ("mode", "ex"), split_axis=0, concat_axis=0, tiled=True)
     names = ("in_y", "in_x", "pair_y", "pair_x", "out_y", "out_x", "lam_x", "lam_y")
     solved = call(
         functools.partial(smooth_kernel, sz),
-        (sz.spots, sz.own, sz.lane_nodes),
-        [terms] + [table[name] for name in names],
+        (sz.n_ex, sz.n_ey * sz.own, sz.lane_nodes),
+        [terms, lax.ppermute(terms, "ey", swap)] + [table[name] for name in names],
         [(PARTS * sz.x_pad, LANES), (PARTS * sz.x_eig, LANES), (PARTS * sz.x_eig, LANES)],
     )
-    solved = lax.all_to_all(solved, ("ex", "ey"), split_axis=0, concat_axis=0, tiled=True)
+    solved = lax.all_to_all(solved, "ex", split_axis=0, concat_axis=0, tiled=True)
     out = call(
         functools.partial(spread_kernel, sz),
         (flat, LANES),
-        [solved.reshape(sz.columns, sz.lane_nodes)],
+        [solved, lax.ppermute(solved, "ey", swap)],
         [(sz.lane_nodes, LANES)],
     )
     return out.reshape(sz.nodes, sz.nodes, sz.elems, sz.rows, sz.columns)

time: 71.2 us -> 74.8 us (1.051)
  waiting for transfers between devices: 0 us -> 3.81 us
  blocking collectives: 52.5 us -> 51.4 us
  Pallas kernels: 12.5 us -> 13.4 us
    ppermute x0 -> x2, waiting for transfers between devices: none -> 3.81 us  [the longest x1 1.91 us: on_device(): lax.ppermute(terms, 'ey', swap)]
    all_to_all x2, blocking collectives: 31.7 us -> 30.7 us  [the longest x1 19.2 us: on_device(): lax.all_to_all(spectra, ('mode', 'ex'), split_axis=0, concat_axis=0, tile...]
    pallas_call x4, Pallas kernels: 12.5 us -> 13.4 us  [call(): pl.pallas_call(kernel, out_shape=jax.ShapeDtypeStruct(out_shape, jnp.floa...]
  transfers between devices with their start and end apart: 0 -> 2, of which waited for: 0 -> 2; matrix products, arithmetic and copies ran while one was open for 0% -> 0% of each run, Pallas kernels for 0% -> 0%
where the time goes in v2:
time: 74.8 us; the launch traced here: 74.4 us
  blocking collectives  51.4 us (69%)
  Pallas kernels  13.4 us (18%)
  local copies, waits for them, and re-layouts  5.67 us (8%)
  waiting for transfers between devices  3.81 us (5%)
    all_to_all x1, blocking collectives, on_device(): weak = lax.all_to_all(weak, 'mode', split_axis=0, concat_axis=0, tiled=True)  20.7 us
    all_to_all x1, blocking collectives, on_device(): lax.all_to_all(spectra, ('mode', 'ex'), split_axis=0, concat_axis=0, tile...  19.2 us
    pallas_call x4, Pallas kernels, call(): pl.pallas_call(kernel, out_shape=jax.ShapeDtypeStruct(out_shape, jnp.floa...  13.4 us
    all_to_all x1, blocking collectives, on_device(): lax.all_to_all(solved, 'ex', split_axis=0, concat_axis=0, tiled=True)  11.5 us
    unnamed x28, local copies, waits for them, and re-layouts  5.67 us
    ppermute x1, waiting for transfers between devices, on_device(): lax.ppermute(terms, 'ey', swap)  1.91 us
    ppermute x1, waiting for transfers between devices, on_device(): lax.ppermute(solved, 'ey', swap)  1.91 us
  transfers between devices with their start and end apart: 2, of which 2 were waited for; matrix products, arithmetic and copies ran while one was open for 0% of the time, Pallas kernels for 0%

profile of v2, /device:TPU:0, one launch (start us, length us, event | category | flops | bytes accessed | tf_op | source)
XLA Modules:
  0.0 74.4 jit_solution(5565477110598454430)
XLA Ops:
  0.0 1.6 %copy-done = bf16[2,264,2016]{2,1,0:T(8,128)(2,1)S(1)} copy-done((bf16[2,264,2016]{2,1,0:T(8,128)(2,1)S(1)}, bf16[2,264,2016]{2,1,0:T(8,128)(2,1)}, u32[]{:S(2)}) %copy-start) | copy-done | bytes 2128920
  1.6 1.2 %copy-done.1 = bf16[1008,432]{1,0:T(8,128)(2,1)S(1)} copy-done((bf16[1008,432]{1,0:T(8,128)(2,1)S(1)}, bf16[1008,432]{1,0:T(8,128)(2,1)}, u32[]{:S(2)}) %copy-start.1) | copy-done | bytes 870936
  2.8 1.1 %copy-done.3 = f32[12,12,4,2,64]{4,3,2,1,0:T(2,128)S(1)} copy-done((f32[12,12,4,2,64]{4,3,2,1,0:T(2,128)S(1)}, f32[12,12,4,2,64]{4,3,2,1,0:T(2,128)}, u32[]{:S(2)}) %copy-start.3) | copy-done | bytes 294936
  3.9 1.1 %copy-done.4 = f32[12,12,4,2,64]{4,3,2,1,0:T(2,128)S(1)} copy-done((f32[12,12,4,2,64]{4,3,2,1,0:T(2,128)S(1)}, f32[12,12,4,2,64]{4,3,2,1,0:T(2,128)}, u32[]{:S(2)}) %copy-start.4) | copy-done | bytes 294936
  5.0 0.7 copy-done.12
  5.6 4.8 %shard_map.136 = f32[4,256,128]{2,1,0:T(8,128)S(1)} custom-call(f32[4]{0:T(128)S(1)} %copy-done.12, f32[1152,64]{1,0:T(8,128)S(1)} %bitcast.5, f32[1152,64]{1,0:T(8,128)S(1)} %bitcast.6, bf16[1008,432]{1,0:T(8,128)(2,1)S(1)} %copy-done.1, bf16[2,264,2016]{2,1,0:T(8,128)(2,1)S(1)} %copy-done), custom_call_target="tpu_custom_call" | custom-call | tf_op jit(solution)/shard_map/pallas_call | solution.py:550
  10.4 0.0 copy-start.2
  10.4 0.0 copy-start.5
  10.5 0.0 copy-start.6
  10.5 0.0 copy-start.8
  10.5 0.0 copy-start.9
  10.5 0.0 copy-start.10
  10.5 0.0 copy-start.11
  10.5 0.0 copy-start.13
  10.5 20.7 %all_to_all.15.weak_ref = f32[4,256,128]{2,1,0:T(8,128)S(1)} all-to-all(f32[4,256,128]{2,1,0:T(8,128)S(1)} %shard_map.136), channel_id=1, replica_groups=mesh['mode'=4,'ex'=4,'ey'=2] {'mode'}, dimensions={0} | all-to-all | bytes 1048576 | tf_op jit(solution)/shard_map/all_to_all | solution.py:584
  31.3 0.6 shard_map.137
  31.8 19.2 %all_to_all.16.mine_ref = f32[16,32,256]{2,1,0:T(8,128)S(1)} all-to-all(f32[16,32,256]{2,1,0:T(8,128)S(1)} %bitcast.4), channel_id=1, replica_groups=mesh['mode'=4,'ex'=4,'ey'=2] {'mode','ex'}, dimensions={0} | all-to-all | bytes 1048576 | tf_op jit(solution)/shard_map/all_to_all | solution.py:592
  51.0 0.0 collective-permute-start
  51.0 1.9 %collective-permute-done.other_ref = f32[16,32,256]{2,1,0:T(8,128)S(1)} collective-permute-done((f32[16,32,256]{2,1,0:T(8,128)S(1)}, f32[16,32,256]{2,1,0:T(8,128)S(1)}, u32[]{:S(2)}, u32[]{:S(2)}) %collective-permute-start) | collective-permute-done | bytes 524320 | tf_op jit(solution)/shard_map/ppermute | solution.py:597
  53.0 6.9 %shard_map.138 = f32[4,32,1024]{2,1,0:T(8,128)S(1)} custom-call(f32[16,32,256]{2,1,0:T(8,128)S(1)} %all_to_all.16.mine_ref, f32[16,32,256]{2,1,0:T(8,128)S(1)} %collective-permute-done.other_ref, bf16[256,256]{1,0:T(8,128)(2,1)S(1)} %copy-done.10, bf16[224,576]{1,0:T(8,128)(2,1)S(1)} %copy-done.6, bf16[384,256]{1,0:T(8,128)(2,1)S(1)} %copy-done.8, ...), custom_call_target="tpu_custom_call" | custom-call | tf_op jit(solution)/shard_map/pallas_call | solution.py:550
  59.9 11.5 %all_to_all.17.mine_ref = f32[4,32,1024]{2,1,0:T(8,128)S(1)} all-to-all(f32[4,32,1024]{2,1,0:T(8,128)S(1)} %shard_map.138), channel_id=1, replica_groups=mesh['mode'=4,'ex'=4,'ey'=2] {'ex'}, dimensions={0} | all-to-all | bytes 1048576 | tf_op jit(solution)/shard_map/all_to_all | solution.py:600
  71.4 0.0 collective-permute-start.1
  71.4 1.9 %collective-permute-done.1.other_ref = f32[4,32,1024]{2,1,0:T(8,128)S(1)} collective-permute-done((f32[4,32,1024]{2,1,0:T(8,128)S(1)}, f32[4,32,1024]{2,1,0:T(8,128)S(1)}, u32[]{:S(2)}, u32[]{:S(2)}) %collective-permute-start.1) | collective-permute-done | bytes 524320 | tf_op jit(solution)/shard_map/ppermute | solution.py:604
  73.3 1.1 %shard_map.139 = f32[1152,128]{1,0:T(8,128)} custom-call(f32[4,32,1024]{2,1,0:T(8,128)S(1)} %all_to_all.17.mine_ref, f32[4,32,1024]{2,1,0:T(8,128)S(1)} %collective-permute-done.1.other_ref), custom_call_target="tpu_custom_call" | custom-call | tf_op jit(solution)/shard_map/pallas_call | solution.py:550
  (15 shorter events, 0.0 us)
Async XLA Ops:
  0.0 1.6 %copy-start = (bf16[2,264,2016]{2,1,0:T(8,128)(2,1)S(1)}, bf16[2,264,2016]{2,1,0:T(8,128)(2,1)}, u32[]{:S(2)}) copy-start(bf16[2,264,2016]{2,1,0:T(8,128)(2,1)} %constant.26.clone.back_hbm) | copy-start | bytes 6386692
  1.6 1.2 %copy-start.1 = (bf16[1008,432]{1,0:T(8,128)(2,1)S(1)}, bf16[1008,432]{1,0:T(8,128)(2,1)}, u32[]{:S(2)}) copy-start(bf16[1008,432]{1,0:T(8,128)(2,1)} %constant.25.clone.lift_hbm) | copy-start | bytes 2612740
  2.8 1.1 %copy-start.3 = (f32[12,12,4,2,64]{4,3,2,1,0:T(2,128)S(1)}, f32[12,12,4,2,64]{4,3,2,1,0:T(2,128)}, u32[]{:S(2)}) copy-start(f32[12,12,4,2,64]{4,3,2,1,0:T(2,128)} %param.14) | copy-start | bytes 884740
  3.9 1.1 %copy-start.4 = (f32[12,12,4,2,64]{4,3,2,1,0:T(2,128)S(1)}, f32[12,12,4,2,64]{4,3,2,1,0:T(2,128)}, u32[]{:S(2)}) copy-start(f32[12,12,4,2,64]{4,3,2,1,0:T(2,128)} %param.15) | copy-start | bytes 884740
  5.0 0.7 copy-start.12
  5.6 25.7 %copy-start.7 = (bf16[2,256,256]{2,1,0:T(8,128)(2,1)S(1)}, bf16[2,256,256]{2,1,0:T(8,128)(2,1)}, u32[]{:S(2)}) copy-start(bf16[2,256,256]{2,1,0:T(8,128)(2,1)} %constant.27.clone.waves_ref) | copy-start | bytes 786436
  10.4 42.5 %copy-start.2 = (bf16[224,1344]{1,0:T(8,128)(2,1)S(1)}, bf16[224,1344]{1,0:T(8,128)(2,1)}, u32[]{:S(2)}) copy-start(bf16[224,1344]{1,0:T(8,128)(2,1)} %constant.31.clone.pair_x_ref) | copy-start | bytes 1806340
  10.4 42.5 %copy-start.5 = (bf16[192,672]{1,0:T(8,128)(2,1)S(1)}, bf16[192,672]{1,0:T(8,128)(2,1)}, u32[]{:S(2)}) copy-start(bf16[192,672]{1,0:T(8,128)(2,1)} %constant.33.clone.out_x_ref) | copy-start | bytes 774148
  10.5 42.5 %copy-start.6 = (bf16[224,576]{1,0:T(8,128)(2,1)S(1)}, bf16[224,576]{1,0:T(8,128)(2,1)}, u32[]{:S(2)}) copy-start(bf16[224,576]{1,0:T(8,128)(2,1)} %constant.29.clone.in_x_ref) | copy-start | bytes 774148
  10.5 42.5 %copy-start.8 = (bf16[384,256]{1,0:T(8,128)(2,1)S(1)}, bf16[384,256]{1,0:T(8,128)(2,1)}, u32[]{:S(2)}) copy-start(bf16[384,256]{1,0:T(8,128)(2,1)} %constant.30.clone.pair_y_ref) | copy-start | bytes 589828
  10.5 42.5 %copy-start.9 = (bf16[256,256]{1,0:T(8,128)(2,1)S(1)}, bf16[256,256]{1,0:T(8,128)(2,1)}, u32[]{:S(2)}) copy-start(bf16[256,256]{1,0:T(8,128)(2,1)} %constant.32.clone.out_y_ref) | copy-start | bytes 393220
  10.5 42.5 %copy-start.10 = (bf16[256,256]{1,0:T(8,128)(2,1)S(1)}, bf16[256,256]{1,0:T(8,128)(2,1)}, u32[]{:S(2)}) copy-start(bf16[256,256]{1,0:T(8,128)(2,1)} %constant.28.clone.in_y_ref) | copy-start | bytes 393220
  10.5 42.5 %copy-start.11 = (f32[224,128]{1,0:T(8,128)S(1)}, f32[224,128]{1,0:T(8,128)}, u32[]{:S(2)}) copy-start(f32[224,128]{1,0:T(8,128)} %constant.34.clone.lam_x_ref) | copy-start | bytes 344068
  10.5 42.5 %copy-start.13 = (f32[1,128]{1,0:T(1,128)S(1)}, f32[1,128]{1,0:T(1,128)}, u32[]{:S(2)}) copy-start(f32[1,128]{1,0:T(1,128)} %constant.35.clone.lam_y_ref) | copy-start | bytes 1540
  51.0 1.9 %collective-permute-start = (f32[16,32,256]{2,1,0:T(8,128)S(1)}, f32[16,32,256]{2,1,0:T(8,128)S(1)}, u32[]{:S(2)}, u32[]{:S(2)}) collective-permute-start(f32[16,32,256]{2,1,0:T(8,128)S(1)} %all_to_all.16.mine_ref), channel_id=1, source_target_pairs={{0,1},{1,0},{2,3},{3,2},{4,5},{5,4},{6,7},{7,6},{8,9},{9,8},{10,11... | collective-permute-start | bytes 1572872 | tf_op jit(solution)/shard_map/ppermute | solution.py:597
  71.4 1.9 %collective-permute-start.1 = (f32[4,32,1024]{2,1,0:T(8,128)S(1)}, f32[4,32,1024]{2,1,0:T(8,128)S(1)}, u32[]{:S(2)}, u32[]{:S(2)}) collective-permute-start(f32[4,32,1024]{2,1,0:T(8,128)S(1)} %all_to_all.17.mine_ref), channel_id=1, source_target_pairs={{0,1},{1,0},{2,3},{3,2},{4,5},{5,4},{6,7},{7,6},{8,9},{9,8},{10,11... | collective-permute-start | bytes 1572872 | tf_op jit(solution)/shard_map/ppermute | solution.py:604

commit v3 on v2

--- a/solution.py
+++ b/solution.py
@@ -190,7 +190,7 @@
         self.fine = ceil_to(self.gauss * self.gauss, 16)
         assert self.own == PARTS * self.folds and self.x_eig % 16 == 0
         assert max(self.y_eig, self.n_ey * self.block_y) <= self.fold_width
-        assert 2 * self.planes == LANES and self.n_ey == 2
+        assert 2 * self.planes == LANES
 
 
 def high_low(table):
@@ -305,25 +305,32 @@
     return jnp.concatenate(split(value), 1)
 
 
+def partner(spot, step, count):
+    if count & (count - 1) == 0:
+        return spot ^ step
+    return (spot + step) % count
+
+
+def origin(spot, step, count):
+    if count & (count - 1) == 0:
+        return spot ^ step
+    return (spot - step + count) % count
+
+
 def lane_index(shape):
     return lax.broadcasted_iota(jnp.int32, shape, len(shape) - 1)
 
 
 def advect_kernel(
     sz,
-    heights_ref,
+    heights,
     stream_hbm,
     normal_hbm,
     lift_hbm,
     back_hbm,
-    out_ref,
-    total_ref,
-    stream_ref,
-    normal_ref,
-    lift_ref,
-    back_ref,
-    arrived,
+    *others,
 ):
+    out_refs, (total_ref, stream_ref, normal_ref, lift_ref, back_ref, arrived) = others[:-6], others[-6:]
     place = lax.axis_index("ey")
     fetched = [
         pltpu.make_async_copy(source, target, arrived.at[i])
@@ -361,7 +368,7 @@
         values = dot(lift_ref[...], below(speeds))
         highs, lows = [], []
         for f in range(rows):
-            height = heights_ref[place * rows + f]
+            height = sum(jnp.where(place == q, heights[q * rows + f], 0.0) for q in range(sz.n_ey))
             mine = values[:, f * LANES : (f + 1) * LANES]
             both, slope_x, slope_y = mine[:fine], mine[fine : 2 * fine], mine[2 * fine :]
             turned = pltpu.roll(both, sz.planes, 1)
@@ -381,16 +388,23 @@
             carry = weak[step:]
         else:
             total_ref[pl.ds(e * step, column), :] = weak
-    for z in range(sz.n_mode):
-        out_ref[z] = total_ref[pl.ds(z * sz.share, sz.share), :]
-
-
-def transform_kernel(sz, weak_ref, waves_ref, out_ref, mixed_ref):
-    turned = [weak_ref[z].T for z in range(sz.n_mode)]
+    spot = lax.axis_index("mode")
+    for step, out_ref in enumerate(out_refs):
+        goal = partner(spot, step, sz.n_mode)
+        out_ref[...] = total_ref[pl.ds(pl.multiple_of(goal * sz.share, 8), sz.share), :]
+
+
+def transform_kernel(sz, *refs):
+    weak_refs, (waves_ref, out_ref, mixed_ref, signal_ref) = refs[:-4], refs[-4:]
+    spot = lax.axis_index("mode")
+    for step, weak_ref in enumerate(weak_refs):
+        turned = weak_ref[...].T
+        first = pl.multiple_of(origin(spot, step, sz.n_mode) * sz.planes, 8)
+        for k in range(2):
+            signal_ref[k, pl.ds(first, sz.planes), :] = turned[k * sz.planes : (k + 1) * sz.planes]
     modes = sz.planes_total
     for k in range(2):
-        signal = jnp.concatenate([piece[k * sz.planes : (k + 1) * sz.planes] for piece in turned], 0)
-        high, low = split(signal)
+        high, low = split(signal_ref[k])
         part = dot(waves_ref[0], high) + dot(waves_ref[0], low) + dot(waves_ref[1], high)
         for t in range(mixed_ref.shape[0]):
             tile = part[:, t * LANES : (t + 1) * LANES]
@@ -402,8 +416,7 @@
 
 def smooth_kernel(
     sz,
-    mine_ref,
-    other_ref,
+    terms_ref,
     in_y_ref,
     in_x_ref,
     pair_y_ref,
@@ -412,17 +425,15 @@
     out_x_ref,
     lam_x_ref,
     lam_y_ref,
-    out_ref,
-    field_ref,
-    first_ref,
-    work_ref,
+    *others,
 ):
+    out_refs, (field_ref, first_ref, work_ref) = others[:-3], others[-3:]
     width, folds, strip = sz.fold_width, sz.folds, sz.block_y
     tiles = -(-sz.lane_nodes // LANES)
     lanes = lane_index((PARTS, LANES))
     x_pad, x_eig = sz.x_pad, sz.x_eig
-    place = lax.axis_index("ey")
-    device = (lax.axis_index("mode") * sz.n_ex + lax.axis_index("ex")) * sz.n_ey + place
+    place, spot = lax.axis_index("ey"), lax.axis_index("ex")
+    device = (lax.axis_index("mode") * sz.n_ex + spot) * sz.n_ey + place
     first_mode = device * (sz.own // 4)
 
     for c in range(PARTS):
@@ -430,13 +441,13 @@
             (x_pad - sz.x_nodes, LANES), jnp.float32
         )
     for p in range(sz.n_ex):
+        block = (spot + p) % sz.n_ex
         held = {}
         for q in range(sz.n_ey):
             for fold in range(folds):
-                rows = pl.ds(pl.multiple_of(place * sz.own + fold * PARTS, PARTS), PARTS)
                 whole = jnp.concatenate(
                     [
-                        jnp.where(place == q, mine_ref[z * sz.n_ex + p, rows, :], other_ref[z * sz.n_ex + p, rows, :])
+                        terms_ref[(z * sz.n_ex + block) * sz.n_ey + q, pl.ds(fold * PARTS, PARTS), :]
                         for z in range(sz.n_mode)
                     ],
                     1,
@@ -511,18 +522,22 @@
                             made[q, fold, tile] = jnp.where((lanes >= low) & (lanes < high), moved, old)
         for (q, fold, tile), value in made.items():
             last = min(LANES, sz.lane_nodes - tile * LANES)
-            out_ref[p, pl.ds(q * sz.own + fold * PARTS, PARTS), pl.ds(tile * LANES, last)] = value[:, :last]
-
-
-def spread_kernel(sz, mine_ref, other_ref, out_ref, turned_ref):
-    place = lax.axis_index("ey")
-    rows = pl.ds(pl.multiple_of(place * sz.own, PARTS), sz.own)
-    solved = [
-        jnp.where(place == q, mine_ref[p, rows, :], other_ref[p, rows, :])
-        for p in range(sz.n_ex)
-        for q in range(sz.n_ey)
-    ]
-    turned_ref[...] = jnp.concatenate(solved, 0).T
+            where = (pl.ds(fold * PARTS, PARTS), pl.ds(tile * LANES, last))
+            for turn in range(sz.n_ey):
+
+                @pl.when((place + turn) % sz.n_ey == q)
+                def _(out_ref=out_refs[p * sz.n_ey + turn], value=value[:, :last], where=where):
+                    out_ref[where] = value
+
+
+def spread_kernel(sz, *refs):
+    solved_refs, (out_ref, stacked_ref, turned_ref) = refs[:-3], refs[-3:]
+    place, spot = lax.axis_index("ey"), lax.axis_index("ex")
+    for step, solved_ref in enumerate(solved_refs):
+        shift, turn = step // sz.n_ey, step % sz.n_ey
+        source = (spot - shift + sz.n_ex) % sz.n_ex * sz.n_ey + (place - turn + sz.n_ey) % sz.n_ey
+        stacked_ref[pl.ds(pl.multiple_of(source * sz.own, PARTS), sz.own), :] = solved_ref[...]
+    turned_ref[...] = stacked_ref[...].T
     spots = sz.elems * sz.rows
     for e in range(sz.elems):
         for f in range(sz.rows):
@@ -545,27 +560,26 @@
             out_ref[pl.ds(first, sz.elems, stride=sz.rows), :] = blank
 
 
-def call(kernel, out_shape, operands, scratch=(), spaces=None):
-    spaces = spaces or [pltpu.VMEM] * len(operands)
-    return pl.pallas_call(
+def call(kernel, shapes, operands, scratch=(), space=pltpu.VMEM, limit=16):
+    made = pl.pallas_call(
         kernel,
-        out_shape=jax.ShapeDtypeStruct(out_shape, jnp.float32),
-        in_specs=[pl.BlockSpec(memory_space=space) for space in spaces],
-        out_specs=pl.BlockSpec(memory_space=pltpu.VMEM),
+        out_shape=[jax.ShapeDtypeStruct(shape, jnp.float32) for shape in shapes],
+        in_specs=[pl.BlockSpec(memory_space=space) for _ in operands],
+        out_specs=[pl.BlockSpec(memory_space=pltpu.VMEM) for _ in shapes],
         scratch_shapes=[pltpu.VMEM(each, jnp.float32) if isinstance(each, tuple) else each for each in scratch],
-        compiler_params=pltpu.CompilerParams(vmem_limit_bytes=16 * 2**20),
+        compiler_params=pltpu.CompilerParams(vmem_limit_bytes=limit * 2**20),
     )(*operands)
+    return list(made)
 
 
 def on_device(sz, tables, stream_speed, normal_speed):
     flat = sz.nodes * sz.nodes * sz.elems * sz.rows
-    swap = [(q, sz.n_ey - 1 - q) for q in range(sz.n_ey)]
-    table = {name: jnp.asarray(value) for name, value in tables.items()}
+    table = {name: jnp.asarray(value) for name, value in tables.items() if name != "heights"}
+    heights = [float(height) for height in tables["heights"]]
     weak = call(
-        functools.partial(advect_kernel, sz),
-        (sz.n_mode, sz.share, LANES),
+        functools.partial(advect_kernel, sz, heights),
+        [(sz.share, LANES)] * sz.n_mode,
         [
-            table["heights"],
             stream_speed.reshape(flat, sz.planes),
             normal_speed.reshape(flat, sz.planes),
             table["lift"],
@@ -579,30 +593,40 @@
             pltpu.VMEM(tables["back"].shape[1:], jnp.bfloat16),
             pltpu.SemaphoreType.DMA((4,)),
         ],
-        [pltpu.SMEM] + [pltpu.HBM] * 4,
-    )
-    weak = lax.all_to_all(weak, "mode", split_axis=0, concat_axis=0, tiled=True)
-    spectra = call(
+        pltpu.HBM,
+        60,
+    )
+    for step in sorted(range(1, sz.n_mode), key=lambda each: (each & -each, each), reverse=True):
+        pairs = [(z, partner(z, step, sz.n_mode)) for z in range(sz.n_mode)]
+        weak[step] = lax.ppermute(weak[step], "mode", pairs)
+    (spectra,) = call(
         functools.partial(transform_kernel, sz),
-        (2 * sz.planes_total, sz.share),
-        [weak, table["waves"]],
-        [(-(-sz.share // LANES), 2 * sz.planes_total, LANES)],
-    )
-    spectra = spectra.reshape(sz.n_mode * sz.n_ex, sz.n_ey * sz.own, sz.share)
-    terms = lax.all_to_all(spectra, ("mode", "ex"), split_axis=0, concat_axis=0, tiled=True)
+        [(2 * sz.planes_total, sz.share)],
+        [*weak, table["waves"]],
+        [(-(-sz.share // LANES), 2 * sz.planes_total, LANES), (2, sz.planes_total, sz.share)],
+    )
+    spectra = spectra.reshape(sz.n_mode * sz.spots, sz.own, sz.share)
+    terms = lax.all_to_all(spectra, ("mode", "ex", "ey"), split_axis=0, concat_axis=0, tiled=True)
     names = ("in_y", "in_x", "pair_y", "pair_x", "out_y", "out_x", "lam_x", "lam_y")
     solved = call(
         functools.partial(smooth_kernel, sz),
-        (sz.n_ex, sz.n_ey * sz.own, sz.lane_nodes),
-        [terms, lax.ppermute(terms, "ey", swap)] + [table[name] for name in names],
+        [(sz.own, sz.lane_nodes)] * sz.spots,
+        [terms] + [table[name] for name in names],
         [(PARTS * sz.x_pad, LANES), (PARTS * sz.x_eig, LANES), (PARTS * sz.x_eig, LANES)],
     )
-    solved = lax.all_to_all(solved, "ex", split_axis=0, concat_axis=0, tiled=True)
-    out = call(
+    for step in range(1, sz.spots):
+        shift, turn = step // sz.n_ey, step % sz.n_ey
+        pairs = [
+            (p * sz.n_ey + q, (p + shift) % sz.n_ex * sz.n_ey + (q + turn) % sz.n_ey)
+            for p in range(sz.n_ex)
+            for q in range(sz.n_ey)
+        ]
+        solved[step] = lax.ppermute(solved[step], ("ex", "ey"), pairs)
+    (out,) = call(
         functools.partial(spread_kernel, sz),
-        (flat, LANES),
-        [solved, lax.ppermute(solved, "ey", swap)],
-        [(sz.lane_nodes, LANES)],
+        [(flat, LANES)],
+        solved,
+        [(sz.columns, sz.lane_nodes), (sz.lane_nodes, LANES)],
     )
     return out.reshape(sz.nodes, sz.nodes, sz.elems, sz.rows, sz.columns)
 

time: 74.8 us -> 63.9 us (0.85)
  blocking collectives: 51.4 us -> 20.6 us
  starting transfers between devices: 0.01 us -> 12 us
  waiting for transfers between devices: 3.81 us -> 14.4 us
  local copies, waits for them, and re-layouts: 5.67 us -> 0.96 us
  Pallas kernels: 13.4 us -> 15.7 us
    all_to_all x3 -> x1, blocking collectives: 51.4 us -> 20.6 us  [on_device(): lax.all_to_all(spectra, ('mode', 'ex', 'ey'), split_axis=0, concat_axis=0...]
    ppermute x2 -> x10, starting transfers between devices: 0.01 us -> 12 us  [the longest x7 6.31 us: on_device(): solved[step] = lax.ppermute(solved[step], ('ex', 'ey'), pairs)]
    ppermute x2 -> x10, waiting for transfers between devices: 3.81 us -> 14.4 us  [the longest x3 10.5 us: on_device(): weak[step] = lax.ppermute(weak[step], 'mode', pairs)]
    unnamed x28 -> x20, local copies, waits for them, and re-layouts: 5.67 us -> 0.96 us
    pallas_call x4, Pallas kernels: 13.4 us -> 15.7 us  [call(): pl.pallas_call(kernel, out_shape=[jax.ShapeDtypeStruct(shape, jnp.float32...]
  transfers between devices with their start and end apart: 2 -> 10, of which waited for: 2 -> 6; matrix products, arithmetic and copies ran while one was open for 0% -> 0% of each run, Pallas kernels for 0% -> 0%
where the time goes in v3:
time: 63.9 us; the launch traced here: 63.7 us
  blocking collectives  20.6 us (32%)
  Pallas kernels  15.7 us (25%)
  waiting for transfers between devices  14.4 us (23%)
  starting transfers between devices  12 us (19%)
  local copies, waits for them, and re-layouts  0.96 us (2%)
    all_to_all x1, blocking collectives, on_device(): lax.all_to_all(spectra, ('mode', 'ex', 'ey'), split_axis=0, concat_axis=0...  20.6 us
    pallas_call x4, Pallas kernels, call(): pl.pallas_call(kernel, out_shape=[jax.ShapeDtypeStruct(shape, jnp.float32...  15.7 us
    ppermute x3, waiting for transfers between devices, on_device(): weak[step] = lax.ppermute(weak[step], 'mode', pairs)  10.5 us
    ppermute x7, starting transfers between devices, on_device(): solved[step] = lax.ppermute(solved[step], ('ex', 'ey'), pairs)  6.31 us
    ppermute x3, starting transfers between devices, on_device(): weak[step] = lax.ppermute(weak[step], 'mode', pairs)  5.72 us
    ppermute x7, waiting for transfers between devices, on_device(): solved[step] = lax.ppermute(solved[step], ('ex', 'ey'), pairs)  3.87 us
  transfers between devices with their start and end apart: 10, of which 6 were waited for; matrix products, arithmetic and copies ran while one was open for 0% of the time, Pallas kernels for 0%

profile of v3, /device:TPU:0, one launch (start us, length us, event | category | flops | bytes accessed | tf_op | source)
XLA Modules:
  0.0 63.7 jit_solution(1276701708026677840)
XLA Ops:
  0.0 5.9 %shard_map.127 = (f32[256,128]{1,0:T(8,128)}, f32[256,128]{1,0:T(8,128)}, f32[256,128]{1,0:T(8,128)}, f32[256,128]{1,0:T(8,128)}) custom-call(f32[1152,64]{1,0:T(8,128)} %bitcast.5, f32[1152,64]{1,0:T(8,128)} %bitcast.6, bf16[1008,432]{1,0:T(8,128)(2,1)} %constant.22.clone.lift_hbm, bf16[2,264,2016]{2,1,0:T(8,128)(2,1)} %constant.23.clone.back_hbm), custom_call_target="tpu_custom_call" | custom-call | tf_op jit(solution)/shard_map/pallas_call | solution.py:564
  5.9 0.0 copy-start
  5.9 0.0 copy-start.2
  5.9 0.0 copy-start.4
  6.0 3.1 %collective-permute-start = (f32[256,128]{1,0:T(8,128)}, f32[256,128]{1,0:T(8,128)S(1)}, u32[]{:S(2)}, u32[]{:S(2)}) collective-permute-start(f32[256,128]{1,0:T(8,128)} %get-tuple-element.18), channel_id=1, source_target_pairs={{0,8},{8,0},{16,24},{24,16},{1,9},{9,1},{17,25},{25,17},{2,10},{10... | collective-permute-start | bytes 393224 | tf_op jit(solution)/shard_map/ppermute | solution.py:601
  9.1 2.6 %collective-permute-start.1 = (f32[256,128]{1,0:T(8,128)}, f32[256,128]{1,0:T(8,128)S(1)}, u32[]{:S(2)}, u32[]{:S(2)}) collective-permute-start(f32[256,128]{1,0:T(8,128)} %get-tuple-element.19), channel_id=1, source_target_pairs={{0,16},{8,24},{16,0},{24,8},{1,17},{9,25},{17,1},{25,9},{2,18},{10... | collective-permute-start | bytes 393224 | tf_op jit(solution)/shard_map/ppermute | solution.py:601
  11.7 2.6 %collective-permute-done.refs_1_ = f32[256,128]{1,0:T(8,128)S(1)} collective-permute-done((f32[256,128]{1,0:T(8,128)}, f32[256,128]{1,0:T(8,128)S(1)}, u32[]{:S(2)}, u32[]{:S(2)}) %collective-permute-start) | collective-permute-done | bytes 131104 | tf_op jit(solution)/shard_map/ppermute | solution.py:601
  14.3 7.9 %collective-permute-done.1.refs_2_ = f32[256,128]{1,0:T(8,128)S(1)} collective-permute-done((f32[256,128]{1,0:T(8,128)}, f32[256,128]{1,0:T(8,128)S(1)}, u32[]{:S(2)}, u32[]{:S(2)}) %collective-permute-start.1) | collective-permute-done | bytes 131104 | tf_op jit(solution)/shard_map/ppermute | solution.py:601
  22.2 0.9 %copy-done.7 = f32[256,128]{1,0:T(8,128)S(1)} copy-done((f32[256,128]{1,0:T(8,128)S(1)}, f32[256,128]{1,0:T(8,128)}, u32[]{:S(2)}) %copy-start.7) | copy-done | bytes 131096
  23.1 0.6 shard_map.128
  23.7 20.6 %all_to_all.5.terms_ref = f32[32,16,256]{2,1,0:T(8,128)S(1)} all-to-all(f32[32,16,256]{2,1,0:T(8,128)S(1)} %bitcast.4), channel_id=1, replica_groups=mesh['mode'=4,'ex'=4,'ey'=2] {'mode','ex','ey'}, dimensions={0} | all-to-all | bytes 1048576 | tf_op jit(solution)/shard_map/all_to_all | solution.py:609
  44.4 8.0 %shard_map.129 = (f32[16,1024]{1,0:T(8,128)S(1)}, f32[16,1024]{1,0:T(8,128)S(1)}, f32[16,1024]{1,0:T(8,128)S(1)}, f32[16,1024]{1,0:T(8,128)S(1)}, f32[16,1024]{1...) custom-call(f32[32,16,256]{2,1,0:T(8,128)S(1)} %all_to_all.5.terms_ref, ...), custom_call_target="tpu_custom_call" | custom-call | tf_op jit(solution)/shard_map/pallas_call | solution.py:564
  52.4 0.1 collective-permute-start.3
  52.5 1.3 %collective-permute-start.4 = (f32[16,1024]{1,0:T(8,128)S(1)}, f32[16,1024]{1,0:T(8,128)S(1)}, u32[]{:S(2)}, u32[]{:S(2)}) collective-permute-start(f32[16,1024]{1,0:T(8,128)S(1)} %get-tuple-element.23), channel_id=1, source_target_pairs={{0,2},{1,3},{2,4},{3,5},{4,6},{5,7},{6,0},{7,1},{8,10},{9,11},{10,... | collective-permute-start | bytes 196616 | tf_op jit(solution)/shard_map/ppermute | solution.py:624
  53.8 1.2 %collective-permute-start.5 = (f32[16,1024]{1,0:T(8,128)S(1)}, f32[16,1024]{1,0:T(8,128)S(1)}, u32[]{:S(2)}, u32[]{:S(2)}) collective-permute-start(f32[16,1024]{1,0:T(8,128)S(1)} %get-tuple-element.24), channel_id=1, source_target_pairs={{0,3},{1,2},{2,5},{3,4},{4,7},{5,6},{6,1},{7,0},{8,11},{9,10},{10,... | collective-permute-start | bytes 196616 | tf_op jit(solution)/shard_map/ppermute | solution.py:624
  55.0 0.8 %collective-permute-start.6 = (f32[16,1024]{1,0:T(8,128)S(1)}, f32[16,1024]{1,0:T(8,128)S(1)}, u32[]{:S(2)}, u32[]{:S(2)}) collective-permute-start(f32[16,1024]{1,0:T(8,128)S(1)} %get-tuple-element.25), channel_id=1, source_target_pairs={{0,4},{1,5},{2,6},{3,7},{4,0},{5,1},{6,2},{7,3},{8,12},{9,13},{10,... | collective-permute-start | bytes 196616 | tf_op jit(solution)/shard_map/ppermute | solution.py:624
  55.8 0.9 %collective-permute-start.7 = (f32[16,1024]{1,0:T(8,128)S(1)}, f32[16,1024]{1,0:T(8,128)S(1)}, u32[]{:S(2)}, u32[]{:S(2)}) collective-permute-start(f32[16,1024]{1,0:T(8,128)S(1)} %get-tuple-element.26), channel_id=1, source_target_pairs={{0,5},{1,4},{2,7},{3,6},{4,1},{5,0},{6,3},{7,2},{8,13},{9,12},{10,... | collective-permute-start | bytes 196616 | tf_op jit(solution)/shard_map/ppermute | solution.py:624
  56.7 1.5 %collective-permute-start.8 = (f32[16,1024]{1,0:T(8,128)S(1)}, f32[16,1024]{1,0:T(8,128)S(1)}, u32[]{:S(2)}, u32[]{:S(2)}) collective-permute-start(f32[16,1024]{1,0:T(8,128)S(1)} %get-tuple-element.27), channel_id=1, source_target_pairs={{0,6},{1,7},{2,0},{3,1},{4,2},{5,3},{6,4},{7,5},{8,14},{9,15},{10,... | collective-permute-start | bytes 196616 | tf_op jit(solution)/shard_map/ppermute | solution.py:624
  58.2 0.5 collective-permute-start.9
  58.8 0.4 collective-permute-done.5.refs_3_
  59.1 1.6 %collective-permute-done.6.refs_4_ = f32[16,1024]{1,0:T(8,128)S(1)} collective-permute-done((f32[16,1024]{1,0:T(8,128)S(1)}, f32[16,1024]{1,0:T(8,128)S(1)}, u32[]{:S(2)}, u32[]{:S(2)}) %collective-permute-start.6) | collective-permute-done | bytes 65568 | tf_op jit(solution)/shard_map/ppermute | solution.py:624
  60.8 1.3 %collective-permute-done.7.refs_5_ = f32[16,1024]{1,0:T(8,128)S(1)} collective-permute-done((f32[16,1024]{1,0:T(8,128)S(1)}, f32[16,1024]{1,0:T(8,128)S(1)}, u32[]{:S(2)}, u32[]{:S(2)}) %collective-permute-start.7) | collective-permute-done | bytes 65568 | tf_op jit(solution)/shard_map/ppermute | solution.py:624
  62.1 0.6 collective-permute-done.9.refs_7_
  62.6 1.1 %shard_map.130 = f32[1152,128]{1,0:T(8,128)} custom-call(f32[16,1024]{1,0:T(8,128)S(1)} %get-tuple-element.21.refs_0_, f32[16,1024]{1,0:T(8,128)S(1)} %collective-permute-done.3.refs_1_, f32[16,1024]{1,0:T(8,128)S(1)} %collective-permute-done.4.refs_2_, f32[16,1024]{1,0:T(8,128)S(1)} %collective-permute-done.5.refs_3_, ...), custom_call_target="tpu_custom_call" | custom-call | tf_op jit(solution)/shard_map/pallas_call | solution.py:564
  (21 shorter events, 0.1 us)
Async XLA Ops:
  0.0 22.2 %copy-start.3 = (bf16[2,256,256]{2,1,0:T(8,128)(2,1)S(1)}, bf16[2,256,256]{2,1,0:T(8,128)(2,1)}, u32[]{:S(2)}) copy-start(bf16[2,256,256]{2,1,0:T(8,128)(2,1)} %constant.24.clone.refs_4_) | copy-start | bytes 786436
  0.0 44.3 %copy-start.8 = (f32[224,128]{1,0:T(8,128)S(1)}, f32[224,128]{1,0:T(8,128)}, u32[]{:S(2)}) copy-start(f32[224,128]{1,0:T(8,128)} %constant.31.clone.lam_x_ref) | copy-start | bytes 344068
  0.0 44.3 %copy-start.9 = (f32[1,128]{1,0:T(1,128)S(1)}, f32[1,128]{1,0:T(1,128)}, u32[]{:S(2)}) copy-start(f32[1,128]{1,0:T(1,128)} %constant.32.clone.lam_y_ref) | copy-start | bytes 1540
  5.9 38.4 %copy-start = (bf16[224,1344]{1,0:T(8,128)(2,1)S(1)}, bf16[224,1344]{1,0:T(8,128)(2,1)}, u32[]{:S(2)}) copy-start(bf16[224,1344]{1,0:T(8,128)(2,1)} %constant.28.clone.pair_x_ref) | copy-start | bytes 1806340
  5.9 38.4 %copy-start.1 = (bf16[192,672]{1,0:T(8,128)(2,1)S(1)}, bf16[192,672]{1,0:T(8,128)(2,1)}, u32[]{:S(2)}) copy-start(bf16[192,672]{1,0:T(8,128)(2,1)} %constant.30.clone.out_x_ref) | copy-start | bytes 774148
  5.9 38.4 %copy-start.2 = (bf16[224,576]{1,0:T(8,128)(2,1)S(1)}, bf16[224,576]{1,0:T(8,128)(2,1)}, u32[]{:S(2)}) copy-start(bf16[224,576]{1,0:T(8,128)(2,1)} %constant.26.clone.in_x_ref) | copy-start | bytes 774148
  5.9 38.4 %copy-start.4 = (bf16[384,256]{1,0:T(8,128)(2,1)S(1)}, bf16[384,256]{1,0:T(8,128)(2,1)}, u32[]{:S(2)}) copy-start(bf16[384,256]{1,0:T(8,128)(2,1)} %constant.27.clone.pair_y_ref) | copy-start | bytes 589828
  5.9 38.4 %copy-start.5 = (bf16[256,256]{1,0:T(8,128)(2,1)S(1)}, bf16[256,256]{1,0:T(8,128)(2,1)}, u32[]{:S(2)}) copy-start(bf16[256,256]{1,0:T(8,128)(2,1)} %constant.29.clone.out_y_ref) | copy-start | bytes 393220
  5.9 38.4 %copy-start.6 = (bf16[256,256]{1,0:T(8,128)(2,1)S(1)}, bf16[256,256]{1,0:T(8,128)(2,1)}, u32[]{:S(2)}) copy-start(bf16[256,256]{1,0:T(8,128)(2,1)} %constant.25.clone.in_y_ref) | copy-start | bytes 393220
  6.0 8.3 %collective-permute-start = (f32[256,128]{1,0:T(8,128)}, f32[256,128]{1,0:T(8,128)S(1)}, u32[]{:S(2)}, u32[]{:S(2)}) collective-permute-start(f32[256,128]{1,0:T(8,128)} %get-tuple-element.18), channel_id=1, source_target_pairs={{0,8},{8,0},{16,24},{24,16},{1,9},{9,1},{17,25},{25,17},{2,10},{10... | collective-permute-start | bytes 393224 | tf_op jit(solution)/shard_map/ppermute | solution.py:601
  9.1 13.1 %collective-permute-start.1 = (f32[256,128]{1,0:T(8,128)}, f32[256,128]{1,0:T(8,128)S(1)}, u32[]{:S(2)}, u32[]{:S(2)}) collective-permute-start(f32[256,128]{1,0:T(8,128)} %get-tuple-element.19), channel_id=1, source_target_pairs={{0,16},{8,24},{16,0},{24,8},{1,17},{9,25},{17,1},{25,9},{2,18},{10... | collective-permute-start | bytes 393224 | tf_op jit(solution)/shard_map/ppermute | solution.py:601
  11.7 10.5 %collective-permute-start.2 = (f32[256,128]{1,0:T(8,128)}, f32[256,128]{1,0:T(8,128)S(1)}, u32[]{:S(2)}, u32[]{:S(2)}) collective-permute-start(f32[256,128]{1,0:T(8,128)} %get-tuple-element.20), channel_id=1, source_target_pairs={{0,24},{8,16},{16,8},{24,0},{1,25},{9,17},{17,9},{25,1},{2,26},{10... | collective-permute-start | bytes 393224 | tf_op jit(solution)/shard_map/ppermute | solution.py:601
  22.2 0.9 %copy-start.7 = (f32[256,128]{1,0:T(8,128)S(1)}, f32[256,128]{1,0:T(8,128)}, u32[]{:S(2)}) copy-start(f32[256,128]{1,0:T(8,128)} %get-tuple-element.17.refs_0_) | copy-start | bytes 393220
  52.4 4.3 %collective-permute-start.3 = (f32[16,1024]{1,0:T(8,128)S(1)}, f32[16,1024]{1,0:T(8,128)S(1)}, u32[]{:S(2)}, u32[]{:S(2)}) collective-permute-start(f32[16,1024]{1,0:T(8,128)S(1)} %get-tuple-element.22), channel_id=1, source_target_pairs={{0,1},{1,0},{2,3},{3,2},{4,5},{5,4},{6,7},{7,6},{8,9},{9,8},{10,11... | collective-permute-start | bytes 196616 | tf_op jit(solution)/shard_map/ppermute | solution.py:624
  52.5 5.7 %collective-permute-start.4 = (f32[16,1024]{1,0:T(8,128)S(1)}, f32[16,1024]{1,0:T(8,128)S(1)}, u32[]{:S(2)}, u32[]{:S(2)}) collective-permute-start(f32[16,1024]{1,0:T(8,128)S(1)} %get-tuple-element.23), channel_id=1, source_target_pairs={{0,2},{1,3},{2,4},{3,5},{4,6},{5,7},{6,0},{7,1},{8,10},{9,11},{10,... | collective-permute-start | bytes 196616 | tf_op jit(solution)/shard_map/ppermute | solution.py:624
  53.8 5.3 %collective-permute-start.5 = (f32[16,1024]{1,0:T(8,128)S(1)}, f32[16,1024]{1,0:T(8,128)S(1)}, u32[]{:S(2)}, u32[]{:S(2)}) collective-permute-start(f32[16,1024]{1,0:T(8,128)S(1)} %get-tuple-element.24), channel_id=1, source_target_pairs={{0,3},{1,2},{2,5},{3,4},{4,7},{5,6},{6,1},{7,0},{8,11},{9,10},{10,... | collective-permute-start | bytes 196616 | tf_op jit(solution)/shard_map/ppermute | solution.py:624
  55.0 5.7 %collective-permute-start.6 = (f32[16,1024]{1,0:T(8,128)S(1)}, f32[16,1024]{1,0:T(8,128)S(1)}, u32[]{:S(2)}, u32[]{:S(2)}) collective-permute-start(f32[16,1024]{1,0:T(8,128)S(1)} %get-tuple-element.25), channel_id=1, source_target_pairs={{0,4},{1,5},{2,6},{3,7},{4,0},{5,1},{6,2},{7,3},{8,12},{9,13},{10,... | collective-permute-start | bytes 196616 | tf_op jit(solution)/shard_map/ppermute | solution.py:624
  55.8 6.2 %collective-permute-start.7 = (f32[16,1024]{1,0:T(8,128)S(1)}, f32[16,1024]{1,0:T(8,128)S(1)}, u32[]{:S(2)}, u32[]{:S(2)}) collective-permute-start(f32[16,1024]{1,0:T(8,128)S(1)} %get-tuple-element.26), channel_id=1, source_target_pairs={{0,5},{1,4},{2,7},{3,6},{4,1},{5,0},{6,3},{7,2},{8,13},{9,12},{10,... | collective-permute-start | bytes 196616 | tf_op jit(solution)/shard_map/ppermute | solution.py:624
  56.7 5.3 %collective-permute-start.8 = (f32[16,1024]{1,0:T(8,128)S(1)}, f32[16,1024]{1,0:T(8,128)S(1)}, u32[]{:S(2)}, u32[]{:S(2)}) collective-permute-start(f32[16,1024]{1,0:T(8,128)S(1)} %get-tuple-element.27), channel_id=1, source_target_pairs={{0,6},{1,7},{2,0},{3,1},{4,2},{5,3},{6,4},{7,5},{8,14},{9,15},{10,... | collective-permute-start | bytes 196616 | tf_op jit(solution)/shard_map/ppermute | solution.py:624
  58.2 4.4 %collective-permute-start.9 = (f32[16,1024]{1,0:T(8,128)S(1)}, f32[16,1024]{1,0:T(8,128)S(1)}, u32[]{:S(2)}, u32[]{:S(2)}) collective-permute-start(f32[16,1024]{1,0:T(8,128)S(1)} %get-tuple-element.28), channel_id=1, source_target_pairs={{0,7},{1,6},{2,1},{3,0},{4,3},{5,2},{6,5},{7,4},{8,15},{9,14},{10,... | collective-permute-start | bytes 196616 | tf_op jit(solution)/shard_map/ppermute | solution.py:624

commit v4 on v3

--- a/solution.py
+++ b/solution.py
@@ -174,17 +174,21 @@
             for p in range(self.n_ey)
         ]
         self.block_y = max(len(found) for found in self.inner)
-        share = -(-(self.block_x * self.block_y + 2) // self.n_mode)
-        self.share = ceil_to(share, LANES if share > 64 else 32)
-        self.lane_nodes = self.share * self.n_mode
+        self.cuts = 2 if self.elems % 2 == 0 else 1
+        self.cut_elems = self.elems // self.cuts
+        self.cut_x = self.order * self.cut_elems + 1
+        share = -(-self.cut_x * self.block_y // self.n_mode)
+        self.share = ceil_to(share, LANES if share > 64 else 16)
+        self.cut_nodes = self.share * self.n_mode
+        self.lane_nodes = ceil_to(self.block_x * self.block_y + 2, LANES)
         self.columns = 2 * self.planes
         self.spots = self.n_ex * self.n_ey
         self.own = self.columns // self.spots
         self.folds = self.own // PARTS
         self.fold_width = LANES // self.folds
         self.points = self.nodes + 2
-        self.x_nodes = self.n_ex * self.block_x
-        self.x_pad = ceil_to(self.x_nodes, 16)
+        self.x_cuts = self.n_ex * self.cuts * self.cut_x
+        self.x_pad = ceil_to(max(self.x_cuts, self.n_ex * self.block_x), 16)
         self.x_eig = self.elems_total * self.points
         self.y_eig = self.rows_total * self.points
         self.fine = ceil_to(self.gauss * self.gauss, 16)
@@ -243,9 +247,13 @@
         mass_y[index] += weights * (heights[f] / 2.0)
     stiff_xx, mass_xx = to_x @ stiff_x @ to_x.T, (to_x * mass_x) @ to_x.T
     stiff_yy, mass_yy = to_y @ stiff_y @ to_y.T, (to_y * mass_y) @ to_y.T
-    list_x = [(sz.order * sz.elems * p + i) % grid_x for p in range(sz.n_ex) for i in range(sz.block_x)]
-    block_x = np.zeros((sz.x_eig, sz.x_pad))
-    block_x[:, : sz.x_nodes] = to_x[:, list_x]
+    def block_x(blocks, elems):
+        length = sz.order * elems + 1
+        nodes_of = [(sz.order * elems * p + i) % grid_x for p in range(blocks) for i in range(length)]
+        table = np.zeros((sz.x_eig, sz.x_pad))
+        table[:, : len(nodes_of)] = to_x[:, nodes_of]
+        return table
+
     width, folds = sz.fold_width, sz.folds
     block_y = np.zeros((width, width))
     for place in range(sz.n_ey):
@@ -276,11 +284,11 @@
         back=np.stack([beside(table) for table in back]),
         waves=np.stack(high_low(waves)),
         in_y=one_dot(block_y),
-        in_x=beside(block_x),
+        in_x=beside(block_x(sz.n_ex * sz.cuts, sz.cut_elems)),
         pair_y=np.concatenate([heads, heads, tails], 0),
         pair_x=beside(np.concatenate([stiff_xx, mass_xx], 1)),
         out_y=one_dot(block_y.T),
-        out_x=beside(block_x.T),
+        out_x=beside(block_x(sz.n_ex, sz.elems).T),
         lam_x=np.asarray(np.tile(lam_x, sz.elems_total)[:, None] * np.ones((1, LANES)), np.float32),
         lam_y=np.asarray(lam_lanes.reshape(1, LANES), np.float32),
     )
@@ -324,6 +332,7 @@
 def advect_kernel(
     sz,
     heights,
+    cut,
     stream_hbm,
     normal_hbm,
     lift_hbm,
@@ -349,17 +358,15 @@
     spots = sz.elems * rows
     half = lane_index((fine, LANES)) < sz.planes
     column, step = sz.nodes * sz.block_y, sz.order * sz.block_y
-    length = sz.block_x * sz.block_y
-    total_ref[pl.ds(length // 8 * 8, sz.lane_nodes - length // 8 * 8), :] = jnp.zeros(
-        (sz.lane_nodes - length // 8 * 8, LANES), jnp.float32
-    )
+    full = sz.cut_x * sz.block_y // 8 * 8
+    total_ref[pl.ds(full, sz.cut_nodes - full), :] = jnp.zeros((sz.cut_nodes - full, LANES), jnp.float32)
     carry = None
     for copy in fetched[:3]:
         copy.wait()
-    for e in range(sz.elems):
+    for e in range(sz.cut_elems):
         speeds = jnp.concatenate(
             [
-                ref[pl.ds(e * rows + f, count, stride=spots), :]
+                ref[pl.ds((cut * sz.cut_elems + e) * rows + f, count, stride=spots), :]
                 for f in range(rows)
                 for ref in (stream_ref, normal_ref)
             ],
@@ -383,7 +390,7 @@
         if carry is not None:
             head = jnp.concatenate([carry, jnp.zeros((column - carry.shape[0], LANES), jnp.float32)], 0)
             weak = weak + head
-        if e < sz.elems - 1:
+        if e < sz.cut_elems - 1:
             total_ref[pl.ds(e * step, step), :] = weak[:step]
             carry = weak[step:]
         else:
@@ -395,7 +402,7 @@
 
 
 def transform_kernel(sz, *refs):
-    weak_refs, (waves_ref, out_ref, mixed_ref, signal_ref) = refs[:-4], refs[-4:]
+    weak_refs, (waves_ref, out_ref, mixed_ref, signal_ref) = refs[: sz.n_mode], refs[-4:]
     spot = lax.axis_index("mode")
     for step, weak_ref in enumerate(weak_refs):
         turned = weak_ref[...].T
@@ -416,20 +423,14 @@
 
 def smooth_kernel(
     sz,
-    terms_ref,
-    in_y_ref,
-    in_x_ref,
-    pair_y_ref,
-    pair_x_ref,
-    out_y_ref,
-    out_x_ref,
-    lam_x_ref,
-    lam_y_ref,
-    *others,
+    *refs,
 ):
-    out_refs, (field_ref, first_ref, work_ref) = others[:-3], others[-3:]
+    terms_refs, out_refs, (field_ref, first_ref, work_ref) = refs[: sz.cuts], refs[sz.cuts + 8 : -3], refs[-3:]
+    in_y_ref, in_x_ref, pair_y_ref, pair_x_ref, out_y_ref, out_x_ref, lam_x_ref, lam_y_ref = refs[
+        sz.cuts : sz.cuts + 8
+    ]
     width, folds, strip = sz.fold_width, sz.folds, sz.block_y
-    tiles = -(-sz.lane_nodes // LANES)
+    tiles = -(-sz.cut_nodes // LANES)
     lanes = lane_index((PARTS, LANES))
     x_pad, x_eig = sz.x_pad, sz.x_eig
     place, spot = lax.axis_index("ey"), lax.axis_index("ex")
@@ -437,23 +438,23 @@
     first_mode = device * (sz.own // 4)
 
     for c in range(PARTS):
-        field_ref[pl.ds(c * x_pad + sz.x_nodes, x_pad - sz.x_nodes), :] = jnp.zeros(
-            (x_pad - sz.x_nodes, LANES), jnp.float32
+        field_ref[pl.ds(c * x_pad + sz.x_cuts, x_pad - sz.x_cuts), :] = jnp.zeros(
+            (x_pad - sz.x_cuts, LANES), jnp.float32
         )
-    for p in range(sz.n_ex):
+    for p, cut in [(p, cut) for p in range(sz.n_ex) for cut in range(sz.cuts)]:
         block = (spot + p) % sz.n_ex
         held = {}
         for q in range(sz.n_ey):
             for fold in range(folds):
                 whole = jnp.concatenate(
                     [
-                        terms_ref[(z * sz.n_ex + block) * sz.n_ey + q, pl.ds(fold * PARTS, PARTS), :]
+                        terms_refs[cut][(z * sz.n_ex + block) * sz.n_ey + q, pl.ds(fold * PARTS, PARTS), :]
                         for z in range(sz.n_mode)
                     ],
                     1,
                 )
                 held[q, fold] = [whole[:, t * LANES : (t + 1) * LANES] for t in range(tiles)]
-        for i in range(sz.block_x):
+        for i in range(sz.cut_x):
             start = i * strip
             t, r = start // LANES, start % LANES
             result = jnp.zeros((PARTS, LANES), jnp.float32)
@@ -465,7 +466,7 @@
                     goal = fold * width + q * strip
                     moved = pltpu.roll(source, (goal - r) % LANES, 1) if goal != r else source
                     result = jnp.where((lanes >= goal) & (lanes < goal + strip), moved, result)
-            field_ref[pl.ds(p * sz.block_x + i, PARTS, stride=x_pad), :] = result
+            field_ref[pl.ds((p * sz.cuts + cut) * sz.cut_x + i, PARTS, stride=x_pad), :] = result
 
     parts = dot(along(field_ref[...]), in_y_ref[...])
     field_ref[...] = parts[:, :LANES] + parts[:, LANES:]
@@ -520,14 +521,14 @@
                             if old is None:
                                 old = jnp.zeros((PARTS, LANES), jnp.float32)
                             made[q, fold, tile] = jnp.where((lanes >= low) & (lanes < high), moved, old)
-        for (q, fold, tile), value in made.items():
-            last = min(LANES, sz.lane_nodes - tile * LANES)
-            where = (pl.ds(fold * PARTS, PARTS), pl.ds(tile * LANES, last))
-            for turn in range(sz.n_ey):
-
-                @pl.when((place + turn) % sz.n_ey == q)
-                def _(out_ref=out_refs[p * sz.n_ey + turn], value=value[:, :last], where=where):
-                    out_ref[where] = value
+        for fold in range(folds):
+            for tile in range(sz.lane_nodes // LANES):
+                for turn in range(sz.n_ey):
+                    chosen = jnp.zeros((PARTS, LANES), jnp.float32)
+                    for q in range(sz.n_ey):
+                        if (q, fold, tile) in made:
+                            chosen = jnp.where((place + turn) % sz.n_ey == q, made[q, fold, tile], chosen)
+                    out_refs[p * sz.n_ey + turn][pl.ds(fold * PARTS, PARTS), pl.ds(tile * LANES, LANES)] = chosen
 
 
 def spread_kernel(sz, *refs):
@@ -560,11 +561,13 @@
             out_ref[pl.ds(first, sz.elems, stride=sz.rows), :] = blank
 
 
-def call(kernel, shapes, operands, scratch=(), space=pltpu.VMEM, limit=16):
+def call(kernel, shapes, operands, scratch=(), spaces=pltpu.VMEM, limit=16):
+    if not isinstance(spaces, list):
+        spaces = [spaces] * len(operands)
     made = pl.pallas_call(
         kernel,
         out_shape=[jax.ShapeDtypeStruct(shape, jnp.float32) for shape in shapes],
-        in_specs=[pl.BlockSpec(memory_space=space) for _ in operands],
+        in_specs=[pl.BlockSpec(memory_space=space) for space in spaces],
         out_specs=[pl.BlockSpec(memory_space=pltpu.VMEM) for _ in shapes],
         scratch_shapes=[pltpu.VMEM(each, jnp.float32) if isinstance(each, tuple) else each for each in scratch],
         compiler_params=pltpu.CompilerParams(vmem_limit_bytes=limit * 2**20),
@@ -576,42 +579,51 @@
     flat = sz.nodes * sz.nodes * sz.elems * sz.rows
     table = {name: jnp.asarray(value) for name, value in tables.items() if name != "heights"}
     heights = [float(height) for height in tables["heights"]]
-    weak = call(
-        functools.partial(advect_kernel, sz, heights),
-        [(sz.share, LANES)] * sz.n_mode,
-        [
-            stream_speed.reshape(flat, sz.planes),
-            normal_speed.reshape(flat, sz.planes),
-            table["lift"],
-            table["back"],
-        ],
-        [
-            (sz.lane_nodes, LANES),
-            (flat, sz.planes),
-            (flat, sz.planes),
-            pltpu.VMEM(tables["lift"].shape, jnp.bfloat16),
-            pltpu.VMEM(tables["back"].shape[1:], jnp.bfloat16),
-            pltpu.SemaphoreType.DMA((4,)),
-        ],
-        pltpu.HBM,
-        60,
-    )
-    for step in sorted(range(1, sz.n_mode), key=lambda each: (each & -each, each), reverse=True):
-        pairs = [(z, partner(z, step, sz.n_mode)) for z in range(sz.n_mode)]
-        weak[step] = lax.ppermute(weak[step], "mode", pairs)
-    (spectra,) = call(
-        functools.partial(transform_kernel, sz),
-        [(2 * sz.planes_total, sz.share)],
-        [*weak, table["waves"]],
-        [(-(-sz.share // LANES), 2 * sz.planes_total, LANES), (2, sz.planes_total, sz.share)],
-    )
-    spectra = spectra.reshape(sz.n_mode * sz.spots, sz.own, sz.share)
-    terms = lax.all_to_all(spectra, ("mode", "ex", "ey"), split_axis=0, concat_axis=0, tiled=True)
+    weak, made = [], []
+    for cut in range(sz.cuts):
+        weak.append(
+            call(
+                functools.partial(advect_kernel, sz, heights, cut),
+                [(sz.share, LANES)] * sz.n_mode,
+                [
+                    stream_speed.reshape(flat, sz.planes),
+                    normal_speed.reshape(flat, sz.planes),
+                    table["lift"],
+                    table["back"],
+                ],
+                [
+                    (sz.cut_nodes, LANES),
+                    (flat, sz.planes),
+                    (flat, sz.planes),
+                    pltpu.VMEM(tables["lift"].shape, jnp.bfloat16),
+                    pltpu.VMEM(tables["back"].shape[1:], jnp.bfloat16),
+                    pltpu.SemaphoreType.DMA((4,)),
+                ],
+                pltpu.HBM,
+                60,
+            )
+        )
+        made.append(weak[cut][0])
+        for step in sorted(range(1, sz.n_mode), key=lambda each: (each & -each, each), reverse=True):
+            pairs = [(z, partner(z, step, sz.n_mode)) for z in range(sz.n_mode)]
+            weak[cut][step] = lax.ppermute(weak[cut][step], "mode", pairs)
+    terms, ahead = [], made[-1]
+    for cut in range(sz.cuts):
+        (spectra,) = call(
+            functools.partial(transform_kernel, sz),
+            [(2 * sz.planes_total, sz.share)],
+            [*weak[cut], ahead, table["waves"]],
+            [(-(-sz.share // LANES), 2 * sz.planes_total, LANES), (2, sz.planes_total, sz.share)],
+            [pltpu.VMEM] * sz.n_mode + [pl.ANY, pltpu.VMEM],
+        )
+        spectra = spectra.reshape(sz.n_mode * sz.spots, sz.own, sz.share)
+        terms.append(lax.all_to_all(spectra, ("mode", "ex", "ey"), split_axis=0, concat_axis=0, tiled=True))
+        ahead = terms[cut]
     names = ("in_y", "in_x", "pair_y", "pair_x", "out_y", "out_x", "lam_x", "lam_y")
     solved = call(
         functools.partial(smooth_kernel, sz),
         [(sz.own, sz.lane_nodes)] * sz.spots,
-        [terms] + [table[name] for name in names],
+        terms + [table[name] for name in names],
         [(PARTS * sz.x_pad, LANES), (PARTS * sz.x_eig, LANES), (PARTS * sz.x_eig, LANES)],
     )
     for step in range(1, sz.spots):

time: 63.9 us -> 71 us (1.11)
  starting transfers between devices: 12 us -> 20.4 us
  blocking collectives: 20.6 us -> 14.1 us
  Pallas kernels: 15.7 us -> 19 us
  waiting for transfers between devices: 14.4 us -> 15.3 us
  local copies, waits for them, and re-layouts: 0.96 us -> 1.74 us
    all_to_all x1, blocking collectives: 20.6 us -> 14.1 us  [on_device(): lax.all_to_all(spectra, ('mode', 'ex', 'ey'), split_axis=0, concat_axis=0...]
    all_to_all x0 -> x1, starting transfers between devices: none -> 4.65 us  [on_device(): lax.all_to_all(spectra, ('mode', 'ex', 'ey'), split_axis=0, concat_axis=0...]
    ppermute x3 -> x6, starting transfers between devices: 5.72 us -> 10.1 us  [on_device(): weak[cut][step] = lax.ppermute(weak[cut][step], 'mode', pairs)]
    pallas_call x4 -> x6, Pallas kernels: 15.7 us -> 19 us  [call(): pl.pallas_call(kernel, out_shape=[jax.ShapeDtypeStruct(shape, jnp.float32...]
    unnamed x20 -> x24, local copies, waits for them, and re-layouts: 0.96 us -> 1.74 us
    ppermute x7, starting transfers between devices: 6.31 us -> 5.6 us  [on_device(): solved[step] = lax.ppermute(solved[step], ('ex', 'ey'), pairs)]
    ppermute x3 -> x6, waiting for transfers between devices: 10.5 us -> 11.1 us  [on_device(): weak[cut][step] = lax.ppermute(weak[cut][step], 'mode', pairs)]
  transfers between devices with their start and end apart: 10 -> 14, of which waited for: 6 -> 9; matrix products, arithmetic and copies ran while one was open for 0% -> 0% of each run, Pallas kernels for 0% -> 7%
where the time goes in v4:
time: 71 us; the launch traced here: 70.7 us
  starting transfers between devices  20.4 us (29%)
  Pallas kernels  19 us (27%)
  waiting for transfers between devices  15.3 us (22%)
  blocking collectives  14.1 us (20%)
  local copies, waits for them, and re-layouts  1.74 us (2%)
    pallas_call x6, Pallas kernels, call(): pl.pallas_call(kernel, out_shape=[jax.ShapeDtypeStruct(shape, jnp.float32...  19 us
    all_to_all x1, blocking collectives, on_device(): lax.all_to_all(spectra, ('mode', 'ex', 'ey'), split_axis=0, concat_axis=0...  14.1 us
    ppermute x6, waiting for transfers between devices, on_device(): weak[cut][step] = lax.ppermute(weak[cut][step], 'mode', pairs)  11.1 us
    ppermute x6, starting transfers between devices, on_device(): weak[cut][step] = lax.ppermute(weak[cut][step], 'mode', pairs)  10.1 us
    ppermute x7, starting transfers between devices, on_device(): solved[step] = lax.ppermute(solved[step], ('ex', 'ey'), pairs)  5.6 us
    all_to_all x1, starting transfers between devices, on_device(): lax.all_to_all(spectra, ('mode', 'ex', 'ey'), split_axis=0, concat_axis=0...  4.65 us
    ppermute x7, waiting for transfers between devices, on_device(): solved[step] = lax.ppermute(solved[step], ('ex', 'ey'), pairs)  4.19 us
    unnamed x24, local copies, waits for them, and re-layouts  1.74 us
  transfers between devices with their start and end apart: 14, of which 9 were waited for; matrix products, arithmetic and copies ran while one was open for 0% of the time, Pallas kernels for 7%

profile of v4, /device:TPU:0, one launch (start us, length us, event | category | flops | bytes accessed | tf_op | source)
XLA Modules:
  0.0 70.7 jit_solution(9889236057425893197)
XLA Ops:
  0.0 4.6 %shard_map.127 = (f32[128,128]{1,0:T(8,128)}, f32[128,128]{1,0:T(8,128)}, f32[128,128]{1,0:T(8,128)}, f32[128,128]{1,0:T(8,128)}) custom-call(f32[1152,64]{1,0:T(8,128)} %bitcast.6, f32[1152,64]{1,0:T(8,128)} %bitcast.8, bf16[1008,432]{1,0:T(8,128)(2,1)} %constant.22.clone.lift_hbm, bf16[2,264,2016]{2,1,0:T(8,128)(2,1)} %constant.23.clone.back_hbm), custom_call_target="tpu_custom_call" | custom-call | tf_op jit(solution)/shard_map/pallas_call | solution.py:567
  4.6 3.1 %collective-permute-start = (f32[128,128]{1,0:T(8,128)}, f32[128,128]{1,0:T(8,128)S(1)}, u32[]{:S(2)}, u32[]{:S(2)}) collective-permute-start(f32[128,128]{1,0:T(8,128)} %get-tuple-element.22), channel_id=1, source_target_pairs={{0,8},{8,0},{16,24},{24,16},{1,9},{9,1},{17,25},{25,17},{2,10},{10... | collective-permute-start | bytes 196616 | tf_op jit(solution)/shard_map/ppermute | solution.py:609
  7.6 2.6 %collective-permute-start.1 = (f32[128,128]{1,0:T(8,128)}, f32[128,128]{1,0:T(8,128)S(1)}, u32[]{:S(2)}, u32[]{:S(2)}) collective-permute-start(f32[128,128]{1,0:T(8,128)} %get-tuple-element.23), channel_id=1, source_target_pairs={{0,16},{8,24},{16,0},{24,8},{1,17},{9,25},{17,1},{25,9},{2,18},{10... | collective-permute-start | bytes 196616 | tf_op jit(solution)/shard_map/ppermute | solution.py:609
  10.3 4.7 %shard_map.128 = (f32[128,128]{1,0:T(8,128)}, f32[128,128]{1,0:T(8,128)}, f32[128,128]{1,0:T(8,128)}, f32[128,128]{1,0:T(8,128)}) custom-call(f32[1152,64]{1,0:T(8,128)} %bitcast.7, f32[1152,64]{1,0:T(8,128)} %bitcast.9, bf16[1008,432]{1,0:T(8,128)(2,1)} %constant.22.clone.lift_hbm, bf16[2,264,2016]{2,1,0:T(8,128)(2,1)} %constant.23.clone.back_hbm), custom_call_target="tpu_custom_call" | custom-call | tf_op jit(solution)/shard_map/pallas_call | solution.py:567
  15.1 1.4 %collective-permute-done.2.refs_3_ = f32[128,128]{1,0:T(8,128)S(1)} collective-permute-done((f32[128,128]{1,0:T(8,128)}, f32[128,128]{1,0:T(8,128)S(1)}, u32[]{:S(2)}, u32[]{:S(2)}) %collective-permute-start.2) | collective-permute-done | bytes 65568 | tf_op jit(solution)/shard_map/ppermute | solution.py:609
  16.5 0.8 %copy-done.4 = f32[128,128]{1,0:T(8,128)S(1)} copy-done((f32[128,128]{1,0:T(8,128)S(1)}, f32[128,128]{1,0:T(8,128)}, u32[]{:S(2)}) %copy-start.4) | copy-done | bytes 65560
  17.4 1.2 %shard_map.129 = f32[512,128]{1,0:T(8,128)} custom-call(f32[128,128]{1,0:T(8,128)S(1)} %copy-done.10, f32[128,128]{1,0:T(8,128)S(1)} %collective-permute-done.refs_1_, f32[128,128]{1,0:T(8,128)S(1)} %collective-permute-done.1.refs_2_, f32[128,128]{1,0:T(8,128)S(1)} %collective-permute-done.2.refs_3_, f32[128,128]{1,0:T(8,128)S(1)} %copy-done.4, ...), custom_call_target="tpu_custom_call" | custom-call | tf_op jit(solution)/shard_map/pallas_call | solution.py:567
  18.6 4.7 %all-to-all-start = ((f32[32,16,128]{2,1,0:T(8,128)}), f32[32,16,128]{2,1,0:T(8,128)S(1)}, u32[]{:S(2)}, u32[]{:S(2)}) async-start(f32[32,16,128]{2,1,0:T(8,128)} %bitcast.2), calls=%async_computation | async-start | bytes 524288 | tf_op jit(solution)/shard_map/all_to_all | solution.py:620
  23.3 1.8 %collective-permute-start.3 = (f32[128,128]{1,0:T(8,128)}, f32[128,128]{1,0:T(8,128)S(1)}, u32[]{:S(2)}, u32[]{:S(2)}) collective-permute-start(f32[128,128]{1,0:T(8,128)} %get-tuple-element.26), channel_id=1, source_target_pairs={{0,8},{8,0},{16,24},{24,16},{1,9},{9,1},{17,25},{25,17},{2,10},{10... | collective-permute-start | bytes 196616 | tf_op jit(solution)/shard_map/ppermute | solution.py:609
  25.1 2.4 %collective-permute-start.4 = (f32[128,128]{1,0:T(8,128)}, f32[128,128]{1,0:T(8,128)S(1)}, u32[]{:S(2)}, u32[]{:S(2)}) collective-permute-start(f32[128,128]{1,0:T(8,128)} %get-tuple-element.27), channel_id=1, source_target_pairs={{0,16},{8,24},{16,0},{24,8},{1,17},{9,25},{17,1},{25,9},{2,18},{10... | collective-permute-start | bytes 196616 | tf_op jit(solution)/shard_map/ppermute | solution.py:609
  27.7 3.0 %collective-permute-done.3.refs_1_ = f32[128,128]{1,0:T(8,128)S(1)} collective-permute-done((f32[128,128]{1,0:T(8,128)}, f32[128,128]{1,0:T(8,128)S(1)}, u32[]{:S(2)}, u32[]{:S(2)}) %collective-permute-start.3) | collective-permute-done | bytes 65568 | tf_op jit(solution)/shard_map/ppermute | solution.py:609
  30.7 6.7 %collective-permute-done.4.refs_2_ = f32[128,128]{1,0:T(8,128)S(1)} collective-permute-done((f32[128,128]{1,0:T(8,128)}, f32[128,128]{1,0:T(8,128)S(1)}, u32[]{:S(2)}, u32[]{:S(2)}) %collective-permute-start.4) | collective-permute-done | bytes 65568 | tf_op jit(solution)/shard_map/ppermute | solution.py:609
  37.3 0.8 %copy-done.5 = f32[128,128]{1,0:T(8,128)S(1)} copy-done((f32[128,128]{1,0:T(8,128)S(1)}, f32[128,128]{1,0:T(8,128)}, u32[]{:S(2)}) %copy-start.5) | copy-done | bytes 65560
  38.7 14.1 %all_to_all.10.refs_1_ = f32[32,16,128]{2,1,0:T(8,128)S(1)} all-to-all(f32[32,16,128]{2,1,0:T(8,128)S(1)} %bitcast.5), channel_id=1, replica_groups=mesh['mode'=4,'ex'=4,'ey'=2] {'mode','ex','ey'}, dimensions={0} | all-to-all | bytes 524288 | tf_op jit(solution)/shard_map/all_to_all | solution.py:620
  52.9 6.9 %shard_map.131 = (f32[16,1024]{1,0:T(8,128)S(1)}, f32[16,1024]{1,0:T(8,128)S(1)}, f32[16,1024]{1,0:T(8,128)S(1)}, f32[16,1024]{1,0:T(8,128)S(1)}, f32[16,1024]{1...) custom-call(f32[32,16,128]{2,1,0:T(8,128)S(1)} %all-to-all-done.refs_4_.refs_0_, ...), custom_call_target="tpu_custom_call" | custom-call | tf_op jit(solution)/shard_map/pallas_call | solution.py:567
  59.9 0.8 %collective-permute-start.7 = (f32[16,1024]{1,0:T(8,128)S(1)}, f32[16,1024]{1,0:T(8,128)S(1)}, u32[]{:S(2)}, u32[]{:S(2)}) collective-permute-start(f32[16,1024]{1,0:T(8,128)S(1)} %get-tuple-element.31), channel_id=1, source_target_pairs={{0,2},{1,3},{2,4},{3,5},{4,6},{5,7},{6,0},{7,1},{8,10},{9,11},{10,... | collective-permute-start | bytes 196616 | tf_op jit(solution)/shard_map/ppermute | solution.py:636
  60.7 1.4 %collective-permute-start.8 = (f32[16,1024]{1,0:T(8,128)S(1)}, f32[16,1024]{1,0:T(8,128)S(1)}, u32[]{:S(2)}, u32[]{:S(2)}) collective-permute-start(f32[16,1024]{1,0:T(8,128)S(1)} %get-tuple-element.32), channel_id=1, source_target_pairs={{0,3},{1,2},{2,5},{3,4},{4,7},{5,6},{6,1},{7,0},{8,11},{9,10},{10,... | collective-permute-start | bytes 196616 | tf_op jit(solution)/shard_map/ppermute | solution.py:636
  62.1 1.1 %collective-permute-start.9 = (f32[16,1024]{1,0:T(8,128)S(1)}, f32[16,1024]{1,0:T(8,128)S(1)}, u32[]{:S(2)}, u32[]{:S(2)}) collective-permute-start(f32[16,1024]{1,0:T(8,128)S(1)} %get-tuple-element.33), channel_id=1, source_target_pairs={{0,4},{1,5},{2,6},{3,7},{4,0},{5,1},{6,2},{7,3},{8,12},{9,13},{10,... | collective-permute-start | bytes 196616 | tf_op jit(solution)/shard_map/ppermute | solution.py:636
  63.2 0.6 collective-permute-start.10
  63.8 1.3 %collective-permute-start.11 = (f32[16,1024]{1,0:T(8,128)S(1)}, f32[16,1024]{1,0:T(8,128)S(1)}, u32[]{:S(2)}, u32[]{:S(2)}) collective-permute-start(f32[16,1024]{1,0:T(8,128)S(1)} %get-tuple-element.35), channel_id=1, source_target_pairs={{0,6},{1,7},{2,0},{3,1},{4,2},{5,3},{6,4},{7,5},{8,14},{9,15},{10,... | collective-permute-start | bytes 196616 | tf_op jit(solution)/shard_map/ppermute | solution.py:636
  65.1 0.7 %collective-permute-done.7.refs_2_ = f32[16,1024]{1,0:T(8,128)S(1)} collective-permute-done((f32[16,1024]{1,0:T(8,128)S(1)}, f32[16,1024]{1,0:T(8,128)S(1)}, u32[]{:S(2)}, u32[]{:S(2)}) %collective-permute-start.7) | collective-permute-done | bytes 65568 | tf_op jit(solution)/shard_map/ppermute | solution.py:636
  66.3 1.8 %collective-permute-done.9.refs_4_ = f32[16,1024]{1,0:T(8,128)S(1)} collective-permute-done((f32[16,1024]{1,0:T(8,128)S(1)}, f32[16,1024]{1,0:T(8,128)S(1)}, u32[]{:S(2)}, u32[]{:S(2)}) %collective-permute-start.9) | collective-permute-done | bytes 65568 | tf_op jit(solution)/shard_map/ppermute | solution.py:636
  68.1 1.3 %collective-permute-done.10.refs_5_ = f32[16,1024]{1,0:T(8,128)S(1)} collective-permute-done((f32[16,1024]{1,0:T(8,128)S(1)}, f32[16,1024]{1,0:T(8,128)S(1)}, u32[]{:S(2)}, u32[]{:S(2)}) %collective-permute-start.10) | collective-permute-done | bytes 65568 | tf_op jit(solution)/shard_map/ppermute | solution.py:636
  69.6 1.1 %shard_map.132 = f32[1152,128]{1,0:T(8,128)} custom-call(f32[16,1024]{1,0:T(8,128)S(1)} %get-tuple-element.29.refs_0_, f32[16,1024]{1,0:T(8,128)S(1)} %collective-permute-done.6.refs_1_, f32[16,1024]{1,0:T(8,128)S(1)} %collective-permute-done.7.refs_2_, f32[16,1024]{1,0:T(8,128)S(1)} %collective-permute-done.8.refs_3_, ...), custom_call_target="tpu_custom_call" | custom-call | tf_op jit(solution)/shard_map/pallas_call | solution.py:567
  (35 shorter events, 1.7 us)
Async XLA Ops:
  4.6 10.5 %collective-permute-start = (f32[128,128]{1,0:T(8,128)}, f32[128,128]{1,0:T(8,128)S(1)}, u32[]{:S(2)}, u32[]{:S(2)}) collective-permute-start(f32[128,128]{1,0:T(8,128)} %get-tuple-element.22), channel_id=1, source_target_pairs={{0,8},{8,0},{16,24},{24,16},{1,9},{9,1},{17,25},{25,17},{2,10},{10... | collective-permute-start | bytes 196616 | tf_op jit(solution)/shard_map/ppermute | solution.py:609
  7.6 7.5 %collective-permute-start.1 = (f32[128,128]{1,0:T(8,128)}, f32[128,128]{1,0:T(8,128)S(1)}, u32[]{:S(2)}, u32[]{:S(2)}) collective-permute-start(f32[128,128]{1,0:T(8,128)} %get-tuple-element.23), channel_id=1, source_target_pairs={{0,16},{8,24},{16,0},{24,8},{1,17},{9,25},{17,1},{25,9},{2,18},{10... | collective-permute-start | bytes 196616 | tf_op jit(solution)/shard_map/ppermute | solution.py:609
  10.2 6.3 %copy-start = (bf16[2,256,256]{2,1,0:T(8,128)(2,1)S(1)}, bf16[2,256,256]{2,1,0:T(8,128)(2,1)}, u32[]{:S(2)}) copy-start(bf16[2,256,256]{2,1,0:T(8,128)(2,1)} %constant.24.clone.refs_5_) | copy-start | bytes 786436
  10.3 6.3 %copy-start.10 = (f32[128,128]{1,0:T(8,128)S(1)}, f32[128,128]{1,0:T(8,128)}, u32[]{:S(2)}) copy-start(f32[128,128]{1,0:T(8,128)} %get-tuple-element.21.refs_0_) | copy-start | bytes 196612
  10.3 6.3 %collective-permute-start.2 = (f32[128,128]{1,0:T(8,128)}, f32[128,128]{1,0:T(8,128)S(1)}, u32[]{:S(2)}, u32[]{:S(2)}) collective-permute-start(f32[128,128]{1,0:T(8,128)} %get-tuple-element.24), channel_id=1, source_target_pairs={{0,24},{8,16},{16,8},{24,0},{1,25},{9,17},{17,9},{25,1},{2,26},{10... | collective-permute-start | bytes 196616 | tf_op jit(solution)/shard_map/ppermute | solution.py:609
  10.3 42.5 %copy-start.6 = (bf16[384,256]{1,0:T(8,128)(2,1)S(1)}, bf16[384,256]{1,0:T(8,128)(2,1)}, u32[]{:S(2)}) copy-start(bf16[384,256]{1,0:T(8,128)(2,1)} %constant.27.clone.refs_4_) | copy-start | bytes 589828
  10.3 42.5 %copy-start.7 = (bf16[256,256]{1,0:T(8,128)(2,1)S(1)}, bf16[256,256]{1,0:T(8,128)(2,1)}, u32[]{:S(2)}) copy-start(bf16[256,256]{1,0:T(8,128)(2,1)} %constant.29.clone.refs_6_) | copy-start | bytes 393220
  10.3 42.5 %copy-start.8 = (bf16[256,256]{1,0:T(8,128)(2,1)S(1)}, bf16[256,256]{1,0:T(8,128)(2,1)}, u32[]{:S(2)}) copy-start(bf16[256,256]{1,0:T(8,128)(2,1)} %constant.25.clone.refs_2_) | copy-start | bytes 393220
  10.3 42.5 %copy-start.9 = (f32[224,128]{1,0:T(8,128)S(1)}, f32[224,128]{1,0:T(8,128)}, u32[]{:S(2)}) copy-start(f32[224,128]{1,0:T(8,128)} %constant.31.clone.refs_8_) | copy-start | bytes 344068
  10.3 42.5 %copy-start.11 = (f32[1,128]{1,0:T(1,128)S(1)}, f32[1,128]{1,0:T(1,128)}, u32[]{:S(2)}) copy-start(f32[1,128]{1,0:T(1,128)} %constant.32.clone.refs_9_) | copy-start | bytes 1540
  15.0 37.9 %copy-start.1 = (bf16[224,1344]{1,0:T(8,128)(2,1)S(1)}, bf16[224,1344]{1,0:T(8,128)(2,1)}, u32[]{:S(2)}) copy-start(bf16[224,1344]{1,0:T(8,128)(2,1)} %constant.28.clone.refs_5_) | copy-start | bytes 1806340
  15.0 37.9 %copy-start.2 = (bf16[192,672]{1,0:T(8,128)(2,1)S(1)}, bf16[192,672]{1,0:T(8,128)(2,1)}, u32[]{:S(2)}) copy-start(bf16[192,672]{1,0:T(8,128)(2,1)} %constant.30.clone.refs_7_) | copy-start | bytes 774148
  15.0 37.9 %copy-start.3 = (bf16[224,576]{1,0:T(8,128)(2,1)S(1)}, bf16[224,576]{1,0:T(8,128)(2,1)}, u32[]{:S(2)}) copy-start(bf16[224,576]{1,0:T(8,128)(2,1)} %constant.26.clone.refs_3_) | copy-start | bytes 774148
  18.6 18.7 %all-to-all-start = ((f32[32,16,128]{2,1,0:T(8,128)}), f32[32,16,128]{2,1,0:T(8,128)S(1)}, u32[]{:S(2)}, u32[]{:S(2)}) async-start(f32[32,16,128]{2,1,0:T(8,128)} %bitcast.2), calls=%async_computation | async-start | bytes 524288 | tf_op jit(solution)/shard_map/all_to_all | solution.py:620
  23.3 7.4 %collective-permute-start.3 = (f32[128,128]{1,0:T(8,128)}, f32[128,128]{1,0:T(8,128)S(1)}, u32[]{:S(2)}, u32[]{:S(2)}) collective-permute-start(f32[128,128]{1,0:T(8,128)} %get-tuple-element.26), channel_id=1, source_target_pairs={{0,8},{8,0},{16,24},{24,16},{1,9},{9,1},{17,25},{25,17},{2,10},{10... | collective-permute-start | bytes 196616 | tf_op jit(solution)/shard_map/ppermute | solution.py:609
  25.1 12.2 %collective-permute-start.4 = (f32[128,128]{1,0:T(8,128)}, f32[128,128]{1,0:T(8,128)S(1)}, u32[]{:S(2)}, u32[]{:S(2)}) collective-permute-start(f32[128,128]{1,0:T(8,128)} %get-tuple-element.27), channel_id=1, source_target_pairs={{0,16},{8,24},{16,0},{24,8},{1,17},{9,25},{17,1},{25,9},{2,18},{10... | collective-permute-start | bytes 196616 | tf_op jit(solution)/shard_map/ppermute | solution.py:609
  27.5 9.8 %collective-permute-start.5 = (f32[128,128]{1,0:T(8,128)}, f32[128,128]{1,0:T(8,128)S(1)}, u32[]{:S(2)}, u32[]{:S(2)}) collective-permute-start(f32[128,128]{1,0:T(8,128)} %get-tuple-element.28), channel_id=1, source_target_pairs={{0,24},{8,16},{16,8},{24,0},{1,25},{9,17},{17,9},{25,1},{2,26},{10... | collective-permute-start | bytes 196616 | tf_op jit(solution)/shard_map/ppermute | solution.py:609
  59.8 3.9 %collective-permute-start.6 = (f32[16,1024]{1,0:T(8,128)S(1)}, f32[16,1024]{1,0:T(8,128)S(1)}, u32[]{:S(2)}, u32[]{:S(2)}) collective-permute-start(f32[16,1024]{1,0:T(8,128)S(1)} %get-tuple-element.30), channel_id=1, source_target_pairs={{0,1},{1,0},{2,3},{3,2},{4,5},{5,4},{6,7},{7,6},{8,9},{9,8},{10,11... | collective-permute-start | bytes 196616 | tf_op jit(solution)/shard_map/ppermute | solution.py:636
  59.9 5.9 %collective-permute-start.7 = (f32[16,1024]{1,0:T(8,128)S(1)}, f32[16,1024]{1,0:T(8,128)S(1)}, u32[]{:S(2)}, u32[]{:S(2)}) collective-permute-start(f32[16,1024]{1,0:T(8,128)S(1)} %get-tuple-element.31), channel_id=1, source_target_pairs={{0,2},{1,3},{2,4},{3,5},{4,6},{5,7},{6,0},{7,1},{8,10},{9,11},{10,... | collective-permute-start | bytes 196616 | tf_op jit(solution)/shard_map/ppermute | solution.py:636
  60.7 5.6 %collective-permute-start.8 = (f32[16,1024]{1,0:T(8,128)S(1)}, f32[16,1024]{1,0:T(8,128)S(1)}, u32[]{:S(2)}, u32[]{:S(2)}) collective-permute-start(f32[16,1024]{1,0:T(8,128)S(1)} %get-tuple-element.32), channel_id=1, source_target_pairs={{0,3},{1,2},{2,5},{3,4},{4,7},{5,6},{6,1},{7,0},{8,11},{9,10},{10,... | collective-permute-start | bytes 196616 | tf_op jit(solution)/shard_map/ppermute | solution.py:636
  62.1 6.1 %collective-permute-start.9 = (f32[16,1024]{1,0:T(8,128)S(1)}, f32[16,1024]{1,0:T(8,128)S(1)}, u32[]{:S(2)}, u32[]{:S(2)}) collective-permute-start(f32[16,1024]{1,0:T(8,128)S(1)} %get-tuple-element.33), channel_id=1, source_target_pairs={{0,4},{1,5},{2,6},{3,7},{4,0},{5,1},{6,2},{7,3},{8,12},{9,13},{10,... | collective-permute-start | bytes 196616 | tf_op jit(solution)/shard_map/ppermute | solution.py:636
  63.2 6.2 %collective-permute-start.10 = (f32[16,1024]{1,0:T(8,128)S(1)}, f32[16,1024]{1,0:T(8,128)S(1)}, u32[]{:S(2)}, u32[]{:S(2)}) collective-permute-start(f32[16,1024]{1,0:T(8,128)S(1)} %get-tuple-element.34), channel_id=1, source_target_pairs={{0,5},{1,4},{2,7},{3,6},{4,1},{5,0},{6,3},{7,2},{8,13},{9,12},{10,... | collective-permute-start | bytes 196616 | tf_op jit(solution)/shard_map/ppermute | solution.py:636
  63.8 5.7 %collective-permute-start.11 = (f32[16,1024]{1,0:T(8,128)S(1)}, f32[16,1024]{1,0:T(8,128)S(1)}, u32[]{:S(2)}, u32[]{:S(2)}) collective-permute-start(f32[16,1024]{1,0:T(8,128)S(1)} %get-tuple-element.35), channel_id=1, source_target_pairs={{0,6},{1,7},{2,0},{3,1},{4,2},{5,3},{6,4},{7,5},{8,14},{9,15},{10,... | collective-permute-start | bytes 196616 | tf_op jit(solution)/shard_map/ppermute | solution.py:636
  65.8 3.8 %collective-permute-start.12 = (f32[16,1024]{1,0:T(8,128)S(1)}, f32[16,1024]{1,0:T(8,128)S(1)}, u32[]{:S(2)}, u32[]{:S(2)}) collective-permute-start(f32[16,1024]{1,0:T(8,128)S(1)} %get-tuple-element.36), channel_id=1, source_target_pairs={{0,7},{1,6},{2,1},{3,0},{4,3},{5,2},{6,5},{7,4},{8,15},{9,14},{10,... | collective-permute-start | bytes 196616 | tf_op jit(solution)/shard_map/ppermute | solution.py:636
  (2 other events, 1.7 us)

commit v5 on v4

--- a/solution.py
+++ b/solution.py
@@ -329,16 +329,7 @@
     return lax.broadcasted_iota(jnp.int32, shape, len(shape) - 1)
 
 
-def advect_kernel(
-    sz,
-    heights,
-    cut,
-    stream_hbm,
-    normal_hbm,
-    lift_hbm,
-    back_hbm,
-    *others,
-):
+def advect_kernel(sz, heights, stream_hbm, normal_hbm, lift_hbm, back_hbm, *others):
     out_refs, (total_ref, stream_ref, normal_ref, lift_ref, back_ref, arrived) = others[:-6], others[-6:]
     place = lax.axis_index("ey")
     fetched = [
@@ -358,47 +349,52 @@
     spots = sz.elems * rows
     half = lane_index((fine, LANES)) < sz.planes
     column, step = sz.nodes * sz.block_y, sz.order * sz.block_y
+    factors = [
+        sum(jnp.where(place == q, heights[q * rows + f] * 0.5, 0.0) for q in range(sz.n_ey)) for f in range(rows)
+    ]
     full = sz.cut_x * sz.block_y // 8 * 8
     total_ref[pl.ds(full, sz.cut_nodes - full), :] = jnp.zeros((sz.cut_nodes - full, LANES), jnp.float32)
-    carry = None
+    spot = lax.axis_index("mode")
     for copy in fetched[:3]:
         copy.wait()
-    for e in range(sz.cut_elems):
-        speeds = jnp.concatenate(
-            [
-                ref[pl.ds((cut * sz.cut_elems + e) * rows + f, count, stride=spots), :]
-                for f in range(rows)
-                for ref in (stream_ref, normal_ref)
-            ],
-            1,
-        )
-        values = dot(lift_ref[...], below(speeds))
-        highs, lows = [], []
-        for f in range(rows):
-            height = sum(jnp.where(place == q, heights[q * rows + f], 0.0) for q in range(sz.n_ey))
-            mine = values[:, f * LANES : (f + 1) * LANES]
-            both, slope_x, slope_y = mine[:fine], mine[fine : 2 * fine], mine[2 * fine :]
-            turned = pltpu.roll(both, sz.planes, 1)
-            stream = jnp.where(half, both, turned)
-            normal = jnp.where(half, turned, both)
-            high, low = split((stream * (height * 0.5)) * slope_x + (normal * (element_width * 0.5)) * slope_y)
-            highs.append(high)
-            lows.append(low)
-        if e == 0:
+    for cut in range(sz.cuts):
+        products = []
+        for e in range(cut * sz.cut_elems, (cut + 1) * sz.cut_elems):
+            speeds = jnp.concatenate(
+                [
+                    ref[pl.ds(e * rows + f, count, stride=spots), :]
+                    for f in range(rows)
+                    for ref in (stream_ref, normal_ref)
+                ],
+                1,
+            )
+            values = dot(lift_ref[...], below(speeds))
+            highs, lows = [], []
+            for f in range(rows):
+                mine = values[:, f * LANES : (f + 1) * LANES]
+                both, slope_x, slope_y = mine[:fine], mine[fine : 2 * fine], mine[2 * fine :]
+                turned = pltpu.roll(both, sz.planes, 1)
+                stream = jnp.where(half, both, turned)
+                normal = jnp.where(half, turned, both)
+                high, low = split((stream * factors[f]) * slope_x + (normal * (element_width * 0.5)) * slope_y)
+                highs.append(high)
+                lows.append(low)
+            products.append(jnp.concatenate(highs + lows + highs, 0))
+        if cut == 0:
             fetched[3].wait()
-        weak = dot(back_ref[...], jnp.concatenate(highs + lows + highs, 0))
-        if carry is not None:
-            head = jnp.concatenate([carry, jnp.zeros((column - carry.shape[0], LANES), jnp.float32)], 0)
-            weak = weak + head
-        if e < sz.cut_elems - 1:
-            total_ref[pl.ds(e * step, step), :] = weak[:step]
-            carry = weak[step:]
-        else:
-            total_ref[pl.ds(e * step, column), :] = weak
-    spot = lax.axis_index("mode")
-    for step, out_ref in enumerate(out_refs):
-        goal = partner(spot, step, sz.n_mode)
-        out_ref[...] = total_ref[pl.ds(pl.multiple_of(goal * sz.share, 8), sz.share), :]
+        weak = dot(back_ref[...], jnp.concatenate(products, 1))
+        carry = None
+        for e in range(sz.cut_elems):
+            mine = weak[:, e * LANES : (e + 1) * LANES]
+            if carry is not None:
+                gap = jnp.zeros((column - carry.shape[0], LANES), jnp.float32)
+                mine = mine + jnp.concatenate([carry, gap], 0)
+            length = step if e < sz.cut_elems - 1 else column
+            total_ref[pl.ds(e * step, length), :] = mine[:length]
+            carry = mine[length:]
+        for turn in range(sz.n_mode):
+            goal = partner(spot, turn, sz.n_mode)
+            out_refs[cut * sz.n_mode + turn][...] = total_ref[pl.ds(pl.multiple_of(goal * sz.share, 8), sz.share), :]
 
 
 def transform_kernel(sz, *refs):
@@ -561,7 +557,7 @@
             out_ref[pl.ds(first, sz.elems, stride=sz.rows), :] = blank
 
 
-def call(kernel, shapes, operands, scratch=(), spaces=pltpu.VMEM, limit=16):
+def call(kernel, shapes, operands, scratch=(), spaces=pltpu.VMEM, limit=16, flops=10**9):
     if not isinstance(spaces, list):
         spaces = [spaces] * len(operands)
     made = pl.pallas_call(
@@ -571,6 +567,7 @@
         out_specs=[pl.BlockSpec(memory_space=pltpu.VMEM) for _ in shapes],
         scratch_shapes=[pltpu.VMEM(each, jnp.float32) if isinstance(each, tuple) else each for each in scratch],
         compiler_params=pltpu.CompilerParams(vmem_limit_bytes=limit * 2**20),
+        cost_estimate=pl.CostEstimate(flops=flops, bytes_accessed=10**6, transcendentals=0),
     )(*operands)
     return list(made)
 
@@ -579,46 +576,44 @@
     flat = sz.nodes * sz.nodes * sz.elems * sz.rows
     table = {name: jnp.asarray(value) for name, value in tables.items() if name != "heights"}
     heights = [float(height) for height in tables["heights"]]
-    weak, made = [], []
+    pieces = call(
+        functools.partial(advect_kernel, sz, heights),
+        [(sz.share, LANES)] * (sz.n_mode * sz.cuts),
+        [
+            stream_speed.reshape(flat, sz.planes),
+            normal_speed.reshape(flat, sz.planes),
+            table["lift"],
+            table["back"],
+        ],
+        [
+            (sz.cut_nodes, LANES),
+            (flat, sz.planes),
+            (flat, sz.planes),
+            pltpu.VMEM(tables["lift"].shape, jnp.bfloat16),
+            pltpu.VMEM(tables["back"].shape[1:], jnp.bfloat16),
+            pltpu.SemaphoreType.DMA((4,)),
+        ],
+        pltpu.HBM,
+        60,
+    )
+    weak = [pieces[cut * sz.n_mode : (cut + 1) * sz.n_mode] for cut in range(sz.cuts)]
     for cut in range(sz.cuts):
-        weak.append(
-            call(
-                functools.partial(advect_kernel, sz, heights, cut),
-                [(sz.share, LANES)] * sz.n_mode,
-                [
-                    stream_speed.reshape(flat, sz.planes),
-                    normal_speed.reshape(flat, sz.planes),
-                    table["lift"],
-                    table["back"],
-                ],
-                [
-                    (sz.cut_nodes, LANES),
-                    (flat, sz.planes),
-                    (flat, sz.planes),
-                    pltpu.VMEM(tables["lift"].shape, jnp.bfloat16),
-                    pltpu.VMEM(tables["back"].shape[1:], jnp.bfloat16),
-                    pltpu.SemaphoreType.DMA((4,)),
-                ],
-                pltpu.HBM,
-                60,
-            )
-        )
-        made.append(weak[cut][0])
         for step in sorted(range(1, sz.n_mode), key=lambda each: (each & -each, each), reverse=True):
             pairs = [(z, partner(z, step, sz.n_mode)) for z in range(sz.n_mode)]
             weak[cut][step] = lax.ppermute(weak[cut][step], "mode", pairs)
-    terms, ahead = [], made[-1]
+    terms, ahead = [], []
     for cut in range(sz.cuts):
         (spectra,) = call(
             functools.partial(transform_kernel, sz),
             [(2 * sz.planes_total, sz.share)],
-            [*weak[cut], ahead, table["waves"]],
+            [*weak[cut], *ahead, table["waves"]],
             [(-(-sz.share // LANES), 2 * sz.planes_total, LANES), (2, sz.planes_total, sz.share)],
-            [pltpu.VMEM] * sz.n_mode + [pl.ANY, pltpu.VMEM],
+            [pltpu.VMEM] * sz.n_mode + [pl.ANY] * len(ahead) + [pltpu.VMEM],
+            flops=10**11 if cut == sz.cuts - 1 else 10**8,
         )
         spectra = spectra.reshape(sz.n_mode * sz.spots, sz.own, sz.share)
         terms.append(lax.all_to_all(spectra, ("mode", "ex", "ey"), split_axis=0, concat_axis=0, tiled=True))
-        ahead = terms[cut]
+        ahead = [spectra]
     names = ("in_y", "in_x", "pair_y", "pair_x", "out_y", "out_x", "lam_x", "lam_y")
     solved = call(
         functools.partial(smooth_kernel, sz),

time: 71 us -> 68.7 us (0.968)
  Pallas kernels: 19 us -> 15 us
  starting transfers between devices: 20.4 us -> 23.1 us
  blocking collectives: 14.1 us -> 12.8 us
    all_to_all x1, waiting for transfers between devices: 0.01 us -> 9.14 us  [on_device(): lax.all_to_all(spectra, ('mode', 'ex', 'ey'), split_axis=0, concat_axis=0...]
    ppermute x6, waiting for transfers between devices: 11.1 us -> 2.25 us  [on_device(): weak[cut][step] = lax.ppermute(weak[cut][step], 'mode', pairs)]
    pallas_call x6 -> x5, Pallas kernels: 19 us -> 15 us  [call(): pl.pallas_call(kernel, out_shape=[jax.ShapeDtypeStruct(shape, jnp.float32...]
    all_to_all x1, starting transfers between devices: 4.65 us -> 7.3 us  [on_device(): lax.all_to_all(spectra, ('mode', 'ex', 'ey'), split_axis=0, concat_axis=0...]
    all_to_all x1, blocking collectives: 14.1 us -> 12.8 us  [on_device(): lax.all_to_all(spectra, ('mode', 'ex', 'ey'), split_axis=0, concat_axis=0...]
    unnamed x24 -> x22, local copies, waits for them, and re-layouts: 1.74 us -> 1.72 us
  transfers between devices with their start and end apart: 14 -> 14, of which waited for: 9 -> 8; matrix products, arithmetic and copies ran while one was open for 0% -> 0% of each run, Pallas kernels for 7% -> 3%
where the time goes in v5:
time: 68.7 us; the launch traced here: 68.4 us
  starting transfers between devices  23.1 us (34%)
  waiting for transfers between devices  15.6 us (23%)
  Pallas kernels  15 us (22%)
  blocking collectives  12.8 us (19%)
  local copies, waits for them, and re-layouts  1.72 us (3%)
    pallas_call x5, Pallas kernels, call(): pl.pallas_call(kernel, out_shape=[jax.ShapeDtypeStruct(shape, jnp.float32...  15 us
    all_to_all x1, blocking collectives, on_device(): lax.all_to_all(spectra, ('mode', 'ex', 'ey'), split_axis=0, concat_axis=0...  12.8 us
    ppermute x6, starting transfers between devices, on_device(): weak[cut][step] = lax.ppermute(weak[cut][step], 'mode', pairs)  10.2 us
    all_to_all x1, waiting for transfers between devices, on_device(): lax.all_to_all(spectra, ('mode', 'ex', 'ey'), split_axis=0, concat_axis=0...  9.14 us
    all_to_all x1, starting transfers between devices, on_device(): lax.all_to_all(spectra, ('mode', 'ex', 'ey'), split_axis=0, concat_axis=0...  7.3 us
    ppermute x7, starting transfers between devices, on_device(): solved[step] = lax.ppermute(solved[step], ('ex', 'ey'), pairs)  5.6 us
    ppermute x7, waiting for transfers between devices, on_device(): solved[step] = lax.ppermute(solved[step], ('ex', 'ey'), pairs)  4.19 us
    ppermute x6, waiting for transfers between devices, on_device(): weak[cut][step] = lax.ppermute(weak[cut][step], 'mode', pairs)  2.25 us
  transfers between devices with their start and end apart: 14, of which 8 were waited for; matrix products, arithmetic and copies ran while one was open for 0% of the time, Pallas kernels for 3%

profile of v5, /device:TPU:0, one launch (start us, length us, event | category | flops | bytes accessed | tf_op | source)
XLA Modules:
  0.0 68.4 jit_solution(5175681954084440169)
XLA Ops:
  0.0 5.2 %shard_map.127 = (f32[128,128]{1,0:T(8,128)}, f32[128,128]{1,0:T(8,128)}, f32[128,128]{1,0:T(8,128)}, f32[128,128]{1,0:T(8,128)}, f32[128,128]{1,0:T(8,128)}, /*...) custom-call(f32[1152,64]{1,0:T(8,128)} %bitcast.6, f32[1152,64]{1,0:T(8,128)} %bitcast.7, ...), custom_call_target="tpu_custom_call" | custom-call | flops 1000000000 | bytes 1000000 | tf_op jit(solution)/shard_map/pallas_call | solution.py:563
  5.2 3.1 %collective-permute-start = (f32[128,128]{1,0:T(8,128)}, f32[128,128]{1,0:T(8,128)S(1)}, u32[]{:S(2)}, u32[]{:S(2)}) collective-permute-start(f32[128,128]{1,0:T(8,128)} %get-tuple-element.22), channel_id=1, source_target_pairs={{0,8},{8,0},{16,24},{24,16},{1,9},{9,1},{17,25},{25,17},{2,10},{10... | collective-permute-start | bytes 196616 | tf_op jit(solution)/shard_map/ppermute | solution.py:603
  8.3 2.6 %collective-permute-start.1 = (f32[128,128]{1,0:T(8,128)}, f32[128,128]{1,0:T(8,128)S(1)}, u32[]{:S(2)}, u32[]{:S(2)}) collective-permute-start(f32[128,128]{1,0:T(8,128)} %get-tuple-element.23), channel_id=1, source_target_pairs={{0,16},{8,24},{16,0},{24,8},{1,17},{9,25},{17,1},{25,9},{2,18},{10... | collective-permute-start | bytes 196616 | tf_op jit(solution)/shard_map/ppermute | solution.py:603
  10.9 0.9 %collective-permute-start.3 = (f32[128,128]{1,0:T(8,128)}, f32[128,128]{1,0:T(8,128)S(1)}, u32[]{:S(2)}, u32[]{:S(2)}) collective-permute-start(f32[128,128]{1,0:T(8,128)} %get-tuple-element.26), channel_id=1, source_target_pairs={{0,8},{8,0},{16,24},{24,16},{1,9},{9,1},{17,25},{25,17},{2,10},{10... | collective-permute-start | bytes 196616 | tf_op jit(solution)/shard_map/ppermute | solution.py:603
  11.8 3.5 %collective-permute-start.4 = (f32[128,128]{1,0:T(8,128)}, f32[128,128]{1,0:T(8,128)S(1)}, u32[]{:S(2)}, u32[]{:S(2)}) collective-permute-start(f32[128,128]{1,0:T(8,128)} %get-tuple-element.27), channel_id=1, source_target_pairs={{0,16},{8,24},{16,0},{24,8},{1,17},{9,25},{17,1},{25,9},{2,18},{10... | collective-permute-start | bytes 196616 | tf_op jit(solution)/shard_map/ppermute | solution.py:603
  15.5 0.5 collective-permute-done.1.refs_2_
  15.9 1.8 %collective-permute-done.2.refs_3_ = f32[128,128]{1,0:T(8,128)S(1)} collective-permute-done((f32[128,128]{1,0:T(8,128)}, f32[128,128]{1,0:T(8,128)S(1)}, u32[]{:S(2)}, u32[]{:S(2)}) %collective-permute-start.2) | collective-permute-done | bytes 65568 | tf_op jit(solution)/shard_map/ppermute | solution.py:603
  17.7 0.8 %copy-done.1 = f32[128,128]{1,0:T(8,128)S(1)} copy-done((f32[128,128]{1,0:T(8,128)S(1)}, f32[128,128]{1,0:T(8,128)}, u32[]{:S(2)}) %copy-start.1) | copy-done | bytes 65560
  18.5 1.2 %shard_map.128 = f32[512,128]{1,0:T(8,128)} custom-call(f32[128,128]{1,0:T(8,128)S(1)} %copy-done.1, f32[128,128]{1,0:T(8,128)S(1)} %collective-permute-done.refs_1_, f32[128,128]{1,0:T(8,128)S(1)} %collective-permute-done.1.refs_2_, f32[128,128]{1,0:T(8,128)S(1)} %collective-permute-done.2.refs_3_, bf16[2,256,256]{2,1,0:T(8,128)(2,1)S(1)} %copy-done), custom_call_target="tpu_custom_call" | custom-call | flops 100000000 | bytes 1000000 | tf_op jit(solution)/shard_map/pallas_call | solution.py:563
  19.8 7.3 %all-to-all-start = ((f32[32,16,128]{2,1,0:T(8,128)}), f32[32,16,128]{2,1,0:T(8,128)S(1)}, u32[]{:S(2)}, u32[]{:S(2)}) async-start(f32[32,16,128]{2,1,0:T(8,128)} %bitcast.2.refs_4_), calls=%async_computation | async-start | bytes 524288 | tf_op jit(solution)/shard_map/all_to_all | solution.py:615
  27.1 0.8 %copy-done.2 = f32[128,128]{1,0:T(8,128)S(1)} copy-done((f32[128,128]{1,0:T(8,128)S(1)}, f32[128,128]{1,0:T(8,128)}, u32[]{:S(2)}) %copy-start.2) | copy-done | bytes 65560
  28.0 0.5 shard_map.129
  28.5 9.1 %all-to-all-done.refs_0_ = f32[32,16,128]{2,1,0:T(8,128)S(1)} async-done(((f32[32,16,128]{2,1,0:T(8,128)}), f32[32,16,128]{2,1,0:T(8,128)S(1)}, u32[]{:S(2)}, u32[]{:S(2)}) %all-to-all-start) | async-done | bytes 262176 | tf_op jit(solution)/shard_map/all_to_all | solution.py:615
  37.7 12.8 %all_to_all.10.refs_1_ = f32[32,16,128]{2,1,0:T(8,128)S(1)} all-to-all(f32[32,16,128]{2,1,0:T(8,128)S(1)} %bitcast.5), channel_id=1, replica_groups=mesh['mode'=4,'ex'=4,'ey'=2] {'mode','ex','ey'}, dimensions={0} | all-to-all | bytes 524288 | tf_op jit(solution)/shard_map/all_to_all | solution.py:615
  50.5 6.9 %shard_map.130 = (f32[16,1024]{1,0:T(8,128)S(1)}, f32[16,1024]{1,0:T(8,128)S(1)}, f32[16,1024]{1,0:T(8,128)S(1)}, f32[16,1024]{1,0:T(8,128)S(1)}, f32[16,1024]{1...) custom-call(f32[32,16,128]{2,1,0:T(8,128)S(1)} %all-to-all-done.refs_0_, ...), custom_call_target="tpu_custom_call" | custom-call | flops 1000000000 | bytes 1000000 | tf_op jit(solution)/shard_map/pallas_call | solution.py:563
  57.6 0.8 %collective-permute-start.7 = (f32[16,1024]{1,0:T(8,128)S(1)}, f32[16,1024]{1,0:T(8,128)S(1)}, u32[]{:S(2)}, u32[]{:S(2)}) collective-permute-start(f32[16,1024]{1,0:T(8,128)S(1)} %get-tuple-element.31), channel_id=1, source_target_pairs={{0,2},{1,3},{2,4},{3,5},{4,6},{5,7},{6,0},{7,1},{8,10},{9,11},{10,... | collective-permute-start | bytes 196616 | tf_op jit(solution)/shard_map/ppermute | solution.py:631
  58.4 1.4 %collective-permute-start.8 = (f32[16,1024]{1,0:T(8,128)S(1)}, f32[16,1024]{1,0:T(8,128)S(1)}, u32[]{:S(2)}, u32[]{:S(2)}) collective-permute-start(f32[16,1024]{1,0:T(8,128)S(1)} %get-tuple-element.32), channel_id=1, source_target_pairs={{0,3},{1,2},{2,5},{3,4},{4,7},{5,6},{6,1},{7,0},{8,11},{9,10},{10,... | collective-permute-start | bytes 196616 | tf_op jit(solution)/shard_map/ppermute | solution.py:631
  59.7 1.1 %collective-permute-start.9 = (f32[16,1024]{1,0:T(8,128)S(1)}, f32[16,1024]{1,0:T(8,128)S(1)}, u32[]{:S(2)}, u32[]{:S(2)}) collective-permute-start(f32[16,1024]{1,0:T(8,128)S(1)} %get-tuple-element.33), channel_id=1, source_target_pairs={{0,4},{1,5},{2,6},{3,7},{4,0},{5,1},{6,2},{7,3},{8,12},{9,13},{10,... | collective-permute-start | bytes 196616 | tf_op jit(solution)/shard_map/ppermute | solution.py:631
  60.9 0.6 collective-permute-start.10
  61.4 1.3 %collective-permute-start.11 = (f32[16,1024]{1,0:T(8,128)S(1)}, f32[16,1024]{1,0:T(8,128)S(1)}, u32[]{:S(2)}, u32[]{:S(2)}) collective-permute-start(f32[16,1024]{1,0:T(8,128)S(1)} %get-tuple-element.35), channel_id=1, source_target_pairs={{0,6},{1,7},{2,0},{3,1},{4,2},{5,3},{6,4},{7,5},{8,14},{9,15},{10,... | collective-permute-start | bytes 196616 | tf_op jit(solution)/shard_map/ppermute | solution.py:631
  62.8 0.7 %collective-permute-done.7.refs_2_ = f32[16,1024]{1,0:T(8,128)S(1)} collective-permute-done((f32[16,1024]{1,0:T(8,128)S(1)}, f32[16,1024]{1,0:T(8,128)S(1)}, u32[]{:S(2)}, u32[]{:S(2)}) %collective-permute-start.7) | collective-permute-done | bytes 65568 | tf_op jit(solution)/shard_map/ppermute | solution.py:631
  64.0 1.8 %collective-permute-done.9.refs_4_ = f32[16,1024]{1,0:T(8,128)S(1)} collective-permute-done((f32[16,1024]{1,0:T(8,128)S(1)}, f32[16,1024]{1,0:T(8,128)S(1)}, u32[]{:S(2)}, u32[]{:S(2)}) %collective-permute-start.9) | collective-permute-done | bytes 65568 | tf_op jit(solution)/shard_map/ppermute | solution.py:631
  65.8 1.3 %collective-permute-done.10.refs_5_ = f32[16,1024]{1,0:T(8,128)S(1)} collective-permute-done((f32[16,1024]{1,0:T(8,128)S(1)}, f32[16,1024]{1,0:T(8,128)S(1)}, u32[]{:S(2)}, u32[]{:S(2)}) %collective-permute-start.10) | collective-permute-done | bytes 65568 | tf_op jit(solution)/shard_map/ppermute | solution.py:631
  67.3 1.1 %shard_map.131 = f32[1152,128]{1,0:T(8,128)} custom-call(f32[16,1024]{1,0:T(8,128)S(1)} %get-tuple-element.29.refs_0_, f32[16,1024]{1,0:T(8,128)S(1)} %collective-permute-done.6.refs_1_, f32[16,1024]{1,0:T(8,128)S(1)} %collective-permute-done.7.refs_2_, f32[16,1024]{1,0:T(8,128)S(1)} %collective-permute-done.8.refs_3_, ...), custom_call_target="tpu_custom_call" | custom-call | flops 1000000000 | bytes 1000000 | tf_op jit(solution)/shard_map/pallas_call | solution.py:563
  (32 shorter events, 1.0 us)
Async XLA Ops:
  0.0 17.7 %copy-start = (bf16[2,256,256]{2,1,0:T(8,128)(2,1)S(1)}, bf16[2,256,256]{2,1,0:T(8,128)(2,1)}, u32[]{:S(2)}) copy-start(bf16[2,256,256]{2,1,0:T(8,128)(2,1)} %constant.24.clone.refs_4_.refs_5_) | copy-start | bytes 786436
  5.2 10.1 %collective-permute-start = (f32[128,128]{1,0:T(8,128)}, f32[128,128]{1,0:T(8,128)S(1)}, u32[]{:S(2)}, u32[]{:S(2)}) collective-permute-start(f32[128,128]{1,0:T(8,128)} %get-tuple-element.22), channel_id=1, source_target_pairs={{0,8},{8,0},{16,24},{24,16},{1,9},{9,1},{17,25},{25,17},{2,10},{10... | collective-permute-start | bytes 196616 | tf_op jit(solution)/shard_map/ppermute | solution.py:603
  8.3 7.6 %collective-permute-start.1 = (f32[128,128]{1,0:T(8,128)}, f32[128,128]{1,0:T(8,128)S(1)}, u32[]{:S(2)}, u32[]{:S(2)}) collective-permute-start(f32[128,128]{1,0:T(8,128)} %get-tuple-element.23), channel_id=1, source_target_pairs={{0,16},{8,24},{16,0},{24,8},{1,17},{9,25},{17,1},{25,9},{2,18},{10... | collective-permute-start | bytes 196616 | tf_op jit(solution)/shard_map/ppermute | solution.py:603
  10.9 6.8 %collective-permute-start.2 = (f32[128,128]{1,0:T(8,128)}, f32[128,128]{1,0:T(8,128)S(1)}, u32[]{:S(2)}, u32[]{:S(2)}) collective-permute-start(f32[128,128]{1,0:T(8,128)} %get-tuple-element.24), channel_id=1, source_target_pairs={{0,24},{8,16},{16,8},{24,0},{1,25},{9,17},{17,9},{25,1},{2,26},{10... | collective-permute-start | bytes 196616 | tf_op jit(solution)/shard_map/ppermute | solution.py:603
  10.9 16.2 %collective-permute-start.3 = (f32[128,128]{1,0:T(8,128)}, f32[128,128]{1,0:T(8,128)S(1)}, u32[]{:S(2)}, u32[]{:S(2)}) collective-permute-start(f32[128,128]{1,0:T(8,128)} %get-tuple-element.26), channel_id=1, source_target_pairs={{0,8},{8,0},{16,24},{24,16},{1,9},{9,1},{17,25},{25,17},{2,10},{10... | collective-permute-start | bytes 196616 | tf_op jit(solution)/shard_map/ppermute | solution.py:603
  11.8 15.3 %collective-permute-start.4 = (f32[128,128]{1,0:T(8,128)}, f32[128,128]{1,0:T(8,128)S(1)}, u32[]{:S(2)}, u32[]{:S(2)}) collective-permute-start(f32[128,128]{1,0:T(8,128)} %get-tuple-element.27), channel_id=1, source_target_pairs={{0,16},{8,24},{16,0},{24,8},{1,17},{9,25},{17,1},{25,9},{2,18},{10... | collective-permute-start | bytes 196616 | tf_op jit(solution)/shard_map/ppermute | solution.py:603
  15.3 11.8 %collective-permute-start.5 = (f32[128,128]{1,0:T(8,128)}, f32[128,128]{1,0:T(8,128)S(1)}, u32[]{:S(2)}, u32[]{:S(2)}) collective-permute-start(f32[128,128]{1,0:T(8,128)} %get-tuple-element.28), channel_id=1, source_target_pairs={{0,24},{8,16},{16,8},{24,0},{1,25},{9,17},{17,9},{25,1},{2,26},{10... | collective-permute-start | bytes 196616 | tf_op jit(solution)/shard_map/ppermute | solution.py:603
  17.7 0.8 %copy-start.1 = (f32[128,128]{1,0:T(8,128)S(1)}, f32[128,128]{1,0:T(8,128)}, u32[]{:S(2)}) copy-start(f32[128,128]{1,0:T(8,128)} %get-tuple-element.21.refs_0_) | copy-start | bytes 196612
  19.8 17.9 %all-to-all-start = ((f32[32,16,128]{2,1,0:T(8,128)}), f32[32,16,128]{2,1,0:T(8,128)S(1)}, u32[]{:S(2)}, u32[]{:S(2)}) async-start(f32[32,16,128]{2,1,0:T(8,128)} %bitcast.2.refs_4_), calls=%async_computation | async-start | bytes 524288 | tf_op jit(solution)/shard_map/all_to_all | solution.py:615
  27.9 22.5 %copy-start.3 = (bf16[224,1344]{1,0:T(8,128)(2,1)S(1)}, bf16[224,1344]{1,0:T(8,128)(2,1)}, u32[]{:S(2)}) copy-start(bf16[224,1344]{1,0:T(8,128)(2,1)} %constant.28.clone.refs_5_) | copy-start | bytes 1806340
  28.0 22.5 %copy-start.4 = (bf16[192,672]{1,0:T(8,128)(2,1)S(1)}, bf16[192,672]{1,0:T(8,128)(2,1)}, u32[]{:S(2)}) copy-start(bf16[192,672]{1,0:T(8,128)(2,1)} %constant.30.clone.refs_7_) | copy-start | bytes 774148
  28.0 22.5 %copy-start.5 = (bf16[224,576]{1,0:T(8,128)(2,1)S(1)}, bf16[224,576]{1,0:T(8,128)(2,1)}, u32[]{:S(2)}) copy-start(bf16[224,576]{1,0:T(8,128)(2,1)} %constant.26.clone.refs_3_) | copy-start | bytes 774148
  28.0 22.5 %copy-start.6 = (bf16[384,256]{1,0:T(8,128)(2,1)S(1)}, bf16[384,256]{1,0:T(8,128)(2,1)}, u32[]{:S(2)}) copy-start(bf16[384,256]{1,0:T(8,128)(2,1)} %constant.27.clone.refs_4_) | copy-start | bytes 589828
  28.0 22.5 %copy-start.7 = (bf16[256,256]{1,0:T(8,128)(2,1)S(1)}, bf16[256,256]{1,0:T(8,128)(2,1)}, u32[]{:S(2)}) copy-start(bf16[256,256]{1,0:T(8,128)(2,1)} %constant.29.clone.refs_6_) | copy-start | bytes 393220
  28.0 22.5 %copy-start.8 = (bf16[256,256]{1,0:T(8,128)(2,1)S(1)}, bf16[256,256]{1,0:T(8,128)(2,1)}, u32[]{:S(2)}) copy-start(bf16[256,256]{1,0:T(8,128)(2,1)} %constant.25.clone.refs_2_) | copy-start | bytes 393220
  28.0 22.5 %copy-start.9 = (f32[224,128]{1,0:T(8,128)S(1)}, f32[224,128]{1,0:T(8,128)}, u32[]{:S(2)}) copy-start(f32[224,128]{1,0:T(8,128)} %constant.31.clone.refs_8_) | copy-start | bytes 344068
  28.0 22.5 %copy-start.10 = (f32[1,128]{1,0:T(1,128)S(1)}, f32[1,128]{1,0:T(1,128)}, u32[]{:S(2)}) copy-start(f32[1,128]{1,0:T(1,128)} %constant.32.clone.refs_9_) | copy-start | bytes 1540
  57.5 4.0 %collective-permute-start.6 = (f32[16,1024]{1,0:T(8,128)S(1)}, f32[16,1024]{1,0:T(8,128)S(1)}, u32[]{:S(2)}, u32[]{:S(2)}) collective-permute-start(f32[16,1024]{1,0:T(8,128)S(1)} %get-tuple-element.30), channel_id=1, source_target_pairs={{0,1},{1,0},{2,3},{3,2},{4,5},{5,4},{6,7},{7,6},{8,9},{9,8},{10,11... | collective-permute-start | bytes 196616 | tf_op jit(solution)/shard_map/ppermute | solution.py:631
  57.6 5.9 %collective-permute-start.7 = (f32[16,1024]{1,0:T(8,128)S(1)}, f32[16,1024]{1,0:T(8,128)S(1)}, u32[]{:S(2)}, u32[]{:S(2)}) collective-permute-start(f32[16,1024]{1,0:T(8,128)S(1)} %get-tuple-element.31), channel_id=1, source_target_pairs={{0,2},{1,3},{2,4},{3,5},{4,6},{5,7},{6,0},{7,1},{8,10},{9,11},{10,... | collective-permute-start | bytes 196616 | tf_op jit(solution)/shard_map/ppermute | solution.py:631
  58.4 5.6 %collective-permute-start.8 = (f32[16,1024]{1,0:T(8,128)S(1)}, f32[16,1024]{1,0:T(8,128)S(1)}, u32[]{:S(2)}, u32[]{:S(2)}) collective-permute-start(f32[16,1024]{1,0:T(8,128)S(1)} %get-tuple-element.32), channel_id=1, source_target_pairs={{0,3},{1,2},{2,5},{3,4},{4,7},{5,6},{6,1},{7,0},{8,11},{9,10},{10,... | collective-permute-start | bytes 196616 | tf_op jit(solution)/shard_map/ppermute | solution.py:631
  59.7 6.1 %collective-permute-start.9 = (f32[16,1024]{1,0:T(8,128)S(1)}, f32[16,1024]{1,0:T(8,128)S(1)}, u32[]{:S(2)}, u32[]{:S(2)}) collective-permute-start(f32[16,1024]{1,0:T(8,128)S(1)} %get-tuple-element.33), channel_id=1, source_target_pairs={{0,4},{1,5},{2,6},{3,7},{4,0},{5,1},{6,2},{7,3},{8,12},{9,13},{10,... | collective-permute-start | bytes 196616 | tf_op jit(solution)/shard_map/ppermute | solution.py:631
  60.9 6.2 %collective-permute-start.10 = (f32[16,1024]{1,0:T(8,128)S(1)}, f32[16,1024]{1,0:T(8,128)S(1)}, u32[]{:S(2)}, u32[]{:S(2)}) collective-permute-start(f32[16,1024]{1,0:T(8,128)S(1)} %get-tuple-element.34), channel_id=1, source_target_pairs={{0,5},{1,4},{2,7},{3,6},{4,1},{5,0},{6,3},{7,2},{8,13},{9,12},{10,... | collective-permute-start | bytes 196616 | tf_op jit(solution)/shard_map/ppermute | solution.py:631
  61.4 5.7 %collective-permute-start.11 = (f32[16,1024]{1,0:T(8,128)S(1)}, f32[16,1024]{1,0:T(8,128)S(1)}, u32[]{:S(2)}, u32[]{:S(2)}) collective-permute-start(f32[16,1024]{1,0:T(8,128)S(1)} %get-tuple-element.35), channel_id=1, source_target_pairs={{0,6},{1,7},{2,0},{3,1},{4,2},{5,3},{6,4},{7,5},{8,14},{9,15},{10,... | collective-permute-start | bytes 196616 | tf_op jit(solution)/shard_map/ppermute | solution.py:631
  63.5 3.8 %collective-permute-start.12 = (f32[16,1024]{1,0:T(8,128)S(1)}, f32[16,1024]{1,0:T(8,128)S(1)}, u32[]{:S(2)}, u32[]{:S(2)}) collective-permute-start(f32[16,1024]{1,0:T(8,128)S(1)} %get-tuple-element.36), channel_id=1, source_target_pairs={{0,7},{1,6},{2,1},{3,0},{4,3},{5,2},{6,5},{7,4},{8,15},{9,14},{10,... | collective-permute-start | bytes 196616 | tf_op jit(solution)/shard_map/ppermute | solution.py:631
  (1 other events, 0.8 us)

commit v6 on v5

--- a/solution.py
+++ b/solution.py
@@ -174,7 +174,7 @@
             for p in range(self.n_ey)
         ]
         self.block_y = max(len(found) for found in self.inner)
-        self.cuts = 2 if self.elems % 2 == 0 else 1
+        self.cuts = 1
         self.cut_elems = self.elems // self.cuts
         self.cut_x = self.order * self.cut_elems + 1
         share = -(-self.cut_x * self.block_y // self.n_mode)
@@ -580,10 +580,13 @@
         functools.partial(advect_kernel, sz, heights),
         [(sz.share, LANES)] * (sz.n_mode * sz.cuts),
         [
-            stream_speed.reshape(flat, sz.planes),
-            normal_speed.reshape(flat, sz.planes),
-            table["lift"],
-            table["back"],
+            pltpu.with_memory_space_constraint(each, pltpu.HBM)
+            for each in (
+                stream_speed.reshape(flat, sz.planes),
+                normal_speed.reshape(flat, sz.planes),
+                table["lift"],
+                table["back"],
+            )
         ],
         [
             (sz.cut_nodes, LANES),
@@ -594,7 +597,6 @@
             pltpu.SemaphoreType.DMA((4,)),
         ],
         pltpu.HBM,
-        60,
     )
     weak = [pieces[cut * sz.n_mode : (cut + 1) * sz.n_mode] for cut in range(sz.cuts)]
     for cut in range(sz.cuts):
@@ -621,7 +623,7 @@
         terms + [table[name] for name in names],
         [(PARTS * sz.x_pad, LANES), (PARTS * sz.x_eig, LANES), (PARTS * sz.x_eig, LANES)],
     )
-    for step in range(1, sz.spots):
+    for step in sorted(range(1, sz.spots), key=lambda each: each // sz.n_ey == 0):
         shift, turn = step // sz.n_ey, step % sz.n_ey
         pairs = [
             (p * sz.n_ey + q, (p + shift) % sz.n_ex * sz.n_ey + (q + turn) % sz.n_ey)

time: 68.7 us -> 59.7 us (0.87)
  starting transfers between devices: 23.1 us -> 12 us
  blocking collectives: 12.8 us -> 20.6 us
  Pallas kernels: 15 us -> 12.6 us
  local copies, waits for them, and re-layouts: 1.72 us -> 0.06 us
  waiting for transfers between devices: 15.6 us -> 14.1 us
    all_to_all x1 -> x0, waiting for transfers between devices: 9.14 us -> none  [on_device(): lax.all_to_all(spectra, ('mode', 'ex', 'ey'), split_axis=0, concat_axis=0...]
    ppermute x6 -> x3, waiting for transfers between devices: 2.25 us -> 10.3 us  [on_device(): weak[cut][step] = lax.ppermute(weak[cut][step], 'mode', pairs)]
    all_to_all x1, blocking collectives: 12.8 us -> 20.6 us  [on_device(): lax.all_to_all(spectra, ('mode', 'ex', 'ey'), split_axis=0, concat_axis=0...]
    all_to_all x1 -> x0, starting transfers between devices: 7.3 us -> none  [on_device(): lax.all_to_all(spectra, ('mode', 'ex', 'ey'), split_axis=0, concat_axis=0...]
    ppermute x6 -> x3, starting transfers between devices: 10.2 us -> 5.7 us  [on_device(): weak[cut][step] = lax.ppermute(weak[cut][step], 'mode', pairs)]
    pallas_call x5 -> x4, Pallas kernels: 15 us -> 12.6 us  [call(): pl.pallas_call(kernel, out_shape=[jax.ShapeDtypeStruct(shape, jnp.float32...]
    unnamed x22 -> x18, local copies, waits for them, and re-layouts: 1.72 us -> 0.06 us
    ppermute x7, starting transfers between devices: 5.6 us -> 6.31 us  [on_device(): solved[step] = lax.ppermute(solved[step], ('ex', 'ey'), pairs)]
  transfers between devices with their start and end apart: 14 -> 10, of which waited for: 8 -> 6; matrix products, arithmetic and copies ran while one was open for 0% -> 0% of each run, Pallas kernels for 3% -> 0%
where the time goes in v6:
time: 59.7 us; the launch traced here: 59.5 us
  blocking collectives  20.6 us (35%)
  waiting for transfers between devices  14.1 us (24%)
  Pallas kernels  12.6 us (21%)
  starting transfers between devices  12 us (20%)
    all_to_all x1, blocking collectives, on_device(): lax.all_to_all(spectra, ('mode', 'ex', 'ey'), split_axis=0, concat_axis=0...  20.6 us
    pallas_call x4, Pallas kernels, call(): pl.pallas_call(kernel, out_shape=[jax.ShapeDtypeStruct(shape, jnp.float32...  12.6 us
    ppermute x3, waiting for transfers between devices, on_device(): weak[cut][step] = lax.ppermute(weak[cut][step], 'mode', pairs)  10.3 us
    ppermute x7, starting transfers between devices, on_device(): solved[step] = lax.ppermute(solved[step], ('ex', 'ey'), pairs)  6.31 us
    ppermute x3, starting transfers between devices, on_device(): weak[cut][step] = lax.ppermute(weak[cut][step], 'mode', pairs)  5.7 us
    ppermute x7, waiting for transfers between devices, on_device(): solved[step] = lax.ppermute(solved[step], ('ex', 'ey'), pairs)  3.8 us
  transfers between devices with their start and end apart: 10, of which 6 were waited for; matrix products, arithmetic and copies ran while one was open for 0% of the time, Pallas kernels for 0%

profile of v6, /device:TPU:0, one launch (start us, length us, event | category | flops | bytes accessed | tf_op | source)
XLA Modules:
  0.0 59.5 jit_solution(4663640500596130256)
XLA Ops:
  0.0 4.0 %shard_map.127 = (f32[256,128]{1,0:T(8,128)S(1)}, f32[256,128]{1,0:T(8,128)S(1)}, f32[256,128]{1,0:T(8,128)S(1)}, f32[256,128]{1,0:T(8,128)S(1)}) custom-call(f32[1152,64]{1,0:T(8,128)} %bitcast.5, f32[1152,64]{1,0:T(8,128)} %bitcast.6, bf16[1008,432]{1,0:T(8,128)(2,1)} %constant.22.clone.lift_hbm, bf16[2,264,2016]{2,1,0:T(8,128)(2,1)} %constant.23.clone.back_hbm), custom_call_target="tpu_custom_call" | custom-call | flops 1000000000 | bytes 1000000 | tf_op jit(solution)/shard_map/pallas_call | solution.py:563
  4.0 3.1 %collective-permute-start = (f32[256,128]{1,0:T(8,128)S(1)}, f32[256,128]{1,0:T(8,128)S(1)}, u32[]{:S(2)}, u32[]{:S(2)}) collective-permute-start(f32[256,128]{1,0:T(8,128)S(1)} %get-tuple-element.18), channel_id=1, source_target_pairs={{0,8},{8,0},{16,24},{24,16},{1,9},{9,1},{17,25},{25,17},{2,10},{10... | collective-permute-start | bytes 393224 | tf_op jit(solution)/shard_map/ppermute | solution.py:605
  7.1 2.6 %collective-permute-start.1 = (f32[256,128]{1,0:T(8,128)S(1)}, f32[256,128]{1,0:T(8,128)S(1)}, u32[]{:S(2)}, u32[]{:S(2)}) collective-permute-start(f32[256,128]{1,0:T(8,128)S(1)} %get-tuple-element.19), channel_id=1, source_target_pairs={{0,16},{8,24},{16,0},{24,8},{1,17},{9,25},{17,1},{25,9},{2,18},{10... | collective-permute-start | bytes 393224 | tf_op jit(solution)/shard_map/ppermute | solution.py:605
  9.7 2.4 %collective-permute-done.refs_1_ = f32[256,128]{1,0:T(8,128)S(1)} collective-permute-done((f32[256,128]{1,0:T(8,128)S(1)}, f32[256,128]{1,0:T(8,128)S(1)}, u32[]{:S(2)}, u32[]{:S(2)}) %collective-permute-start) | collective-permute-done | bytes 131104 | tf_op jit(solution)/shard_map/ppermute | solution.py:605
  12.1 7.9 %collective-permute-done.1.refs_2_ = f32[256,128]{1,0:T(8,128)S(1)} collective-permute-done((f32[256,128]{1,0:T(8,128)S(1)}, f32[256,128]{1,0:T(8,128)S(1)}, u32[]{:S(2)}, u32[]{:S(2)}) %collective-permute-start.1) | collective-permute-done | bytes 131104 | tf_op jit(solution)/shard_map/ppermute | solution.py:605
  20.0 0.0 copy-start.1
  20.0 0.0 copy-start.2
  20.0 0.0 copy-start.4
  20.1 0.0 copy-start.6
  20.1 0.6 %shard_map.128 = f32[512,256]{1,0:T(8,128)S(1)} custom-call(f32[256,128]{1,0:T(8,128)S(1)} %get-tuple-element.17.refs_0_, f32[256,128]{1,0:T(8,128)S(1)} %collective-permute-done.refs_1_, f32[256,128]{1,0:T(8,128)S(1)} %collective-permute-done.1.refs_2_, f32[256,128]{1,0:T(8,128)S(1)} %collective-permute-done.2.refs_3_, bf16[2,256,256]{2,1,0:T(8,128)(2,1)S(1)} %copy-done.3), custom_call_target="tpu_custom_call" | custom-call | flops 99999997952 | bytes 1000000 | tf_op jit(solution)/shard_map/pallas_call | solution.py:563
  20.7 20.6 %all_to_all.5.refs_0_ = f32[32,16,256]{2,1,0:T(8,128)S(1)} all-to-all(f32[32,16,256]{2,1,0:T(8,128)S(1)} %bitcast.4), channel_id=1, replica_groups=mesh['mode'=4,'ex'=4,'ey'=2] {'mode','ex','ey'}, dimensions={0} | all-to-all | bytes 1048576 | tf_op jit(solution)/shard_map/all_to_all | solution.py:617
  41.3 6.9 %shard_map.129 = (f32[16,1024]{1,0:T(8,128)S(1)}, f32[16,1024]{1,0:T(8,128)S(1)}, f32[16,1024]{1,0:T(8,128)S(1)}, f32[16,1024]{1,0:T(8,128)S(1)}, f32[16,1024]{1...) custom-call(f32[32,16,256]{2,1,0:T(8,128)S(1)} %all_to_all.5.refs_0_, ...), custom_call_target="tpu_custom_call" | custom-call | flops 1000000000 | bytes 1000000 | tf_op jit(solution)/shard_map/pallas_call | solution.py:563
  48.3 0.1 collective-permute-start.3
  48.3 1.3 %collective-permute-start.4 = (f32[16,1024]{1,0:T(8,128)S(1)}, f32[16,1024]{1,0:T(8,128)S(1)}, u32[]{:S(2)}, u32[]{:S(2)}) collective-permute-start(f32[16,1024]{1,0:T(8,128)S(1)} %get-tuple-element.23), channel_id=1, source_target_pairs={{0,2},{1,3},{2,4},{3,5},{4,6},{5,7},{6,0},{7,1},{8,10},{9,11},{10,... | collective-permute-start | bytes 196616 | tf_op jit(solution)/shard_map/ppermute | solution.py:633
  49.6 1.2 %collective-permute-start.5 = (f32[16,1024]{1,0:T(8,128)S(1)}, f32[16,1024]{1,0:T(8,128)S(1)}, u32[]{:S(2)}, u32[]{:S(2)}) collective-permute-start(f32[16,1024]{1,0:T(8,128)S(1)} %get-tuple-element.24), channel_id=1, source_target_pairs={{0,3},{1,2},{2,5},{3,4},{4,7},{5,6},{6,1},{7,0},{8,11},{9,10},{10,... | collective-permute-start | bytes 196616 | tf_op jit(solution)/shard_map/ppermute | solution.py:633
  50.9 0.8 %collective-permute-start.6 = (f32[16,1024]{1,0:T(8,128)S(1)}, f32[16,1024]{1,0:T(8,128)S(1)}, u32[]{:S(2)}, u32[]{:S(2)}) collective-permute-start(f32[16,1024]{1,0:T(8,128)S(1)} %get-tuple-element.25), channel_id=1, source_target_pairs={{0,4},{1,5},{2,6},{3,7},{4,0},{5,1},{6,2},{7,3},{8,12},{9,13},{10,... | collective-permute-start | bytes 196616 | tf_op jit(solution)/shard_map/ppermute | solution.py:633
  51.7 0.9 %collective-permute-start.7 = (f32[16,1024]{1,0:T(8,128)S(1)}, f32[16,1024]{1,0:T(8,128)S(1)}, u32[]{:S(2)}, u32[]{:S(2)}) collective-permute-start(f32[16,1024]{1,0:T(8,128)S(1)} %get-tuple-element.26), channel_id=1, source_target_pairs={{0,5},{1,4},{2,7},{3,6},{4,1},{5,0},{6,3},{7,2},{8,13},{9,12},{10,... | collective-permute-start | bytes 196616 | tf_op jit(solution)/shard_map/ppermute | solution.py:633
  52.6 1.5 %collective-permute-start.8 = (f32[16,1024]{1,0:T(8,128)S(1)}, f32[16,1024]{1,0:T(8,128)S(1)}, u32[]{:S(2)}, u32[]{:S(2)}) collective-permute-start(f32[16,1024]{1,0:T(8,128)S(1)} %get-tuple-element.27), channel_id=1, source_target_pairs={{0,6},{1,7},{2,0},{3,1},{4,2},{5,3},{6,4},{7,5},{8,14},{9,15},{10,... | collective-permute-start | bytes 196616 | tf_op jit(solution)/shard_map/ppermute | solution.py:633
  54.0 0.5 collective-permute-start.9
  54.6 0.4 collective-permute-done.5.refs_3_
  55.0 1.6 %collective-permute-done.6.refs_4_ = f32[16,1024]{1,0:T(8,128)S(1)} collective-permute-done((f32[16,1024]{1,0:T(8,128)S(1)}, f32[16,1024]{1,0:T(8,128)S(1)}, u32[]{:S(2)}, u32[]{:S(2)}) %collective-permute-start.6) | collective-permute-done | bytes 65568 | tf_op jit(solution)/shard_map/ppermute | solution.py:633
  56.6 1.3 %collective-permute-done.7.refs_5_ = f32[16,1024]{1,0:T(8,128)S(1)} collective-permute-done((f32[16,1024]{1,0:T(8,128)S(1)}, f32[16,1024]{1,0:T(8,128)S(1)}, u32[]{:S(2)}, u32[]{:S(2)}) %collective-permute-start.7) | collective-permute-done | bytes 65568 | tf_op jit(solution)/shard_map/ppermute | solution.py:633
  57.9 0.5 collective-permute-done.9.refs_7_
  58.4 1.1 %shard_map.130 = f32[1152,128]{1,0:T(8,128)} custom-call(f32[16,1024]{1,0:T(8,128)S(1)} %get-tuple-element.21.refs_0_, f32[16,1024]{1,0:T(8,128)S(1)} %collective-permute-done.3.refs_1_, f32[16,1024]{1,0:T(8,128)S(1)} %collective-permute-done.4.refs_2_, f32[16,1024]{1,0:T(8,128)S(1)} %collective-permute-done.5.refs_3_, ...), custom_call_target="tpu_custom_call" | custom-call | flops 1000000000 | bytes 1000000 | tf_op jit(solution)/shard_map/pallas_call | solution.py:563
  (19 shorter events, 0.0 us)
Async XLA Ops:
  0.0 20.0 %copy-start.3 = (bf16[2,256,256]{2,1,0:T(8,128)(2,1)S(1)}, bf16[2,256,256]{2,1,0:T(8,128)(2,1)}, u32[]{:S(2)}) copy-start(bf16[2,256,256]{2,1,0:T(8,128)(2,1)} %constant.24.clone.refs_4_) | copy-start | bytes 786436
  4.0 8.1 %collective-permute-start = (f32[256,128]{1,0:T(8,128)S(1)}, f32[256,128]{1,0:T(8,128)S(1)}, u32[]{:S(2)}, u32[]{:S(2)}) collective-permute-start(f32[256,128]{1,0:T(8,128)S(1)} %get-tuple-element.18), channel_id=1, source_target_pairs={{0,8},{8,0},{16,24},{24,16},{1,9},{9,1},{17,25},{25,17},{2,10},{10... | collective-permute-start | bytes 393224 | tf_op jit(solution)/shard_map/ppermute | solution.py:605
  7.1 12.9 %collective-permute-start.1 = (f32[256,128]{1,0:T(8,128)S(1)}, f32[256,128]{1,0:T(8,128)S(1)}, u32[]{:S(2)}, u32[]{:S(2)}) collective-permute-start(f32[256,128]{1,0:T(8,128)S(1)} %get-tuple-element.19), channel_id=1, source_target_pairs={{0,16},{8,24},{16,0},{24,8},{1,17},{9,25},{17,1},{25,9},{2,18},{10... | collective-permute-start | bytes 393224 | tf_op jit(solution)/shard_map/ppermute | solution.py:605
  9.7 10.3 %collective-permute-start.2 = (f32[256,128]{1,0:T(8,128)S(1)}, f32[256,128]{1,0:T(8,128)S(1)}, u32[]{:S(2)}, u32[]{:S(2)}) collective-permute-start(f32[256,128]{1,0:T(8,128)S(1)} %get-tuple-element.20), channel_id=1, source_target_pairs={{0,24},{8,16},{16,8},{24,0},{1,25},{9,17},{17,9},{25,1},{2,26},{10... | collective-permute-start | bytes 393224 | tf_op jit(solution)/shard_map/ppermute | solution.py:605
  20.0 21.3 %copy-start = (bf16[224,1344]{1,0:T(8,128)(2,1)S(1)}, bf16[224,1344]{1,0:T(8,128)(2,1)}, u32[]{:S(2)}) copy-start(bf16[224,1344]{1,0:T(8,128)(2,1)} %constant.28.clone.refs_4_) | copy-start | bytes 1806340
  20.0 21.3 %copy-start.1 = (bf16[192,672]{1,0:T(8,128)(2,1)S(1)}, bf16[192,672]{1,0:T(8,128)(2,1)}, u32[]{:S(2)}) copy-start(bf16[192,672]{1,0:T(8,128)(2,1)} %constant.30.clone.refs_6_) | copy-start | bytes 774148
  20.0 21.3 %copy-start.2 = (bf16[224,576]{1,0:T(8,128)(2,1)S(1)}, bf16[224,576]{1,0:T(8,128)(2,1)}, u32[]{:S(2)}) copy-start(bf16[224,576]{1,0:T(8,128)(2,1)} %constant.26.clone.refs_2_) | copy-start | bytes 774148
  20.0 21.3 %copy-start.4 = (bf16[384,256]{1,0:T(8,128)(2,1)S(1)}, bf16[384,256]{1,0:T(8,128)(2,1)}, u32[]{:S(2)}) copy-start(bf16[384,256]{1,0:T(8,128)(2,1)} %constant.27.clone.refs_3_) | copy-start | bytes 589828
  20.0 21.3 %copy-start.5 = (bf16[256,256]{1,0:T(8,128)(2,1)S(1)}, bf16[256,256]{1,0:T(8,128)(2,1)}, u32[]{:S(2)}) copy-start(bf16[256,256]{1,0:T(8,128)(2,1)} %constant.29.clone.refs_5_) | copy-start | bytes 393220
  20.1 21.3 %copy-start.6 = (bf16[256,256]{1,0:T(8,128)(2,1)S(1)}, bf16[256,256]{1,0:T(8,128)(2,1)}, u32[]{:S(2)}) copy-start(bf16[256,256]{1,0:T(8,128)(2,1)} %constant.25.clone.refs_1_) | copy-start | bytes 393220
  20.1 21.3 %copy-start.7 = (f32[224,128]{1,0:T(8,128)S(1)}, f32[224,128]{1,0:T(8,128)}, u32[]{:S(2)}) copy-start(f32[224,128]{1,0:T(8,128)} %constant.31.clone.refs_7_) | copy-start | bytes 344068
  20.1 21.3 %copy-start.8 = (f32[1,128]{1,0:T(1,128)S(1)}, f32[1,128]{1,0:T(1,128)}, u32[]{:S(2)}) copy-start(f32[1,128]{1,0:T(1,128)} %constant.32.clone.refs_8_) | copy-start | bytes 1540
  48.3 4.3 %collective-permute-start.3 = (f32[16,1024]{1,0:T(8,128)S(1)}, f32[16,1024]{1,0:T(8,128)S(1)}, u32[]{:S(2)}, u32[]{:S(2)}) collective-permute-start(f32[16,1024]{1,0:T(8,128)S(1)} %get-tuple-element.22), channel_id=1, source_target_pairs={{0,1},{1,0},{2,3},{3,2},{4,5},{5,4},{6,7},{7,6},{8,9},{9,8},{10,11... | collective-permute-start | bytes 196616 | tf_op jit(solution)/shard_map/ppermute | solution.py:633
  48.3 5.7 %collective-permute-start.4 = (f32[16,1024]{1,0:T(8,128)S(1)}, f32[16,1024]{1,0:T(8,128)S(1)}, u32[]{:S(2)}, u32[]{:S(2)}) collective-permute-start(f32[16,1024]{1,0:T(8,128)S(1)} %get-tuple-element.23), channel_id=1, source_target_pairs={{0,2},{1,3},{2,4},{3,5},{4,6},{5,7},{6,0},{7,1},{8,10},{9,11},{10,... | collective-permute-start | bytes 196616 | tf_op jit(solution)/shard_map/ppermute | solution.py:633
  49.6 5.3 %collective-permute-start.5 = (f32[16,1024]{1,0:T(8,128)S(1)}, f32[16,1024]{1,0:T(8,128)S(1)}, u32[]{:S(2)}, u32[]{:S(2)}) collective-permute-start(f32[16,1024]{1,0:T(8,128)S(1)} %get-tuple-element.24), channel_id=1, source_target_pairs={{0,3},{1,2},{2,5},{3,4},{4,7},{5,6},{6,1},{7,0},{8,11},{9,10},{10,... | collective-permute-start | bytes 196616 | tf_op jit(solution)/shard_map/ppermute | solution.py:633
  50.9 5.7 %collective-permute-start.6 = (f32[16,1024]{1,0:T(8,128)S(1)}, f32[16,1024]{1,0:T(8,128)S(1)}, u32[]{:S(2)}, u32[]{:S(2)}) collective-permute-start(f32[16,1024]{1,0:T(8,128)S(1)} %get-tuple-element.25), channel_id=1, source_target_pairs={{0,4},{1,5},{2,6},{3,7},{4,0},{5,1},{6,2},{7,3},{8,12},{9,13},{10,... | collective-permute-start | bytes 196616 | tf_op jit(solution)/shard_map/ppermute | solution.py:633
  51.7 6.2 %collective-permute-start.7 = (f32[16,1024]{1,0:T(8,128)S(1)}, f32[16,1024]{1,0:T(8,128)S(1)}, u32[]{:S(2)}, u32[]{:S(2)}) collective-permute-start(f32[16,1024]{1,0:T(8,128)S(1)} %get-tuple-element.26), channel_id=1, source_target_pairs={{0,5},{1,4},{2,7},{3,6},{4,1},{5,0},{6,3},{7,2},{8,13},{9,12},{10,... | collective-permute-start | bytes 196616 | tf_op jit(solution)/shard_map/ppermute | solution.py:633
  52.6 5.3 %collective-permute-start.8 = (f32[16,1024]{1,0:T(8,128)S(1)}, f32[16,1024]{1,0:T(8,128)S(1)}, u32[]{:S(2)}, u32[]{:S(2)}) collective-permute-start(f32[16,1024]{1,0:T(8,128)S(1)} %get-tuple-element.27), channel_id=1, source_target_pairs={{0,6},{1,7},{2,0},{3,1},{4,2},{5,3},{6,4},{7,5},{8,14},{9,15},{10,... | collective-permute-start | bytes 196616 | tf_op jit(solution)/shard_map/ppermute | solution.py:633
  54.0 4.3 %collective-permute-start.9 = (f32[16,1024]{1,0:T(8,128)S(1)}, f32[16,1024]{1,0:T(8,128)S(1)}, u32[]{:S(2)}, u32[]{:S(2)}) collective-permute-start(f32[16,1024]{1,0:T(8,128)S(1)} %get-tuple-element.28), channel_id=1, source_target_pairs={{0,7},{1,6},{2,1},{3,0},{4,3},{5,2},{6,5},{7,4},{8,15},{9,14},{10,... | collective-permute-start | bytes 196616 | tf_op jit(solution)/shard_map/ppermute | solution.py:633

commit v7 on v6

--- a/solution.py
+++ b/solution.py
@@ -284,14 +284,18 @@
         back=np.stack([beside(table) for table in back]),
         waves=np.stack(high_low(waves)),
         in_y=one_dot(block_y),
-        in_x=beside(block_x(sz.n_ex * sz.cuts, sz.cut_elems)),
+        in_x=stacked(block_x(sz.n_ex * sz.cuts, sz.cut_elems)),
         pair_y=np.concatenate([heads, heads, tails], 0),
-        pair_x=beside(np.concatenate([stiff_xx, mass_xx], 1)),
+        pair_x=stacked(np.concatenate([stiff_xx, mass_xx], 1)),
         out_y=one_dot(block_y.T),
-        out_x=beside(block_x(sz.n_ex, sz.elems).T),
+        out_x=stacked(block_x(sz.n_ex, sz.elems).T),
         lam_x=np.asarray(np.tile(lam_x, sz.elems_total)[:, None] * np.ones((1, LANES)), np.float32),
         lam_y=np.asarray(lam_lanes.reshape(1, LANES), np.float32),
     )
+
+
+def stacked(table):
+    return np.concatenate(high_low(table), 0)
 
 
 def split(value):
@@ -307,6 +311,13 @@
 def below(value):
     high, low = split(value)
     return jnp.concatenate([high, low, high], 0)
+
+
+def left_dot(table_ref, value):
+    rows = table_ref.shape[0] // 2
+    high, low = split(value)
+    both = dot(table_ref[...], high)
+    return both[:rows] + both[rows:] + dot(table_ref[:rows, :], low)
 
 
 def along(value):
@@ -421,7 +432,8 @@
     sz,
     *refs,
 ):
-    terms_refs, out_refs, (field_ref, first_ref, work_ref) = refs[: sz.cuts], refs[sz.cuts + 8 : -3], refs[-3:]
+    terms_refs, out_refs = refs[: sz.cuts], refs[sz.cuts + 8 : -4]
+    field_ref, first_ref, work_ref, stiff_ref = refs[-4:]
     in_y_ref, in_x_ref, pair_y_ref, pair_x_ref, out_y_ref, out_x_ref, lam_x_ref, lam_y_ref = refs[
         sz.cuts : sz.cuts + 8
     ]
@@ -475,28 +487,32 @@
         inverses.append(1.0 / (lam_x_ref[...] + (lam_y_ref[...] + shift)))
     for c in range(0, PARTS, 2):
         pair = jnp.concatenate([field_ref[pl.ds((c + d) * x_pad, x_pad), :] for d in range(2)], 1)
-        forced = dot(in_x_ref[...], below(pair))
+        forced = left_dot(in_x_ref, pair)
         for d in range(2):
             mine = forced[:, d * LANES : (d + 1) * LANES]
             first_ref[pl.ds((c + d) * x_eig, x_eig), :] = mine
             work_ref[pl.ds((c + d) * x_eig, x_eig), :] = mine * inverses[(c + d) // 4]
+    high, low = split(work_ref[...])
+    both = dot(jnp.concatenate([high, low, high], 1), pair_y_ref[...])
+    work_ref[...] = both[:, :LANES]
+    stiff_ref[...] = both[:, LANES:]
     for c in range(0, PARTS, 2):
-        shift = shifts[c // 4]
         masses, stiffs = [], []
         for d in range(2):
-            high, low = split(work_ref[pl.ds((c + d) * x_eig, x_eig), :])
-            both = dot(jnp.concatenate([high, low, high], 1), pair_y_ref[...])
-            masses.append(both[:, :LANES])
-            stiffs.append(both[:, LANES:] + shift * both[:, :LANES])
-        stacked = jnp.concatenate([jnp.concatenate(masses, 1), jnp.concatenate(stiffs, 1)], 0)
-        applied = dot(pair_x_ref[...], below(stacked))
+            rows = pl.ds((c + d) * x_eig, x_eig)
+            masses.append(work_ref[rows, :])
+            stiffs.append(stiff_ref[rows, :] + shifts[c // 4] * masses[d])
+        stacked_pair = jnp.concatenate([jnp.concatenate(masses, 1), jnp.concatenate(stiffs, 1)], 0)
+        applied = left_dot(pair_x_ref, stacked_pair)
         for d in range(2):
             rows = pl.ds((c + d) * x_eig, x_eig)
-            total = (2.0 * first_ref[rows, :] - applied[:, d * LANES : (d + 1) * LANES]) * inverses[c // 4]
-            parts = dot(along(total), out_y_ref[...])
-            work_ref[rows, :] = parts[:, :LANES] + parts[:, LANES:]
+            mine = applied[:, d * LANES : (d + 1) * LANES]
+            first_ref[rows, :] = (2.0 * first_ref[rows, :] - mine) * inverses[c // 4]
+    parts = dot(along(first_ref[...]), out_y_ref[...])
+    work_ref[...] = parts[:, :LANES] + parts[:, LANES:]
+    for c in range(0, PARTS, 2):
         pair = jnp.concatenate([work_ref[pl.ds((c + d) * x_eig, x_eig), :] for d in range(2)], 1)
-        solved = dot(out_x_ref[...], below(pair))
+        solved = left_dot(out_x_ref, pair)
         for d in range(2):
             field_ref[pl.ds((c + d) * x_pad, x_pad), :] = solved[:, d * LANES : (d + 1) * LANES]
 
@@ -621,7 +637,7 @@
         functools.partial(smooth_kernel, sz),
         [(sz.own, sz.lane_nodes)] * sz.spots,
         terms + [table[name] for name in names],
-        [(PARTS * sz.x_pad, LANES), (PARTS * sz.x_eig, LANES), (PARTS * sz.x_eig, LANES)],
+        [(PARTS * sz.x_pad, LANES)] + [(PARTS * sz.x_eig, LANES)] * 3,
     )
     for step in sorted(range(1, sz.spots), key=lambda each: each // sz.n_ey == 0):
         shift, turn = step // sz.n_ey, step % sz.n_ey

time: 59.7 us -> 58.1 us (0.973)
  Pallas kernels: 12.6 us -> 10.9 us
    pallas_call x4, Pallas kernels: 12.6 us -> 10.9 us  [call(): pl.pallas_call(kernel, out_shape=[jax.ShapeDtypeStruct(shape, jnp.float32...]
where the time goes in v7:
time: 58.1 us; the launch traced here: 57.9 us
  blocking collectives  20.6 us (35%)
  waiting for transfers between devices  14.2 us (24%)
  starting transfers between devices  12 us (21%)
  Pallas kernels  10.9 us (19%)
    all_to_all x1, blocking collectives, on_device(): lax.all_to_all(spectra, ('mode', 'ex', 'ey'), split_axis=0, concat_axis=0...  20.6 us
    pallas_call x4, Pallas kernels, call(): pl.pallas_call(kernel, out_shape=[jax.ShapeDtypeStruct(shape, jnp.float32...  10.9 us
    ppermute x3, waiting for transfers between devices, on_device(): weak[cut][step] = lax.ppermute(weak[cut][step], 'mode', pairs)  10.3 us
    ppermute x7, starting transfers between devices, on_device(): solved[step] = lax.ppermute(solved[step], ('ex', 'ey'), pairs)  6.31 us
    ppermute x3, starting transfers between devices, on_device(): weak[cut][step] = lax.ppermute(weak[cut][step], 'mode', pairs)  5.7 us
    ppermute x7, waiting for transfers between devices, on_device(): solved[step] = lax.ppermute(solved[step], ('ex', 'ey'), pairs)  3.87 us
  transfers between devices with their start and end apart: 10, of which 6 were waited for; matrix products, arithmetic and copies ran while one was open for 0% of the time, Pallas kernels for 0%

profile of v7, /device:TPU:0, one launch (start us, length us, event | category | flops | bytes accessed | tf_op | source)
XLA Modules:
  0.0 57.9 jit_solution(14551049649034312475)
XLA Ops:
  0.0 4.0 %shard_map.127 = (f32[256,128]{1,0:T(8,128)S(1)}, f32[256,128]{1,0:T(8,128)S(1)}, f32[256,128]{1,0:T(8,128)S(1)}, f32[256,128]{1,0:T(8,128)S(1)}) custom-call(f32[1152,64]{1,0:T(8,128)} %bitcast.5, f32[1152,64]{1,0:T(8,128)} %bitcast.6, bf16[1008,432]{1,0:T(8,128)(2,1)} %constant.22.clone.lift_hbm, bf16[2,264,2016]{2,1,0:T(8,128)(2,1)} %constant.23.clone.back_hbm), custom_call_target="tpu_custom_call" | custom-call | flops 1000000000 | bytes 1000000 | tf_op jit(solution)/shard_map/pallas_call | solution.py:579
  4.0 3.1 %collective-permute-start = (f32[256,128]{1,0:T(8,128)S(1)}, f32[256,128]{1,0:T(8,128)S(1)}, u32[]{:S(2)}, u32[]{:S(2)}) collective-permute-start(f32[256,128]{1,0:T(8,128)S(1)} %get-tuple-element.18), channel_id=1, source_target_pairs={{0,8},{8,0},{16,24},{24,16},{1,9},{9,1},{17,25},{25,17},{2,10},{10... | collective-permute-start | bytes 393224 | tf_op jit(solution)/shard_map/ppermute | solution.py:621
  7.1 2.6 %collective-permute-start.1 = (f32[256,128]{1,0:T(8,128)S(1)}, f32[256,128]{1,0:T(8,128)S(1)}, u32[]{:S(2)}, u32[]{:S(2)}) collective-permute-start(f32[256,128]{1,0:T(8,128)S(1)} %get-tuple-element.19), channel_id=1, source_target_pairs={{0,16},{8,24},{16,0},{24,8},{1,17},{9,25},{17,1},{25,9},{2,18},{10... | collective-permute-start | bytes 393224 | tf_op jit(solution)/shard_map/ppermute | solution.py:621
  9.7 2.4 %collective-permute-done.refs_1_ = f32[256,128]{1,0:T(8,128)S(1)} collective-permute-done((f32[256,128]{1,0:T(8,128)S(1)}, f32[256,128]{1,0:T(8,128)S(1)}, u32[]{:S(2)}, u32[]{:S(2)}) %collective-permute-start) | collective-permute-done | bytes 131104 | tf_op jit(solution)/shard_map/ppermute | solution.py:621
  12.1 7.9 %collective-permute-done.1.refs_2_ = f32[256,128]{1,0:T(8,128)S(1)} collective-permute-done((f32[256,128]{1,0:T(8,128)S(1)}, f32[256,128]{1,0:T(8,128)S(1)}, u32[]{:S(2)}, u32[]{:S(2)}) %collective-permute-start.1) | collective-permute-done | bytes 131104 | tf_op jit(solution)/shard_map/ppermute | solution.py:621
  20.0 0.0 copy-start.2
  20.0 0.0 copy-start.3
  20.0 0.0 copy-start.4
  20.1 0.0 copy-start.6
  20.1 0.6 %shard_map.128 = f32[512,256]{1,0:T(8,128)S(1)} custom-call(f32[256,128]{1,0:T(8,128)S(1)} %get-tuple-element.17.refs_0_, f32[256,128]{1,0:T(8,128)S(1)} %collective-permute-done.refs_1_, f32[256,128]{1,0:T(8,128)S(1)} %collective-permute-done.1.refs_2_, f32[256,128]{1,0:T(8,128)S(1)} %collective-permute-done.2.refs_3_, bf16[2,256,256]{2,1,0:T(8,128)(2,1)S(1)} %copy-done.1), custom_call_target="tpu_custom_call" | custom-call | flops 99999997952 | bytes 1000000 | tf_op jit(solution)/shard_map/pallas_call | solution.py:579
  20.7 20.6 %all_to_all.5.refs_0_ = f32[32,16,256]{2,1,0:T(8,128)S(1)} all-to-all(f32[32,16,256]{2,1,0:T(8,128)S(1)} %bitcast.4), channel_id=1, replica_groups=mesh['mode'=4,'ex'=4,'ey'=2] {'mode','ex','ey'}, dimensions={0} | all-to-all | bytes 1048576 | tf_op jit(solution)/shard_map/all_to_all | solution.py:633
  41.3 5.2 %shard_map.129 = (f32[16,1024]{1,0:T(8,128)S(1)}, f32[16,1024]{1,0:T(8,128)S(1)}, f32[16,1024]{1,0:T(8,128)S(1)}, f32[16,1024]{1,0:T(8,128)S(1)}, f32[16,1024]{1...) custom-call(f32[32,16,256]{2,1,0:T(8,128)S(1)} %all_to_all.5.refs_0_, ...), custom_call_target="tpu_custom_call" | custom-call | flops 1000000000 | bytes 1000000 | tf_op jit(solution)/shard_map/pallas_call | solution.py:579
  46.6 0.1 collective-permute-start.3
  46.7 1.3 %collective-permute-start.4 = (f32[16,1024]{1,0:T(8,128)S(1)}, f32[16,1024]{1,0:T(8,128)S(1)}, u32[]{:S(2)}, u32[]{:S(2)}) collective-permute-start(f32[16,1024]{1,0:T(8,128)S(1)} %get-tuple-element.23), channel_id=1, source_target_pairs={{0,2},{1,3},{2,4},{3,5},{4,6},{5,7},{6,0},{7,1},{8,10},{9,11},{10,... | collective-permute-start | bytes 196616 | tf_op jit(solution)/shard_map/ppermute | solution.py:649
  48.0 1.2 %collective-permute-start.5 = (f32[16,1024]{1,0:T(8,128)S(1)}, f32[16,1024]{1,0:T(8,128)S(1)}, u32[]{:S(2)}, u32[]{:S(2)}) collective-permute-start(f32[16,1024]{1,0:T(8,128)S(1)} %get-tuple-element.24), channel_id=1, source_target_pairs={{0,3},{1,2},{2,5},{3,4},{4,7},{5,6},{6,1},{7,0},{8,11},{9,10},{10,... | collective-permute-start | bytes 196616 | tf_op jit(solution)/shard_map/ppermute | solution.py:649
  49.2 0.8 %collective-permute-start.6 = (f32[16,1024]{1,0:T(8,128)S(1)}, f32[16,1024]{1,0:T(8,128)S(1)}, u32[]{:S(2)}, u32[]{:S(2)}) collective-permute-start(f32[16,1024]{1,0:T(8,128)S(1)} %get-tuple-element.25), channel_id=1, source_target_pairs={{0,4},{1,5},{2,6},{3,7},{4,0},{5,1},{6,2},{7,3},{8,12},{9,13},{10,... | collective-permute-start | bytes 196616 | tf_op jit(solution)/shard_map/ppermute | solution.py:649
  50.0 0.9 %collective-permute-start.7 = (f32[16,1024]{1,0:T(8,128)S(1)}, f32[16,1024]{1,0:T(8,128)S(1)}, u32[]{:S(2)}, u32[]{:S(2)}) collective-permute-start(f32[16,1024]{1,0:T(8,128)S(1)} %get-tuple-element.26), channel_id=1, source_target_pairs={{0,5},{1,4},{2,7},{3,6},{4,1},{5,0},{6,3},{7,2},{8,13},{9,12},{10,... | collective-permute-start | bytes 196616 | tf_op jit(solution)/shard_map/ppermute | solution.py:649
  50.9 1.5 %collective-permute-start.8 = (f32[16,1024]{1,0:T(8,128)S(1)}, f32[16,1024]{1,0:T(8,128)S(1)}, u32[]{:S(2)}, u32[]{:S(2)}) collective-permute-start(f32[16,1024]{1,0:T(8,128)S(1)} %get-tuple-element.27), channel_id=1, source_target_pairs={{0,6},{1,7},{2,0},{3,1},{4,2},{5,3},{6,4},{7,5},{8,14},{9,15},{10,... | collective-permute-start | bytes 196616 | tf_op jit(solution)/shard_map/ppermute | solution.py:649
  52.4 0.5 collective-permute-start.9
  52.9 0.4 collective-permute-done.5.refs_3_
  53.3 1.6 %collective-permute-done.6.refs_4_ = f32[16,1024]{1,0:T(8,128)S(1)} collective-permute-done((f32[16,1024]{1,0:T(8,128)S(1)}, f32[16,1024]{1,0:T(8,128)S(1)}, u32[]{:S(2)}, u32[]{:S(2)}) %collective-permute-start.6) | collective-permute-done | bytes 65568 | tf_op jit(solution)/shard_map/ppermute | solution.py:649
  54.9 1.3 %collective-permute-done.7.refs_5_ = f32[16,1024]{1,0:T(8,128)S(1)} collective-permute-done((f32[16,1024]{1,0:T(8,128)S(1)}, f32[16,1024]{1,0:T(8,128)S(1)}, u32[]{:S(2)}, u32[]{:S(2)}) %collective-permute-start.7) | collective-permute-done | bytes 65568 | tf_op jit(solution)/shard_map/ppermute | solution.py:649
  56.2 0.6 collective-permute-done.9.refs_7_
  56.8 1.1 %shard_map.130 = f32[1152,128]{1,0:T(8,128)} custom-call(f32[16,1024]{1,0:T(8,128)S(1)} %get-tuple-element.21.refs_0_, f32[16,1024]{1,0:T(8,128)S(1)} %collective-permute-done.3.refs_1_, f32[16,1024]{1,0:T(8,128)S(1)} %collective-permute-done.4.refs_2_, f32[16,1024]{1,0:T(8,128)S(1)} %collective-permute-done.5.refs_3_, ...), custom_call_target="tpu_custom_call" | custom-call | flops 1000000000 | bytes 1000000 | tf_op jit(solution)/shard_map/pallas_call | solution.py:579
  (19 shorter events, 0.0 us)
Async XLA Ops:
  0.0 20.0 %copy-start.1 = (bf16[2,256,256]{2,1,0:T(8,128)(2,1)S(1)}, bf16[2,256,256]{2,1,0:T(8,128)(2,1)}, u32[]{:S(2)}) copy-start(bf16[2,256,256]{2,1,0:T(8,128)(2,1)} %constant.24.clone.refs_4_) | copy-start | bytes 786436
  4.0 8.1 %collective-permute-start = (f32[256,128]{1,0:T(8,128)S(1)}, f32[256,128]{1,0:T(8,128)S(1)}, u32[]{:S(2)}, u32[]{:S(2)}) collective-permute-start(f32[256,128]{1,0:T(8,128)S(1)} %get-tuple-element.18), channel_id=1, source_target_pairs={{0,8},{8,0},{16,24},{24,16},{1,9},{9,1},{17,25},{25,17},{2,10},{10... | collective-permute-start | bytes 393224 | tf_op jit(solution)/shard_map/ppermute | solution.py:621
  7.1 12.9 %collective-permute-start.1 = (f32[256,128]{1,0:T(8,128)S(1)}, f32[256,128]{1,0:T(8,128)S(1)}, u32[]{:S(2)}, u32[]{:S(2)}) collective-permute-start(f32[256,128]{1,0:T(8,128)S(1)} %get-tuple-element.19), channel_id=1, source_target_pairs={{0,16},{8,24},{16,0},{24,8},{1,17},{9,25},{17,1},{25,9},{2,18},{10... | collective-permute-start | bytes 393224 | tf_op jit(solution)/shard_map/ppermute | solution.py:621
  9.7 10.3 %collective-permute-start.2 = (f32[256,128]{1,0:T(8,128)S(1)}, f32[256,128]{1,0:T(8,128)S(1)}, u32[]{:S(2)}, u32[]{:S(2)}) collective-permute-start(f32[256,128]{1,0:T(8,128)S(1)} %get-tuple-element.20), channel_id=1, source_target_pairs={{0,24},{8,16},{16,8},{24,0},{1,25},{9,17},{17,9},{25,1},{2,26},{10... | collective-permute-start | bytes 393224 | tf_op jit(solution)/shard_map/ppermute | solution.py:621
  20.0 21.3 %copy-start = (bf16[448,448]{1,0:T(8,128)(2,1)S(1)}, bf16[448,448]{1,0:T(8,128)(2,1)}, u32[]{:S(2)}) copy-start(bf16[448,448]{1,0:T(8,128)(2,1)} %constant.28.clone.refs_4_) | copy-start | bytes 1204228
  20.0 21.3 %copy-start.2 = (bf16[448,192]{1,0:T(8,128)(2,1)S(1)}, bf16[448,192]{1,0:T(8,128)(2,1)}, u32[]{:S(2)}) copy-start(bf16[448,192]{1,0:T(8,128)(2,1)} %constant.26.clone.refs_2_) | copy-start | bytes 516100
  20.0 21.3 %copy-start.3 = (bf16[384,224]{1,0:T(8,128)(2,1)S(1)}, bf16[384,224]{1,0:T(8,128)(2,1)}, u32[]{:S(2)}) copy-start(bf16[384,224]{1,0:T(8,128)(2,1)} %constant.30.clone.refs_6_) | copy-start | bytes 516100
  20.0 21.3 %copy-start.4 = (bf16[384,256]{1,0:T(8,128)(2,1)S(1)}, bf16[384,256]{1,0:T(8,128)(2,1)}, u32[]{:S(2)}) copy-start(bf16[384,256]{1,0:T(8,128)(2,1)} %constant.27.clone.refs_3_) | copy-start | bytes 589828
  20.0 21.3 %copy-start.5 = (bf16[256,256]{1,0:T(8,128)(2,1)S(1)}, bf16[256,256]{1,0:T(8,128)(2,1)}, u32[]{:S(2)}) copy-start(bf16[256,256]{1,0:T(8,128)(2,1)} %constant.29.clone.refs_5_) | copy-start | bytes 393220
  20.1 21.3 %copy-start.6 = (bf16[256,256]{1,0:T(8,128)(2,1)S(1)}, bf16[256,256]{1,0:T(8,128)(2,1)}, u32[]{:S(2)}) copy-start(bf16[256,256]{1,0:T(8,128)(2,1)} %constant.25.clone.refs_1_) | copy-start | bytes 393220
  20.1 21.3 %copy-start.7 = (f32[224,128]{1,0:T(8,128)S(1)}, f32[224,128]{1,0:T(8,128)}, u32[]{:S(2)}) copy-start(f32[224,128]{1,0:T(8,128)} %constant.31.clone.refs_7_) | copy-start | bytes 344068
  20.1 21.3 %copy-start.8 = (f32[1,128]{1,0:T(1,128)S(1)}, f32[1,128]{1,0:T(1,128)}, u32[]{:S(2)}) copy-start(f32[1,128]{1,0:T(1,128)} %constant.32.clone.refs_8_) | copy-start | bytes 1540
  46.6 4.3 %collective-permute-start.3 = (f32[16,1024]{1,0:T(8,128)S(1)}, f32[16,1024]{1,0:T(8,128)S(1)}, u32[]{:S(2)}, u32[]{:S(2)}) collective-permute-start(f32[16,1024]{1,0:T(8,128)S(1)} %get-tuple-element.22), channel_id=1, source_target_pairs={{0,1},{1,0},{2,3},{3,2},{4,5},{5,4},{6,7},{7,6},{8,9},{9,8},{10,11... | collective-permute-start | bytes 196616 | tf_op jit(solution)/shard_map/ppermute | solution.py:649
  46.7 5.7 %collective-permute-start.4 = (f32[16,1024]{1,0:T(8,128)S(1)}, f32[16,1024]{1,0:T(8,128)S(1)}, u32[]{:S(2)}, u32[]{:S(2)}) collective-permute-start(f32[16,1024]{1,0:T(8,128)S(1)} %get-tuple-element.23), channel_id=1, source_target_pairs={{0,2},{1,3},{2,4},{3,5},{4,6},{5,7},{6,0},{7,1},{8,10},{9,11},{10,... | collective-permute-start | bytes 196616 | tf_op jit(solution)/shard_map/ppermute | solution.py:649
  48.0 5.3 %collective-permute-start.5 = (f32[16,1024]{1,0:T(8,128)S(1)}, f32[16,1024]{1,0:T(8,128)S(1)}, u32[]{:S(2)}, u32[]{:S(2)}) collective-permute-start(f32[16,1024]{1,0:T(8,128)S(1)} %get-tuple-element.24), channel_id=1, source_target_pairs={{0,3},{1,2},{2,5},{3,4},{4,7},{5,6},{6,1},{7,0},{8,11},{9,10},{10,... | collective-permute-start | bytes 196616 | tf_op jit(solution)/shard_map/ppermute | solution.py:649
  49.2 5.7 %collective-permute-start.6 = (f32[16,1024]{1,0:T(8,128)S(1)}, f32[16,1024]{1,0:T(8,128)S(1)}, u32[]{:S(2)}, u32[]{:S(2)}) collective-permute-start(f32[16,1024]{1,0:T(8,128)S(1)} %get-tuple-element.25), channel_id=1, source_target_pairs={{0,4},{1,5},{2,6},{3,7},{4,0},{5,1},{6,2},{7,3},{8,12},{9,13},{10,... | collective-permute-start | bytes 196616 | tf_op jit(solution)/shard_map/ppermute | solution.py:649
  50.0 6.2 %collective-permute-start.7 = (f32[16,1024]{1,0:T(8,128)S(1)}, f32[16,1024]{1,0:T(8,128)S(1)}, u32[]{:S(2)}, u32[]{:S(2)}) collective-permute-start(f32[16,1024]{1,0:T(8,128)S(1)} %get-tuple-element.26), channel_id=1, source_target_pairs={{0,5},{1,4},{2,7},{3,6},{4,1},{5,0},{6,3},{7,2},{8,13},{9,12},{10,... | collective-permute-start | bytes 196616 | tf_op jit(solution)/shard_map/ppermute | solution.py:649
  50.9 5.3 %collective-permute-start.8 = (f32[16,1024]{1,0:T(8,128)S(1)}, f32[16,1024]{1,0:T(8,128)S(1)}, u32[]{:S(2)}, u32[]{:S(2)}) collective-permute-start(f32[16,1024]{1,0:T(8,128)S(1)} %get-tuple-element.27), channel_id=1, source_target_pairs={{0,6},{1,7},{2,0},{3,1},{4,2},{5,3},{6,4},{7,5},{8,14},{9,15},{10,... | collective-permute-start | bytes 196616 | tf_op jit(solution)/shard_map/ppermute | solution.py:649
  52.4 4.4 %collective-permute-start.9 = (f32[16,1024]{1,0:T(8,128)S(1)}, f32[16,1024]{1,0:T(8,128)S(1)}, u32[]{:S(2)}, u32[]{:S(2)}) collective-permute-start(f32[16,1024]{1,0:T(8,128)S(1)} %get-tuple-element.28), channel_id=1, source_target_pairs={{0,7},{1,6},{2,1},{3,0},{4,3},{5,2},{6,5},{7,4},{8,15},{9,14},{10,... | collective-permute-start | bytes 196616 | tf_op jit(solution)/shard_map/ppermute | solution.py:649

commit v8 on v7

--- a/solution.py
+++ b/solution.py
@@ -178,14 +178,16 @@
         self.cut_elems = self.elems // self.cuts
         self.cut_x = self.order * self.cut_elems + 1
         share = -(-self.cut_x * self.block_y // self.n_mode)
-        self.share = ceil_to(share, LANES if share > 64 else 16)
-        self.cut_nodes = self.share * self.n_mode
+        self.sent = ceil_to(share, 8)
+        self.share = ceil_to(self.sent, LANES if share > 64 else 16)
+        self.cut_nodes = self.sent * self.n_mode
         self.lane_nodes = ceil_to(self.block_x * self.block_y + 2, LANES)
         self.columns = 2 * self.planes
         self.spots = self.n_ex * self.n_ey
         self.own = self.columns // self.spots
         self.folds = self.own // PARTS
         self.fold_width = LANES // self.folds
+        self.stripe = self.fold_width // self.n_ey
         self.points = self.nodes + 2
         self.x_cuts = self.n_ex * self.cuts * self.cut_x
         self.x_pad = ceil_to(max(self.x_cuts, self.n_ex * self.block_x), 16)
@@ -193,7 +195,7 @@
         self.y_eig = self.rows_total * self.points
         self.fine = ceil_to(self.gauss * self.gauss, 16)
         assert self.own == PARTS * self.folds and self.x_eig % 16 == 0
-        assert max(self.y_eig, self.n_ey * self.block_y) <= self.fold_width
+        assert self.y_eig <= self.fold_width and self.block_y < self.stripe
         assert 2 * self.planes == LANES
 
 
@@ -255,10 +257,11 @@
         return table
 
     width, folds = sz.fold_width, sz.folds
-    block_y = np.zeros((width, width))
+    enter_y, leave_y = np.zeros((width, width)), np.zeros((width, width))
     for place in range(sz.n_ey):
         for jj, j in enumerate(sz.inner[place]):
-            block_y[place * sz.block_y + jj, : sz.y_eig] = to_y[:, sz.order * sz.rows * place + j]
+            enter_y[place * sz.stripe + jj, : sz.y_eig] = to_y[:, sz.order * sz.rows * place + j]
+            leave_y[: sz.y_eig, place * sz.stripe + j] = to_y[:, sz.order * sz.rows * place + j]
 
     def folded(table):
         padded = np.zeros((width, width))
@@ -283,11 +286,11 @@
         lift=beside(lift),
         back=np.stack([beside(table) for table in back]),
         waves=np.stack(high_low(waves)),
-        in_y=one_dot(block_y),
+        in_y=one_dot(enter_y),
         in_x=stacked(block_x(sz.n_ex * sz.cuts, sz.cut_elems)),
         pair_y=np.concatenate([heads, heads, tails], 0),
         pair_x=stacked(np.concatenate([stiff_xx, mass_xx], 1)),
-        out_y=one_dot(block_y.T),
+        out_y=one_dot(leave_y),
         out_x=stacked(block_x(sz.n_ex, sz.elems).T),
         lam_x=np.asarray(np.tile(lam_x, sz.elems_total)[:, None] * np.ones((1, LANES)), np.float32),
         lam_y=np.asarray(lam_lanes.reshape(1, LANES), np.float32),
@@ -334,6 +337,29 @@
     if count & (count - 1) == 0:
         return spot ^ step
     return (spot - step + count) % count
+
+
+def rotate(tiles, shift):
+    width = tiles[0].shape[-1]
+    whole, part = shift % (width * len(tiles)) // width, shift % width
+    if part == 0:
+        return [tiles[t - whole] for t in range(len(tiles))]
+    moved = [pltpu.roll(tile, part, tile.ndim - 1) for tile in tiles]
+    crossed = lane_index(tiles[0].shape) < part
+    return [jnp.where(crossed, moved[t - whole - 1], moved[t - whole]) for t in range(len(tiles))]
+
+
+def runs(sz, i, shift, start, count, size, share):
+    found = []
+    for j in range(start, start + count):
+        n = i * sz.block_y + j
+        part, lane = n // size, (n % size + shift) % share
+        key = (part, lane // LANES)
+        if found and found[-1][:2] == key and found[-1][2] + found[-1][4] == lane % LANES:
+            found[-1][4] += 1
+        else:
+            found.append([*key, lane % LANES, shift + j, 1])
+    return found
 
 
 def lane_index(shape):
@@ -405,27 +431,40 @@
             carry = mine[length:]
         for turn in range(sz.n_mode):
             goal = partner(spot, turn, sz.n_mode)
-            out_refs[cut * sz.n_mode + turn][...] = total_ref[pl.ds(pl.multiple_of(goal * sz.share, 8), sz.share), :]
+            out_refs[cut * sz.n_mode + turn][...] = total_ref[pl.ds(pl.multiple_of(goal * sz.sent, 8), sz.sent), :]
 
 
 def transform_kernel(sz, *refs):
-    weak_refs, (waves_ref, out_ref, mixed_ref, signal_ref) = refs[: sz.n_mode], refs[-4:]
-    spot = lax.axis_index("mode")
+    weak_refs, (waves_ref, out_ref, mixed_ref, signal_ref, stage_ref) = refs[: sz.n_mode], refs[-5:]
+    spot, place = lax.axis_index("mode"), lax.axis_index("ey")
+    if sz.share > sz.sent:
+        stage_ref[...] = jnp.zeros(stage_ref.shape, jnp.float32)
     for step, weak_ref in enumerate(weak_refs):
-        turned = weak_ref[...].T
+        for q in range(sz.n_ey):
+
+            @pl.when(place == q)
+            def _(begin=q * sz.stripe % sz.share, weak_ref=weak_ref):
+                end = min(begin + sz.sent, sz.share)
+                stage_ref[begin:end, :] = weak_ref[: end - begin, :]
+                if end - begin < sz.sent:
+                    stage_ref[: sz.sent - (end - begin), :] = weak_ref[end - begin :, :]
+
+        turned = stage_ref[...].T
         first = pl.multiple_of(origin(spot, step, sz.n_mode) * sz.planes, 8)
         for k in range(2):
             signal_ref[k, pl.ds(first, sz.planes), :] = turned[k * sz.planes : (k + 1) * sz.planes]
-    modes = sz.planes_total
+    modes, tiles = sz.planes_total, mixed_ref.shape[0]
+    last = min(LANES, sz.share)
     for k in range(2):
         high, low = split(signal_ref[k])
         part = dot(waves_ref[0], high) + dot(waves_ref[0], low) + dot(waves_ref[1], high)
-        for t in range(mixed_ref.shape[0]):
-            tile = part[:, t * LANES : (t + 1) * LANES]
-            mixed_ref[t, pl.ds(k, modes, stride=2), pl.ds(0, tile.shape[1])] = tile
-    for t in range(mixed_ref.shape[0]):
-        last = min(LANES, sz.share - t * LANES)
-        out_ref[:, pl.ds(t * LANES, last)] = mixed_ref[t, :, pl.ds(0, last)]
+        for t in range(tiles):
+            mixed_ref[t, pl.ds(k, modes, stride=2), pl.ds(0, last)] = part[:, t * LANES : (t + 1) * LANES]
+    shape = (sz.n_mode * sz.spots, sz.folds, PARTS, last)
+    mixed = [mixed_ref[t, :, pl.ds(0, last)].reshape(shape) for t in range(tiles)]
+    for fold in range(sz.folds):
+        for t, tile in enumerate(rotate([each[:, fold] for each in mixed], fold * sz.fold_width % sz.share)):
+            out_ref[:, fold, :, pl.ds(t * LANES, last)] = tile
 
 
 def smooth_kernel(
@@ -437,13 +476,21 @@
     in_y_ref, in_x_ref, pair_y_ref, pair_x_ref, out_y_ref, out_x_ref, lam_x_ref, lam_y_ref = refs[
         sz.cuts : sz.cuts + 8
     ]
-    width, folds, strip = sz.fold_width, sz.folds, sz.block_y
-    tiles = -(-sz.cut_nodes // LANES)
+    width, folds = sz.fold_width, sz.folds
+    tiles = -(-sz.share // LANES)
     lanes = lane_index((PARTS, LANES))
     x_pad, x_eig = sz.x_pad, sz.x_eig
     place, spot = lax.axis_index("ey"), lax.axis_index("ex")
     device = (lax.axis_index("mode") * sz.n_ex + spot) * sz.n_ey + place
     first_mode = device * (sz.own // 4)
+    masks = {}
+
+    def within(low, length):
+        if (low, length) not in masks:
+            masks[low, length] = (lanes >= low) & (lanes < low + length)
+        return masks[low, length]
+
+    strips = [(q, fold, fold * width + q * sz.stripe) for q in range(sz.n_ey) for fold in range(folds)]
 
     for c in range(PARTS):
         field_ref[pl.ds(c * x_pad + sz.x_cuts, x_pad - sz.x_cuts), :] = jnp.zeros(
@@ -452,28 +499,31 @@
     for p, cut in [(p, cut) for p in range(sz.n_ex) for cut in range(sz.cuts)]:
         block = (spot + p) % sz.n_ex
         held = {}
-        for q in range(sz.n_ey):
-            for fold in range(folds):
-                whole = jnp.concatenate(
-                    [
-                        terms_refs[cut][(z * sz.n_ex + block) * sz.n_ey + q, pl.ds(fold * PARTS, PARTS), :]
-                        for z in range(sz.n_mode)
-                    ],
-                    1,
-                )
-                held[q, fold] = [whole[:, t * LANES : (t + 1) * LANES] for t in range(tiles)]
+        for q, fold, _ in strips:
+            for z in range(sz.n_mode):
+                whole = terms_refs[cut][(z * sz.n_ex + block) * sz.n_ey + q, pl.ds(fold * PARTS, PARTS), :]
+                if sz.share < LANES:
+                    whole = jnp.concatenate([whole] * (LANES // sz.share), 1)
+                for t in range(tiles):
+                    held[q, fold, z, t] = whole[:, t * LANES : (t + 1) * LANES]
         for i in range(sz.cut_x):
-            start = i * strip
-            t, r = start // LANES, start % LANES
-            result = jnp.zeros((PARTS, LANES), jnp.float32)
-            for fold in range(folds):
-                for q in range(sz.n_ey):
-                    source = held[q, fold][t]
-                    if r + strip > LANES:
-                        source = jnp.where(lanes >= r, source, held[q, fold][t + 1])
-                    goal = fold * width + q * strip
-                    moved = pltpu.roll(source, (goal - r) % LANES, 1) if goal != r else source
-                    result = jnp.where((lanes >= goal) & (lanes < goal + strip), moved, result)
+            groups = {}
+            for q, fold, goal in strips:
+                for z, t, lane, end, length in runs(sz, i, goal, 0, len(sz.inner[q]), sz.sent, sz.share):
+                    source = held[q, fold, z, t]
+                    shift = (end - lane) % LANES
+                    old = groups.get(shift)
+                    if old is not None:
+                        source = jnp.where(within(lane, length), source, old[0])
+                    groups[shift] = (source, (old[1] if old else []) + [(end, length)])
+            result = None
+            for shift, (source, spans) in groups.items():
+                moved = pltpu.roll(source, shift, 1) if shift else source
+                if result is None:
+                    result = moved
+                else:
+                    for low, length in spans:
+                        result = jnp.where(within(low, length), moved, result)
             field_ref[pl.ds((p * sz.cuts + cut) * sz.cut_x + i, PARTS, stride=x_pad), :] = result
 
     parts = dot(along(field_ref[...]), in_y_ref[...])
@@ -520,19 +570,17 @@
         made = {}
         for i in range(sz.block_x):
             source = field_ref[pl.ds(p * sz.block_x + i, PARTS, stride=x_pad), :]
-            for q in range(sz.n_ey):
-                begin = i * strip + sz.inner[q][0]
-                count = len(sz.inner[q])
-                t, r = begin // LANES, begin % LANES
-                for fold in range(folds):
-                    origin = fold * width + q * strip
-                    moved = pltpu.roll(source, (r - origin) % LANES, 1) if origin != r else source
-                    for tile, low, high in ((t, r, r + count), (t + 1, 0, r + count - LANES)):
-                        if high > 0:
-                            old = made.get((q, fold, tile))
-                            if old is None:
-                                old = jnp.zeros((PARTS, LANES), jnp.float32)
-                            made[q, fold, tile] = jnp.where((lanes >= low) & (lanes < high), moved, old)
+            shift = i * sz.block_y % LANES
+            moved = pltpu.roll(source, shift, 1) if shift else source
+            for q, fold, goal in strips:
+                inner = sz.inner[q]
+                for _, tile, lane, _, length in runs(
+                    sz, i, goal, inner[0], len(inner), sz.lane_nodes, sz.lane_nodes
+                ):
+                    old = made.get((q, fold, tile), moved)
+                    if old is not moved:
+                        old = jnp.where(within(lane, length), moved, old)
+                    made[q, fold, tile] = old
         for fold in range(folds):
             for tile in range(sz.lane_nodes // LANES):
                 for turn in range(sz.n_ey):
@@ -549,7 +597,20 @@
     for step, solved_ref in enumerate(solved_refs):
         shift, turn = step // sz.n_ey, step % sz.n_ey
         source = (spot - shift + sz.n_ex) % sz.n_ex * sz.n_ey + (place - turn + sz.n_ey) % sz.n_ey
-        stacked_ref[pl.ds(pl.multiple_of(source * sz.own, PARTS), sz.own), :] = solved_ref[...]
+        for q in range(sz.n_ey):
+
+            @pl.when(place == q)
+            def _(q=q, solved_ref=solved_ref, source=source):
+                for fold in range(sz.folds):
+                    shift = -(fold * sz.fold_width + q * sz.stripe)
+                    tiles = [
+                        solved_ref[pl.ds(fold * PARTS, PARTS), pl.ds(t * LANES, LANES)]
+                        for t in range(sz.lane_nodes // LANES)
+                    ]
+                    rows = pl.ds(pl.multiple_of(source * sz.own + fold * PARTS, PARTS), PARTS)
+                    for t, tile in enumerate(rotate(tiles, shift)):
+                        stacked_ref[rows, pl.ds(t * LANES, LANES)] = tile
+
     turned_ref[...] = stacked_ref[...].T
     spots = sz.elems * sz.rows
     for e in range(sz.elems):
@@ -594,7 +655,7 @@
     heights = [float(height) for height in tables["heights"]]
     pieces = call(
         functools.partial(advect_kernel, sz, heights),
-        [(sz.share, LANES)] * (sz.n_mode * sz.cuts),
+        [(sz.sent, LANES)] * (sz.n_mode * sz.cuts),
         [
             pltpu.with_memory_space_constraint(each, pltpu.HBM)
             for each in (
@@ -623,9 +684,13 @@
     for cut in range(sz.cuts):
         (spectra,) = call(
             functools.partial(transform_kernel, sz),
-            [(2 * sz.planes_total, sz.share)],
+            [(sz.n_mode * sz.spots, sz.folds, PARTS, sz.share)],
             [*weak[cut], *ahead, table["waves"]],
-            [(-(-sz.share // LANES), 2 * sz.planes_total, LANES), (2, sz.planes_total, sz.share)],
+            [
+                (-(-sz.share // LANES), 2 * sz.planes_total, LANES),
+                (2, sz.planes_total, sz.share),
+                (sz.share, LANES),
+            ],
             [pltpu.VMEM] * sz.n_mode + [pl.ANY] * len(ahead) + [pltpu.VMEM],
             flops=10**11 if cut == sz.cuts - 1 else 10**8,
         )

time: 58.1 us -> 63.4 us (1.091)
  Pallas kernels: 10.9 us -> 16.6 us
    pallas_call x4, Pallas kernels: 10.9 us -> 16.6 us  [call(): pl.pallas_call(kernel, out_shape=[jax.ShapeDtypeStruct(shape, jnp.float32...]
where the time goes in v8:
time: 63.4 us; the launch traced here: 63.2 us
  blocking collectives  20.5 us (32%)
  Pallas kernels  16.6 us (26%)
  waiting for transfers between devices  13.9 us (22%)
  starting transfers between devices  12 us (19%)
    all_to_all x1, blocking collectives, on_device(): lax.all_to_all(spectra, ('mode', 'ex', 'ey'), split_axis=0, concat_axis=0...  20.5 us
    pallas_call x4, Pallas kernels, call(): pl.pallas_call(kernel, out_shape=[jax.ShapeDtypeStruct(shape, jnp.float32...  16.6 us
    ppermute x3, waiting for transfers between devices, on_device(): weak[cut][step] = lax.ppermute(weak[cut][step], 'mode', pairs)  10 us
    ppermute x7, starting transfers between devices, on_device(): solved[step] = lax.ppermute(solved[step], ('ex', 'ey'), pairs)  6.31 us
    ppermute x3, starting transfers between devices, on_device(): weak[cut][step] = lax.ppermute(weak[cut][step], 'mode', pairs)  5.71 us
    ppermute x7, waiting for transfers between devices, on_device(): solved[step] = lax.ppermute(solved[step], ('ex', 'ey'), pairs)  3.87 us
  transfers between devices with their start and end apart: 10, of which 6 were waited for; matrix products, arithmetic and copies ran while one was open for 0% of the time, Pallas kernels for 0%

profile of v8, /device:TPU:0, one launch (start us, length us, event | category | flops | bytes accessed | tf_op | source)
XLA Modules:
  0.0 63.2 jit_solution(12124392980536385721)
XLA Ops:
  0.0 4.0 %shard_map.127 = (f32[248,128]{1,0:T(8,128)S(1)}, f32[248,128]{1,0:T(8,128)S(1)}, f32[248,128]{1,0:T(8,128)S(1)}, f32[248,128]{1,0:T(8,128)S(1)}) custom-call(f32[1152,64]{1,0:T(8,128)} %bitcast.5, f32[1152,64]{1,0:T(8,128)} %bitcast.6, bf16[1008,432]{1,0:T(8,128)(2,1)} %constant.22.clone.lift_hbm, bf16[2,264,2016]{2,1,0:T(8,128)(2,1)} %constant.23.clone.back_hbm), custom_call_target="tpu_custom_call" | custom-call | flops 1000000000 | bytes 1000000 | tf_op jit(solution)/shard_map/pallas_call | solution.py:640
  4.0 3.1 %collective-permute-start = (f32[248,128]{1,0:T(8,128)S(1)}, f32[248,128]{1,0:T(8,128)S(1)}, u32[]{:S(2)}, u32[]{:S(2)}) collective-permute-start(f32[248,128]{1,0:T(8,128)S(1)} %get-tuple-element.18), channel_id=1, source_target_pairs={{0,8},{8,0},{16,24},{24,16},{1,9},{9,1},{17,25},{25,17},{2,10},{10... | collective-permute-start | bytes 380936 | tf_op jit(solution)/shard_map/ppermute | solution.py:682
  7.1 2.6 %collective-permute-start.1 = (f32[248,128]{1,0:T(8,128)S(1)}, f32[248,128]{1,0:T(8,128)S(1)}, u32[]{:S(2)}, u32[]{:S(2)}) collective-permute-start(f32[248,128]{1,0:T(8,128)S(1)} %get-tuple-element.19), channel_id=1, source_target_pairs={{0,16},{8,24},{16,0},{24,8},{1,17},{9,25},{17,1},{25,9},{2,18},{10... | collective-permute-start | bytes 380936 | tf_op jit(solution)/shard_map/ppermute | solution.py:682
  9.7 2.2 %collective-permute-done.refs_1_ = f32[248,128]{1,0:T(8,128)S(1)} collective-permute-done((f32[248,128]{1,0:T(8,128)S(1)}, f32[248,128]{1,0:T(8,128)S(1)}, u32[]{:S(2)}, u32[]{:S(2)}) %collective-permute-start) | collective-permute-done | bytes 127008 | tf_op jit(solution)/shard_map/ppermute | solution.py:682
  11.9 7.8 %collective-permute-done.1.refs_2_ = f32[248,128]{1,0:T(8,128)S(1)} collective-permute-done((f32[248,128]{1,0:T(8,128)S(1)}, f32[248,128]{1,0:T(8,128)S(1)}, u32[]{:S(2)}, u32[]{:S(2)}) %collective-permute-start.1) | collective-permute-done | bytes 127008 | tf_op jit(solution)/shard_map/ppermute | solution.py:682
  19.7 0.0 copy-start.2
  19.7 0.0 copy-start.3
  19.7 0.0 copy-start.4
  19.7 0.0 copy-start.5
  19.8 0.9 %shard_map.128 = f32[32,2,8,256]{3,2,1,0:T(8,128)S(1)} custom-call(f32[248,128]{1,0:T(8,128)S(1)} %get-tuple-element.17.refs_0_, f32[248,128]{1,0:T(8,128)S(1)} %collective-permute-done.refs_1_, f32[248,128]{1,0:T(8,128)S(1)} %collective-permute-done.1.refs_2_, f32[248,128]{1,0:T(8,128)S(1)} %collective-permute-done.2.refs_3_, bf16[2,256,256]{2,1,0:T(8,128)(2,1)S(1)} %copy-done.1), custom_call_target="tpu_custom_call" | custom-call | flops 99999997952 | bytes 1000000 | tf_op jit(solution)/shard_map/pallas_call | solution.py:640
  20.7 20.5 %all_to_all.5.refs_0_ = f32[32,16,256]{2,1,0:T(8,128)S(1)} all-to-all(f32[32,16,256]{2,1,0:T(8,128)S(1)} %bitcast.4), channel_id=1, replica_groups=mesh['mode'=4,'ex'=4,'ey'=2] {'mode','ex','ey'}, dimensions={0} | all-to-all | bytes 1048576 | tf_op jit(solution)/shard_map/all_to_all | solution.py:698
  41.3 10.0 %shard_map.129 = (f32[16,1024]{1,0:T(8,128)S(1)}, f32[16,1024]{1,0:T(8,128)S(1)}, f32[16,1024]{1,0:T(8,128)S(1)}, f32[16,1024]{1,0:T(8,128)S(1)}, f32[16,1024]{1...) custom-call(f32[32,16,256]{2,1,0:T(8,128)S(1)} %all_to_all.5.refs_0_, ...), custom_call_target="tpu_custom_call" | custom-call | flops 1000000000 | bytes 1000000 | tf_op jit(solution)/shard_map/pallas_call | solution.py:640
  51.4 0.1 collective-permute-start.3
  51.4 1.3 %collective-permute-start.4 = (f32[16,1024]{1,0:T(8,128)S(1)}, f32[16,1024]{1,0:T(8,128)S(1)}, u32[]{:S(2)}, u32[]{:S(2)}) collective-permute-start(f32[16,1024]{1,0:T(8,128)S(1)} %get-tuple-element.23), channel_id=1, source_target_pairs={{0,2},{1,3},{2,4},{3,5},{4,6},{5,7},{6,0},{7,1},{8,10},{9,11},{10,... | collective-permute-start | bytes 196616 | tf_op jit(solution)/shard_map/ppermute | solution.py:714
  52.7 1.2 %collective-permute-start.5 = (f32[16,1024]{1,0:T(8,128)S(1)}, f32[16,1024]{1,0:T(8,128)S(1)}, u32[]{:S(2)}, u32[]{:S(2)}) collective-permute-start(f32[16,1024]{1,0:T(8,128)S(1)} %get-tuple-element.24), channel_id=1, source_target_pairs={{0,3},{1,2},{2,5},{3,4},{4,7},{5,6},{6,1},{7,0},{8,11},{9,10},{10,... | collective-permute-start | bytes 196616 | tf_op jit(solution)/shard_map/ppermute | solution.py:714
  54.0 0.8 %collective-permute-start.6 = (f32[16,1024]{1,0:T(8,128)S(1)}, f32[16,1024]{1,0:T(8,128)S(1)}, u32[]{:S(2)}, u32[]{:S(2)}) collective-permute-start(f32[16,1024]{1,0:T(8,128)S(1)} %get-tuple-element.25), channel_id=1, source_target_pairs={{0,4},{1,5},{2,6},{3,7},{4,0},{5,1},{6,2},{7,3},{8,12},{9,13},{10,... | collective-permute-start | bytes 196616 | tf_op jit(solution)/shard_map/ppermute | solution.py:714
  54.8 0.9 %collective-permute-start.7 = (f32[16,1024]{1,0:T(8,128)S(1)}, f32[16,1024]{1,0:T(8,128)S(1)}, u32[]{:S(2)}, u32[]{:S(2)}) collective-permute-start(f32[16,1024]{1,0:T(8,128)S(1)} %get-tuple-element.26), channel_id=1, source_target_pairs={{0,5},{1,4},{2,7},{3,6},{4,1},{5,0},{6,3},{7,2},{8,13},{9,12},{10,... | collective-permute-start | bytes 196616 | tf_op jit(solution)/shard_map/ppermute | solution.py:714
  55.7 1.5 %collective-permute-start.8 = (f32[16,1024]{1,0:T(8,128)S(1)}, f32[16,1024]{1,0:T(8,128)S(1)}, u32[]{:S(2)}, u32[]{:S(2)}) collective-permute-start(f32[16,1024]{1,0:T(8,128)S(1)} %get-tuple-element.27), channel_id=1, source_target_pairs={{0,6},{1,7},{2,0},{3,1},{4,2},{5,3},{6,4},{7,5},{8,14},{9,15},{10,... | collective-permute-start | bytes 196616 | tf_op jit(solution)/shard_map/ppermute | solution.py:714
  57.2 0.5 collective-permute-start.9
  57.7 0.4 collective-permute-done.5.refs_3_
  58.1 1.6 %collective-permute-done.6.refs_4_ = f32[16,1024]{1,0:T(8,128)S(1)} collective-permute-done((f32[16,1024]{1,0:T(8,128)S(1)}, f32[16,1024]{1,0:T(8,128)S(1)}, u32[]{:S(2)}, u32[]{:S(2)}) %collective-permute-start.6) | collective-permute-done | bytes 65568 | tf_op jit(solution)/shard_map/ppermute | solution.py:714
  59.7 1.3 %collective-permute-done.7.refs_5_ = f32[16,1024]{1,0:T(8,128)S(1)} collective-permute-done((f32[16,1024]{1,0:T(8,128)S(1)}, f32[16,1024]{1,0:T(8,128)S(1)}, u32[]{:S(2)}, u32[]{:S(2)}) %collective-permute-start.7) | collective-permute-done | bytes 65568 | tf_op jit(solution)/shard_map/ppermute | solution.py:714
  61.0 0.6 collective-permute-done.9.refs_7_
  61.5 1.7 %shard_map.130 = f32[1152,128]{1,0:T(8,128)} custom-call(f32[16,1024]{1,0:T(8,128)S(1)} %get-tuple-element.21.refs_0_, f32[16,1024]{1,0:T(8,128)S(1)} %collective-permute-done.3.refs_1_, f32[16,1024]{1,0:T(8,128)S(1)} %collective-permute-done.4.refs_2_, f32[16,1024]{1,0:T(8,128)S(1)} %collective-permute-done.5.refs_3_, ...), custom_call_target="tpu_custom_call" | custom-call | flops 1000000000 | bytes 1000000 | tf_op jit(solution)/shard_map/pallas_call | solution.py:640
  (19 shorter events, 0.0 us)
Async XLA Ops:
  0.0 19.7 %copy-start.1 = (bf16[2,256,256]{2,1,0:T(8,128)(2,1)S(1)}, bf16[2,256,256]{2,1,0:T(8,128)(2,1)}, u32[]{:S(2)}) copy-start(bf16[2,256,256]{2,1,0:T(8,128)(2,1)} %constant.24.clone.refs_4_) | copy-start | bytes 786436
  4.0 7.9 %collective-permute-start = (f32[248,128]{1,0:T(8,128)S(1)}, f32[248,128]{1,0:T(8,128)S(1)}, u32[]{:S(2)}, u32[]{:S(2)}) collective-permute-start(f32[248,128]{1,0:T(8,128)S(1)} %get-tuple-element.18), channel_id=1, source_target_pairs={{0,8},{8,0},{16,24},{24,16},{1,9},{9,1},{17,25},{25,17},{2,10},{10... | collective-permute-start | bytes 380936 | tf_op jit(solution)/shard_map/ppermute | solution.py:682
  7.1 12.6 %collective-permute-start.1 = (f32[248,128]{1,0:T(8,128)S(1)}, f32[248,128]{1,0:T(8,128)S(1)}, u32[]{:S(2)}, u32[]{:S(2)}) collective-permute-start(f32[248,128]{1,0:T(8,128)S(1)} %get-tuple-element.19), channel_id=1, source_target_pairs={{0,16},{8,24},{16,0},{24,8},{1,17},{9,25},{17,1},{25,9},{2,18},{10... | collective-permute-start | bytes 380936 | tf_op jit(solution)/shard_map/ppermute | solution.py:682
  9.7 10.0 %collective-permute-start.2 = (f32[248,128]{1,0:T(8,128)S(1)}, f32[248,128]{1,0:T(8,128)S(1)}, u32[]{:S(2)}, u32[]{:S(2)}) collective-permute-start(f32[248,128]{1,0:T(8,128)S(1)} %get-tuple-element.20), channel_id=1, source_target_pairs={{0,24},{8,16},{16,8},{24,0},{1,25},{9,17},{17,9},{25,1},{2,26},{10... | collective-permute-start | bytes 380936 | tf_op jit(solution)/shard_map/ppermute | solution.py:682
  19.7 21.6 %copy-start = (bf16[448,448]{1,0:T(8,128)(2,1)S(1)}, bf16[448,448]{1,0:T(8,128)(2,1)}, u32[]{:S(2)}) copy-start(bf16[448,448]{1,0:T(8,128)(2,1)} %constant.28.clone.refs_4_) | copy-start | bytes 1204228
  19.7 21.6 %copy-start.2 = (bf16[448,192]{1,0:T(8,128)(2,1)S(1)}, bf16[448,192]{1,0:T(8,128)(2,1)}, u32[]{:S(2)}) copy-start(bf16[448,192]{1,0:T(8,128)(2,1)} %constant.26.clone.refs_2_) | copy-start | bytes 516100
  19.7 21.5 %copy-start.3 = (bf16[384,224]{1,0:T(8,128)(2,1)S(1)}, bf16[384,224]{1,0:T(8,128)(2,1)}, u32[]{:S(2)}) copy-start(bf16[384,224]{1,0:T(8,128)(2,1)} %constant.30.clone.refs_6_) | copy-start | bytes 516100
  19.7 21.5 %copy-start.4 = (bf16[384,256]{1,0:T(8,128)(2,1)S(1)}, bf16[384,256]{1,0:T(8,128)(2,1)}, u32[]{:S(2)}) copy-start(bf16[384,256]{1,0:T(8,128)(2,1)} %constant.27.clone.refs_3_) | copy-start | bytes 589828
  19.7 21.5 %copy-start.5 = (bf16[256,256]{1,0:T(8,128)(2,1)S(1)}, bf16[256,256]{1,0:T(8,128)(2,1)}, u32[]{:S(2)}) copy-start(bf16[256,256]{1,0:T(8,128)(2,1)} %constant.29.clone.refs_5_) | copy-start | bytes 393220
  19.7 21.5 %copy-start.6 = (bf16[256,256]{1,0:T(8,128)(2,1)S(1)}, bf16[256,256]{1,0:T(8,128)(2,1)}, u32[]{:S(2)}) copy-start(bf16[256,256]{1,0:T(8,128)(2,1)} %constant.25.clone.refs_1_) | copy-start | bytes 393220
  19.8 21.5 %copy-start.7 = (f32[224,128]{1,0:T(8,128)S(1)}, f32[224,128]{1,0:T(8,128)}, u32[]{:S(2)}) copy-start(f32[224,128]{1,0:T(8,128)} %constant.31.clone.refs_7_) | copy-start | bytes 344068
  19.8 21.5 %copy-start.8 = (f32[1,128]{1,0:T(1,128)S(1)}, f32[1,128]{1,0:T(1,128)}, u32[]{:S(2)}) copy-start(f32[1,128]{1,0:T(1,128)} %constant.32.clone.refs_8_) | copy-start | bytes 1540
  51.4 4.3 %collective-permute-start.3 = (f32[16,1024]{1,0:T(8,128)S(1)}, f32[16,1024]{1,0:T(8,128)S(1)}, u32[]{:S(2)}, u32[]{:S(2)}) collective-permute-start(f32[16,1024]{1,0:T(8,128)S(1)} %get-tuple-element.22), channel_id=1, source_target_pairs={{0,1},{1,0},{2,3},{3,2},{4,5},{5,4},{6,7},{7,6},{8,9},{9,8},{10,11... | collective-permute-start | bytes 196616 | tf_op jit(solution)/shard_map/ppermute | solution.py:714
  51.4 5.7 %collective-permute-start.4 = (f32[16,1024]{1,0:T(8,128)S(1)}, f32[16,1024]{1,0:T(8,128)S(1)}, u32[]{:S(2)}, u32[]{:S(2)}) collective-permute-start(f32[16,1024]{1,0:T(8,128)S(1)} %get-tuple-element.23), channel_id=1, source_target_pairs={{0,2},{1,3},{2,4},{3,5},{4,6},{5,7},{6,0},{7,1},{8,10},{9,11},{10,... | collective-permute-start | bytes 196616 | tf_op jit(solution)/shard_map/ppermute | solution.py:714
  52.7 5.3 %collective-permute-start.5 = (f32[16,1024]{1,0:T(8,128)S(1)}, f32[16,1024]{1,0:T(8,128)S(1)}, u32[]{:S(2)}, u32[]{:S(2)}) collective-permute-start(f32[16,1024]{1,0:T(8,128)S(1)} %get-tuple-element.24), channel_id=1, source_target_pairs={{0,3},{1,2},{2,5},{3,4},{4,7},{5,6},{6,1},{7,0},{8,11},{9,10},{10,... | collective-permute-start | bytes 196616 | tf_op jit(solution)/shard_map/ppermute | solution.py:714
  54.0 5.7 %collective-permute-start.6 = (f32[16,1024]{1,0:T(8,128)S(1)}, f32[16,1024]{1,0:T(8,128)S(1)}, u32[]{:S(2)}, u32[]{:S(2)}) collective-permute-start(f32[16,1024]{1,0:T(8,128)S(1)} %get-tuple-element.25), channel_id=1, source_target_pairs={{0,4},{1,5},{2,6},{3,7},{4,0},{5,1},{6,2},{7,3},{8,12},{9,13},{10,... | collective-permute-start | bytes 196616 | tf_op jit(solution)/shard_map/ppermute | solution.py:714
  54.8 6.2 %collective-permute-start.7 = (f32[16,1024]{1,0:T(8,128)S(1)}, f32[16,1024]{1,0:T(8,128)S(1)}, u32[]{:S(2)}, u32[]{:S(2)}) collective-permute-start(f32[16,1024]{1,0:T(8,128)S(1)} %get-tuple-element.26), channel_id=1, source_target_pairs={{0,5},{1,4},{2,7},{3,6},{4,1},{5,0},{6,3},{7,2},{8,13},{9,12},{10,... | collective-permute-start | bytes 196616 | tf_op jit(solution)/shard_map/ppermute | solution.py:714
  55.7 5.3 %collective-permute-start.8 = (f32[16,1024]{1,0:T(8,128)S(1)}, f32[16,1024]{1,0:T(8,128)S(1)}, u32[]{:S(2)}, u32[]{:S(2)}) collective-permute-start(f32[16,1024]{1,0:T(8,128)S(1)} %get-tuple-element.27), channel_id=1, source_target_pairs={{0,6},{1,7},{2,0},{3,1},{4,2},{5,3},{6,4},{7,5},{8,14},{9,15},{10,... | collective-permute-start | bytes 196616 | tf_op jit(solution)/shard_map/ppermute | solution.py:714
  57.2 4.4 %collective-permute-start.9 = (f32[16,1024]{1,0:T(8,128)S(1)}, f32[16,1024]{1,0:T(8,128)S(1)}, u32[]{:S(2)}, u32[]{:S(2)}) collective-permute-start(f32[16,1024]{1,0:T(8,128)S(1)} %get-tuple-element.28), channel_id=1, source_target_pairs={{0,7},{1,6},{2,1},{3,0},{4,3},{5,2},{6,5},{7,4},{8,15},{9,14},{10,... | collective-permute-start | bytes 196616 | tf_op jit(solution)/shard_map/ppermute | solution.py:714

commit v9 on v7

--- a/solution.py
+++ b/solution.py
@@ -174,7 +174,7 @@
             for p in range(self.n_ey)
         ]
         self.block_y = max(len(found) for found in self.inner)
-        self.cuts = 1
+        self.cuts = 2 if self.elems % 2 == 0 else 1
         self.cut_elems = self.elems // self.cuts
         self.cut_x = self.order * self.cut_elems + 1
         share = -(-self.cut_x * self.block_y // self.n_mode)
@@ -340,7 +340,7 @@
     return lax.broadcasted_iota(jnp.int32, shape, len(shape) - 1)
 
 
-def advect_kernel(sz, heights, stream_hbm, normal_hbm, lift_hbm, back_hbm, *others):
+def advect_kernel(sz, heights, cut, stream_hbm, normal_hbm, lift_hbm, back_hbm, *others):
     out_refs, (total_ref, stream_ref, normal_ref, lift_ref, back_ref, arrived) = others[:-6], others[-6:]
     place = lax.axis_index("ey")
     fetched = [
@@ -368,55 +368,56 @@
     spot = lax.axis_index("mode")
     for copy in fetched[:3]:
         copy.wait()
-    for cut in range(sz.cuts):
-        products = []
-        for e in range(cut * sz.cut_elems, (cut + 1) * sz.cut_elems):
-            speeds = jnp.concatenate(
-                [
-                    ref[pl.ds(e * rows + f, count, stride=spots), :]
-                    for f in range(rows)
-                    for ref in (stream_ref, normal_ref)
-                ],
-                1,
-            )
-            values = dot(lift_ref[...], below(speeds))
-            highs, lows = [], []
-            for f in range(rows):
-                mine = values[:, f * LANES : (f + 1) * LANES]
-                both, slope_x, slope_y = mine[:fine], mine[fine : 2 * fine], mine[2 * fine :]
-                turned = pltpu.roll(both, sz.planes, 1)
-                stream = jnp.where(half, both, turned)
-                normal = jnp.where(half, turned, both)
-                high, low = split((stream * factors[f]) * slope_x + (normal * (element_width * 0.5)) * slope_y)
-                highs.append(high)
-                lows.append(low)
-            products.append(jnp.concatenate(highs + lows + highs, 0))
-        if cut == 0:
-            fetched[3].wait()
-        weak = dot(back_ref[...], jnp.concatenate(products, 1))
-        carry = None
-        for e in range(sz.cut_elems):
-            mine = weak[:, e * LANES : (e + 1) * LANES]
-            if carry is not None:
-                gap = jnp.zeros((column - carry.shape[0], LANES), jnp.float32)
-                mine = mine + jnp.concatenate([carry, gap], 0)
-            length = step if e < sz.cut_elems - 1 else column
-            total_ref[pl.ds(e * step, length), :] = mine[:length]
-            carry = mine[length:]
-        for turn in range(sz.n_mode):
-            goal = partner(spot, turn, sz.n_mode)
-            out_refs[cut * sz.n_mode + turn][...] = total_ref[pl.ds(pl.multiple_of(goal * sz.share, 8), sz.share), :]
+    products = []
+    for e in range(cut * sz.cut_elems, (cut + 1) * sz.cut_elems):
+        speeds = jnp.concatenate(
+            [
+                ref[pl.ds(e * rows + f, count, stride=spots), :]
+                for f in range(rows)
+                for ref in (stream_ref, normal_ref)
+            ],
+            1,
+        )
+        values = dot(lift_ref[...], below(speeds))
+        highs, lows = [], []
+        for f in range(rows):
+            mine = values[:, f * LANES : (f + 1) * LANES]
+            both, slope_x, slope_y = mine[:fine], mine[fine : 2 * fine], mine[2 * fine :]
+            turned = pltpu.roll(both, sz.planes, 1)
+            stream = jnp.where(half, both, turned)
+            normal = jnp.where(half, turned, both)
+            high, low = split((stream * factors[f]) * slope_x + (normal * (element_width * 0.5)) * slope_y)
+            highs.append(high)
+            lows.append(low)
+        products.append(jnp.concatenate(highs + lows + highs, 0))
+    fetched[3].wait()
+    weak = dot(back_ref[...], jnp.concatenate(products, 1))
+    carry = None
+    for e in range(sz.cut_elems):
+        mine = weak[:, e * LANES : (e + 1) * LANES]
+        if carry is not None:
+            gap = jnp.zeros((column - carry.shape[0], LANES), jnp.float32)
+            mine = mine + jnp.concatenate([carry, gap], 0)
+        length = step if e < sz.cut_elems - 1 else column
+        total_ref[pl.ds(e * step, length), :] = mine[:length]
+        carry = mine[length:]
+    for turn in range(sz.n_mode):
+        goal = partner(spot, turn, sz.n_mode)
+        out_refs[turn][...] = total_ref[pl.ds(pl.multiple_of(goal * sz.share, 8), sz.share), :]
 
 
 def transform_kernel(sz, *refs):
-    weak_refs, (waves_ref, out_ref, mixed_ref, signal_ref) = refs[: sz.n_mode], refs[-4:]
+    weak_refs, (waves_ref, out_ref, mixed_ref, signal_ref) = refs[:-4], refs[-4:]
     spot = lax.axis_index("mode")
-    for step, weak_ref in enumerate(weak_refs):
+    for number, weak_ref in enumerate(weak_refs):
+        cut, step = number // sz.n_mode, number % sz.n_mode
         turned = weak_ref[...].T
         first = pl.multiple_of(origin(spot, step, sz.n_mode) * sz.planes, 8)
         for k in range(2):
-            signal_ref[k, pl.ds(first, sz.planes), :] = turned[k * sz.planes : (k + 1) * sz.planes]
-    modes = sz.planes_total
+            signal_ref[k, pl.ds(first, sz.planes), pl.ds(cut * sz.share, sz.share)] = turned[
+                k * sz.planes : (k + 1) * sz.planes
+            ]
+    modes, width = sz.planes_total, sz.cuts * sz.share
     for k in range(2):
         high, low = split(signal_ref[k])
         part = dot(waves_ref[0], high) + dot(waves_ref[0], low) + dot(waves_ref[1], high)
@@ -424,7 +425,7 @@
             tile = part[:, t * LANES : (t + 1) * LANES]
             mixed_ref[t, pl.ds(k, modes, stride=2), pl.ds(0, tile.shape[1])] = tile
     for t in range(mixed_ref.shape[0]):
-        last = min(LANES, sz.share - t * LANES)
+        last = min(LANES, width - t * LANES)
         out_ref[:, pl.ds(t * LANES, last)] = mixed_ref[t, :, pl.ds(0, last)]
 
 
@@ -432,11 +433,9 @@
     sz,
     *refs,
 ):
-    terms_refs, out_refs = refs[: sz.cuts], refs[sz.cuts + 8 : -4]
+    terms_ref, out_refs = refs[0], refs[9:-4]
     field_ref, first_ref, work_ref, stiff_ref = refs[-4:]
-    in_y_ref, in_x_ref, pair_y_ref, pair_x_ref, out_y_ref, out_x_ref, lam_x_ref, lam_y_ref = refs[
-        sz.cuts : sz.cuts + 8
-    ]
+    in_y_ref, in_x_ref, pair_y_ref, pair_x_ref, out_y_ref, out_x_ref, lam_x_ref, lam_y_ref = refs[1:9]
     width, folds, strip = sz.fold_width, sz.folds, sz.block_y
     tiles = -(-sz.cut_nodes // LANES)
     lanes = lane_index((PARTS, LANES))
@@ -456,7 +455,11 @@
             for fold in range(folds):
                 whole = jnp.concatenate(
                     [
-                        terms_refs[cut][(z * sz.n_ex + block) * sz.n_ey + q, pl.ds(fold * PARTS, PARTS), :]
+                        terms_ref[
+                            (z * sz.n_ex + block) * sz.n_ey + q,
+                            pl.ds(fold * PARTS, PARTS),
+                            pl.ds(cut * sz.share, sz.share),
+                        ]
                         for z in range(sz.n_mode)
                     ],
                     1,
@@ -592,51 +595,48 @@
     flat = sz.nodes * sz.nodes * sz.elems * sz.rows
     table = {name: jnp.asarray(value) for name, value in tables.items() if name != "heights"}
     heights = [float(height) for height in tables["heights"]]
-    pieces = call(
-        functools.partial(advect_kernel, sz, heights),
-        [(sz.share, LANES)] * (sz.n_mode * sz.cuts),
-        [
-            pltpu.with_memory_space_constraint(each, pltpu.HBM)
-            for each in (
-                stream_speed.reshape(flat, sz.planes),
-                normal_speed.reshape(flat, sz.planes),
-                table["lift"],
-                table["back"],
-            )
-        ],
-        [
-            (sz.cut_nodes, LANES),
-            (flat, sz.planes),
-            (flat, sz.planes),
-            pltpu.VMEM(tables["lift"].shape, jnp.bfloat16),
-            pltpu.VMEM(tables["back"].shape[1:], jnp.bfloat16),
-            pltpu.SemaphoreType.DMA((4,)),
-        ],
-        pltpu.HBM,
-    )
-    weak = [pieces[cut * sz.n_mode : (cut + 1) * sz.n_mode] for cut in range(sz.cuts)]
+    weak = []
     for cut in range(sz.cuts):
+        pieces = call(
+            functools.partial(advect_kernel, sz, heights, cut),
+            [(sz.share, LANES)] * sz.n_mode,
+            [
+                pltpu.with_memory_space_constraint(each, pltpu.HBM)
+                for each in (
+                    stream_speed.reshape(flat, sz.planes),
+                    normal_speed.reshape(flat, sz.planes),
+                    table["lift"],
+                    table["back"],
+                )
+            ],
+            [
+                (sz.cut_nodes, LANES),
+                (flat, sz.planes),
+                (flat, sz.planes),
+                pltpu.VMEM(tables["lift"].shape, jnp.bfloat16),
+                pltpu.VMEM(tables["back"].shape[1:], jnp.bfloat16),
+                pltpu.SemaphoreType.DMA((4,)),
+            ],
+            pltpu.HBM,
+        )
         for step in sorted(range(1, sz.n_mode), key=lambda each: (each & -each, each), reverse=True):
             pairs = [(z, partner(z, step, sz.n_mode)) for z in range(sz.n_mode)]
-            weak[cut][step] = lax.ppermute(weak[cut][step], "mode", pairs)
-    terms, ahead = [], []
-    for cut in range(sz.cuts):
-        (spectra,) = call(
-            functools.partial(transform_kernel, sz),
-            [(2 * sz.planes_total, sz.share)],
-            [*weak[cut], *ahead, table["waves"]],
-            [(-(-sz.share // LANES), 2 * sz.planes_total, LANES), (2, sz.planes_total, sz.share)],
-            [pltpu.VMEM] * sz.n_mode + [pl.ANY] * len(ahead) + [pltpu.VMEM],
-            flops=10**11 if cut == sz.cuts - 1 else 10**8,
-        )
-        spectra = spectra.reshape(sz.n_mode * sz.spots, sz.own, sz.share)
-        terms.append(lax.all_to_all(spectra, ("mode", "ex", "ey"), split_axis=0, concat_axis=0, tiled=True))
-        ahead = [spectra]
+            pieces[step] = lax.ppermute(pieces[step], "mode", pairs)
+        weak += pieces
+    width = sz.cuts * sz.share
+    (spectra,) = call(
+        functools.partial(transform_kernel, sz),
+        [(2 * sz.planes_total, width)],
+        [*weak, table["waves"]],
+        [(-(-width // LANES), 2 * sz.planes_total, LANES), (2, sz.planes_total, width)],
+    )
+    spectra = spectra.reshape(sz.n_mode * sz.spots, sz.own, width)
+    terms = lax.all_to_all(spectra, ("mode", "ex", "ey"), split_axis=0, concat_axis=0, tiled=True)
     names = ("in_y", "in_x", "pair_y", "pair_x", "out_y", "out_x", "lam_x", "lam_y")
     solved = call(
         functools.partial(smooth_kernel, sz),
         [(sz.own, sz.lane_nodes)] * sz.spots,
-        terms + [table[name] for name in names],
+        [terms] + [table[name] for name in names],
         [(PARTS * sz.x_pad, LANES)] + [(PARTS * sz.x_eig, LANES)] * 3,
     )
     for step in sorted(range(1, sz.spots), key=lambda each: each // sz.n_ey == 0):

time: 58.1 us -> 59.1 us (1.017)
  starting transfers between devices: 12 us -> 16.5 us
  waiting for transfers between devices: 14.2 us -> 9.9 us
  Pallas kernels: 10.9 us -> 13.9 us
  blocking collectives: 20.6 us -> 18.5 us
    ppermute x3 -> x6, starting transfers between devices: 5.7 us -> 10.2 us  [on_device(): pieces[step] = lax.ppermute(pieces[step], 'mode', pairs)]
    ppermute x3 -> x6, waiting for transfers between devices: 10.3 us -> 6.04 us  [on_device(): pieces[step] = lax.ppermute(pieces[step], 'mode', pairs)]
    pallas_call x4 -> x5, Pallas kernels: 10.9 us -> 13.9 us  [call(): pl.pallas_call(kernel, out_shape=[jax.ShapeDtypeStruct(shape, jnp.float32...]
    all_to_all x1, blocking collectives: 20.6 us -> 18.5 us  [on_device(): lax.all_to_all(spectra, ('mode', 'ex', 'ey'), split_axis=0, concat_axis=0...]
  transfers between devices with their start and end apart: 10 -> 13, of which waited for: 6 -> 7; matrix products, arithmetic and copies ran while one was open for 0% -> 0% of each run, Pallas kernels for 0% -> 6%
where the time goes in v9:
time: 59.1 us; the launch traced here: 58.9 us
  blocking collectives  18.5 us (31%)
  starting transfers between devices  16.5 us (28%)
  Pallas kernels  13.9 us (24%)
  waiting for transfers between devices  9.9 us (17%)
    all_to_all x1, blocking collectives, on_device(): lax.all_to_all(spectra, ('mode', 'ex', 'ey'), split_axis=0, concat_axis=0...  18.5 us
    pallas_call x5, Pallas kernels, call(): pl.pallas_call(kernel, out_shape=[jax.ShapeDtypeStruct(shape, jnp.float32...  13.9 us
    ppermute x6, starting transfers between devices, on_device(): pieces[step] = lax.ppermute(pieces[step], 'mode', pairs)  10.2 us
    ppermute x7, starting transfers between devices, on_device(): solved[step] = lax.ppermute(solved[step], ('ex', 'ey'), pairs)  6.31 us
    ppermute x6, waiting for transfers between devices, on_device(): pieces[step] = lax.ppermute(pieces[step], 'mode', pairs)  6.04 us
    ppermute x7, waiting for transfers between devices, on_device(): solved[step] = lax.ppermute(solved[step], ('ex', 'ey'), pairs)  3.86 us
  transfers between devices with their start and end apart: 13, of which 7 were waited for; matrix products, arithmetic and copies ran while one was open for 0% of the time, Pallas kernels for 6%

profile of v9, /device:TPU:0, one launch (start us, length us, event | category | flops | bytes accessed | tf_op | source)
XLA Modules:
  0.0 58.9 jit_solution(6371240941589180115)
XLA Ops:
  0.0 3.4 %shard_map.128 = (f32[128,128]{1,0:T(8,128)S(1)}, f32[128,128]{1,0:T(8,128)S(1)}, f32[128,128]{1,0:T(8,128)S(1)}, f32[128,128]{1,0:T(8,128)S(1)}) custom-call(f32[1152,64]{1,0:T(8,128)} %bitcast.5, f32[1152,64]{1,0:T(8,128)} %bitcast.7, bf16[1008,432]{1,0:T(8,128)(2,1)} %constant.22.clone.lift_hbm, bf16[2,264,2016]{2,1,0:T(8,128)(2,1)} %constant.23.clone.back_hbm), custom_call_target="tpu_custom_call" | custom-call | flops 1000000000 | bytes 1000000 | tf_op jit(solution)/shard_map/pallas_call | solution.py:582
  3.4 3.1 %collective-permute-start.3 = (f32[128,128]{1,0:T(8,128)S(1)}, f32[128,128]{1,0:T(8,128)S(1)}, u32[]{:S(2)}, u32[]{:S(2)}) collective-permute-start(f32[128,128]{1,0:T(8,128)S(1)} %get-tuple-element.26), channel_id=1, source_target_pairs={{0,8},{8,0},{16,24},{24,16},{1,9},{9,1},{17,25},{25,17},{2,10},{10... | collective-permute-start | bytes 196616 | tf_op jit(solution)/shard_map/ppermute | solution.py:624
  6.5 2.6 %collective-permute-start.4 = (f32[128,128]{1,0:T(8,128)S(1)}, f32[128,128]{1,0:T(8,128)S(1)}, u32[]{:S(2)}, u32[]{:S(2)}) collective-permute-start(f32[128,128]{1,0:T(8,128)S(1)} %get-tuple-element.27), channel_id=1, source_target_pairs={{0,16},{8,24},{16,0},{24,8},{1,17},{9,25},{17,1},{25,9},{2,18},{10... | collective-permute-start | bytes 196616 | tf_op jit(solution)/shard_map/ppermute | solution.py:624
  9.1 3.5 %shard_map.127 = (f32[128,128]{1,0:T(8,128)S(1)}, f32[128,128]{1,0:T(8,128)S(1)}, f32[128,128]{1,0:T(8,128)S(1)}, f32[128,128]{1,0:T(8,128)S(1)}) custom-call(f32[1152,64]{1,0:T(8,128)} %bitcast.6, f32[1152,64]{1,0:T(8,128)} %bitcast.8, bf16[1008,432]{1,0:T(8,128)(2,1)} %constant.22.clone.lift_hbm, bf16[2,264,2016]{2,1,0:T(8,128)(2,1)} %constant.23.clone.back_hbm), custom_call_target="tpu_custom_call" | custom-call | flops 1000000000 | bytes 1000000 | tf_op jit(solution)/shard_map/pallas_call | solution.py:582
  12.6 0.9 %collective-permute-start = (f32[128,128]{1,0:T(8,128)S(1)}, f32[128,128]{1,0:T(8,128)S(1)}, u32[]{:S(2)}, u32[]{:S(2)}) collective-permute-start(f32[128,128]{1,0:T(8,128)S(1)} %get-tuple-element.22), channel_id=1, source_target_pairs={{0,8},{8,0},{16,24},{24,16},{1,9},{9,1},{17,25},{25,17},{2,10},{10... | collective-permute-start | bytes 196616 | tf_op jit(solution)/shard_map/ppermute | solution.py:624
  13.5 3.5 %collective-permute-start.1 = (f32[128,128]{1,0:T(8,128)S(1)}, f32[128,128]{1,0:T(8,128)S(1)}, u32[]{:S(2)}, u32[]{:S(2)}) collective-permute-start(f32[128,128]{1,0:T(8,128)S(1)} %get-tuple-element.23), channel_id=1, source_target_pairs={{0,16},{8,24},{16,0},{24,8},{1,17},{9,25},{17,1},{25,9},{2,18},{10... | collective-permute-start | bytes 196616 | tf_op jit(solution)/shard_map/ppermute | solution.py:624
  17.1 0.4 collective-permute-done.refs_1_
  17.4 3.4 %collective-permute-done.1.refs_2_ = f32[128,128]{1,0:T(8,128)S(1)} collective-permute-done((f32[128,128]{1,0:T(8,128)S(1)}, f32[128,128]{1,0:T(8,128)S(1)}, u32[]{:S(2)}, u32[]{:S(2)}) %collective-permute-start.1) | collective-permute-done | bytes 65568 | tf_op jit(solution)/shard_map/ppermute | solution.py:624
  20.8 2.3 %collective-permute-done.2.refs_3_ = f32[128,128]{1,0:T(8,128)S(1)} collective-permute-done((f32[128,128]{1,0:T(8,128)S(1)}, f32[128,128]{1,0:T(8,128)S(1)}, u32[]{:S(2)}, u32[]{:S(2)}) %collective-permute-start.2) | collective-permute-done | bytes 65568 | tf_op jit(solution)/shard_map/ppermute | solution.py:624
  23.2 0.6 %shard_map.129 = f32[512,256]{1,0:T(8,128)S(1)} custom-call(f32[128,128]{1,0:T(8,128)S(1)} %get-tuple-element.21.refs_0_, f32[128,128]{1,0:T(8,128)S(1)} %collective-permute-done.refs_1_, f32[128,128]{1,0:T(8,128)S(1)} %collective-permute-done.1.refs_2_, f32[128,128]{1,0:T(8,128)S(1)} %collective-permute-done.2.refs_3_, ...), custom_call_target="tpu_custom_call" | custom-call | flops 1000000000 | bytes 1000000 | tf_op jit(solution)/shard_map/pallas_call | solution.py:582
  23.8 18.5 %all_to_all.5.refs_0_ = f32[32,16,256]{2,1,0:T(8,128)S(1)} all-to-all(f32[32,16,256]{2,1,0:T(8,128)S(1)} %bitcast.4), channel_id=1, replica_groups=mesh['mode'=4,'ex'=4,'ey'=2] {'mode','ex','ey'}, dimensions={0} | all-to-all | bytes 1048576 | tf_op jit(solution)/shard_map/all_to_all | solution.py:634
  42.3 5.3 %shard_map.130 = (f32[16,1024]{1,0:T(8,128)S(1)}, f32[16,1024]{1,0:T(8,128)S(1)}, f32[16,1024]{1,0:T(8,128)S(1)}, f32[16,1024]{1,0:T(8,128)S(1)}, f32[16,1024]{1...) custom-call(f32[32,16,256]{2,1,0:T(8,128)S(1)} %all_to_all.5.refs_0_, ...), custom_call_target="tpu_custom_call" | custom-call | flops 1000000000 | bytes 1000000 | tf_op jit(solution)/shard_map/pallas_call | solution.py:582
  47.6 0.1 collective-permute-start.6
  47.7 1.3 %collective-permute-start.7 = (f32[16,1024]{1,0:T(8,128)S(1)}, f32[16,1024]{1,0:T(8,128)S(1)}, u32[]{:S(2)}, u32[]{:S(2)}) collective-permute-start(f32[16,1024]{1,0:T(8,128)S(1)} %get-tuple-element.31), channel_id=1, source_target_pairs={{0,2},{1,3},{2,4},{3,5},{4,6},{5,7},{6,0},{7,1},{8,10},{9,11},{10,... | collective-permute-start | bytes 196616 | tf_op jit(solution)/shard_map/ppermute | solution.py:649
  49.0 1.2 %collective-permute-start.8 = (f32[16,1024]{1,0:T(8,128)S(1)}, f32[16,1024]{1,0:T(8,128)S(1)}, u32[]{:S(2)}, u32[]{:S(2)}) collective-permute-start(f32[16,1024]{1,0:T(8,128)S(1)} %get-tuple-element.32), channel_id=1, source_target_pairs={{0,3},{1,2},{2,5},{3,4},{4,7},{5,6},{6,1},{7,0},{8,11},{9,10},{10,... | collective-permute-start | bytes 196616 | tf_op jit(solution)/shard_map/ppermute | solution.py:649
  50.2 0.8 %collective-permute-start.9 = (f32[16,1024]{1,0:T(8,128)S(1)}, f32[16,1024]{1,0:T(8,128)S(1)}, u32[]{:S(2)}, u32[]{:S(2)}) collective-permute-start(f32[16,1024]{1,0:T(8,128)S(1)} %get-tuple-element.33), channel_id=1, source_target_pairs={{0,4},{1,5},{2,6},{3,7},{4,0},{5,1},{6,2},{7,3},{8,12},{9,13},{10,... | collective-permute-start | bytes 196616 | tf_op jit(solution)/shard_map/ppermute | solution.py:649
  51.0 0.9 %collective-permute-start.10 = (f32[16,1024]{1,0:T(8,128)S(1)}, f32[16,1024]{1,0:T(8,128)S(1)}, u32[]{:S(2)}, u32[]{:S(2)}) collective-permute-start(f32[16,1024]{1,0:T(8,128)S(1)} %get-tuple-element.34), channel_id=1, source_target_pairs={{0,5},{1,4},{2,7},{3,6},{4,1},{5,0},{6,3},{7,2},{8,13},{9,12},{10,... | collective-permute-start | bytes 196616 | tf_op jit(solution)/shard_map/ppermute | solution.py:649
  51.9 1.5 %collective-permute-start.11 = (f32[16,1024]{1,0:T(8,128)S(1)}, f32[16,1024]{1,0:T(8,128)S(1)}, u32[]{:S(2)}, u32[]{:S(2)}) collective-permute-start(f32[16,1024]{1,0:T(8,128)S(1)} %get-tuple-element.35), channel_id=1, source_target_pairs={{0,6},{1,7},{2,0},{3,1},{4,2},{5,3},{6,4},{7,5},{8,14},{9,15},{10,... | collective-permute-start | bytes 196616 | tf_op jit(solution)/shard_map/ppermute | solution.py:649
  53.4 0.5 collective-permute-start.12
  53.9 0.4 collective-permute-done.8.refs_3_
  54.3 1.6 %collective-permute-done.9.refs_4_ = f32[16,1024]{1,0:T(8,128)S(1)} collective-permute-done((f32[16,1024]{1,0:T(8,128)S(1)}, f32[16,1024]{1,0:T(8,128)S(1)}, u32[]{:S(2)}, u32[]{:S(2)}) %collective-permute-start.9) | collective-permute-done | bytes 65568 | tf_op jit(solution)/shard_map/ppermute | solution.py:649
  55.9 1.3 %collective-permute-done.10.refs_5_ = f32[16,1024]{1,0:T(8,128)S(1)} collective-permute-done((f32[16,1024]{1,0:T(8,128)S(1)}, f32[16,1024]{1,0:T(8,128)S(1)}, u32[]{:S(2)}, u32[]{:S(2)}) %collective-permute-start.10) | collective-permute-done | bytes 65568 | tf_op jit(solution)/shard_map/ppermute | solution.py:649
  57.2 0.6 collective-permute-done.12.refs_7_
  57.8 1.1 %shard_map.131 = f32[1152,128]{1,0:T(8,128)} custom-call(f32[16,1024]{1,0:T(8,128)S(1)} %get-tuple-element.29.refs_0_, f32[16,1024]{1,0:T(8,128)S(1)} %collective-permute-done.6.refs_1_, f32[16,1024]{1,0:T(8,128)S(1)} %collective-permute-done.7.refs_2_, f32[16,1024]{1,0:T(8,128)S(1)} %collective-permute-done.8.refs_3_, ...), custom_call_target="tpu_custom_call" | custom-call | flops 1000000000 | bytes 1000000 | tf_op jit(solution)/shard_map/pallas_call | solution.py:582
  (26 shorter events, 0.1 us)
Async XLA Ops:
  3.4 13.6 %collective-permute-start.3 = (f32[128,128]{1,0:T(8,128)S(1)}, f32[128,128]{1,0:T(8,128)S(1)}, u32[]{:S(2)}, u32[]{:S(2)}) collective-permute-start(f32[128,128]{1,0:T(8,128)S(1)} %get-tuple-element.26), channel_id=1, source_target_pairs={{0,8},{8,0},{16,24},{24,16},{1,9},{9,1},{17,25},{25,17},{2,10},{10... | collective-permute-start | bytes 196616 | tf_op jit(solution)/shard_map/ppermute | solution.py:624
  6.5 10.5 %collective-permute-start.4 = (f32[128,128]{1,0:T(8,128)S(1)}, f32[128,128]{1,0:T(8,128)S(1)}, u32[]{:S(2)}, u32[]{:S(2)}) collective-permute-start(f32[128,128]{1,0:T(8,128)S(1)} %get-tuple-element.27), channel_id=1, source_target_pairs={{0,16},{8,24},{16,0},{24,8},{1,17},{9,25},{17,1},{25,9},{2,18},{10... | collective-permute-start | bytes 196616 | tf_op jit(solution)/shard_map/ppermute | solution.py:624
  9.1 14.0 %copy-start.1 = (bf16[2,256,256]{2,1,0:T(8,128)(2,1)S(1)}, bf16[2,256,256]{2,1,0:T(8,128)(2,1)}, u32[]{:S(2)}) copy-start(bf16[2,256,256]{2,1,0:T(8,128)(2,1)} %constant.24.clone.refs_8_) | copy-start | bytes 786436
  9.1 7.9 %collective-permute-start.5 = (f32[128,128]{1,0:T(8,128)S(1)}, f32[128,128]{1,0:T(8,128)S(1)}, u32[]{:S(2)}, u32[]{:S(2)}) collective-permute-start(f32[128,128]{1,0:T(8,128)S(1)} %get-tuple-element.28), channel_id=1, source_target_pairs={{0,24},{8,16},{16,8},{24,0},{1,25},{9,17},{17,9},{25,1},{2,26},{10... | collective-permute-start | bytes 196616 | tf_op jit(solution)/shard_map/ppermute | solution.py:624
  12.6 4.9 %collective-permute-start = (f32[128,128]{1,0:T(8,128)S(1)}, f32[128,128]{1,0:T(8,128)S(1)}, u32[]{:S(2)}, u32[]{:S(2)}) collective-permute-start(f32[128,128]{1,0:T(8,128)S(1)} %get-tuple-element.22), channel_id=1, source_target_pairs={{0,8},{8,0},{16,24},{24,16},{1,9},{9,1},{17,25},{25,17},{2,10},{10... | collective-permute-start | bytes 196616 | tf_op jit(solution)/shard_map/ppermute | solution.py:624
  13.5 7.3 %collective-permute-start.1 = (f32[128,128]{1,0:T(8,128)S(1)}, f32[128,128]{1,0:T(8,128)S(1)}, u32[]{:S(2)}, u32[]{:S(2)}) collective-permute-start(f32[128,128]{1,0:T(8,128)S(1)} %get-tuple-element.23), channel_id=1, source_target_pairs={{0,16},{8,24},{16,0},{24,8},{1,17},{9,25},{17,1},{25,9},{2,18},{10... | collective-permute-start | bytes 196616 | tf_op jit(solution)/shard_map/ppermute | solution.py:624
  17.0 6.1 %collective-permute-start.2 = (f32[128,128]{1,0:T(8,128)S(1)}, f32[128,128]{1,0:T(8,128)S(1)}, u32[]{:S(2)}, u32[]{:S(2)}) collective-permute-start(f32[128,128]{1,0:T(8,128)S(1)} %get-tuple-element.24), channel_id=1, source_target_pairs={{0,24},{8,16},{16,8},{24,0},{1,25},{9,17},{17,9},{25,1},{2,26},{10... | collective-permute-start | bytes 196616 | tf_op jit(solution)/shard_map/ppermute | solution.py:624
  23.1 19.2 %copy-start = (bf16[448,448]{1,0:T(8,128)(2,1)S(1)}, bf16[448,448]{1,0:T(8,128)(2,1)}, u32[]{:S(2)}) copy-start(bf16[448,448]{1,0:T(8,128)(2,1)} %constant.28.clone.refs_4_) | copy-start | bytes 1204228
  23.1 19.2 %copy-start.2 = (bf16[448,192]{1,0:T(8,128)(2,1)S(1)}, bf16[448,192]{1,0:T(8,128)(2,1)}, u32[]{:S(2)}) copy-start(bf16[448,192]{1,0:T(8,128)(2,1)} %constant.26.clone.refs_2_) | copy-start | bytes 516100
  23.1 19.2 %copy-start.3 = (bf16[384,224]{1,0:T(8,128)(2,1)S(1)}, bf16[384,224]{1,0:T(8,128)(2,1)}, u32[]{:S(2)}) copy-start(bf16[384,224]{1,0:T(8,128)(2,1)} %constant.30.clone.refs_6_) | copy-start | bytes 516100
  23.1 19.2 %copy-start.4 = (bf16[384,256]{1,0:T(8,128)(2,1)S(1)}, bf16[384,256]{1,0:T(8,128)(2,1)}, u32[]{:S(2)}) copy-start(bf16[384,256]{1,0:T(8,128)(2,1)} %constant.27.clone.refs_3_) | copy-start | bytes 589828
  23.1 19.2 %copy-start.5 = (bf16[256,256]{1,0:T(8,128)(2,1)S(1)}, bf16[256,256]{1,0:T(8,128)(2,1)}, u32[]{:S(2)}) copy-start(bf16[256,256]{1,0:T(8,128)(2,1)} %constant.29.clone.refs_5_) | copy-start | bytes 393220
  23.1 19.2 %copy-start.6 = (bf16[256,256]{1,0:T(8,128)(2,1)S(1)}, bf16[256,256]{1,0:T(8,128)(2,1)}, u32[]{:S(2)}) copy-start(bf16[256,256]{1,0:T(8,128)(2,1)} %constant.25.clone.refs_1_) | copy-start | bytes 393220
  23.1 19.2 %copy-start.7 = (f32[224,128]{1,0:T(8,128)S(1)}, f32[224,128]{1,0:T(8,128)}, u32[]{:S(2)}) copy-start(f32[224,128]{1,0:T(8,128)} %constant.31.clone.refs_7_) | copy-start | bytes 344068
  23.2 19.2 %copy-start.8 = (f32[1,128]{1,0:T(1,128)S(1)}, f32[1,128]{1,0:T(1,128)}, u32[]{:S(2)}) copy-start(f32[1,128]{1,0:T(1,128)} %constant.32.clone.refs_8_) | copy-start | bytes 1540
  47.6 4.3 %collective-permute-start.6 = (f32[16,1024]{1,0:T(8,128)S(1)}, f32[16,1024]{1,0:T(8,128)S(1)}, u32[]{:S(2)}, u32[]{:S(2)}) collective-permute-start(f32[16,1024]{1,0:T(8,128)S(1)} %get-tuple-element.30), channel_id=1, source_target_pairs={{0,1},{1,0},{2,3},{3,2},{4,5},{5,4},{6,7},{7,6},{8,9},{9,8},{10,11... | collective-permute-start | bytes 196616 | tf_op jit(solution)/shard_map/ppermute | solution.py:649
  47.7 5.7 %collective-permute-start.7 = (f32[16,1024]{1,0:T(8,128)S(1)}, f32[16,1024]{1,0:T(8,128)S(1)}, u32[]{:S(2)}, u32[]{:S(2)}) collective-permute-start(f32[16,1024]{1,0:T(8,128)S(1)} %get-tuple-element.31), channel_id=1, source_target_pairs={{0,2},{1,3},{2,4},{3,5},{4,6},{5,7},{6,0},{7,1},{8,10},{9,11},{10,... | collective-permute-start | bytes 196616 | tf_op jit(solution)/shard_map/ppermute | solution.py:649
  49.0 5.3 %collective-permute-start.8 = (f32[16,1024]{1,0:T(8,128)S(1)}, f32[16,1024]{1,0:T(8,128)S(1)}, u32[]{:S(2)}, u32[]{:S(2)}) collective-permute-start(f32[16,1024]{1,0:T(8,128)S(1)} %get-tuple-element.32), channel_id=1, source_target_pairs={{0,3},{1,2},{2,5},{3,4},{4,7},{5,6},{6,1},{7,0},{8,11},{9,10},{10,... | collective-permute-start | bytes 196616 | tf_op jit(solution)/shard_map/ppermute | solution.py:649
  50.2 5.7 %collective-permute-start.9 = (f32[16,1024]{1,0:T(8,128)S(1)}, f32[16,1024]{1,0:T(8,128)S(1)}, u32[]{:S(2)}, u32[]{:S(2)}) collective-permute-start(f32[16,1024]{1,0:T(8,128)S(1)} %get-tuple-element.33), channel_id=1, source_target_pairs={{0,4},{1,5},{2,6},{3,7},{4,0},{5,1},{6,2},{7,3},{8,12},{9,13},{10,... | collective-permute-start | bytes 196616 | tf_op jit(solution)/shard_map/ppermute | solution.py:649
  51.0 6.2 %collective-permute-start.10 = (f32[16,1024]{1,0:T(8,128)S(1)}, f32[16,1024]{1,0:T(8,128)S(1)}, u32[]{:S(2)}, u32[]{:S(2)}) collective-permute-start(f32[16,1024]{1,0:T(8,128)S(1)} %get-tuple-element.34), channel_id=1, source_target_pairs={{0,5},{1,4},{2,7},{3,6},{4,1},{5,0},{6,3},{7,2},{8,13},{9,12},{10,... | collective-permute-start | bytes 196616 | tf_op jit(solution)/shard_map/ppermute | solution.py:649
  51.9 5.3 %collective-permute-start.11 = (f32[16,1024]{1,0:T(8,128)S(1)}, f32[16,1024]{1,0:T(8,128)S(1)}, u32[]{:S(2)}, u32[]{:S(2)}) collective-permute-start(f32[16,1024]{1,0:T(8,128)S(1)} %get-tuple-element.35), channel_id=1, source_target_pairs={{0,6},{1,7},{2,0},{3,1},{4,2},{5,3},{6,4},{7,5},{8,14},{9,15},{10,... | collective-permute-start | bytes 196616 | tf_op jit(solution)/shard_map/ppermute | solution.py:649
  53.4 4.4 %collective-permute-start.12 = (f32[16,1024]{1,0:T(8,128)S(1)}, f32[16,1024]{1,0:T(8,128)S(1)}, u32[]{:S(2)}, u32[]{:S(2)}) collective-permute-start(f32[16,1024]{1,0:T(8,128)S(1)} %get-tuple-element.36), channel_id=1, source_target_pairs={{0,7},{1,6},{2,1},{3,0},{4,3},{5,2},{6,5},{7,4},{8,15},{9,14},{10,... | collective-permute-start | bytes 196616 | tf_op jit(solution)/shard_map/ppermute | solution.py:649

commit v10 on v7

--- a/solution.py
+++ b/solution.py
@@ -178,8 +178,9 @@
         self.cut_elems = self.elems // self.cuts
         self.cut_x = self.order * self.cut_elems + 1
         share = -(-self.cut_x * self.block_y // self.n_mode)
-        self.share = ceil_to(share, LANES if share > 64 else 16)
-        self.cut_nodes = self.share * self.n_mode
+        self.sent = ceil_to(share, 8)
+        self.share = ceil_to(self.sent, LANES if share > 64 else 16)
+        self.cut_nodes = self.sent * self.n_mode
         self.lane_nodes = ceil_to(self.block_x * self.block_y + 2, LANES)
         self.columns = 2 * self.planes
         self.spots = self.n_ex * self.n_ey
@@ -281,7 +282,7 @@
     return dict(
         heights=np.asarray(heights, np.float32),
         lift=beside(lift),
-        back=np.stack([beside(table) for table in back]),
+        back=np.stack([stacked(table) for table in back]),
         waves=np.stack(high_low(waves)),
         in_y=one_dot(block_y),
         in_x=stacked(block_x(sz.n_ex * sz.cuts, sz.cut_elems)),
@@ -354,7 +355,7 @@
             )
         )
     ]
-    for copy in fetched:
+    for copy in fetched[:3]:
         copy.start()
     count, fine, rows = sz.nodes * sz.nodes, sz.fine, sz.rows
     spots = sz.elems * rows
@@ -368,8 +369,9 @@
     spot = lax.axis_index("mode")
     for copy in fetched[:3]:
         copy.wait()
+    fetched[3].start()
     for cut in range(sz.cuts):
-        products = []
+        high_parts, low_parts = [], []
         for e in range(cut * sz.cut_elems, (cut + 1) * sz.cut_elems):
             speeds = jnp.concatenate(
                 [
@@ -390,10 +392,12 @@
                 high, low = split((stream * factors[f]) * slope_x + (normal * (element_width * 0.5)) * slope_y)
                 highs.append(high)
                 lows.append(low)
-            products.append(jnp.concatenate(highs + lows + highs, 0))
+            high_parts.append(jnp.concatenate(highs, 0))
+            low_parts.append(jnp.concatenate(lows, 0))
         if cut == 0:
             fetched[3].wait()
-        weak = dot(back_ref[...], jnp.concatenate(products, 1))
+        both = dot(back_ref[...], jnp.concatenate(high_parts, 1))
+        weak = both[:column] + both[column:] + dot(back_ref[:column, :], jnp.concatenate(low_parts, 1))
         carry = None
         for e in range(sz.cut_elems):
             mine = weak[:, e * LANES : (e + 1) * LANES]
@@ -405,17 +409,19 @@
             carry = mine[length:]
         for turn in range(sz.n_mode):
             goal = partner(spot, turn, sz.n_mode)
-            out_refs[cut * sz.n_mode + turn][...] = total_ref[pl.ds(pl.multiple_of(goal * sz.share, 8), sz.share), :]
+            out_refs[cut * sz.n_mode + turn][...] = total_ref[pl.ds(pl.multiple_of(goal * sz.sent, 8), sz.sent), :]
 
 
 def transform_kernel(sz, *refs):
     weak_refs, (waves_ref, out_ref, mixed_ref, signal_ref) = refs[: sz.n_mode], refs[-4:]
     spot = lax.axis_index("mode")
+    if sz.share > sz.sent:
+        signal_ref[...] = jnp.zeros(signal_ref.shape, jnp.float32)
     for step, weak_ref in enumerate(weak_refs):
         turned = weak_ref[...].T
         first = pl.multiple_of(origin(spot, step, sz.n_mode) * sz.planes, 8)
         for k in range(2):
-            signal_ref[k, pl.ds(first, sz.planes), :] = turned[k * sz.planes : (k + 1) * sz.planes]
+            signal_ref[k, pl.ds(first, sz.planes), pl.ds(0, sz.sent)] = turned[k * sz.planes : (k + 1) * sz.planes]
     modes = sz.planes_total
     for k in range(2):
         high, low = split(signal_ref[k])
@@ -438,7 +444,7 @@
         sz.cuts : sz.cuts + 8
     ]
     width, folds, strip = sz.fold_width, sz.folds, sz.block_y
-    tiles = -(-sz.cut_nodes // LANES)
+    tiles = -(-(sz.share * sz.n_mode) // LANES)
     lanes = lane_index((PARTS, LANES))
     x_pad, x_eig = sz.x_pad, sz.x_eig
     place, spot = lax.axis_index("ey"), lax.axis_index("ex")
@@ -463,17 +469,20 @@
                 )
                 held[q, fold] = [whole[:, t * LANES : (t + 1) * LANES] for t in range(tiles)]
         for i in range(sz.cut_x):
-            start = i * strip
-            t, r = start // LANES, start % LANES
+            cutting = sorted({0, strip} | {n - i * strip for n in range(0, sz.cut_nodes, sz.sent)} & set(range(strip)))
+            cutting = [0] + [n for n in cutting if n > 0]
             result = jnp.zeros((PARTS, LANES), jnp.float32)
-            for fold in range(folds):
-                for q in range(sz.n_ey):
-                    source = held[q, fold][t]
-                    if r + strip > LANES:
-                        source = jnp.where(lanes >= r, source, held[q, fold][t + 1])
-                    goal = fold * width + q * strip
-                    moved = pltpu.roll(source, (goal - r) % LANES, 1) if goal != r else source
-                    result = jnp.where((lanes >= goal) & (lanes < goal + strip), moved, result)
+            for begin, end in zip(cutting[:-1], cutting[1:]):
+                piece, row = (i * strip + begin) // sz.sent, (i * strip + begin) % sz.sent
+                t, r = (piece * sz.share + row) // LANES, (piece * sz.share + row) % LANES
+                for fold in range(folds):
+                    for q in range(sz.n_ey):
+                        source = held[q, fold][t]
+                        if r + end - begin > LANES:
+                            source = jnp.where(lanes >= r, source, held[q, fold][t + 1])
+                        goal = fold * width + q * strip + begin
+                        moved = pltpu.roll(source, (goal - r) % LANES, 1) if goal != r else source
+                        result = jnp.where((lanes >= goal) & (lanes < goal + end - begin), moved, result)
             field_ref[pl.ds((p * sz.cuts + cut) * sz.cut_x + i, PARTS, stride=x_pad), :] = result
 
     parts = dot(along(field_ref[...]), in_y_ref[...])
@@ -594,7 +603,7 @@
     heights = [float(height) for height in tables["heights"]]
     pieces = call(
         functools.partial(advect_kernel, sz, heights),
-        [(sz.share, LANES)] * (sz.n_mode * sz.cuts),
+        [(sz.sent, LANES)] * (sz.n_mode * sz.cuts),
         [
             pltpu.with_memory_space_constraint(each, pltpu.HBM)
             for each in (

time: 58.1 us -> 57.9 us (level)
  no operation moved by 1% of the time
where the time goes in v10:
time: 57.9 us; the launch traced here: 57.7 us
  blocking collectives  20.5 us (35%)
  waiting for transfers between devices  13.9 us (24%)
  starting transfers between devices  12 us (21%)
  Pallas kernels  11.1 us (19%)
    all_to_all x1, blocking collectives, on_device(): lax.all_to_all(spectra, ('mode', 'ex', 'ey'), split_axis=0, concat_axis=0...  20.5 us
    pallas_call x4, Pallas kernels, call(): pl.pallas_call(kernel, out_shape=[jax.ShapeDtypeStruct(shape, jnp.float32...  11.1 us
    ppermute x3, waiting for transfers between devices, on_device(): weak[cut][step] = lax.ppermute(weak[cut][step], 'mode', pairs)  10 us
    ppermute x7, starting transfers between devices, on_device(): solved[step] = lax.ppermute(solved[step], ('ex', 'ey'), pairs)  6.31 us
    ppermute x3, starting transfers between devices, on_device(): weak[cut][step] = lax.ppermute(weak[cut][step], 'mode', pairs)  5.69 us
    ppermute x7, waiting for transfers between devices, on_device(): solved[step] = lax.ppermute(solved[step], ('ex', 'ey'), pairs)  3.86 us
  transfers between devices with their start and end apart: 10, of which 6 were waited for; matrix products, arithmetic and copies ran while one was open for 0% of the time, Pallas kernels for 0%

profile of v10, /device:TPU:0, one launch (start us, length us, event | category | flops | bytes accessed | tf_op | source)
XLA Modules:
  0.0 57.7 jit_solution(6045542303030138010)
XLA Ops:
  0.0 4.0 %shard_map.127 = (f32[248,128]{1,0:T(8,128)S(1)}, f32[248,128]{1,0:T(8,128)S(1)}, f32[248,128]{1,0:T(8,128)S(1)}, f32[248,128]{1,0:T(8,128)S(1)}) custom-call(f32[1152,64]{1,0:T(8,128)} %bitcast.5, f32[1152,64]{1,0:T(8,128)} %bitcast.6, bf16[1008,432]{1,0:T(8,128)(2,1)} %constant.22.clone.lift_hbm, bf16[2,528,672]{2,1,0:T(8,128)(2,1)} %constant.23.clone.back_hbm), custom_call_target="tpu_custom_call" | custom-call | flops 1000000000 | bytes 1000000 | tf_op jit(solution)/shard_map/pallas_call | solution.py:588
  4.0 3.1 %collective-permute-start = (f32[248,128]{1,0:T(8,128)S(1)}, f32[248,128]{1,0:T(8,128)S(1)}, u32[]{:S(2)}, u32[]{:S(2)}) collective-permute-start(f32[248,128]{1,0:T(8,128)S(1)} %get-tuple-element.18), channel_id=1, source_target_pairs={{0,8},{8,0},{16,24},{24,16},{1,9},{9,1},{17,25},{25,17},{2,10},{10... | collective-permute-start | bytes 380936 | tf_op jit(solution)/shard_map/ppermute | solution.py:630
  7.1 2.6 %collective-permute-start.1 = (f32[248,128]{1,0:T(8,128)S(1)}, f32[248,128]{1,0:T(8,128)S(1)}, u32[]{:S(2)}, u32[]{:S(2)}) collective-permute-start(f32[248,128]{1,0:T(8,128)S(1)} %get-tuple-element.19), channel_id=1, source_target_pairs={{0,16},{8,24},{16,0},{24,8},{1,17},{9,25},{17,1},{25,9},{2,18},{10... | collective-permute-start | bytes 380936 | tf_op jit(solution)/shard_map/ppermute | solution.py:630
  9.7 2.2 %collective-permute-done.refs_1_ = f32[248,128]{1,0:T(8,128)S(1)} collective-permute-done((f32[248,128]{1,0:T(8,128)S(1)}, f32[248,128]{1,0:T(8,128)S(1)}, u32[]{:S(2)}, u32[]{:S(2)}) %collective-permute-start) | collective-permute-done | bytes 127008 | tf_op jit(solution)/shard_map/ppermute | solution.py:630
  12.0 7.8 %collective-permute-done.1.refs_2_ = f32[248,128]{1,0:T(8,128)S(1)} collective-permute-done((f32[248,128]{1,0:T(8,128)S(1)}, f32[248,128]{1,0:T(8,128)S(1)}, u32[]{:S(2)}, u32[]{:S(2)}) %collective-permute-start.1) | collective-permute-done | bytes 127008 | tf_op jit(solution)/shard_map/ppermute | solution.py:630
  19.8 0.0 copy-start.3
  19.8 0.0 copy-start.4
  19.8 0.0 copy-start.5
  19.8 0.0 copy-start.6
  19.9 0.6 %shard_map.128 = f32[512,256]{1,0:T(8,128)S(1)} custom-call(f32[248,128]{1,0:T(8,128)S(1)} %get-tuple-element.17.refs_0_, f32[248,128]{1,0:T(8,128)S(1)} %collective-permute-done.refs_1_, f32[248,128]{1,0:T(8,128)S(1)} %collective-permute-done.1.refs_2_, f32[248,128]{1,0:T(8,128)S(1)} %collective-permute-done.2.refs_3_, bf16[2,256,256]{2,1,0:T(8,128)(2,1)S(1)} %copy-done.1), custom_call_target="tpu_custom_call" | custom-call | flops 99999997952 | bytes 1000000 | tf_op jit(solution)/shard_map/pallas_call | solution.py:588
  20.5 20.5 %all_to_all.5.refs_0_ = f32[32,16,256]{2,1,0:T(8,128)S(1)} all-to-all(f32[32,16,256]{2,1,0:T(8,128)S(1)} %bitcast.4), channel_id=1, replica_groups=mesh['mode'=4,'ex'=4,'ey'=2] {'mode','ex','ey'}, dimensions={0} | all-to-all | bytes 1048576 | tf_op jit(solution)/shard_map/all_to_all | solution.py:642
  41.1 5.3 %shard_map.129 = (f32[16,1024]{1,0:T(8,128)S(1)}, f32[16,1024]{1,0:T(8,128)S(1)}, f32[16,1024]{1,0:T(8,128)S(1)}, f32[16,1024]{1,0:T(8,128)S(1)}, f32[16,1024]{1...) custom-call(f32[32,16,256]{2,1,0:T(8,128)S(1)} %all_to_all.5.refs_0_, ...), custom_call_target="tpu_custom_call" | custom-call | flops 1000000000 | bytes 1000000 | tf_op jit(solution)/shard_map/pallas_call | solution.py:588
  46.4 0.1 collective-permute-start.3
  46.5 1.3 %collective-permute-start.4 = (f32[16,1024]{1,0:T(8,128)S(1)}, f32[16,1024]{1,0:T(8,128)S(1)}, u32[]{:S(2)}, u32[]{:S(2)}) collective-permute-start(f32[16,1024]{1,0:T(8,128)S(1)} %get-tuple-element.23), channel_id=1, source_target_pairs={{0,2},{1,3},{2,4},{3,5},{4,6},{5,7},{6,0},{7,1},{8,10},{9,11},{10,... | collective-permute-start | bytes 196616 | tf_op jit(solution)/shard_map/ppermute | solution.py:658
  47.8 1.2 %collective-permute-start.5 = (f32[16,1024]{1,0:T(8,128)S(1)}, f32[16,1024]{1,0:T(8,128)S(1)}, u32[]{:S(2)}, u32[]{:S(2)}) collective-permute-start(f32[16,1024]{1,0:T(8,128)S(1)} %get-tuple-element.24), channel_id=1, source_target_pairs={{0,3},{1,2},{2,5},{3,4},{4,7},{5,6},{6,1},{7,0},{8,11},{9,10},{10,... | collective-permute-start | bytes 196616 | tf_op jit(solution)/shard_map/ppermute | solution.py:658
  49.0 0.8 %collective-permute-start.6 = (f32[16,1024]{1,0:T(8,128)S(1)}, f32[16,1024]{1,0:T(8,128)S(1)}, u32[]{:S(2)}, u32[]{:S(2)}) collective-permute-start(f32[16,1024]{1,0:T(8,128)S(1)} %get-tuple-element.25), channel_id=1, source_target_pairs={{0,4},{1,5},{2,6},{3,7},{4,0},{5,1},{6,2},{7,3},{8,12},{9,13},{10,... | collective-permute-start | bytes 196616 | tf_op jit(solution)/shard_map/ppermute | solution.py:658
  49.8 0.9 %collective-permute-start.7 = (f32[16,1024]{1,0:T(8,128)S(1)}, f32[16,1024]{1,0:T(8,128)S(1)}, u32[]{:S(2)}, u32[]{:S(2)}) collective-permute-start(f32[16,1024]{1,0:T(8,128)S(1)} %get-tuple-element.26), channel_id=1, source_target_pairs={{0,5},{1,4},{2,7},{3,6},{4,1},{5,0},{6,3},{7,2},{8,13},{9,12},{10,... | collective-permute-start | bytes 196616 | tf_op jit(solution)/shard_map/ppermute | solution.py:658
  50.7 1.5 %collective-permute-start.8 = (f32[16,1024]{1,0:T(8,128)S(1)}, f32[16,1024]{1,0:T(8,128)S(1)}, u32[]{:S(2)}, u32[]{:S(2)}) collective-permute-start(f32[16,1024]{1,0:T(8,128)S(1)} %get-tuple-element.27), channel_id=1, source_target_pairs={{0,6},{1,7},{2,0},{3,1},{4,2},{5,3},{6,4},{7,5},{8,14},{9,15},{10,... | collective-permute-start | bytes 196616 | tf_op jit(solution)/shard_map/ppermute | solution.py:658
  52.2 0.5 collective-permute-start.9
  52.7 0.4 collective-permute-done.5.refs_3_
  53.1 1.6 %collective-permute-done.6.refs_4_ = f32[16,1024]{1,0:T(8,128)S(1)} collective-permute-done((f32[16,1024]{1,0:T(8,128)S(1)}, f32[16,1024]{1,0:T(8,128)S(1)}, u32[]{:S(2)}, u32[]{:S(2)}) %collective-permute-start.6) | collective-permute-done | bytes 65568 | tf_op jit(solution)/shard_map/ppermute | solution.py:658
  54.7 1.3 %collective-permute-done.7.refs_5_ = f32[16,1024]{1,0:T(8,128)S(1)} collective-permute-done((f32[16,1024]{1,0:T(8,128)S(1)}, f32[16,1024]{1,0:T(8,128)S(1)}, u32[]{:S(2)}, u32[]{:S(2)}) %collective-permute-start.7) | collective-permute-done | bytes 65568 | tf_op jit(solution)/shard_map/ppermute | solution.py:658
  56.0 0.6 collective-permute-done.9.refs_7_
  56.6 1.1 %shard_map.130 = f32[1152,128]{1,0:T(8,128)} custom-call(f32[16,1024]{1,0:T(8,128)S(1)} %get-tuple-element.21.refs_0_, f32[16,1024]{1,0:T(8,128)S(1)} %collective-permute-done.3.refs_1_, f32[16,1024]{1,0:T(8,128)S(1)} %collective-permute-done.4.refs_2_, f32[16,1024]{1,0:T(8,128)S(1)} %collective-permute-done.5.refs_3_, ...), custom_call_target="tpu_custom_call" | custom-call | flops 1000000000 | bytes 1000000 | tf_op jit(solution)/shard_map/pallas_call | solution.py:588
  (19 shorter events, 0.0 us)
Async XLA Ops:
  0.0 19.8 %copy-start.1 = (bf16[2,256,256]{2,1,0:T(8,128)(2,1)S(1)}, bf16[2,256,256]{2,1,0:T(8,128)(2,1)}, u32[]{:S(2)}) copy-start(bf16[2,256,256]{2,1,0:T(8,128)(2,1)} %constant.24.clone.refs_4_) | copy-start | bytes 786436
  4.0 7.9 %collective-permute-start = (f32[248,128]{1,0:T(8,128)S(1)}, f32[248,128]{1,0:T(8,128)S(1)}, u32[]{:S(2)}, u32[]{:S(2)}) collective-permute-start(f32[248,128]{1,0:T(8,128)S(1)} %get-tuple-element.18), channel_id=1, source_target_pairs={{0,8},{8,0},{16,24},{24,16},{1,9},{9,1},{17,25},{25,17},{2,10},{10... | collective-permute-start | bytes 380936 | tf_op jit(solution)/shard_map/ppermute | solution.py:630
  7.1 12.6 %collective-permute-start.1 = (f32[248,128]{1,0:T(8,128)S(1)}, f32[248,128]{1,0:T(8,128)S(1)}, u32[]{:S(2)}, u32[]{:S(2)}) collective-permute-start(f32[248,128]{1,0:T(8,128)S(1)} %get-tuple-element.19), channel_id=1, source_target_pairs={{0,16},{8,24},{16,0},{24,8},{1,17},{9,25},{17,1},{25,9},{2,18},{10... | collective-permute-start | bytes 380936 | tf_op jit(solution)/shard_map/ppermute | solution.py:630
  9.7 10.0 %collective-permute-start.2 = (f32[248,128]{1,0:T(8,128)S(1)}, f32[248,128]{1,0:T(8,128)S(1)}, u32[]{:S(2)}, u32[]{:S(2)}) collective-permute-start(f32[248,128]{1,0:T(8,128)S(1)} %get-tuple-element.20), channel_id=1, source_target_pairs={{0,24},{8,16},{16,8},{24,0},{1,25},{9,17},{17,9},{25,1},{2,26},{10... | collective-permute-start | bytes 380936 | tf_op jit(solution)/shard_map/ppermute | solution.py:630
  19.8 21.3 %copy-start = (bf16[448,448]{1,0:T(8,128)(2,1)S(1)}, bf16[448,448]{1,0:T(8,128)(2,1)}, u32[]{:S(2)}) copy-start(bf16[448,448]{1,0:T(8,128)(2,1)} %constant.28.clone.refs_4_) | copy-start | bytes 1204228
  19.8 21.2 %copy-start.2 = (bf16[448,192]{1,0:T(8,128)(2,1)S(1)}, bf16[448,192]{1,0:T(8,128)(2,1)}, u32[]{:S(2)}) copy-start(bf16[448,192]{1,0:T(8,128)(2,1)} %constant.26.clone.refs_2_) | copy-start | bytes 516100
  19.8 21.2 %copy-start.3 = (bf16[384,224]{1,0:T(8,128)(2,1)S(1)}, bf16[384,224]{1,0:T(8,128)(2,1)}, u32[]{:S(2)}) copy-start(bf16[384,224]{1,0:T(8,128)(2,1)} %constant.30.clone.refs_6_) | copy-start | bytes 516100
  19.8 21.2 %copy-start.4 = (bf16[384,256]{1,0:T(8,128)(2,1)S(1)}, bf16[384,256]{1,0:T(8,128)(2,1)}, u32[]{:S(2)}) copy-start(bf16[384,256]{1,0:T(8,128)(2,1)} %constant.27.clone.refs_3_) | copy-start | bytes 589828
  19.8 21.2 %copy-start.5 = (bf16[256,256]{1,0:T(8,128)(2,1)S(1)}, bf16[256,256]{1,0:T(8,128)(2,1)}, u32[]{:S(2)}) copy-start(bf16[256,256]{1,0:T(8,128)(2,1)} %constant.29.clone.refs_5_) | copy-start | bytes 393220
  19.8 21.2 %copy-start.6 = (bf16[256,256]{1,0:T(8,128)(2,1)S(1)}, bf16[256,256]{1,0:T(8,128)(2,1)}, u32[]{:S(2)}) copy-start(bf16[256,256]{1,0:T(8,128)(2,1)} %constant.25.clone.refs_1_) | copy-start | bytes 393220
  19.8 21.2 %copy-start.7 = (f32[224,128]{1,0:T(8,128)S(1)}, f32[224,128]{1,0:T(8,128)}, u32[]{:S(2)}) copy-start(f32[224,128]{1,0:T(8,128)} %constant.31.clone.refs_7_) | copy-start | bytes 344068
  19.8 21.2 %copy-start.8 = (f32[1,128]{1,0:T(1,128)S(1)}, f32[1,128]{1,0:T(1,128)}, u32[]{:S(2)}) copy-start(f32[1,128]{1,0:T(1,128)} %constant.32.clone.refs_8_) | copy-start | bytes 1540
  46.4 4.3 %collective-permute-start.3 = (f32[16,1024]{1,0:T(8,128)S(1)}, f32[16,1024]{1,0:T(8,128)S(1)}, u32[]{:S(2)}, u32[]{:S(2)}) collective-permute-start(f32[16,1024]{1,0:T(8,128)S(1)} %get-tuple-element.22), channel_id=1, source_target_pairs={{0,1},{1,0},{2,3},{3,2},{4,5},{5,4},{6,7},{7,6},{8,9},{9,8},{10,11... | collective-permute-start | bytes 196616 | tf_op jit(solution)/shard_map/ppermute | solution.py:658
  46.5 5.7 %collective-permute-start.4 = (f32[16,1024]{1,0:T(8,128)S(1)}, f32[16,1024]{1,0:T(8,128)S(1)}, u32[]{:S(2)}, u32[]{:S(2)}) collective-permute-start(f32[16,1024]{1,0:T(8,128)S(1)} %get-tuple-element.23), channel_id=1, source_target_pairs={{0,2},{1,3},{2,4},{3,5},{4,6},{5,7},{6,0},{7,1},{8,10},{9,11},{10,... | collective-permute-start | bytes 196616 | tf_op jit(solution)/shard_map/ppermute | solution.py:658
  47.8 5.3 %collective-permute-start.5 = (f32[16,1024]{1,0:T(8,128)S(1)}, f32[16,1024]{1,0:T(8,128)S(1)}, u32[]{:S(2)}, u32[]{:S(2)}) collective-permute-start(f32[16,1024]{1,0:T(8,128)S(1)} %get-tuple-element.24), channel_id=1, source_target_pairs={{0,3},{1,2},{2,5},{3,4},{4,7},{5,6},{6,1},{7,0},{8,11},{9,10},{10,... | collective-permute-start | bytes 196616 | tf_op jit(solution)/shard_map/ppermute | solution.py:658
  49.0 5.7 %collective-permute-start.6 = (f32[16,1024]{1,0:T(8,128)S(1)}, f32[16,1024]{1,0:T(8,128)S(1)}, u32[]{:S(2)}, u32[]{:S(2)}) collective-permute-start(f32[16,1024]{1,0:T(8,128)S(1)} %get-tuple-element.25), channel_id=1, source_target_pairs={{0,4},{1,5},{2,6},{3,7},{4,0},{5,1},{6,2},{7,3},{8,12},{9,13},{10,... | collective-permute-start | bytes 196616 | tf_op jit(solution)/shard_map/ppermute | solution.py:658
  49.8 6.2 %collective-permute-start.7 = (f32[16,1024]{1,0:T(8,128)S(1)}, f32[16,1024]{1,0:T(8,128)S(1)}, u32[]{:S(2)}, u32[]{:S(2)}) collective-permute-start(f32[16,1024]{1,0:T(8,128)S(1)} %get-tuple-element.26), channel_id=1, source_target_pairs={{0,5},{1,4},{2,7},{3,6},{4,1},{5,0},{6,3},{7,2},{8,13},{9,12},{10,... | collective-permute-start | bytes 196616 | tf_op jit(solution)/shard_map/ppermute | solution.py:658
  50.7 5.3 %collective-permute-start.8 = (f32[16,1024]{1,0:T(8,128)S(1)}, f32[16,1024]{1,0:T(8,128)S(1)}, u32[]{:S(2)}, u32[]{:S(2)}) collective-permute-start(f32[16,1024]{1,0:T(8,128)S(1)} %get-tuple-element.27), channel_id=1, source_target_pairs={{0,6},{1,7},{2,0},{3,1},{4,2},{5,3},{6,4},{7,5},{8,14},{9,15},{10,... | collective-permute-start | bytes 196616 | tf_op jit(solution)/shard_map/ppermute | solution.py:658
  52.2 4.4 %collective-permute-start.9 = (f32[16,1024]{1,0:T(8,128)S(1)}, f32[16,1024]{1,0:T(8,128)S(1)}, u32[]{:S(2)}, u32[]{:S(2)}) collective-permute-start(f32[16,1024]{1,0:T(8,128)S(1)} %get-tuple-element.28), channel_id=1, source_target_pairs={{0,7},{1,6},{2,1},{3,0},{4,3},{5,2},{6,5},{7,4},{8,15},{9,14},{10,... | collective-permute-start | bytes 196616 | tf_op jit(solution)/shard_map/ppermute | solution.py:658

commit v11 on v10

--- a/solution.py
+++ b/solution.py
@@ -355,7 +355,7 @@
             )
         )
     ]
-    for copy in fetched[:3]:
+    for copy in fetched:
         copy.start()
     count, fine, rows = sz.nodes * sz.nodes, sz.fine, sz.rows
     spots = sz.elems * rows
@@ -369,7 +369,6 @@
     spot = lax.axis_index("mode")
     for copy in fetched[:3]:
         copy.wait()
-    fetched[3].start()
     for cut in range(sz.cuts):
         high_parts, low_parts = [], []
         for e in range(cut * sz.cut_elems, (cut + 1) * sz.cut_elems):
@@ -549,7 +548,7 @@
                     for q in range(sz.n_ey):
                         if (q, fold, tile) in made:
                             chosen = jnp.where((place + turn) % sz.n_ey == q, made[q, fold, tile], chosen)
-                    out_refs[p * sz.n_ey + turn][pl.ds(fold * PARTS, PARTS), pl.ds(tile * LANES, LANES)] = chosen
+                    out_refs[p][pl.ds(turn * sz.own + fold * PARTS, PARTS), pl.ds(tile * LANES, LANES)] = chosen
 
 
 def spread_kernel(sz, *refs):
@@ -558,7 +557,8 @@
     for step, solved_ref in enumerate(solved_refs):
         shift, turn = step // sz.n_ey, step % sz.n_ey
         source = (spot - shift + sz.n_ex) % sz.n_ex * sz.n_ey + (place - turn + sz.n_ey) % sz.n_ey
-        stacked_ref[pl.ds(pl.multiple_of(source * sz.own, PARTS), sz.own), :] = solved_ref[...]
+        rows = pl.ds(pl.multiple_of(source * sz.own, PARTS), sz.own)
+        stacked_ref[rows, :] = solved_ref[pl.ds(turn * sz.own, sz.own), :]
     turned_ref[...] = stacked_ref[...].T
     spots = sz.elems * sz.rows
     for e in range(sz.elems):
@@ -644,22 +644,22 @@
     names = ("in_y", "in_x", "pair_y", "pair_x", "out_y", "out_x", "lam_x", "lam_y")
     solved = call(
         functools.partial(smooth_kernel, sz),
-        [(sz.own, sz.lane_nodes)] * sz.spots,
+        [(sz.n_ey * sz.own, sz.lane_nodes)] * sz.n_ex,
         terms + [table[name] for name in names],
         [(PARTS * sz.x_pad, LANES)] + [(PARTS * sz.x_eig, LANES)] * 3,
     )
-    for step in sorted(range(1, sz.spots), key=lambda each: each // sz.n_ey == 0):
-        shift, turn = step // sz.n_ey, step % sz.n_ey
-        pairs = [
-            (p * sz.n_ey + q, (p + shift) % sz.n_ex * sz.n_ey + (q + turn) % sz.n_ey)
-            for p in range(sz.n_ex)
-            for q in range(sz.n_ey)
-        ]
-        solved[step] = lax.ppermute(solved[step], ("ex", "ey"), pairs)
+    for shift in sorted(range(1, sz.n_ex), key=lambda each: (each & -each, each), reverse=True):
+        pairs = [(p, (p + shift) % sz.n_ex) for p in range(sz.n_ex)]
+        solved[shift] = lax.ppermute(solved[shift], "ex", pairs)
+    arrived = []
+    for shift in range(sz.n_ex):
+        for turn in range(sz.n_ey):
+            pairs = [(q, (q + turn) % sz.n_ey) for q in range(sz.n_ey)]
+            arrived.append(lax.ppermute(solved[shift], "ey", pairs) if turn else solved[shift])
     (out,) = call(
         functools.partial(spread_kernel, sz),
         [(flat, LANES)],
-        solved,
+        arrived,
         [(sz.columns, sz.lane_nodes), (sz.lane_nodes, LANES)],
     )
     return out.reshape(sz.nodes, sz.nodes, sz.elems, sz.rows, sz.columns)

time: 57.9 us -> 58.3 us (level)
  waiting for transfers between devices: 13.9 us -> 15.9 us
  starting transfers between devices: 12 us -> 10.4 us
    ppermute x7, waiting for transfers between devices: 3.86 us -> 5.86 us  [the longest x3 4.84 us: on_device(): solved[shift] = lax.ppermute(solved[shift], 'ex', pairs)]
    ppermute x7, starting transfers between devices: 6.31 us -> 4.73 us  [the longest x3 4.22 us: on_device(): solved[shift] = lax.ppermute(solved[shift], 'ex', pairs)]
where the time goes in v11:
time: 58.3 us; the launch traced here: 58.1 us
  blocking collectives  20.5 us (35%)
  waiting for transfers between devices  15.9 us (27%)
  Pallas kernels  11.1 us (19%)
  starting transfers between devices  10.4 us (18%)
    all_to_all x1, blocking collectives, on_device(): lax.all_to_all(spectra, ('mode', 'ex', 'ey'), split_axis=0, concat_axis=0...  20.5 us
    pallas_call x4, Pallas kernels, call(): pl.pallas_call(kernel, out_shape=[jax.ShapeDtypeStruct(shape, jnp.float32...  11.1 us
    ppermute x3, waiting for transfers between devices, on_device(): weak[cut][step] = lax.ppermute(weak[cut][step], 'mode', pairs)  10 us
    ppermute x3, starting transfers between devices, on_device(): weak[cut][step] = lax.ppermute(weak[cut][step], 'mode', pairs)  5.7 us
    ppermute x3, waiting for transfers between devices, on_device(): solved[shift] = lax.ppermute(solved[shift], 'ex', pairs)  4.84 us
    ppermute x3, starting transfers between devices, on_device(): solved[shift] = lax.ppermute(solved[shift], 'ex', pairs)  4.22 us
  transfers between devices with their start and end apart: 10, of which 6 were waited for; matrix products, arithmetic and copies ran while one was open for 0% of the time, Pallas kernels for 0%

profile of v11, /device:TPU:0, one launch (start us, length us, event | category | flops | bytes accessed | tf_op | source)
XLA Modules:
  0.0 58.1 jit_solution(13957792464923582632)
XLA Ops:
  0.0 4.0 %shard_map.127 = (f32[248,128]{1,0:T(8,128)S(1)}, f32[248,128]{1,0:T(8,128)S(1)}, f32[248,128]{1,0:T(8,128)S(1)}, f32[248,128]{1,0:T(8,128)S(1)}) custom-call(f32[1152,64]{1,0:T(8,128)} %bitcast.5, f32[1152,64]{1,0:T(8,128)} %bitcast.6, bf16[1008,432]{1,0:T(8,128)(2,1)} %constant.22.clone.lift_hbm, bf16[2,528,672]{2,1,0:T(8,128)(2,1)} %constant.23.clone.back_hbm), custom_call_target="tpu_custom_call" | custom-call | flops 1000000000 | bytes 1000000 | tf_op jit(solution)/shard_map/pallas_call | solution.py:588
  4.0 3.1 %collective-permute-start = (f32[248,128]{1,0:T(8,128)S(1)}, f32[248,128]{1,0:T(8,128)S(1)}, u32[]{:S(2)}, u32[]{:S(2)}) collective-permute-start(f32[248,128]{1,0:T(8,128)S(1)} %get-tuple-element.14), channel_id=1, source_target_pairs={{0,8},{8,0},{16,24},{24,16},{1,9},{9,1},{17,25},{25,17},{2,10},{10... | collective-permute-start | bytes 380936 | tf_op jit(solution)/shard_map/ppermute | solution.py:630
  7.1 2.6 %collective-permute-start.1 = (f32[248,128]{1,0:T(8,128)S(1)}, f32[248,128]{1,0:T(8,128)S(1)}, u32[]{:S(2)}, u32[]{:S(2)}) collective-permute-start(f32[248,128]{1,0:T(8,128)S(1)} %get-tuple-element.15), channel_id=1, source_target_pairs={{0,16},{8,24},{16,0},{24,8},{1,17},{9,25},{17,1},{25,9},{2,18},{10... | collective-permute-start | bytes 380936 | tf_op jit(solution)/shard_map/ppermute | solution.py:630
  9.7 2.2 %collective-permute-done.refs_1_ = f32[248,128]{1,0:T(8,128)S(1)} collective-permute-done((f32[248,128]{1,0:T(8,128)S(1)}, f32[248,128]{1,0:T(8,128)S(1)}, u32[]{:S(2)}, u32[]{:S(2)}) %collective-permute-start) | collective-permute-done | bytes 127008 | tf_op jit(solution)/shard_map/ppermute | solution.py:630
  12.0 7.8 %collective-permute-done.1.refs_2_ = f32[248,128]{1,0:T(8,128)S(1)} collective-permute-done((f32[248,128]{1,0:T(8,128)S(1)}, f32[248,128]{1,0:T(8,128)S(1)}, u32[]{:S(2)}, u32[]{:S(2)}) %collective-permute-start.1) | collective-permute-done | bytes 127008 | tf_op jit(solution)/shard_map/ppermute | solution.py:630
  19.8 0.0 copy-start.2
  19.8 0.0 copy-start.4
  19.8 0.0 copy-start.5
  19.8 0.0 copy-start.6
  19.8 0.0 copy-start.7
  19.8 0.0 copy-start.8
  19.9 0.6 %shard_map.128 = f32[512,256]{1,0:T(8,128)S(1)} custom-call(f32[248,128]{1,0:T(8,128)S(1)} %get-tuple-element.13.refs_0_, f32[248,128]{1,0:T(8,128)S(1)} %collective-permute-done.refs_1_, f32[248,128]{1,0:T(8,128)S(1)} %collective-permute-done.1.refs_2_, f32[248,128]{1,0:T(8,128)S(1)} %collective-permute-done.2.refs_3_, bf16[2,256,256]{2,1,0:T(8,128)(2,1)S(1)} %copy-done.1), custom_call_target="tpu_custom_call" | custom-call | flops 99999997952 | bytes 1000000 | tf_op jit(solution)/shard_map/pallas_call | solution.py:588
  20.5 20.5 %all_to_all.5.refs_0_ = f32[32,16,256]{2,1,0:T(8,128)S(1)} all-to-all(f32[32,16,256]{2,1,0:T(8,128)S(1)} %bitcast.4), channel_id=1, replica_groups=mesh['mode'=4,'ex'=4,'ey'=2] {'mode','ex','ey'}, dimensions={0} | all-to-all | bytes 1048576 | tf_op jit(solution)/shard_map/all_to_all | solution.py:642
  41.1 5.3 %shard_map.129 = (f32[32,1024]{1,0:T(8,128)S(1)}, f32[32,1024]{1,0:T(8,128)S(1)}, f32[32,1024]{1,0:T(8,128)S(1)}, f32[32,1024]{1,0:T(8,128)S(1)}) custom-call(f32[32,16,256]{2,1,0:T(8,128)S(1)} %all_to_all.5.refs_0_, bf16[256,256]{1,0:T(8,128)(2,1)S(1)} %copy-done.6, bf16[448,192]{1,0:T(8,128)(2,1)S(1)} %copy-done.2, bf16[384,256]{1,0:T(8,128)(2,1)S(1)} %copy-done.4, ...), custom_call_target="tpu_custom_call" | custom-call | flops 1000000000 | bytes 1000000 | tf_op jit(solution)/shard_map/pallas_call | solution.py:588
  46.4 1.0 %collective-permute-start.4 = (f32[32,1024]{1,0:T(8,128)S(1)}, f32[32,1024]{1,0:T(8,128)S(1)}, u32[]{:S(2)}, u32[]{:S(2)}) collective-permute-start(f32[32,1024]{1,0:T(8,128)S(1)} %get-tuple-element.18), channel_id=1, source_target_pairs={{0,2},{2,4},{4,6},{6,0},{1,3},{3,5},{5,7},{7,1},{8,10},{10,12},{12... | collective-permute-start | bytes 393224 | tf_op jit(solution)/shard_map/ppermute | solution.py:653
  47.3 1.5 %collective-permute-start.6 = (f32[32,1024]{1,0:T(8,128)S(1)}, f32[32,1024]{1,0:T(8,128)S(1)}, u32[]{:S(2)}, u32[]{:S(2)}) collective-permute-start(f32[32,1024]{1,0:T(8,128)S(1)} %get-tuple-element.19), channel_id=1, source_target_pairs={{0,4},{2,6},{4,0},{6,2},{1,5},{3,7},{5,1},{7,3},{8,12},{10,14},{12... | collective-permute-start | bytes 393224 | tf_op jit(solution)/shard_map/ppermute | solution.py:653
  48.8 1.8 %collective-permute-start.8 = (f32[32,1024]{1,0:T(8,128)S(1)}, f32[32,1024]{1,0:T(8,128)S(1)}, u32[]{:S(2)}, u32[]{:S(2)}) collective-permute-start(f32[32,1024]{1,0:T(8,128)S(1)} %get-tuple-element.20), channel_id=1, source_target_pairs={{0,6},{2,0},{4,2},{6,4},{1,7},{3,1},{5,3},{7,5},{8,14},{10,8},{12,... | collective-permute-start | bytes 393224 | tf_op jit(solution)/shard_map/ppermute | solution.py:653
  50.6 3.1 %collective-permute-done.4.refs_2_ = f32[32,1024]{1,0:T(8,128)S(1)} collective-permute-done((f32[32,1024]{1,0:T(8,128)S(1)}, f32[32,1024]{1,0:T(8,128)S(1)}, u32[]{:S(2)}, u32[]{:S(2)}) %collective-permute-start.4) | collective-permute-done | bytes 131104 | tf_op jit(solution)/shard_map/ppermute | solution.py:653
  53.7 1.7 %collective-permute-done.6.refs_4_ = f32[32,1024]{1,0:T(8,128)S(1)} collective-permute-done((f32[32,1024]{1,0:T(8,128)S(1)}, f32[32,1024]{1,0:T(8,128)S(1)}, u32[]{:S(2)}, u32[]{:S(2)}) %collective-permute-start.6) | collective-permute-done | bytes 131104 | tf_op jit(solution)/shard_map/ppermute | solution.py:653
  55.4 0.0 collective-permute-start.7
  55.5 0.5 collective-permute-start.9
  56.0 0.8 %collective-permute-done.7.refs_5_ = f32[32,1024]{1,0:T(8,128)S(1)} collective-permute-done((f32[32,1024]{1,0:T(8,128)S(1)}, f32[32,1024]{1,0:T(8,128)S(1)}, u32[]{:S(2)}, u32[]{:S(2)}) %collective-permute-start.7) | collective-permute-done | bytes 131104 | tf_op jit(solution)/shard_map/ppermute | solution.py:658
  56.8 0.2 collective-permute-done.9.refs_7_
  57.0 1.1 %shard_map.130 = f32[1152,128]{1,0:T(8,128)} custom-call(f32[32,1024]{1,0:T(8,128)S(1)} %get-tuple-element.17.refs_0_, f32[32,1024]{1,0:T(8,128)S(1)} %collective-permute-done.3.refs_1_, f32[32,1024]{1,0:T(8,128)S(1)} %collective-permute-done.4.refs_2_, f32[32,1024]{1,0:T(8,128)S(1)} %collective-permute-done.5.refs_3_, ...), custom_call_target="tpu_custom_call" | custom-call | flops 1000000000 | bytes 1000000 | tf_op jit(solution)/shard_map/pallas_call | solution.py:588
  (19 shorter events, 0.0 us)
Async XLA Ops:
  0.0 19.8 %copy-start.1 = (bf16[2,256,256]{2,1,0:T(8,128)(2,1)S(1)}, bf16[2,256,256]{2,1,0:T(8,128)(2,1)}, u32[]{:S(2)}) copy-start(bf16[2,256,256]{2,1,0:T(8,128)(2,1)} %constant.24.clone.refs_4_) | copy-start | bytes 786436
  4.0 7.9 %collective-permute-start = (f32[248,128]{1,0:T(8,128)S(1)}, f32[248,128]{1,0:T(8,128)S(1)}, u32[]{:S(2)}, u32[]{:S(2)}) collective-permute-start(f32[248,128]{1,0:T(8,128)S(1)} %get-tuple-element.14), channel_id=1, source_target_pairs={{0,8},{8,0},{16,24},{24,16},{1,9},{9,1},{17,25},{25,17},{2,10},{10... | collective-permute-start | bytes 380936 | tf_op jit(solution)/shard_map/ppermute | solution.py:630
  7.1 12.6 %collective-permute-start.1 = (f32[248,128]{1,0:T(8,128)S(1)}, f32[248,128]{1,0:T(8,128)S(1)}, u32[]{:S(2)}, u32[]{:S(2)}) collective-permute-start(f32[248,128]{1,0:T(8,128)S(1)} %get-tuple-element.15), channel_id=1, source_target_pairs={{0,16},{8,24},{16,0},{24,8},{1,17},{9,25},{17,1},{25,9},{2,18},{10... | collective-permute-start | bytes 380936 | tf_op jit(solution)/shard_map/ppermute | solution.py:630
  9.7 10.0 %collective-permute-start.2 = (f32[248,128]{1,0:T(8,128)S(1)}, f32[248,128]{1,0:T(8,128)S(1)}, u32[]{:S(2)}, u32[]{:S(2)}) collective-permute-start(f32[248,128]{1,0:T(8,128)S(1)} %get-tuple-element.16), channel_id=1, source_target_pairs={{0,24},{8,16},{16,8},{24,0},{1,25},{9,17},{17,9},{25,1},{2,26},{10... | collective-permute-start | bytes 380936 | tf_op jit(solution)/shard_map/ppermute | solution.py:630
  19.8 21.3 %copy-start = (bf16[448,448]{1,0:T(8,128)(2,1)S(1)}, bf16[448,448]{1,0:T(8,128)(2,1)}, u32[]{:S(2)}) copy-start(bf16[448,448]{1,0:T(8,128)(2,1)} %constant.28.clone.refs_4_) | copy-start | bytes 1204228
  19.8 21.2 %copy-start.2 = (bf16[448,192]{1,0:T(8,128)(2,1)S(1)}, bf16[448,192]{1,0:T(8,128)(2,1)}, u32[]{:S(2)}) copy-start(bf16[448,192]{1,0:T(8,128)(2,1)} %constant.26.clone.refs_2_) | copy-start | bytes 516100
  19.8 21.2 %copy-start.3 = (bf16[384,224]{1,0:T(8,128)(2,1)S(1)}, bf16[384,224]{1,0:T(8,128)(2,1)}, u32[]{:S(2)}) copy-start(bf16[384,224]{1,0:T(8,128)(2,1)} %constant.30.clone.refs_6_) | copy-start | bytes 516100
  19.8 21.2 %copy-start.4 = (bf16[384,256]{1,0:T(8,128)(2,1)S(1)}, bf16[384,256]{1,0:T(8,128)(2,1)}, u32[]{:S(2)}) copy-start(bf16[384,256]{1,0:T(8,128)(2,1)} %constant.27.clone.refs_3_) | copy-start | bytes 589828
  19.8 21.2 %copy-start.5 = (bf16[256,256]{1,0:T(8,128)(2,1)S(1)}, bf16[256,256]{1,0:T(8,128)(2,1)}, u32[]{:S(2)}) copy-start(bf16[256,256]{1,0:T(8,128)(2,1)} %constant.29.clone.refs_5_) | copy-start | bytes 393220
  19.8 21.2 %copy-start.6 = (bf16[256,256]{1,0:T(8,128)(2,1)S(1)}, bf16[256,256]{1,0:T(8,128)(2,1)}, u32[]{:S(2)}) copy-start(bf16[256,256]{1,0:T(8,128)(2,1)} %constant.25.clone.refs_1_) | copy-start | bytes 393220
  19.8 21.2 %copy-start.7 = (f32[224,128]{1,0:T(8,128)S(1)}, f32[224,128]{1,0:T(8,128)}, u32[]{:S(2)}) copy-start(f32[224,128]{1,0:T(8,128)} %constant.31.clone.refs_7_) | copy-start | bytes 344068
  19.8 21.2 %copy-start.8 = (f32[1,128]{1,0:T(1,128)S(1)}, f32[1,128]{1,0:T(1,128)}, u32[]{:S(2)}) copy-start(f32[1,128]{1,0:T(1,128)} %constant.32.clone.refs_8_) | copy-start | bytes 1540
  46.4 7.3 %collective-permute-start.4 = (f32[32,1024]{1,0:T(8,128)S(1)}, f32[32,1024]{1,0:T(8,128)S(1)}, u32[]{:S(2)}, u32[]{:S(2)}) collective-permute-start(f32[32,1024]{1,0:T(8,128)S(1)} %get-tuple-element.18), channel_id=1, source_target_pairs={{0,2},{2,4},{4,6},{6,0},{1,3},{3,5},{5,7},{7,1},{8,10},{10,12},{12... | collective-permute-start | bytes 393224 | tf_op jit(solution)/shard_map/ppermute | solution.py:653
  47.3 8.1 %collective-permute-start.6 = (f32[32,1024]{1,0:T(8,128)S(1)}, f32[32,1024]{1,0:T(8,128)S(1)}, u32[]{:S(2)}, u32[]{:S(2)}) collective-permute-start(f32[32,1024]{1,0:T(8,128)S(1)} %get-tuple-element.19), channel_id=1, source_target_pairs={{0,4},{2,6},{4,0},{6,2},{1,5},{3,7},{5,1},{7,3},{8,12},{10,14},{12... | collective-permute-start | bytes 393224 | tf_op jit(solution)/shard_map/ppermute | solution.py:653
  48.8 6.6 %collective-permute-start.8 = (f32[32,1024]{1,0:T(8,128)S(1)}, f32[32,1024]{1,0:T(8,128)S(1)}, u32[]{:S(2)}, u32[]{:S(2)}) collective-permute-start(f32[32,1024]{1,0:T(8,128)S(1)} %get-tuple-element.20), channel_id=1, source_target_pairs={{0,6},{2,0},{4,2},{6,4},{1,7},{3,1},{5,3},{7,5},{8,14},{10,8},{12,... | collective-permute-start | bytes 393224 | tf_op jit(solution)/shard_map/ppermute | solution.py:653
  50.6 5.4 %collective-permute-start.3 = (f32[32,1024]{1,0:T(8,128)S(1)}, f32[32,1024]{1,0:T(8,128)S(1)}, u32[]{:S(2)}, u32[]{:S(2)}) collective-permute-start(f32[32,1024]{1,0:T(8,128)S(1)} %get-tuple-element.17.refs_0_), channel_id=1, source_target_pairs={{0,1},{1,0},{2,3},{3,2},{4,5},{5,4},{6,7},{7,6},{8,9},{9,8},{10,11... | collective-permute-start | bytes 393224 | tf_op jit(solution)/shard_map/ppermute | solution.py:658
  53.7 2.3 %collective-permute-start.5 = (f32[32,1024]{1,0:T(8,128)S(1)}, f32[32,1024]{1,0:T(8,128)S(1)}, u32[]{:S(2)}, u32[]{:S(2)}) collective-permute-start(f32[32,1024]{1,0:T(8,128)S(1)} %collective-permute-done.4.refs_2_), channel_id=1, source_target_pairs={{0,1},{1,0},{2,3},{3,2},{4,5},{5,4},{6,7},{7,6},{8,9},{9,8},{10,11... | collective-permute-start | bytes 393224 | tf_op jit(solution)/shard_map/ppermute | solution.py:658
  55.4 1.3 %collective-permute-start.7 = (f32[32,1024]{1,0:T(8,128)S(1)}, f32[32,1024]{1,0:T(8,128)S(1)}, u32[]{:S(2)}, u32[]{:S(2)}) collective-permute-start(f32[32,1024]{1,0:T(8,128)S(1)} %collective-permute-done.6.refs_4_), channel_id=1, source_target_pairs={{0,1},{1,0},{2,3},{3,2},{4,5},{5,4},{6,7},{7,6},{8,9},{9,8},{10,11... | collective-permute-start | bytes 393224 | tf_op jit(solution)/shard_map/ppermute | solution.py:658
  55.5 1.5 %collective-permute-start.9 = (f32[32,1024]{1,0:T(8,128)S(1)}, f32[32,1024]{1,0:T(8,128)S(1)}, u32[]{:S(2)}, u32[]{:S(2)}) collective-permute-start(f32[32,1024]{1,0:T(8,128)S(1)} %collective-permute-done.8.refs_6_), channel_id=1, source_target_pairs={{0,1},{1,0},{2,3},{3,2},{4,5},{5,4},{6,7},{7,6},{8,9},{9,8},{10,11... | collective-permute-start | bytes 393224 | tf_op jit(solution)/shard_map/ppermute | solution.py:658

commit v12 on v10

--- a/solution.py
+++ b/solution.py
@@ -282,7 +282,7 @@
     return dict(
         heights=np.asarray(heights, np.float32),
         lift=beside(lift),
-        back=np.stack([stacked(table) for table in back]),
+        back=np.stack([beside(table) for table in back]),
         waves=np.stack(high_low(waves)),
         in_y=one_dot(block_y),
         in_x=stacked(block_x(sz.n_ex * sz.cuts, sz.cut_elems)),
@@ -355,7 +355,7 @@
             )
         )
     ]
-    for copy in fetched[:3]:
+    for copy in fetched:
         copy.start()
     count, fine, rows = sz.nodes * sz.nodes, sz.fine, sz.rows
     spots = sz.elems * rows
@@ -369,9 +369,8 @@
     spot = lax.axis_index("mode")
     for copy in fetched[:3]:
         copy.wait()
-    fetched[3].start()
     for cut in range(sz.cuts):
-        high_parts, low_parts = [], []
+        products = []
         for e in range(cut * sz.cut_elems, (cut + 1) * sz.cut_elems):
             speeds = jnp.concatenate(
                 [
@@ -392,12 +391,10 @@
                 high, low = split((stream * factors[f]) * slope_x + (normal * (element_width * 0.5)) * slope_y)
                 highs.append(high)
                 lows.append(low)
-            high_parts.append(jnp.concatenate(highs, 0))
-            low_parts.append(jnp.concatenate(lows, 0))
+            products.append(jnp.concatenate(highs + lows + highs, 0))
         if cut == 0:
             fetched[3].wait()
-        both = dot(back_ref[...], jnp.concatenate(high_parts, 1))
-        weak = both[:column] + both[column:] + dot(back_ref[:column, :], jnp.concatenate(low_parts, 1))
+        weak = dot(back_ref[...], jnp.concatenate(products, 1))
         carry = None
         for e in range(sz.cut_elems):
             mine = weak[:, e * LANES : (e + 1) * LANES]
@@ -625,7 +622,7 @@
     )
     weak = [pieces[cut * sz.n_mode : (cut + 1) * sz.n_mode] for cut in range(sz.cuts)]
     for cut in range(sz.cuts):
-        for step in sorted(range(1, sz.n_mode), key=lambda each: (each & -each, each), reverse=True):
+        for step in range(sz.n_mode - 1, 0, -1):
             pairs = [(z, partner(z, step, sz.n_mode)) for z in range(sz.n_mode)]
             weak[cut][step] = lax.ppermute(weak[cut][step], "mode", pairs)
     terms, ahead = [], []

time: 57.9 us -> 57.8 us (level)
  no operation moved by 1% of the time
where the time goes in v12:
time: 57.8 us; the launch traced here: 57.6 us
  blocking collectives  20.5 us (35%)
  waiting for transfers between devices  13.9 us (24%)
  starting transfers between devices  12 us (21%)
  Pallas kernels  11 us (19%)
    all_to_all x1, blocking collectives, on_device(): lax.all_to_all(spectra, ('mode', 'ex', 'ey'), split_axis=0, concat_axis=0...  20.5 us
    pallas_call x4, Pallas kernels, call(): pl.pallas_call(kernel, out_shape=[jax.ShapeDtypeStruct(shape, jnp.float32...  11 us
    ppermute x3, waiting for transfers between devices, on_device(): weak[cut][step] = lax.ppermute(weak[cut][step], 'mode', pairs)  10 us
    ppermute x7, starting transfers between devices, on_device(): solved[step] = lax.ppermute(solved[step], ('ex', 'ey'), pairs)  6.31 us
    ppermute x3, starting transfers between devices, on_device(): weak[cut][step] = lax.ppermute(weak[cut][step], 'mode', pairs)  5.71 us
    ppermute x7, waiting for transfers between devices, on_device(): solved[step] = lax.ppermute(solved[step], ('ex', 'ey'), pairs)  3.86 us
  transfers between devices with their start and end apart: 10, of which 6 were waited for; matrix products, arithmetic and copies ran while one was open for 0% of the time, Pallas kernels for 0%

profile of v12, /device:TPU:0, one launch (start us, length us, event | category | flops | bytes accessed | tf_op | source)
XLA Modules:
  0.0 57.6 jit_solution(17192847037334787486)
XLA Ops:
  0.0 4.0 %shard_map.127 = (f32[248,128]{1,0:T(8,128)S(1)}, f32[248,128]{1,0:T(8,128)S(1)}, f32[248,128]{1,0:T(8,128)S(1)}, f32[248,128]{1,0:T(8,128)S(1)}) custom-call(f32[1152,64]{1,0:T(8,128)} %bitcast.5, f32[1152,64]{1,0:T(8,128)} %bitcast.6, bf16[1008,432]{1,0:T(8,128)(2,1)} %constant.22.clone.lift_hbm, bf16[2,264,2016]{2,1,0:T(8,128)(2,1)} %constant.23.clone.back_hbm), custom_call_target="tpu_custom_call" | custom-call | flops 1000000000 | bytes 1000000 | tf_op jit(solution)/shard_map/pallas_call | solution.py:585
  4.0 3.1 %collective-permute-start = (f32[248,128]{1,0:T(8,128)S(1)}, f32[248,128]{1,0:T(8,128)S(1)}, u32[]{:S(2)}, u32[]{:S(2)}) collective-permute-start(f32[248,128]{1,0:T(8,128)S(1)} %get-tuple-element.18), channel_id=1, source_target_pairs={{0,8},{8,0},{16,24},{24,16},{1,9},{9,1},{17,25},{25,17},{2,10},{10... | collective-permute-start | bytes 380936 | tf_op jit(solution)/shard_map/ppermute | solution.py:627
  7.1 2.6 %collective-permute-start.1 = (f32[248,128]{1,0:T(8,128)S(1)}, f32[248,128]{1,0:T(8,128)S(1)}, u32[]{:S(2)}, u32[]{:S(2)}) collective-permute-start(f32[248,128]{1,0:T(8,128)S(1)} %get-tuple-element.19), channel_id=1, source_target_pairs={{0,16},{8,24},{16,0},{24,8},{1,17},{9,25},{17,1},{25,9},{2,18},{10... | collective-permute-start | bytes 380936 | tf_op jit(solution)/shard_map/ppermute | solution.py:627
  9.7 2.2 %collective-permute-done.refs_1_ = f32[248,128]{1,0:T(8,128)S(1)} collective-permute-done((f32[248,128]{1,0:T(8,128)S(1)}, f32[248,128]{1,0:T(8,128)S(1)}, u32[]{:S(2)}, u32[]{:S(2)}) %collective-permute-start) | collective-permute-done | bytes 127008 | tf_op jit(solution)/shard_map/ppermute | solution.py:627
  11.9 7.8 %collective-permute-done.1.refs_2_ = f32[248,128]{1,0:T(8,128)S(1)} collective-permute-done((f32[248,128]{1,0:T(8,128)S(1)}, f32[248,128]{1,0:T(8,128)S(1)}, u32[]{:S(2)}, u32[]{:S(2)}) %collective-permute-start.1) | collective-permute-done | bytes 127008 | tf_op jit(solution)/shard_map/ppermute | solution.py:627
  19.7 0.0 copy-start.2
  19.7 0.0 copy-start.3
  19.7 0.0 copy-start.4
  19.7 0.0 copy-start.5
  19.8 0.6 %shard_map.128 = f32[512,256]{1,0:T(8,128)S(1)} custom-call(f32[248,128]{1,0:T(8,128)S(1)} %get-tuple-element.17.refs_0_, f32[248,128]{1,0:T(8,128)S(1)} %collective-permute-done.refs_1_, f32[248,128]{1,0:T(8,128)S(1)} %collective-permute-done.1.refs_2_, f32[248,128]{1,0:T(8,128)S(1)} %collective-permute-done.2.refs_3_, bf16[2,256,256]{2,1,0:T(8,128)(2,1)S(1)} %copy-done.1), custom_call_target="tpu_custom_call" | custom-call | flops 99999997952 | bytes 1000000 | tf_op jit(solution)/shard_map/pallas_call | solution.py:585
  20.4 20.5 %all_to_all.5.refs_0_ = f32[32,16,256]{2,1,0:T(8,128)S(1)} all-to-all(f32[32,16,256]{2,1,0:T(8,128)S(1)} %bitcast.4), channel_id=1, replica_groups=mesh['mode'=4,'ex'=4,'ey'=2] {'mode','ex','ey'}, dimensions={0} | all-to-all | bytes 1048576 | tf_op jit(solution)/shard_map/all_to_all | solution.py:639
  41.0 5.3 %shard_map.129 = (f32[16,1024]{1,0:T(8,128)S(1)}, f32[16,1024]{1,0:T(8,128)S(1)}, f32[16,1024]{1,0:T(8,128)S(1)}, f32[16,1024]{1,0:T(8,128)S(1)}, f32[16,1024]{1...) custom-call(f32[32,16,256]{2,1,0:T(8,128)S(1)} %all_to_all.5.refs_0_, ...), custom_call_target="tpu_custom_call" | custom-call | flops 1000000000 | bytes 1000000 | tf_op jit(solution)/shard_map/pallas_call | solution.py:585
  46.3 0.1 collective-permute-start.3
  46.4 1.3 %collective-permute-start.4 = (f32[16,1024]{1,0:T(8,128)S(1)}, f32[16,1024]{1,0:T(8,128)S(1)}, u32[]{:S(2)}, u32[]{:S(2)}) collective-permute-start(f32[16,1024]{1,0:T(8,128)S(1)} %get-tuple-element.23), channel_id=1, source_target_pairs={{0,2},{1,3},{2,4},{3,5},{4,6},{5,7},{6,0},{7,1},{8,10},{9,11},{10,... | collective-permute-start | bytes 196616 | tf_op jit(solution)/shard_map/ppermute | solution.py:655
  47.7 1.2 %collective-permute-start.5 = (f32[16,1024]{1,0:T(8,128)S(1)}, f32[16,1024]{1,0:T(8,128)S(1)}, u32[]{:S(2)}, u32[]{:S(2)}) collective-permute-start(f32[16,1024]{1,0:T(8,128)S(1)} %get-tuple-element.24), channel_id=1, source_target_pairs={{0,3},{1,2},{2,5},{3,4},{4,7},{5,6},{6,1},{7,0},{8,11},{9,10},{10,... | collective-permute-start | bytes 196616 | tf_op jit(solution)/shard_map/ppermute | solution.py:655
  48.9 0.8 %collective-permute-start.6 = (f32[16,1024]{1,0:T(8,128)S(1)}, f32[16,1024]{1,0:T(8,128)S(1)}, u32[]{:S(2)}, u32[]{:S(2)}) collective-permute-start(f32[16,1024]{1,0:T(8,128)S(1)} %get-tuple-element.25), channel_id=1, source_target_pairs={{0,4},{1,5},{2,6},{3,7},{4,0},{5,1},{6,2},{7,3},{8,12},{9,13},{10,... | collective-permute-start | bytes 196616 | tf_op jit(solution)/shard_map/ppermute | solution.py:655
  49.7 0.9 %collective-permute-start.7 = (f32[16,1024]{1,0:T(8,128)S(1)}, f32[16,1024]{1,0:T(8,128)S(1)}, u32[]{:S(2)}, u32[]{:S(2)}) collective-permute-start(f32[16,1024]{1,0:T(8,128)S(1)} %get-tuple-element.26), channel_id=1, source_target_pairs={{0,5},{1,4},{2,7},{3,6},{4,1},{5,0},{6,3},{7,2},{8,13},{9,12},{10,... | collective-permute-start | bytes 196616 | tf_op jit(solution)/shard_map/ppermute | solution.py:655
  50.6 1.5 %collective-permute-start.8 = (f32[16,1024]{1,0:T(8,128)S(1)}, f32[16,1024]{1,0:T(8,128)S(1)}, u32[]{:S(2)}, u32[]{:S(2)}) collective-permute-start(f32[16,1024]{1,0:T(8,128)S(1)} %get-tuple-element.27), channel_id=1, source_target_pairs={{0,6},{1,7},{2,0},{3,1},{4,2},{5,3},{6,4},{7,5},{8,14},{9,15},{10,... | collective-permute-start | bytes 196616 | tf_op jit(solution)/shard_map/ppermute | solution.py:655
  52.1 0.5 collective-permute-start.9
  52.6 0.4 collective-permute-done.5.refs_3_
  53.0 1.6 %collective-permute-done.6.refs_4_ = f32[16,1024]{1,0:T(8,128)S(1)} collective-permute-done((f32[16,1024]{1,0:T(8,128)S(1)}, f32[16,1024]{1,0:T(8,128)S(1)}, u32[]{:S(2)}, u32[]{:S(2)}) %collective-permute-start.6) | collective-permute-done | bytes 65568 | tf_op jit(solution)/shard_map/ppermute | solution.py:655
  54.6 1.3 %collective-permute-done.7.refs_5_ = f32[16,1024]{1,0:T(8,128)S(1)} collective-permute-done((f32[16,1024]{1,0:T(8,128)S(1)}, f32[16,1024]{1,0:T(8,128)S(1)}, u32[]{:S(2)}, u32[]{:S(2)}) %collective-permute-start.7) | collective-permute-done | bytes 65568 | tf_op jit(solution)/shard_map/ppermute | solution.py:655
  55.9 0.6 collective-permute-done.9.refs_7_
  56.5 1.1 %shard_map.130 = f32[1152,128]{1,0:T(8,128)} custom-call(f32[16,1024]{1,0:T(8,128)S(1)} %get-tuple-element.21.refs_0_, f32[16,1024]{1,0:T(8,128)S(1)} %collective-permute-done.3.refs_1_, f32[16,1024]{1,0:T(8,128)S(1)} %collective-permute-done.4.refs_2_, f32[16,1024]{1,0:T(8,128)S(1)} %collective-permute-done.5.refs_3_, ...), custom_call_target="tpu_custom_call" | custom-call | flops 1000000000 | bytes 1000000 | tf_op jit(solution)/shard_map/pallas_call | solution.py:585
  (19 shorter events, 0.0 us)
Async XLA Ops:
  0.0 19.7 %copy-start.1 = (bf16[2,256,256]{2,1,0:T(8,128)(2,1)S(1)}, bf16[2,256,256]{2,1,0:T(8,128)(2,1)}, u32[]{:S(2)}) copy-start(bf16[2,256,256]{2,1,0:T(8,128)(2,1)} %constant.24.clone.refs_4_) | copy-start | bytes 786436
  4.0 7.9 %collective-permute-start = (f32[248,128]{1,0:T(8,128)S(1)}, f32[248,128]{1,0:T(8,128)S(1)}, u32[]{:S(2)}, u32[]{:S(2)}) collective-permute-start(f32[248,128]{1,0:T(8,128)S(1)} %get-tuple-element.18), channel_id=1, source_target_pairs={{0,8},{8,0},{16,24},{24,16},{1,9},{9,1},{17,25},{25,17},{2,10},{10... | collective-permute-start | bytes 380936 | tf_op jit(solution)/shard_map/ppermute | solution.py:627
  7.1 12.6 %collective-permute-start.1 = (f32[248,128]{1,0:T(8,128)S(1)}, f32[248,128]{1,0:T(8,128)S(1)}, u32[]{:S(2)}, u32[]{:S(2)}) collective-permute-start(f32[248,128]{1,0:T(8,128)S(1)} %get-tuple-element.19), channel_id=1, source_target_pairs={{0,16},{8,24},{16,0},{24,8},{1,17},{9,25},{17,1},{25,9},{2,18},{10... | collective-permute-start | bytes 380936 | tf_op jit(solution)/shard_map/ppermute | solution.py:627
  9.7 10.0 %collective-permute-start.2 = (f32[248,128]{1,0:T(8,128)S(1)}, f32[248,128]{1,0:T(8,128)S(1)}, u32[]{:S(2)}, u32[]{:S(2)}) collective-permute-start(f32[248,128]{1,0:T(8,128)S(1)} %get-tuple-element.20), channel_id=1, source_target_pairs={{0,24},{8,16},{16,8},{24,0},{1,25},{9,17},{17,9},{25,1},{2,26},{10... | collective-permute-start | bytes 380936 | tf_op jit(solution)/shard_map/ppermute | solution.py:627
  19.7 21.3 %copy-start = (bf16[448,448]{1,0:T(8,128)(2,1)S(1)}, bf16[448,448]{1,0:T(8,128)(2,1)}, u32[]{:S(2)}) copy-start(bf16[448,448]{1,0:T(8,128)(2,1)} %constant.28.clone.refs_4_) | copy-start | bytes 1204228
  19.7 21.2 %copy-start.2 = (bf16[448,192]{1,0:T(8,128)(2,1)S(1)}, bf16[448,192]{1,0:T(8,128)(2,1)}, u32[]{:S(2)}) copy-start(bf16[448,192]{1,0:T(8,128)(2,1)} %constant.26.clone.refs_2_) | copy-start | bytes 516100
  19.7 21.2 %copy-start.3 = (bf16[384,224]{1,0:T(8,128)(2,1)S(1)}, bf16[384,224]{1,0:T(8,128)(2,1)}, u32[]{:S(2)}) copy-start(bf16[384,224]{1,0:T(8,128)(2,1)} %constant.30.clone.refs_6_) | copy-start | bytes 516100
  19.7 21.2 %copy-start.4 = (bf16[384,256]{1,0:T(8,128)(2,1)S(1)}, bf16[384,256]{1,0:T(8,128)(2,1)}, u32[]{:S(2)}) copy-start(bf16[384,256]{1,0:T(8,128)(2,1)} %constant.27.clone.refs_3_) | copy-start | bytes 589828
  19.7 21.2 %copy-start.5 = (bf16[256,256]{1,0:T(8,128)(2,1)S(1)}, bf16[256,256]{1,0:T(8,128)(2,1)}, u32[]{:S(2)}) copy-start(bf16[256,256]{1,0:T(8,128)(2,1)} %constant.29.clone.refs_5_) | copy-start | bytes 393220
  19.7 21.2 %copy-start.6 = (bf16[256,256]{1,0:T(8,128)(2,1)S(1)}, bf16[256,256]{1,0:T(8,128)(2,1)}, u32[]{:S(2)}) copy-start(bf16[256,256]{1,0:T(8,128)(2,1)} %constant.25.clone.refs_1_) | copy-start | bytes 393220
  19.8 21.2 %copy-start.7 = (f32[224,128]{1,0:T(8,128)S(1)}, f32[224,128]{1,0:T(8,128)}, u32[]{:S(2)}) copy-start(f32[224,128]{1,0:T(8,128)} %constant.31.clone.refs_7_) | copy-start | bytes 344068
  19.8 21.2 %copy-start.8 = (f32[1,128]{1,0:T(1,128)S(1)}, f32[1,128]{1,0:T(1,128)}, u32[]{:S(2)}) copy-start(f32[1,128]{1,0:T(1,128)} %constant.32.clone.refs_8_) | copy-start | bytes 1540
  46.3 4.3 %collective-permute-start.3 = (f32[16,1024]{1,0:T(8,128)S(1)}, f32[16,1024]{1,0:T(8,128)S(1)}, u32[]{:S(2)}, u32[]{:S(2)}) collective-permute-start(f32[16,1024]{1,0:T(8,128)S(1)} %get-tuple-element.22), channel_id=1, source_target_pairs={{0,1},{1,0},{2,3},{3,2},{4,5},{5,4},{6,7},{7,6},{8,9},{9,8},{10,11... | collective-permute-start | bytes 196616 | tf_op jit(solution)/shard_map/ppermute | solution.py:655
  46.4 5.7 %collective-permute-start.4 = (f32[16,1024]{1,0:T(8,128)S(1)}, f32[16,1024]{1,0:T(8,128)S(1)}, u32[]{:S(2)}, u32[]{:S(2)}) collective-permute-start(f32[16,1024]{1,0:T(8,128)S(1)} %get-tuple-element.23), channel_id=1, source_target_pairs={{0,2},{1,3},{2,4},{3,5},{4,6},{5,7},{6,0},{7,1},{8,10},{9,11},{10,... | collective-permute-start | bytes 196616 | tf_op jit(solution)/shard_map/ppermute | solution.py:655
  47.7 5.3 %collective-permute-start.5 = (f32[16,1024]{1,0:T(8,128)S(1)}, f32[16,1024]{1,0:T(8,128)S(1)}, u32[]{:S(2)}, u32[]{:S(2)}) collective-permute-start(f32[16,1024]{1,0:T(8,128)S(1)} %get-tuple-element.24), channel_id=1, source_target_pairs={{0,3},{1,2},{2,5},{3,4},{4,7},{5,6},{6,1},{7,0},{8,11},{9,10},{10,... | collective-permute-start | bytes 196616 | tf_op jit(solution)/shard_map/ppermute | solution.py:655
  48.9 5.7 %collective-permute-start.6 = (f32[16,1024]{1,0:T(8,128)S(1)}, f32[16,1024]{1,0:T(8,128)S(1)}, u32[]{:S(2)}, u32[]{:S(2)}) collective-permute-start(f32[16,1024]{1,0:T(8,128)S(1)} %get-tuple-element.25), channel_id=1, source_target_pairs={{0,4},{1,5},{2,6},{3,7},{4,0},{5,1},{6,2},{7,3},{8,12},{9,13},{10,... | collective-permute-start | bytes 196616 | tf_op jit(solution)/shard_map/ppermute | solution.py:655
  49.7 6.2 %collective-permute-start.7 = (f32[16,1024]{1,0:T(8,128)S(1)}, f32[16,1024]{1,0:T(8,128)S(1)}, u32[]{:S(2)}, u32[]{:S(2)}) collective-permute-start(f32[16,1024]{1,0:T(8,128)S(1)} %get-tuple-element.26), channel_id=1, source_target_pairs={{0,5},{1,4},{2,7},{3,6},{4,1},{5,0},{6,3},{7,2},{8,13},{9,12},{10,... | collective-permute-start | bytes 196616 | tf_op jit(solution)/shard_map/ppermute | solution.py:655
  50.6 5.3 %collective-permute-start.8 = (f32[16,1024]{1,0:T(8,128)S(1)}, f32[16,1024]{1,0:T(8,128)S(1)}, u32[]{:S(2)}, u32[]{:S(2)}) collective-permute-start(f32[16,1024]{1,0:T(8,128)S(1)} %get-tuple-element.27), channel_id=1, source_target_pairs={{0,6},{1,7},{2,0},{3,1},{4,2},{5,3},{6,4},{7,5},{8,14},{9,15},{10,... | collective-permute-start | bytes 196616 | tf_op jit(solution)/shard_map/ppermute | solution.py:655
  52.1 4.4 %collective-permute-start.9 = (f32[16,1024]{1,0:T(8,128)S(1)}, f32[16,1024]{1,0:T(8,128)S(1)}, u32[]{:S(2)}, u32[]{:S(2)}) collective-permute-start(f32[16,1024]{1,0:T(8,128)S(1)} %get-tuple-element.28), channel_id=1, source_target_pairs={{0,7},{1,6},{2,1},{3,0},{4,3},{5,2},{6,5},{7,4},{8,15},{9,14},{10,... | collective-permute-start | bytes 196616 | tf_op jit(solution)/shard_map/ppermute | solution.py:655

commit v13 on v12

--- a/solution.py
+++ b/solution.py
@@ -350,7 +350,10 @@
             (
                 (stream_hbm, stream_ref),
                 (normal_hbm, normal_ref),
-                (lift_hbm, lift_ref),
+                *(
+                    (lift_hbm.at[pl.ds(part * sz.fine, sz.fine)], lift_ref.at[pl.ds(part * sz.fine, sz.fine)])
+                    for part in range(3)
+                ),
                 (back_hbm.at[place], back_ref),
             )
         )
@@ -367,8 +370,9 @@
     full = sz.cut_x * sz.block_y // 8 * 8
     total_ref[pl.ds(full, sz.cut_nodes - full), :] = jnp.zeros((sz.cut_nodes - full, LANES), jnp.float32)
     spot = lax.axis_index("mode")
-    for copy in fetched[:3]:
+    for copy in fetched[:2]:
         copy.wait()
+    waiting = fetched[2:5]
     for cut in range(sz.cuts):
         products = []
         for e in range(cut * sz.cut_elems, (cut + 1) * sz.cut_elems):
@@ -380,11 +384,15 @@
                 ],
                 1,
             )
-            values = dot(lift_ref[...], below(speeds))
+            spread = below(speeds)
+            values = []
+            for part in range(3):
+                if waiting:
+                    waiting.pop(0).wait()
+                values.append(dot(lift_ref[pl.ds(part * fine, fine), :], spread))
             highs, lows = [], []
             for f in range(rows):
-                mine = values[:, f * LANES : (f + 1) * LANES]
-                both, slope_x, slope_y = mine[:fine], mine[fine : 2 * fine], mine[2 * fine :]
+                both, slope_x, slope_y = (part[:, f * LANES : (f + 1) * LANES] for part in values)
                 turned = pltpu.roll(both, sz.planes, 1)
                 stream = jnp.where(half, both, turned)
                 normal = jnp.where(half, turned, both)
@@ -393,7 +401,7 @@
                 lows.append(low)
             products.append(jnp.concatenate(highs + lows + highs, 0))
         if cut == 0:
-            fetched[3].wait()
+            fetched[5].wait()
         weak = dot(back_ref[...], jnp.concatenate(products, 1))
         carry = None
         for e in range(sz.cut_elems):
@@ -616,7 +624,7 @@
             (flat, sz.planes),
             pltpu.VMEM(tables["lift"].shape, jnp.bfloat16),
             pltpu.VMEM(tables["back"].shape[1:], jnp.bfloat16),
-            pltpu.SemaphoreType.DMA((4,)),
+            pltpu.SemaphoreType.DMA((6,)),
         ],
         pltpu.HBM,
     )

time: 57.8 us -> 57.9 us (level)
  no operation moved by 1% of the time
where the time goes in v13:
time: 57.9 us; the launch traced here: 57.7 us
  blocking collectives  20.5 us (35%)
  waiting for transfers between devices  13.9 us (24%)
  starting transfers between devices  12 us (21%)
  Pallas kernels  11.1 us (19%)
    all_to_all x1, blocking collectives, on_device(): lax.all_to_all(spectra, ('mode', 'ex', 'ey'), split_axis=0, concat_axis=0...  20.5 us
    pallas_call x4, Pallas kernels, call(): pl.pallas_call(kernel, out_shape=[jax.ShapeDtypeStruct(shape, jnp.float32...  11.1 us
    ppermute x3, waiting for transfers between devices, on_device(): weak[cut][step] = lax.ppermute(weak[cut][step], 'mode', pairs)  10 us
    ppermute x7, starting transfers between devices, on_device(): solved[step] = lax.ppermute(solved[step], ('ex', 'ey'), pairs)  6.31 us
    ppermute x3, starting transfers between devices, on_device(): weak[cut][step] = lax.ppermute(weak[cut][step], 'mode', pairs)  5.7 us
    ppermute x7, waiting for transfers between devices, on_device(): solved[step] = lax.ppermute(solved[step], ('ex', 'ey'), pairs)  3.86 us
  transfers between devices with their start and end apart: 10, of which 6 were waited for; matrix products, arithmetic and copies ran while one was open for 0% of the time, Pallas kernels for 0%

profile of v13, /device:TPU:0, one launch (start us, length us, event | category | flops | bytes accessed | tf_op | source)
XLA Modules:
  0.0 57.7 jit_solution(16617183128861829075)
XLA Ops:
  0.0 4.1 %shard_map.127 = (f32[248,128]{1,0:T(8,128)S(1)}, f32[248,128]{1,0:T(8,128)S(1)}, f32[248,128]{1,0:T(8,128)S(1)}, f32[248,128]{1,0:T(8,128)S(1)}) custom-call(f32[1152,64]{1,0:T(8,128)} %bitcast.5, f32[1152,64]{1,0:T(8,128)} %bitcast.6, bf16[1008,432]{1,0:T(8,128)(2,1)} %constant.22.clone.lift_hbm, bf16[2,264,2016]{2,1,0:T(8,128)(2,1)} %constant.23.clone.back_hbm), custom_call_target="tpu_custom_call" | custom-call | flops 1000000000 | bytes 1000000 | tf_op jit(solution)/shard_map/pallas_call | solution.py:593
  4.1 3.1 %collective-permute-start = (f32[248,128]{1,0:T(8,128)S(1)}, f32[248,128]{1,0:T(8,128)S(1)}, u32[]{:S(2)}, u32[]{:S(2)}) collective-permute-start(f32[248,128]{1,0:T(8,128)S(1)} %get-tuple-element.18), channel_id=1, source_target_pairs={{0,8},{8,0},{16,24},{24,16},{1,9},{9,1},{17,25},{25,17},{2,10},{10... | collective-permute-start | bytes 380936 | tf_op jit(solution)/shard_map/ppermute | solution.py:635
  7.2 2.6 %collective-permute-start.1 = (f32[248,128]{1,0:T(8,128)S(1)}, f32[248,128]{1,0:T(8,128)S(1)}, u32[]{:S(2)}, u32[]{:S(2)}) collective-permute-start(f32[248,128]{1,0:T(8,128)S(1)} %get-tuple-element.19), channel_id=1, source_target_pairs={{0,16},{8,24},{16,0},{24,8},{1,17},{9,25},{17,1},{25,9},{2,18},{10... | collective-permute-start | bytes 380936 | tf_op jit(solution)/shard_map/ppermute | solution.py:635
  9.8 2.2 %collective-permute-done.refs_1_ = f32[248,128]{1,0:T(8,128)S(1)} collective-permute-done((f32[248,128]{1,0:T(8,128)S(1)}, f32[248,128]{1,0:T(8,128)S(1)}, u32[]{:S(2)}, u32[]{:S(2)}) %collective-permute-start) | collective-permute-done | bytes 127008 | tf_op jit(solution)/shard_map/ppermute | solution.py:635
  12.0 7.8 %collective-permute-done.1.refs_2_ = f32[248,128]{1,0:T(8,128)S(1)} collective-permute-done((f32[248,128]{1,0:T(8,128)S(1)}, f32[248,128]{1,0:T(8,128)S(1)}, u32[]{:S(2)}, u32[]{:S(2)}) %collective-permute-start.1) | collective-permute-done | bytes 127008 | tf_op jit(solution)/shard_map/ppermute | solution.py:635
  19.8 0.0 copy-start.2
  19.8 0.0 copy-start.3
  19.8 0.0 copy-start.4
  19.9 0.0 copy-start.6
  19.9 0.6 %shard_map.128 = f32[512,256]{1,0:T(8,128)S(1)} custom-call(f32[248,128]{1,0:T(8,128)S(1)} %get-tuple-element.17.refs_0_, f32[248,128]{1,0:T(8,128)S(1)} %collective-permute-done.refs_1_, f32[248,128]{1,0:T(8,128)S(1)} %collective-permute-done.1.refs_2_, f32[248,128]{1,0:T(8,128)S(1)} %collective-permute-done.2.refs_3_, bf16[2,256,256]{2,1,0:T(8,128)(2,1)S(1)} %copy-done.1), custom_call_target="tpu_custom_call" | custom-call | flops 99999997952 | bytes 1000000 | tf_op jit(solution)/shard_map/pallas_call | solution.py:593
  20.5 20.5 %all_to_all.5.refs_0_ = f32[32,16,256]{2,1,0:T(8,128)S(1)} all-to-all(f32[32,16,256]{2,1,0:T(8,128)S(1)} %bitcast.4), channel_id=1, replica_groups=mesh['mode'=4,'ex'=4,'ey'=2] {'mode','ex','ey'}, dimensions={0} | all-to-all | bytes 1048576 | tf_op jit(solution)/shard_map/all_to_all | solution.py:647
  41.1 5.3 %shard_map.129 = (f32[16,1024]{1,0:T(8,128)S(1)}, f32[16,1024]{1,0:T(8,128)S(1)}, f32[16,1024]{1,0:T(8,128)S(1)}, f32[16,1024]{1,0:T(8,128)S(1)}, f32[16,1024]{1...) custom-call(f32[32,16,256]{2,1,0:T(8,128)S(1)} %all_to_all.5.refs_0_, ...), custom_call_target="tpu_custom_call" | custom-call | flops 1000000000 | bytes 1000000 | tf_op jit(solution)/shard_map/pallas_call | solution.py:593
  46.4 0.1 collective-permute-start.3
  46.5 1.3 %collective-permute-start.4 = (f32[16,1024]{1,0:T(8,128)S(1)}, f32[16,1024]{1,0:T(8,128)S(1)}, u32[]{:S(2)}, u32[]{:S(2)}) collective-permute-start(f32[16,1024]{1,0:T(8,128)S(1)} %get-tuple-element.23), channel_id=1, source_target_pairs={{0,2},{1,3},{2,4},{3,5},{4,6},{5,7},{6,0},{7,1},{8,10},{9,11},{10,... | collective-permute-start | bytes 196616 | tf_op jit(solution)/shard_map/ppermute | solution.py:663
  47.8 1.2 %collective-permute-start.5 = (f32[16,1024]{1,0:T(8,128)S(1)}, f32[16,1024]{1,0:T(8,128)S(1)}, u32[]{:S(2)}, u32[]{:S(2)}) collective-permute-start(f32[16,1024]{1,0:T(8,128)S(1)} %get-tuple-element.24), channel_id=1, source_target_pairs={{0,3},{1,2},{2,5},{3,4},{4,7},{5,6},{6,1},{7,0},{8,11},{9,10},{10,... | collective-permute-start | bytes 196616 | tf_op jit(solution)/shard_map/ppermute | solution.py:663
  49.0 0.8 %collective-permute-start.6 = (f32[16,1024]{1,0:T(8,128)S(1)}, f32[16,1024]{1,0:T(8,128)S(1)}, u32[]{:S(2)}, u32[]{:S(2)}) collective-permute-start(f32[16,1024]{1,0:T(8,128)S(1)} %get-tuple-element.25), channel_id=1, source_target_pairs={{0,4},{1,5},{2,6},{3,7},{4,0},{5,1},{6,2},{7,3},{8,12},{9,13},{10,... | collective-permute-start | bytes 196616 | tf_op jit(solution)/shard_map/ppermute | solution.py:663
  49.8 0.9 %collective-permute-start.7 = (f32[16,1024]{1,0:T(8,128)S(1)}, f32[16,1024]{1,0:T(8,128)S(1)}, u32[]{:S(2)}, u32[]{:S(2)}) collective-permute-start(f32[16,1024]{1,0:T(8,128)S(1)} %get-tuple-element.26), channel_id=1, source_target_pairs={{0,5},{1,4},{2,7},{3,6},{4,1},{5,0},{6,3},{7,2},{8,13},{9,12},{10,... | collective-permute-start | bytes 196616 | tf_op jit(solution)/shard_map/ppermute | solution.py:663
  50.7 1.5 %collective-permute-start.8 = (f32[16,1024]{1,0:T(8,128)S(1)}, f32[16,1024]{1,0:T(8,128)S(1)}, u32[]{:S(2)}, u32[]{:S(2)}) collective-permute-start(f32[16,1024]{1,0:T(8,128)S(1)} %get-tuple-element.27), channel_id=1, source_target_pairs={{0,6},{1,7},{2,0},{3,1},{4,2},{5,3},{6,4},{7,5},{8,14},{9,15},{10,... | collective-permute-start | bytes 196616 | tf_op jit(solution)/shard_map/ppermute | solution.py:663
  52.2 0.5 collective-permute-start.9
  52.7 0.4 collective-permute-done.5.refs_3_
  53.1 1.6 %collective-permute-done.6.refs_4_ = f32[16,1024]{1,0:T(8,128)S(1)} collective-permute-done((f32[16,1024]{1,0:T(8,128)S(1)}, f32[16,1024]{1,0:T(8,128)S(1)}, u32[]{:S(2)}, u32[]{:S(2)}) %collective-permute-start.6) | collective-permute-done | bytes 65568 | tf_op jit(solution)/shard_map/ppermute | solution.py:663
  54.7 1.3 %collective-permute-done.7.refs_5_ = f32[16,1024]{1,0:T(8,128)S(1)} collective-permute-done((f32[16,1024]{1,0:T(8,128)S(1)}, f32[16,1024]{1,0:T(8,128)S(1)}, u32[]{:S(2)}, u32[]{:S(2)}) %collective-permute-start.7) | collective-permute-done | bytes 65568 | tf_op jit(solution)/shard_map/ppermute | solution.py:663
  56.0 0.6 collective-permute-done.9.refs_7_
  56.6 1.1 %shard_map.130 = f32[1152,128]{1,0:T(8,128)} custom-call(f32[16,1024]{1,0:T(8,128)S(1)} %get-tuple-element.21.refs_0_, f32[16,1024]{1,0:T(8,128)S(1)} %collective-permute-done.3.refs_1_, f32[16,1024]{1,0:T(8,128)S(1)} %collective-permute-done.4.refs_2_, f32[16,1024]{1,0:T(8,128)S(1)} %collective-permute-done.5.refs_3_, ...), custom_call_target="tpu_custom_call" | custom-call | flops 1000000000 | bytes 1000000 | tf_op jit(solution)/shard_map/pallas_call | solution.py:593
  (19 shorter events, 0.0 us)
Async XLA Ops:
  0.0 19.8 %copy-start.1 = (bf16[2,256,256]{2,1,0:T(8,128)(2,1)S(1)}, bf16[2,256,256]{2,1,0:T(8,128)(2,1)}, u32[]{:S(2)}) copy-start(bf16[2,256,256]{2,1,0:T(8,128)(2,1)} %constant.24.clone.refs_4_) | copy-start | bytes 786436
  4.1 7.9 %collective-permute-start = (f32[248,128]{1,0:T(8,128)S(1)}, f32[248,128]{1,0:T(8,128)S(1)}, u32[]{:S(2)}, u32[]{:S(2)}) collective-permute-start(f32[248,128]{1,0:T(8,128)S(1)} %get-tuple-element.18), channel_id=1, source_target_pairs={{0,8},{8,0},{16,24},{24,16},{1,9},{9,1},{17,25},{25,17},{2,10},{10... | collective-permute-start | bytes 380936 | tf_op jit(solution)/shard_map/ppermute | solution.py:635
  7.2 12.6 %collective-permute-start.1 = (f32[248,128]{1,0:T(8,128)S(1)}, f32[248,128]{1,0:T(8,128)S(1)}, u32[]{:S(2)}, u32[]{:S(2)}) collective-permute-start(f32[248,128]{1,0:T(8,128)S(1)} %get-tuple-element.19), channel_id=1, source_target_pairs={{0,16},{8,24},{16,0},{24,8},{1,17},{9,25},{17,1},{25,9},{2,18},{10... | collective-permute-start | bytes 380936 | tf_op jit(solution)/shard_map/ppermute | solution.py:635
  9.8 10.0 %collective-permute-start.2 = (f32[248,128]{1,0:T(8,128)S(1)}, f32[248,128]{1,0:T(8,128)S(1)}, u32[]{:S(2)}, u32[]{:S(2)}) collective-permute-start(f32[248,128]{1,0:T(8,128)S(1)} %get-tuple-element.20), channel_id=1, source_target_pairs={{0,24},{8,16},{16,8},{24,0},{1,25},{9,17},{17,9},{25,1},{2,26},{10... | collective-permute-start | bytes 380936 | tf_op jit(solution)/shard_map/ppermute | solution.py:635
  19.8 21.3 %copy-start = (bf16[448,448]{1,0:T(8,128)(2,1)S(1)}, bf16[448,448]{1,0:T(8,128)(2,1)}, u32[]{:S(2)}) copy-start(bf16[448,448]{1,0:T(8,128)(2,1)} %constant.28.clone.refs_4_) | copy-start | bytes 1204228
  19.8 21.2 %copy-start.2 = (bf16[448,192]{1,0:T(8,128)(2,1)S(1)}, bf16[448,192]{1,0:T(8,128)(2,1)}, u32[]{:S(2)}) copy-start(bf16[448,192]{1,0:T(8,128)(2,1)} %constant.26.clone.refs_2_) | copy-start | bytes 516100
  19.8 21.2 %copy-start.3 = (bf16[384,224]{1,0:T(8,128)(2,1)S(1)}, bf16[384,224]{1,0:T(8,128)(2,1)}, u32[]{:S(2)}) copy-start(bf16[384,224]{1,0:T(8,128)(2,1)} %constant.30.clone.refs_6_) | copy-start | bytes 516100
  19.8 21.2 %copy-start.4 = (bf16[384,256]{1,0:T(8,128)(2,1)S(1)}, bf16[384,256]{1,0:T(8,128)(2,1)}, u32[]{:S(2)}) copy-start(bf16[384,256]{1,0:T(8,128)(2,1)} %constant.27.clone.refs_3_) | copy-start | bytes 589828
  19.8 21.2 %copy-start.5 = (bf16[256,256]{1,0:T(8,128)(2,1)S(1)}, bf16[256,256]{1,0:T(8,128)(2,1)}, u32[]{:S(2)}) copy-start(bf16[256,256]{1,0:T(8,128)(2,1)} %constant.29.clone.refs_5_) | copy-start | bytes 393220
  19.9 21.2 %copy-start.6 = (bf16[256,256]{1,0:T(8,128)(2,1)S(1)}, bf16[256,256]{1,0:T(8,128)(2,1)}, u32[]{:S(2)}) copy-start(bf16[256,256]{1,0:T(8,128)(2,1)} %constant.25.clone.refs_1_) | copy-start | bytes 393220
  19.9 21.2 %copy-start.7 = (f32[224,128]{1,0:T(8,128)S(1)}, f32[224,128]{1,0:T(8,128)}, u32[]{:S(2)}) copy-start(f32[224,128]{1,0:T(8,128)} %constant.31.clone.refs_7_) | copy-start | bytes 344068
  19.9 21.2 %copy-start.8 = (f32[1,128]{1,0:T(1,128)S(1)}, f32[1,128]{1,0:T(1,128)}, u32[]{:S(2)}) copy-start(f32[1,128]{1,0:T(1,128)} %constant.32.clone.refs_8_) | copy-start | bytes 1540
  46.4 4.3 %collective-permute-start.3 = (f32[16,1024]{1,0:T(8,128)S(1)}, f32[16,1024]{1,0:T(8,128)S(1)}, u32[]{:S(2)}, u32[]{:S(2)}) collective-permute-start(f32[16,1024]{1,0:T(8,128)S(1)} %get-tuple-element.22), channel_id=1, source_target_pairs={{0,1},{1,0},{2,3},{3,2},{4,5},{5,4},{6,7},{7,6},{8,9},{9,8},{10,11... | collective-permute-start | bytes 196616 | tf_op jit(solution)/shard_map/ppermute | solution.py:663
  46.5 5.7 %collective-permute-start.4 = (f32[16,1024]{1,0:T(8,128)S(1)}, f32[16,1024]{1,0:T(8,128)S(1)}, u32[]{:S(2)}, u32[]{:S(2)}) collective-permute-start(f32[16,1024]{1,0:T(8,128)S(1)} %get-tuple-element.23), channel_id=1, source_target_pairs={{0,2},{1,3},{2,4},{3,5},{4,6},{5,7},{6,0},{7,1},{8,10},{9,11},{10,... | collective-permute-start | bytes 196616 | tf_op jit(solution)/shard_map/ppermute | solution.py:663
  47.8 5.3 %collective-permute-start.5 = (f32[16,1024]{1,0:T(8,128)S(1)}, f32[16,1024]{1,0:T(8,128)S(1)}, u32[]{:S(2)}, u32[]{:S(2)}) collective-permute-start(f32[16,1024]{1,0:T(8,128)S(1)} %get-tuple-element.24), channel_id=1, source_target_pairs={{0,3},{1,2},{2,5},{3,4},{4,7},{5,6},{6,1},{7,0},{8,11},{9,10},{10,... | collective-permute-start | bytes 196616 | tf_op jit(solution)/shard_map/ppermute | solution.py:663
  49.0 5.7 %collective-permute-start.6 = (f32[16,1024]{1,0:T(8,128)S(1)}, f32[16,1024]{1,0:T(8,128)S(1)}, u32[]{:S(2)}, u32[]{:S(2)}) collective-permute-start(f32[16,1024]{1,0:T(8,128)S(1)} %get-tuple-element.25), channel_id=1, source_target_pairs={{0,4},{1,5},{2,6},{3,7},{4,0},{5,1},{6,2},{7,3},{8,12},{9,13},{10,... | collective-permute-start | bytes 196616 | tf_op jit(solution)/shard_map/ppermute | solution.py:663
  49.8 6.2 %collective-permute-start.7 = (f32[16,1024]{1,0:T(8,128)S(1)}, f32[16,1024]{1,0:T(8,128)S(1)}, u32[]{:S(2)}, u32[]{:S(2)}) collective-permute-start(f32[16,1024]{1,0:T(8,128)S(1)} %get-tuple-element.26), channel_id=1, source_target_pairs={{0,5},{1,4},{2,7},{3,6},{4,1},{5,0},{6,3},{7,2},{8,13},{9,12},{10,... | collective-permute-start | bytes 196616 | tf_op jit(solution)/shard_map/ppermute | solution.py:663
  50.7 5.3 %collective-permute-start.8 = (f32[16,1024]{1,0:T(8,128)S(1)}, f32[16,1024]{1,0:T(8,128)S(1)}, u32[]{:S(2)}, u32[]{:S(2)}) collective-permute-start(f32[16,1024]{1,0:T(8,128)S(1)} %get-tuple-element.27), channel_id=1, source_target_pairs={{0,6},{1,7},{2,0},{3,1},{4,2},{5,3},{6,4},{7,5},{8,14},{9,15},{10,... | collective-permute-start | bytes 196616 | tf_op jit(solution)/shard_map/ppermute | solution.py:663
  52.2 4.4 %collective-permute-start.9 = (f32[16,1024]{1,0:T(8,128)S(1)}, f32[16,1024]{1,0:T(8,128)S(1)}, u32[]{:S(2)}, u32[]{:S(2)}) collective-permute-start(f32[16,1024]{1,0:T(8,128)S(1)} %get-tuple-element.28), channel_id=1, source_target_pairs={{0,7},{1,6},{2,1},{3,0},{4,3},{5,2},{6,5},{7,4},{8,15},{9,14},{10,... | collective-permute-start | bytes 196616 | tf_op jit(solution)/shard_map/ppermute | solution.py:663

commit v14 on v10

--- a/solution.py
+++ b/solution.py
@@ -553,7 +553,7 @@
 
 
 def spread_kernel(sz, *refs):
-    solved_refs, (out_ref, stacked_ref, turned_ref) = refs[:-3], refs[-3:]
+    solved_refs, (out_ref, stacked_ref, turned_ref, made_ref, left) = refs[:-5], refs[-5:]
     place, spot = lax.axis_index("ey"), lax.axis_index("ex")
     for step, solved_ref in enumerate(solved_refs):
         shift, turn = step // sz.n_ey, step % sz.n_ey
@@ -561,35 +561,42 @@
         stacked_ref[pl.ds(pl.multiple_of(source * sz.own, PARTS), sz.own), :] = solved_ref[...]
     turned_ref[...] = stacked_ref[...].T
     spots = sz.elems * sz.rows
-    for e in range(sz.elems):
-        for f in range(sz.rows):
-            for a in range(sz.nodes):
+    slab = sz.nodes * spots
+    blank = jnp.zeros((sz.elems, LANES), jnp.float32)
+    group = 3 if sz.nodes % 3 == 0 else 1
+    copies = []
+    for a in range(sz.nodes):
+        for e in range(sz.elems):
+            for f in range(sz.rows):
                 start = sz.block_y * (sz.order * e + a) + sz.order * f
-                out_ref[pl.ds(a * sz.nodes * spots + e * sz.rows + f, sz.nodes, stride=spots), :] = turned_ref[
+                made_ref[pl.ds(a * slab + e * sz.rows + f, sz.nodes, stride=spots), :] = turned_ref[
                     pl.ds(start, sz.nodes), :
                 ]
-    blank = jnp.zeros((sz.elems, LANES), jnp.float32)
-
-    @pl.when(place == 0)
-    def _():
-        for a in range(sz.nodes):
-            out_ref[pl.ds(a * sz.nodes * spots, sz.elems, stride=sz.rows), :] = blank
-
-    @pl.when(place == sz.n_ey - 1)
-    def _():
-        for a in range(sz.nodes):
-            first = ((a + 1) * sz.nodes - 1) * spots + sz.rows - 1
-            out_ref[pl.ds(first, sz.elems, stride=sz.rows), :] = blank
-
-
-def call(kernel, shapes, operands, scratch=(), spaces=pltpu.VMEM, limit=16, flops=10**9):
+
+        @pl.when(place == 0)
+        def _(a=a):
+            made_ref[pl.ds(a * slab, sz.elems, stride=sz.rows), :] = blank
+
+        @pl.when(place == sz.n_ey - 1)
+        def _(a=a):
+            made_ref[pl.ds((a + 1) * slab - spots + sz.rows - 1, sz.elems, stride=sz.rows), :] = blank
+
+        if a % group == group - 1:
+            rows = pl.ds((a + 1 - group) * slab, group * slab)
+            copies.append(pltpu.make_async_copy(made_ref.at[rows], out_ref.at[rows], left.at[len(copies)]))
+            copies[-1].start()
+    for copy in copies:
+        copy.wait()
+
+
+def call(kernel, shapes, operands, scratch=(), spaces=pltpu.VMEM, limit=16, flops=10**9, out_space=pltpu.VMEM):
     if not isinstance(spaces, list):
         spaces = [spaces] * len(operands)
     made = pl.pallas_call(
         kernel,
         out_shape=[jax.ShapeDtypeStruct(shape, jnp.float32) for shape in shapes],
         in_specs=[pl.BlockSpec(memory_space=space) for space in spaces],
-        out_specs=[pl.BlockSpec(memory_space=pltpu.VMEM) for _ in shapes],
+        out_specs=[pl.BlockSpec(memory_space=out_space) for _ in shapes],
         scratch_shapes=[pltpu.VMEM(each, jnp.float32) if isinstance(each, tuple) else each for each in scratch],
         compiler_params=pltpu.CompilerParams(vmem_limit_bytes=limit * 2**20),
         cost_estimate=pl.CostEstimate(flops=flops, bytes_accessed=10**6, transcendentals=0),
@@ -660,7 +667,8 @@
         functools.partial(spread_kernel, sz),
         [(flat, LANES)],
         solved,
-        [(sz.columns, sz.lane_nodes), (sz.lane_nodes, LANES)],
+        [(sz.columns, sz.lane_nodes), (sz.lane_nodes, LANES), (flat, LANES), pltpu.SemaphoreType.DMA((sz.nodes,))],
+        out_space=pltpu.HBM,
     )
     return out.reshape(sz.nodes, sz.nodes, sz.elems, sz.rows, sz.columns)
 

time: 57.9 us -> 57.9 us (level)
  no operation moved by 1% of the time
where the time goes in v14:
time: 57.9 us; the launch traced here: 57.8 us
  blocking collectives  20.5 us (35%)
  waiting for transfers between devices  13.9 us (24%)
  starting transfers between devices  12 us (21%)
  Pallas kernels  11.2 us (19%)
    all_to_all x1, blocking collectives, on_device(): lax.all_to_all(spectra, ('mode', 'ex', 'ey'), split_axis=0, concat_axis=0...  20.5 us
    pallas_call x4, Pallas kernels, call(): pl.pallas_call(kernel, out_shape=[jax.ShapeDtypeStruct(shape, jnp.float32...  11.2 us
    ppermute x3, waiting for transfers between devices, on_device(): weak[cut][step] = lax.ppermute(weak[cut][step], 'mode', pairs)  10 us
    ppermute x7, starting transfers between devices, on_device(): solved[step] = lax.ppermute(solved[step], ('ex', 'ey'), pairs)  6.31 us
    ppermute x3, starting transfers between devices, on_device(): weak[cut][step] = lax.ppermute(weak[cut][step], 'mode', pairs)  5.69 us
    ppermute x7, waiting for transfers between devices, on_device(): solved[step] = lax.ppermute(solved[step], ('ex', 'ey'), pairs)  3.86 us
  transfers between devices with their start and end apart: 10, of which 6 were waited for; matrix products, arithmetic and copies ran while one was open for 0% of the time, Pallas kernels for 0%

profile of v14, /device:TPU:0, one launch (start us, length us, event | category | flops | bytes accessed | tf_op | source)
XLA Modules:
  0.0 57.8 jit_solution(11954251393430382752)
XLA Ops:
  0.0 4.0 %shard_map.127 = (f32[248,128]{1,0:T(8,128)S(1)}, f32[248,128]{1,0:T(8,128)S(1)}, f32[248,128]{1,0:T(8,128)S(1)}, f32[248,128]{1,0:T(8,128)S(1)}) custom-call(f32[1152,64]{1,0:T(8,128)} %bitcast.5, f32[1152,64]{1,0:T(8,128)} %bitcast.6, bf16[1008,432]{1,0:T(8,128)(2,1)} %constant.22.clone.lift_hbm, bf16[2,528,672]{2,1,0:T(8,128)(2,1)} %constant.23.clone.back_hbm), custom_call_target="tpu_custom_call" | custom-call | flops 1000000000 | bytes 1000000 | tf_op jit(solution)/shard_map/pallas_call | solution.py:595
  4.0 3.1 %collective-permute-start = (f32[248,128]{1,0:T(8,128)S(1)}, f32[248,128]{1,0:T(8,128)S(1)}, u32[]{:S(2)}, u32[]{:S(2)}) collective-permute-start(f32[248,128]{1,0:T(8,128)S(1)} %get-tuple-element.18), channel_id=1, source_target_pairs={{0,8},{8,0},{16,24},{24,16},{1,9},{9,1},{17,25},{25,17},{2,10},{10... | collective-permute-start | bytes 380936 | tf_op jit(solution)/shard_map/ppermute | solution.py:637
  7.1 2.6 %collective-permute-start.1 = (f32[248,128]{1,0:T(8,128)S(1)}, f32[248,128]{1,0:T(8,128)S(1)}, u32[]{:S(2)}, u32[]{:S(2)}) collective-permute-start(f32[248,128]{1,0:T(8,128)S(1)} %get-tuple-element.19), channel_id=1, source_target_pairs={{0,16},{8,24},{16,0},{24,8},{1,17},{9,25},{17,1},{25,9},{2,18},{10... | collective-permute-start | bytes 380936 | tf_op jit(solution)/shard_map/ppermute | solution.py:637
  9.7 2.2 %collective-permute-done.refs_1_ = f32[248,128]{1,0:T(8,128)S(1)} collective-permute-done((f32[248,128]{1,0:T(8,128)S(1)}, f32[248,128]{1,0:T(8,128)S(1)}, u32[]{:S(2)}, u32[]{:S(2)}) %collective-permute-start) | collective-permute-done | bytes 127008 | tf_op jit(solution)/shard_map/ppermute | solution.py:637
  12.0 7.8 %collective-permute-done.1.refs_2_ = f32[248,128]{1,0:T(8,128)S(1)} collective-permute-done((f32[248,128]{1,0:T(8,128)S(1)}, f32[248,128]{1,0:T(8,128)S(1)}, u32[]{:S(2)}, u32[]{:S(2)}) %collective-permute-start.1) | collective-permute-done | bytes 127008 | tf_op jit(solution)/shard_map/ppermute | solution.py:637
  19.8 0.0 copy-start.2
  19.8 0.0 copy-start.3
  19.8 0.0 copy-start.4
  19.8 0.0 copy-start.6
  19.9 0.6 %shard_map.128 = f32[512,256]{1,0:T(8,128)S(1)} custom-call(f32[248,128]{1,0:T(8,128)S(1)} %get-tuple-element.17.refs_0_, f32[248,128]{1,0:T(8,128)S(1)} %collective-permute-done.refs_1_, f32[248,128]{1,0:T(8,128)S(1)} %collective-permute-done.1.refs_2_, f32[248,128]{1,0:T(8,128)S(1)} %collective-permute-done.2.refs_3_, bf16[2,256,256]{2,1,0:T(8,128)(2,1)S(1)} %copy-done.1), custom_call_target="tpu_custom_call" | custom-call | flops 99999997952 | bytes 1000000 | tf_op jit(solution)/shard_map/pallas_call | solution.py:595
  20.5 20.5 %all_to_all.5.refs_0_ = f32[32,16,256]{2,1,0:T(8,128)S(1)} all-to-all(f32[32,16,256]{2,1,0:T(8,128)S(1)} %bitcast.4), channel_id=1, replica_groups=mesh['mode'=4,'ex'=4,'ey'=2] {'mode','ex','ey'}, dimensions={0} | all-to-all | bytes 1048576 | tf_op jit(solution)/shard_map/all_to_all | solution.py:649
  41.1 5.3 %shard_map.129 = (f32[16,1024]{1,0:T(8,128)S(1)}, f32[16,1024]{1,0:T(8,128)S(1)}, f32[16,1024]{1,0:T(8,128)S(1)}, f32[16,1024]{1,0:T(8,128)S(1)}, f32[16,1024]{1...) custom-call(f32[32,16,256]{2,1,0:T(8,128)S(1)} %all_to_all.5.refs_0_, ...), custom_call_target="tpu_custom_call" | custom-call | flops 1000000000 | bytes 1000000 | tf_op jit(solution)/shard_map/pallas_call | solution.py:595
  46.4 0.1 collective-permute-start.3
  46.5 1.3 %collective-permute-start.4 = (f32[16,1024]{1,0:T(8,128)S(1)}, f32[16,1024]{1,0:T(8,128)S(1)}, u32[]{:S(2)}, u32[]{:S(2)}) collective-permute-start(f32[16,1024]{1,0:T(8,128)S(1)} %get-tuple-element.23), channel_id=1, source_target_pairs={{0,2},{1,3},{2,4},{3,5},{4,6},{5,7},{6,0},{7,1},{8,10},{9,11},{10,... | collective-permute-start | bytes 196616 | tf_op jit(solution)/shard_map/ppermute | solution.py:665
  47.8 1.2 %collective-permute-start.5 = (f32[16,1024]{1,0:T(8,128)S(1)}, f32[16,1024]{1,0:T(8,128)S(1)}, u32[]{:S(2)}, u32[]{:S(2)}) collective-permute-start(f32[16,1024]{1,0:T(8,128)S(1)} %get-tuple-element.24), channel_id=1, source_target_pairs={{0,3},{1,2},{2,5},{3,4},{4,7},{5,6},{6,1},{7,0},{8,11},{9,10},{10,... | collective-permute-start | bytes 196616 | tf_op jit(solution)/shard_map/ppermute | solution.py:665
  49.0 0.8 %collective-permute-start.6 = (f32[16,1024]{1,0:T(8,128)S(1)}, f32[16,1024]{1,0:T(8,128)S(1)}, u32[]{:S(2)}, u32[]{:S(2)}) collective-permute-start(f32[16,1024]{1,0:T(8,128)S(1)} %get-tuple-element.25), channel_id=1, source_target_pairs={{0,4},{1,5},{2,6},{3,7},{4,0},{5,1},{6,2},{7,3},{8,12},{9,13},{10,... | collective-permute-start | bytes 196616 | tf_op jit(solution)/shard_map/ppermute | solution.py:665
  49.8 0.9 %collective-permute-start.7 = (f32[16,1024]{1,0:T(8,128)S(1)}, f32[16,1024]{1,0:T(8,128)S(1)}, u32[]{:S(2)}, u32[]{:S(2)}) collective-permute-start(f32[16,1024]{1,0:T(8,128)S(1)} %get-tuple-element.26), channel_id=1, source_target_pairs={{0,5},{1,4},{2,7},{3,6},{4,1},{5,0},{6,3},{7,2},{8,13},{9,12},{10,... | collective-permute-start | bytes 196616 | tf_op jit(solution)/shard_map/ppermute | solution.py:665
  50.7 1.5 %collective-permute-start.8 = (f32[16,1024]{1,0:T(8,128)S(1)}, f32[16,1024]{1,0:T(8,128)S(1)}, u32[]{:S(2)}, u32[]{:S(2)}) collective-permute-start(f32[16,1024]{1,0:T(8,128)S(1)} %get-tuple-element.27), channel_id=1, source_target_pairs={{0,6},{1,7},{2,0},{3,1},{4,2},{5,3},{6,4},{7,5},{8,14},{9,15},{10,... | collective-permute-start | bytes 196616 | tf_op jit(solution)/shard_map/ppermute | solution.py:665
  52.2 0.5 collective-permute-start.9
  52.7 0.4 collective-permute-done.5.refs_3_
  53.1 1.6 %collective-permute-done.6.refs_4_ = f32[16,1024]{1,0:T(8,128)S(1)} collective-permute-done((f32[16,1024]{1,0:T(8,128)S(1)}, f32[16,1024]{1,0:T(8,128)S(1)}, u32[]{:S(2)}, u32[]{:S(2)}) %collective-permute-start.6) | collective-permute-done | bytes 65568 | tf_op jit(solution)/shard_map/ppermute | solution.py:665
  54.7 1.3 %collective-permute-done.7.refs_5_ = f32[16,1024]{1,0:T(8,128)S(1)} collective-permute-done((f32[16,1024]{1,0:T(8,128)S(1)}, f32[16,1024]{1,0:T(8,128)S(1)}, u32[]{:S(2)}, u32[]{:S(2)}) %collective-permute-start.7) | collective-permute-done | bytes 65568 | tf_op jit(solution)/shard_map/ppermute | solution.py:665
  56.0 0.6 collective-permute-done.9.refs_7_
  56.6 1.2 %shard_map.130 = f32[1152,128]{1,0:T(8,128)} custom-call(f32[16,1024]{1,0:T(8,128)S(1)} %get-tuple-element.21.refs_0_, f32[16,1024]{1,0:T(8,128)S(1)} %collective-permute-done.3.refs_1_, f32[16,1024]{1,0:T(8,128)S(1)} %collective-permute-done.4.refs_2_, f32[16,1024]{1,0:T(8,128)S(1)} %collective-permute-done.5.refs_3_, ...), custom_call_target="tpu_custom_call" | custom-call | flops 1000000000 | bytes 1000000 | tf_op jit(solution)/shard_map/pallas_call | solution.py:595
  (19 shorter events, 0.0 us)
Async XLA Ops:
  0.0 19.8 %copy-start.1 = (bf16[2,256,256]{2,1,0:T(8,128)(2,1)S(1)}, bf16[2,256,256]{2,1,0:T(8,128)(2,1)}, u32[]{:S(2)}) copy-start(bf16[2,256,256]{2,1,0:T(8,128)(2,1)} %constant.24.clone.refs_4_) | copy-start | bytes 786436
  4.0 7.9 %collective-permute-start = (f32[248,128]{1,0:T(8,128)S(1)}, f32[248,128]{1,0:T(8,128)S(1)}, u32[]{:S(2)}, u32[]{:S(2)}) collective-permute-start(f32[248,128]{1,0:T(8,128)S(1)} %get-tuple-element.18), channel_id=1, source_target_pairs={{0,8},{8,0},{16,24},{24,16},{1,9},{9,1},{17,25},{25,17},{2,10},{10... | collective-permute-start | bytes 380936 | tf_op jit(solution)/shard_map/ppermute | solution.py:637
  7.1 12.6 %collective-permute-start.1 = (f32[248,128]{1,0:T(8,128)S(1)}, f32[248,128]{1,0:T(8,128)S(1)}, u32[]{:S(2)}, u32[]{:S(2)}) collective-permute-start(f32[248,128]{1,0:T(8,128)S(1)} %get-tuple-element.19), channel_id=1, source_target_pairs={{0,16},{8,24},{16,0},{24,8},{1,17},{9,25},{17,1},{25,9},{2,18},{10... | collective-permute-start | bytes 380936 | tf_op jit(solution)/shard_map/ppermute | solution.py:637
  9.7 10.0 %collective-permute-start.2 = (f32[248,128]{1,0:T(8,128)S(1)}, f32[248,128]{1,0:T(8,128)S(1)}, u32[]{:S(2)}, u32[]{:S(2)}) collective-permute-start(f32[248,128]{1,0:T(8,128)S(1)} %get-tuple-element.20), channel_id=1, source_target_pairs={{0,24},{8,16},{16,8},{24,0},{1,25},{9,17},{17,9},{25,1},{2,26},{10... | collective-permute-start | bytes 380936 | tf_op jit(solution)/shard_map/ppermute | solution.py:637
  19.8 21.3 %copy-start = (bf16[448,448]{1,0:T(8,128)(2,1)S(1)}, bf16[448,448]{1,0:T(8,128)(2,1)}, u32[]{:S(2)}) copy-start(bf16[448,448]{1,0:T(8,128)(2,1)} %constant.28.clone.refs_4_) | copy-start | bytes 1204228
  19.8 21.2 %copy-start.2 = (bf16[448,192]{1,0:T(8,128)(2,1)S(1)}, bf16[448,192]{1,0:T(8,128)(2,1)}, u32[]{:S(2)}) copy-start(bf16[448,192]{1,0:T(8,128)(2,1)} %constant.26.clone.refs_2_) | copy-start | bytes 516100
  19.8 21.2 %copy-start.3 = (bf16[384,224]{1,0:T(8,128)(2,1)S(1)}, bf16[384,224]{1,0:T(8,128)(2,1)}, u32[]{:S(2)}) copy-start(bf16[384,224]{1,0:T(8,128)(2,1)} %constant.30.clone.refs_6_) | copy-start | bytes 516100
  19.8 21.2 %copy-start.4 = (bf16[384,256]{1,0:T(8,128)(2,1)S(1)}, bf16[384,256]{1,0:T(8,128)(2,1)}, u32[]{:S(2)}) copy-start(bf16[384,256]{1,0:T(8,128)(2,1)} %constant.27.clone.refs_3_) | copy-start | bytes 589828
  19.8 21.2 %copy-start.5 = (bf16[256,256]{1,0:T(8,128)(2,1)S(1)}, bf16[256,256]{1,0:T(8,128)(2,1)}, u32[]{:S(2)}) copy-start(bf16[256,256]{1,0:T(8,128)(2,1)} %constant.29.clone.refs_5_) | copy-start | bytes 393220
  19.8 21.2 %copy-start.6 = (bf16[256,256]{1,0:T(8,128)(2,1)S(1)}, bf16[256,256]{1,0:T(8,128)(2,1)}, u32[]{:S(2)}) copy-start(bf16[256,256]{1,0:T(8,128)(2,1)} %constant.25.clone.refs_1_) | copy-start | bytes 393220
  19.8 21.2 %copy-start.7 = (f32[224,128]{1,0:T(8,128)S(1)}, f32[224,128]{1,0:T(8,128)}, u32[]{:S(2)}) copy-start(f32[224,128]{1,0:T(8,128)} %constant.31.clone.refs_7_) | copy-start | bytes 344068
  19.8 21.2 %copy-start.8 = (f32[1,128]{1,0:T(1,128)S(1)}, f32[1,128]{1,0:T(1,128)}, u32[]{:S(2)}) copy-start(f32[1,128]{1,0:T(1,128)} %constant.32.clone.refs_8_) | copy-start | bytes 1540
  46.4 4.3 %collective-permute-start.3 = (f32[16,1024]{1,0:T(8,128)S(1)}, f32[16,1024]{1,0:T(8,128)S(1)}, u32[]{:S(2)}, u32[]{:S(2)}) collective-permute-start(f32[16,1024]{1,0:T(8,128)S(1)} %get-tuple-element.22), channel_id=1, source_target_pairs={{0,1},{1,0},{2,3},{3,2},{4,5},{5,4},{6,7},{7,6},{8,9},{9,8},{10,11... | collective-permute-start | bytes 196616 | tf_op jit(solution)/shard_map/ppermute | solution.py:665
  46.5 5.7 %collective-permute-start.4 = (f32[16,1024]{1,0:T(8,128)S(1)}, f32[16,1024]{1,0:T(8,128)S(1)}, u32[]{:S(2)}, u32[]{:S(2)}) collective-permute-start(f32[16,1024]{1,0:T(8,128)S(1)} %get-tuple-element.23), channel_id=1, source_target_pairs={{0,2},{1,3},{2,4},{3,5},{4,6},{5,7},{6,0},{7,1},{8,10},{9,11},{10,... | collective-permute-start | bytes 196616 | tf_op jit(solution)/shard_map/ppermute | solution.py:665
  47.8 5.3 %collective-permute-start.5 = (f32[16,1024]{1,0:T(8,128)S(1)}, f32[16,1024]{1,0:T(8,128)S(1)}, u32[]{:S(2)}, u32[]{:S(2)}) collective-permute-start(f32[16,1024]{1,0:T(8,128)S(1)} %get-tuple-element.24), channel_id=1, source_target_pairs={{0,3},{1,2},{2,5},{3,4},{4,7},{5,6},{6,1},{7,0},{8,11},{9,10},{10,... | collective-permute-start | bytes 196616 | tf_op jit(solution)/shard_map/ppermute | solution.py:665
  49.0 5.7 %collective-permute-start.6 = (f32[16,1024]{1,0:T(8,128)S(1)}, f32[16,1024]{1,0:T(8,128)S(1)}, u32[]{:S(2)}, u32[]{:S(2)}) collective-permute-start(f32[16,1024]{1,0:T(8,128)S(1)} %get-tuple-element.25), channel_id=1, source_target_pairs={{0,4},{1,5},{2,6},{3,7},{4,0},{5,1},{6,2},{7,3},{8,12},{9,13},{10,... | collective-permute-start | bytes 196616 | tf_op jit(solution)/shard_map/ppermute | solution.py:665
  49.8 6.2 %collective-permute-start.7 = (f32[16,1024]{1,0:T(8,128)S(1)}, f32[16,1024]{1,0:T(8,128)S(1)}, u32[]{:S(2)}, u32[]{:S(2)}) collective-permute-start(f32[16,1024]{1,0:T(8,128)S(1)} %get-tuple-element.26), channel_id=1, source_target_pairs={{0,5},{1,4},{2,7},{3,6},{4,1},{5,0},{6,3},{7,2},{8,13},{9,12},{10,... | collective-permute-start | bytes 196616 | tf_op jit(solution)/shard_map/ppermute | solution.py:665
  50.7 5.3 %collective-permute-start.8 = (f32[16,1024]{1,0:T(8,128)S(1)}, f32[16,1024]{1,0:T(8,128)S(1)}, u32[]{:S(2)}, u32[]{:S(2)}) collective-permute-start(f32[16,1024]{1,0:T(8,128)S(1)} %get-tuple-element.27), channel_id=1, source_target_pairs={{0,6},{1,7},{2,0},{3,1},{4,2},{5,3},{6,4},{7,5},{8,14},{9,15},{10,... | collective-permute-start | bytes 196616 | tf_op jit(solution)/shard_map/ppermute | solution.py:665
  52.2 4.4 %collective-permute-start.9 = (f32[16,1024]{1,0:T(8,128)S(1)}, f32[16,1024]{1,0:T(8,128)S(1)}, u32[]{:S(2)}, u32[]{:S(2)}) collective-permute-start(f32[16,1024]{1,0:T(8,128)S(1)} %get-tuple-element.28), channel_id=1, source_target_pairs={{0,7},{1,6},{2,1},{3,0},{4,3},{5,2},{6,5},{7,4},{8,15},{9,14},{10,... | collective-permute-start | bytes 196616 | tf_op jit(solution)/shard_map/ppermute | solution.py:665
